TPU v7x, 32 devices: a whole 2x2x4 slice. The times are simulated.
32 devices in a mesh: groups: 2 (over x), expert: 16 (over z, y, core).
Axes of the slice: x: 2, y: 2, z: 4, core: 2. Of those that a mesh axis runs over, the one named last changes fastest.
Arguments:
- tokens: bfloat16 [2048, 7168], P(('groups', 'expert')), parts along dimension 0, may hold values from -6 to 6
- expert_ids: int32 [2048, 8], P(('groups', 'expert')), parts along dimension 0, may hold values from 0 to 255, as said below
- route_logits: float32 [2048, 8], P(('groups', 'expert')), parts along dimension 0, may hold values from -6 to 6
- w_gate: bfloat16 [7168, 4096], P(None, 'expert'), may hold values from -0.0625 to 0.0625
- w_up: bfloat16 [7168, 4096], P(None, 'expert'), may hold values from -0.0625 to 0.0625
- w_down: bfloat16 [4096, 7168], P('expert'), may hold values from -0.125 to 0.125
Outputs:
- blended: bfloat16 [2048, 7168], P(('groups', 'expert')), parts along dimension 0
There are 2 independent parts, one for each index of `groups`. A program takes and returns all parts, laid end to end along the dimension named above; an argument that names none is the same for every part. Nothing has to cross between parts.
Inputs may be any that keep to these rules, and one draw needn't show every extreme that they name: `expert_ids`: each row names 8 different experts. Within the rows of one device (aligned blocks of 64 rows) no expert is named by more than 5 rows, and one and the same expert below 2 is named by exactly 5 rows in every block.
All inputs are finite; a program needn't handle non-finite values.
Results may differ from a plain program's by a relative error of at most 0.0049.
Values may be sent and summed in bfloat16 or wider, within the bound.
No kernel may reach another device: no remote copies, remote signals or barrier semaphores. Data moves between devices by JAX's collectives and lax.ppermute only.
A program may use at most 128 MiB of HBM per device.

v0:
```python
import jax
import jax.numpy as jnp
from jax import lax
from jax.sharding import PartitionSpec as P

SPLIT = 8
CAP = 5


route_scale = 2.5


def route_tables(expert_ids, route_logits, in_flight, capacity):
    count_of_rows, pick_count = expert_ids.shape
    flat_ids = expert_ids.reshape(count_of_rows * pick_count)
    labels = jnp.arange(in_flight, dtype=jnp.int32)
    hit_table = (flat_ids[:, None] == labels[None, :]).astype(jnp.int32)
    earlier = jnp.cumsum(hit_table, axis=0) - hit_table
    slot_index = jnp.sum(earlier * hit_table, axis=1)
    live_mask = jnp.sum(hit_table, axis=1)
    target = jnp.sum(hit_table * labels[None, :], axis=1)
    column = jnp.where(live_mask > 0, target * capacity + slot_index, -1)
    positions = jnp.arange(in_flight * capacity, dtype=jnp.int32)
    pick_place = (column[:, None] == positions[None, :]).reshape(
        count_of_rows, pick_count, in_flight * capacity
    )
    lifted = jax.nn.sigmoid(route_logits)
    gate_values = route_scale * lifted / jnp.sum(lifted, axis=1, keepdims=True)
    expert_weight = jnp.sum(pick_place.astype(gate_values.dtype) * gate_values[:, :, None], axis=1)
    device_assignment = jnp.transpose(jnp.sum(pick_place.astype(jnp.int32), axis=1)).astype(
        jnp.bfloat16
    )
    return (device_assignment, expert_weight)


def expert_rows(rows_in, gate_cols, up_cols, down_rows):
    gate_act = jnp.dot(rows_in, gate_cols, preferred_element_type=jnp.float32)
    up_act = jnp.dot(rows_in, up_cols, preferred_element_type=jnp.float32)
    hidden = (jax.nn.silu(gate_act) * up_act).astype(jnp.bfloat16)
    return jnp.dot(hidden, down_rows, preferred_element_type=jnp.float32)


def body(tokens, expert_ids, route_logits, w_gate, w_up, w_down):
    devices = lax.axis_size("expert")
    in_flight = devices // SPLIT
    features = tokens.shape[1]
    device_assignment, expert_weight = route_tables(expert_ids, route_logits, in_flight, CAP)
    buffer = jnp.dot(device_assignment, tokens, preferred_element_type=jnp.float32).astype(
        jnp.bfloat16
    )
    buffer = buffer.reshape(in_flight, CAP, features)
    outbound = jnp.broadcast_to(buffer[:, None], (in_flight, SPLIT, CAP, features)).reshape(
        devices, CAP, features
    )
    received = lax.all_to_all(outbound, "expert", split_axis=0, concat_axis=0, tiled=True)
    slot_count = received.shape[1]
    produced = expert_rows(received.reshape(devices * slot_count, features), w_gate, w_up, w_down)
    returned = lax.all_to_all(
        produced.reshape(devices, slot_count, features),
        "expert",
        split_axis=0,
        concat_axis=0,
        tiled=True,
    )
    summed = jnp.sum(returned.reshape(in_flight, SPLIT, CAP, features), axis=1)
    blended = jnp.dot(
        expert_weight,
        summed.reshape(in_flight * CAP, features),
        precision=lax.Precision.HIGHEST,
        preferred_element_type=jnp.float32,
    )
    return blended.astype(jnp.bfloat16)


def solution(mesh):
    placed = (
        P(("groups", "expert"), None),
        P(("groups", "expert"), None),
        P(("groups", "expert"), None),
        P(None, "expert"),
        P(None, "expert"),
        P("expert", None),
    )
    return jax.shard_map(
        body, mesh=mesh, in_specs=placed, out_specs=P(("groups", "expert"), None), check_vma=False
    )
```

profile of v0, /device:TPU:13, one launch (start us, length us, event | category | flops | bytes accessed | tf_op | source)
XLA Modules:
  0.0 157.2 jit_solution(1786096589378637928)
XLA Ops:
  0.0 0.0 copy-start
  0.0 0.9 copy.11
  0.9 0.1 eq.46
  0.9 0.1 eq.41
  1.0 0.6 reduce-window.6
  1.7 0.2 slice_reduce_fusion
  1.9 0.2 reduce-window.9
  2.1 0.1 add_bitcast_fusion
  2.2 0.1 select_n.12
  2.3 0.1 copy.13
  2.4 0.0 copy-done
  2.4 0.2 convolution_convert_fusion.1
  2.6 0.1 broadcast_in_dim.9
  2.7 0.2 broadcast_in_dim.10
  2.9 48.1 %all_to_all.10 = bf16[16,5,7168]{2,1,0:T(8,128)(2,1)} all-to-all(bf16[16,5,7168]{2,1,0:T(8,128)(2,1)S(1)} %bitcast.22), channel_id=1, replica_groups=mesh['groups'=2,'expert'=16] {'expert'}, dimensions={0} | all-to-all | bytes 2293760 | tf_op jit(solution)/shard_map/all_to_all | solution.py:55
  51.0 1.7 %reshape.66 = bf16[80,7168]{1,0:T(8,128)(2,1)S(1)} reshape(bf16[16,5,7168]{2,1,0:T(8,128)(2,1)} %all_to_all.10) | data formatting | bytes 2293760 | tf_op jit(solution)/shard_map/reshape | solution.py:57
  52.8 2.8 %fusion.14 = f32[80,256]{1,0:T(8,128)S(1)} fusion(bf16[80,7168]{1,0:T(8,128)(2,1)S(1)} %reshape.66, bf16[7168,256]{1,0:T(8,128)(2,1)} %param.9), kind=kOutput, calls=%fused_computation.32 | convolution fusion | flops 293601280 | bytes 4898816 | tf_op jit(solution)/shard_map/dot_general | solution.py:37
  55.6 6.7 %fusion.1 = f32[80,7168]{1,0:T(8,128)} fusion(bf16[256,7168]{1,0:T(8,128)(2,1)} %param.11, bf16[80,7168]{1,0:T(8,128)(2,1)S(1)} %reshape.66, bf16[7168,256]{1,0:T(8,128)(2,1)} %param.10, f32[80,256]{1,0:T(8,128)S(1)} %fusion.14), kind=kOutput, calls=%fused_computation.5 | convolution fusion | flops 587325440 | bytes 10862592 | tf_op jit(solution)/shard_map/dot_general | solution.py:40
  62.3 3.2 %reshape.67 = f32[16,5,7168]{2,1,0:T(8,128)} reshape(f32[80,7168]{1,0:T(8,128)} %fusion.1) | data formatting | bytes 4587520 | tf_op jit(solution)/shard_map/reshape | solution.py:59
  65.5 0.0 copy-start.1
  65.5 5.6 %all-to-all-start.1 = ((f32[16,5,7168]{2,1,0:T(8,128)}), f32[16,5,7168]{2,1,0:T(8,128)}, u32[]{:S(2)}, u32[]{:S(2)}) async-start(f32[16,5,7168]{2,1,0:T(8,128)} %reshape.67), calls=%async_computation.1 | async-start | bytes 7340032 | tf_op jit(solution)/shard_map/all_to_all | solution.py:58
  71.1 0.0 copy-done.1
  71.2 81.2 %all-to-all-done.1 = f32[16,5,7168]{2,1,0:T(8,128)} async-done(((f32[16,5,7168]{2,1,0:T(8,128)}), f32[16,5,7168]{2,1,0:T(8,128)}, u32[]{:S(2)}, u32[]{:S(2)}) %all-to-all-start.1) | async-done | bytes 2293792 | tf_op jit(solution)/shard_map/all_to_all | solution.py:58
  152.3 2.3 %bitcast_reduce_fusion = f32[2,5,7168]{2,1,0:T(8,128)S(1)} fusion(f32[16,5,7168]{2,1,0:T(8,128)} %all-to-all-done.1), kind=kLoop, calls=%fused_computation.2 | loop fusion | flops 501760 | bytes 2580480 | tf_op jit(solution)/shard_map/reduce_sum | solution.py:65
  154.6 0.1 reshape.69
  154.7 2.6 %convolution_convert_fusion = bf16[64,7168]{1,0:T(8,128)(2,1)} fusion(f32[64,10]{0,1:T(8,128)S(1)} %select_reduce_fusion, f32[10,7168]{1,0:T(8,128)S(1)} %reshape.69), kind=kOutput, calls=%fused_computation | convolution fusion | flops 55508992 | bytes 1206784 | tf_op jit(solution)/shard_map/dot_general | solution.py:66
  (7 shorter events, 0.2 us)
Async XLA Ops:
  0.0 2.4 %copy-start = (bf16[64,7168]{1,0:T(8,128)(2,1)S(1)}, bf16[64,7168]{1,0:T(8,128)(2,1)}, u32[]{:S(2)}) copy-start(bf16[64,7168]{1,0:T(8,128)(2,1)} %param.6) | copy-start | bytes 2752516
  65.5 5.6 %copy-start.1 = (f32[64,8]{0,1:T(8,128)S(1)}, f32[64,8]{0,1:T(8,128)}, u32[]{:S(2)}) copy-start(f32[64,8]{0,1:T(8,128)} %param.8) | copy-start | bytes 6148
  65.5 86.8 %all-to-all-start.1 = ((f32[16,5,7168]{2,1,0:T(8,128)}), f32[16,5,7168]{2,1,0:T(8,128)}, u32[]{:S(2)}, u32[]{:S(2)}) async-start(f32[16,5,7168]{2,1,0:T(8,128)} %reshape.67), calls=%async_computation.1 | async-start | bytes 7340032 | tf_op jit(solution)/shard_map/all_to_all | solution.py:58
where the time goes:
time: 158 us; the launch traced here: 157 us
  waiting for transfers between devices  81.2 us (51%)
  blocking collectives  48.1 us (30%)
  matrix products  12.3 us (8%)
  local copies, waits for them, and re-layouts  6.65 us (4%)
  starting transfers between devices  5.57 us (4%)
  other arithmetic  3.3 us (2%)
    all_to_all x1, waiting for transfers between devices, body(): lax.all_to_all(produced.reshape(devices, slot_count, features), 'expert',...  81.2 us
    all_to_all x1, blocking collectives, body(): lax.all_to_all(outbound, 'expert', split_axis=0, concat_axis=0, tiled=True)  48.1 us
    dot_general x1, matrix products, expert_rows(): return jnp.dot(hidden, down_rows, preferred_element_type=jnp.float32)  6.7 us
    all_to_all x1, starting transfers between devices, body(): lax.all_to_all(produced.reshape(devices, slot_count, features), 'expert',...  5.57 us
    reshape x1, local copies, waits for them, and re-layouts, body(): produced.reshape(devices, slot_count, features)  3.23 us
  transfers between devices with their start and end apart: 1, of which 1 were waited for; matrix products, arithmetic and copies ran while one was open for 0% of the time, Pallas kernels for 0%

commit v1 on v0

--- a/solution.py
+++ b/solution.py
@@ -40,32 +40,45 @@
     return jnp.dot(hidden, down_rows, preferred_element_type=jnp.float32)
 
 
+def swap_teams(blocks, teams):
+    got = [blocks[0]]
+    count = teams * SPLIT
+    for k in range(1, teams):
+        pairs = [(i, (i + k * SPLIT) % count) for i in range(count)]
+        got.append(lax.ppermute(blocks[k], "expert", pairs))
+    return got
+
+
 def body(tokens, expert_ids, route_logits, w_gate, w_up, w_down):
     devices = lax.axis_size("expert")
-    in_flight = devices // SPLIT
+    teams = devices // SPLIT
+    mine = lax.axis_index("expert") // SPLIT
     features = tokens.shape[1]
-    device_assignment, expert_weight = route_tables(expert_ids, route_logits, in_flight, CAP)
-    buffer = jnp.dot(device_assignment, tokens, preferred_element_type=jnp.float32).astype(
-        jnp.bfloat16
+    groups = [[t * SPLIT + p for p in range(SPLIT)] for t in range(teams)]
+    device_assignment, expert_weight = route_tables(expert_ids, route_logits, teams, CAP)
+    assignment = jnp.roll(device_assignment.reshape(teams, CAP, -1), -mine, axis=0)
+    weight = jnp.roll(expert_weight.reshape(-1, teams, CAP), -mine, axis=1)
+    sent = [
+        jnp.dot(assignment[k], tokens, preferred_element_type=jnp.float32).astype(jnp.bfloat16)
+        for k in range(teams)
+    ]
+    got = swap_teams(sent, teams)
+    rows = lax.all_gather(
+        jnp.concatenate(got, axis=0), "expert", axis_index_groups=groups, tiled=True
     )
-    buffer = buffer.reshape(in_flight, CAP, features)
-    outbound = jnp.broadcast_to(buffer[:, None], (in_flight, SPLIT, CAP, features)).reshape(
-        devices, CAP, features
+    produced = expert_rows(rows, w_gate, w_up, w_down)
+    mixed = lax.psum_scatter(
+        produced, "expert", scatter_dimension=0, axis_index_groups=groups, tiled=True
     )
-    received = lax.all_to_all(outbound, "expert", split_axis=0, concat_axis=0, tiled=True)
-    slot_count = received.shape[1]
-    produced = expert_rows(received.reshape(devices * slot_count, features), w_gate, w_up, w_down)
-    returned = lax.all_to_all(
-        produced.reshape(devices, slot_count, features),
-        "expert",
-        split_axis=0,
-        concat_axis=0,
-        tiled=True,
-    )
-    summed = jnp.sum(returned.reshape(in_flight, SPLIT, CAP, features), axis=1)
+    mixed = mixed.reshape(teams, CAP, features)
+    count = devices
+    back = [mixed[0]]
+    for k in range(1, teams):
+        pairs = [(i, (i - k * SPLIT) % count) for i in range(count)]
+        back.append(lax.ppermute(mixed[k], "expert", pairs))
     blended = jnp.dot(
-        expert_weight,
-        summed.reshape(in_flight * CAP, features),
+        weight.reshape(-1, teams * CAP),
+        jnp.concatenate(back, axis=0),
         precision=lax.Precision.HIGHEST,
         preferred_element_type=jnp.float32,
     )

time: 158 us -> 142 us (0.90)
  the two profiles are of different devices: /device:TPU:13 before, /device:TPU:0 now
where the time goes in v1:
time: 142 us
  waiting for transfers between devices  101 us (71%)
  between operations  14.2 us (10%)
  matrix products  12.4 us (9%)
  starting transfers between devices  7.01 us (5%)
  local copies, waits for them, and re-layouts  5.52 us (4%)
  other arithmetic  1.84 us (1%)
    unnamed x3, waiting for transfers between devices  61.6 us
    all_gather x1, waiting for transfers between devices, body(): lax.all_gather(jnp.concatenate(got, axis=0), 'expert', axis_index_groups=...  22.4 us
    ppermute x1, waiting for transfers between devices, body(): back.append(lax.ppermute(mixed[k], 'expert', pairs))  11.3 us
    dot_general x1, matrix products, expert_rows(): return jnp.dot(hidden, down_rows, preferred_element_type=jnp.float32)  6.67 us
    ppermute x1, waiting for transfers between devices, swap_teams(): got.append(lax.ppermute(blocks[k], 'expert', pairs))  5.38 us
    ppermute x1, starting transfers between devices, swap_teams(): got.append(lax.ppermute(blocks[k], 'expert', pairs))  4.1 us
    unnamed x9, local copies, waits for them, and re-layouts  3.76 us
    ppermute x1, starting transfers between devices, body(): back.append(lax.ppermute(mixed[k], 'expert', pairs))  2.86 us
  transfers between devices with their start and end apart: 4, of which 4 were waited for; matrix products, arithmetic and copies ran while one was open for 1% of the time, Pallas kernels for 0%

profile of v1, /device:TPU:0, one launch (start us, length us, event | category | flops | bytes accessed | tf_op | source)
XLA Modules:
  0.0 141.7 jit_solution(13064667549135947143)
XLA Ops:
  6.5 0.0 copy-start
  6.5 0.0 all-gather.3.cloned.1.call-start
  6.5 0.9 copy.14
  7.4 0.1 eq.51
  7.5 0.1 eq.46
  7.6 0.6 reduce-window.6
  8.2 0.2 slice_reduce_fusion
  8.4 0.2 reduce-window.9
  8.6 0.1 add_bitcast_fusion
  8.7 0.1 select_n.35
  8.8 0.1 copy.16
  9.0 0.0 copy-done
  9.0 0.2 convolution_convert_fusion.1
  9.2 4.1 %collective-permute-start = (bf16[5,7168]{1,0:T(8,128)(2,1)S(1)}, bf16[5,7168]{1,0:T(8,128)(2,1)S(1)}, u32[]{:S(2)}, u32[]{:S(2)}) collective-permute-start(bf16[5,7168]{1,0:T(8,128)(2,1)S(1)} %convolution_convert_fusion.1), channel_id=1, source_target_pairs={{0,8},{1,9},{2,10},{3,11},{4,12},{5,13},{6,14},{7,15},{8,0},{9,1},... | collective-permute-start | bytes 215048 | tf_op jit(solution)/shard_map/ppermute | solution.py:48
  13.3 0.2 convolution_convert_fusion.2
  13.6 5.4 %collective-permute-done = bf16[5,7168]{1,0:T(8,128)(2,1)S(1)} collective-permute-done((bf16[5,7168]{1,0:T(8,128)(2,1)S(1)}, bf16[5,7168]{1,0:T(8,128)(2,1)S(1)}, u32[]{:S(2)}, u32[]{:S(2)}) %collective-permute-start) | collective-permute-done | bytes 71712 | tf_op jit(solution)/shard_map/ppermute | solution.py:48
  18.9 0.8 maximum_bitcast_fusion
  19.7 0.0 all-gather.3.cloned.1.call-update
  19.7 0.0 all-reduce.3.cloned.1.call-start
  19.8 22.4 %all-gather.3.cloned.1.call-done = bf16[8,10,7168]{2,1,0:T(8,128)(2,1)} async-done(((bf16[1,10,7168]{2,1,0:T(8,128)(2,1)}), bf16[8,10,7168]{2,1,0:T(8,128)(2,1)}) %all-gather.3.cloned.1.call-update) | async-done | bytes 1146896 | tf_op jit(solution)/shard_map/all_gather | solution.py:66
  42.2 1.7 %reshape.67 = bf16[80,7168]{1,0:T(8,128)(2,1)S(1)} reshape(bf16[8,10,7168]{2,1,0:T(8,128)(2,1)} %all-gather.3.cloned.1.call-done) | data formatting | bytes 2293760
  43.9 2.8 %fusion.19 = f32[80,256]{1,0:T(8,128)S(1)} fusion(bf16[80,7168]{1,0:T(8,128)(2,1)S(1)} %reshape.67, bf16[7168,256]{1,0:T(8,128)(2,1)} %param.9), kind=kOutput, calls=%fused_computation.47 | convolution fusion | flops 293601280 | bytes 4898816 | tf_op jit(solution)/shard_map/dot_general | solution.py:37
  46.7 6.7 %fusion.1 = f32[80,7168]{1,0:T(8,128)} fusion(bf16[256,7168]{1,0:T(8,128)(2,1)} %param.11, bf16[80,7168]{1,0:T(8,128)(2,1)S(1)} %reshape.67, bf16[7168,256]{1,0:T(8,128)(2,1)} %param.10, f32[80,256]{1,0:T(8,128)S(1)} %fusion.19), kind=kOutput, calls=%fused_computation.5 | convolution fusion | flops 587325440 | bytes 10862592 | tf_op jit(solution)/shard_map/dot_general | solution.py:40
  53.4 0.0 copy-start.2
  53.4 0.0 copy-start.1
  53.4 0.0 all-reduce.3.cloned.1.call-update
  53.4 0.6 copy-done.2
  54.0 0.6 dynamic-slice
  55.2 0.0 copy-done.1
  55.3 61.6 %all-reduce.3.cloned.1.call-done = f32[80,7168]{1,0:T(8,128)} async-done(((f32[80,7168]{1,0:T(8,128)}), f32[80,7168]{1,0:T(8,128)}) %all-reduce.3.cloned.1.call-update) | async-done | bytes 2293776
  116.9 1.2 constant_dynamic-slice_fusion
  118.1 2.9 %collective-permute-start.1 = (f32[5,7168]{1,0:T(8,128)S(1)}, f32[5,7168]{1,0:T(8,128)S(1)}, u32[]{:S(2)}, u32[]{:S(2)}) collective-permute-start(f32[5,7168]{1,0:T(8,128)S(1)} %get-tuple-element.9), channel_id=1, source_target_pairs={{0,8},{1,9},{2,10},{3,11},{4,12},{5,13},{6,14},{7,15},{8,0},{9,1},... | collective-permute-start | bytes 430088 | tf_op jit(solution)/shard_map/ppermute | solution.py:78
  121.0 11.3 %collective-permute-done.1 = f32[5,7168]{1,0:T(8,128)S(1)} collective-permute-done((f32[5,7168]{1,0:T(8,128)S(1)}, f32[5,7168]{1,0:T(8,128)S(1)}, u32[]{:S(2)}, u32[]{:S(2)}) %collective-permute-start.1) | collective-permute-done | bytes 143392 | tf_op jit(solution)/shard_map/ppermute | solution.py:78
  132.3 2.6 %convolution_convert_fusion = bf16[64,7168]{1,0:T(8,128)(2,1)} fusion(f32[64,10]{0,1:T(8,128)S(1)} %reshape.64, f32[5,7168]{1,0:T(8,128)S(1)} %collective-permute-done.1, f32[5,7168]{1,0:T(8,128)S(1)} %get-tuple-element.8), kind=kOutput, calls=%fused_computation | convolution fusion | flops 55580672 | bytes 1206784 | tf_op jit(solution)/shard_map/dot_general | solution.py:79
  (13 shorter events, 0.2 us)
Async XLA Ops:
  6.5 2.5 %copy-start = (bf16[64,7168]{1,0:T(8,128)(2,1)S(1)}, bf16[64,7168]{1,0:T(8,128)(2,1)}, u32[]{:S(2)}) copy-start(bf16[64,7168]{1,0:T(8,128)(2,1)} %param.6) | copy-start | bytes 2752516
  6.5 35.7 %all-gather.3.cloned.1.call-start = ((), (), s32[]{:S(2)}) async-start(), calls=%async_computation | async-start | bytes 2064384 | tf_op jit(solution)/shard_map/all_gather | solution.py:66
  9.2 9.7 %collective-permute-start = (bf16[5,7168]{1,0:T(8,128)(2,1)S(1)}, bf16[5,7168]{1,0:T(8,128)(2,1)S(1)}, u32[]{:S(2)}, u32[]{:S(2)}) collective-permute-start(bf16[5,7168]{1,0:T(8,128)(2,1)S(1)} %convolution_convert_fusion.1), channel_id=1, source_target_pairs={{0,8},{1,9},{2,10},{3,11},{4,12},{5,13},{6,14},{7,15},{8,0},{9,1},... | collective-permute-start | bytes 215048 | tf_op jit(solution)/shard_map/ppermute | solution.py:48
  19.7 97.1 %all-reduce.3.cloned.1.call-start = ((), (), s32[]{:S(2)}) async-start(), calls=%async_computation.1 | async-start | bytes 4587520
  53.4 0.7 copy-start.2
  53.4 1.9 %copy-start.1 = (f32[64,8]{0,1:T(8,128)S(1)}, f32[64,8]{0,1:T(8,128)}, u32[]{:S(2)}) copy-start(f32[64,8]{0,1:T(8,128)} %param.8) | copy-start | bytes 6148
  118.1 14.2 %collective-permute-start.1 = (f32[5,7168]{1,0:T(8,128)S(1)}, f32[5,7168]{1,0:T(8,128)S(1)}, u32[]{:S(2)}, u32[]{:S(2)}) collective-permute-start(f32[5,7168]{1,0:T(8,128)S(1)} %get-tuple-element.9), channel_id=1, source_target_pairs={{0,8},{1,9},{2,10},{3,11},{4,12},{5,13},{6,14},{7,15},{8,0},{9,1},... | collective-permute-start | bytes 430088 | tf_op jit(solution)/shard_map/ppermute | solution.py:78
Sparse Core Ops, SparseCore 0:
  19.9 22.2 all-gather.2
  53.5 63.3 all-reduce.2

commit v2 on v0

--- a/solution.py
+++ b/solution.py
@@ -40,32 +40,50 @@
     return jnp.dot(hidden, down_rows, preferred_element_type=jnp.float32)
 
 
+CORES = 2
+SEGMENTS = 8
+
+
 def body(tokens, expert_ids, route_logits, w_gate, w_up, w_down):
     devices = lax.axis_size("expert")
-    in_flight = devices // SPLIT
+    teams = devices // SPLIT
+    chips = SPLIT // CORES
     features = tokens.shape[1]
-    device_assignment, expert_weight = route_tables(expert_ids, route_logits, in_flight, CAP)
+    wide = features // SEGMENTS
+    same_core = [[i for i in range(devices) if i % CORES == c] for c in range(CORES)]
+    other_core = [(i, i + 1 - 2 * (i % CORES)) for i in range(devices)]
+    device_assignment, expert_weight = route_tables(expert_ids, route_logits, teams, CAP)
     buffer = jnp.dot(device_assignment, tokens, preferred_element_type=jnp.float32).astype(
         jnp.bfloat16
     )
-    buffer = buffer.reshape(in_flight, CAP, features)
-    outbound = jnp.broadcast_to(buffer[:, None], (in_flight, SPLIT, CAP, features)).reshape(
-        devices, CAP, features
+    packed = buffer.reshape(teams, CAP * SEGMENTS, wide)
+    outbound = jnp.broadcast_to(
+        packed[:, None], (teams, chips, CAP * SEGMENTS, wide)
+    ).reshape(teams * chips, CAP * SEGMENTS, wide)
+    here = lax.all_to_all(
+        outbound, "expert", split_axis=0, concat_axis=0, axis_index_groups=same_core, tiled=True
     )
-    received = lax.all_to_all(outbound, "expert", split_axis=0, concat_axis=0, tiled=True)
-    slot_count = received.shape[1]
-    produced = expert_rows(received.reshape(devices * slot_count, features), w_gate, w_up, w_down)
+    there = lax.ppermute(here, "expert", other_core)
+    count = teams * chips * CAP
+    rows = jnp.concatenate([here.reshape(count, features), there.reshape(count, features)], axis=0)
+    produced = expert_rows(rows, w_gate, w_up, w_down)
+    kept, given = produced[:count], produced[count:].astype(jnp.bfloat16)
+    taken = lax.ppermute(given, "expert", other_core)
+    part = (kept + taken.astype(jnp.float32)).astype(jnp.bfloat16)
     returned = lax.all_to_all(
-        produced.reshape(devices, slot_count, features),
+        part.reshape(teams * chips, CAP * SEGMENTS, wide),
         "expert",
         split_axis=0,
         concat_axis=0,
+        axis_index_groups=same_core,
         tiled=True,
     )
-    summed = jnp.sum(returned.reshape(in_flight, SPLIT, CAP, features), axis=1)
+    summed = jnp.sum(
+        returned.astype(jnp.float32).reshape(teams, chips, CAP * SEGMENTS, wide), axis=1
+    )
     blended = jnp.dot(
         expert_weight,
-        summed.reshape(in_flight * CAP, features),
+        summed.reshape(teams * CAP, features),
         precision=lax.Precision.HIGHEST,
         preferred_element_type=jnp.float32,
     )

time: 158 us -> 68 us (0.43)
  the two profiles are of different devices: /device:TPU:13 before, /device:TPU:0 now
where the time goes in v2:
time: 68 us; the launch traced here: 67.6 us
  blocking collectives  23.4 us (34%)
  waiting for transfers between devices  19.8 us (29%)
  matrix products  12.3 us (18%)
  local copies, waits for them, and re-layouts  5.64 us (8%)
  starting transfers between devices  3.82 us (6%)
  other arithmetic  2.46 us (4%)
    all_to_all x1, blocking collectives, body(): lax.all_to_all(outbound, 'expert', split_axis=0, concat_axis=0, axis_inde...  23.4 us
    all_to_all x1, waiting for transfers between devices, body(): lax.all_to_all(part.reshape(teams * chips, CAP * SEGMENTS, wide), 'expert...  16 us
    dot_general x1, matrix products, expert_rows(): return jnp.dot(hidden, down_rows, preferred_element_type=jnp.float32)  6.7 us
    all_to_all x1, starting transfers between devices, body(): lax.all_to_all(part.reshape(teams * chips, CAP * SEGMENTS, wide), 'expert...  3.54 us
    dot_general x1, matrix products, expert_rows(): gate_act = jnp.dot(rows_in, gate_cols, preferred_element_type=jnp.float32)  2.79 us
    dot_general x1, matrix products, body(): jnp.dot(expert_weight, summed.reshape(teams * CAP, features), precision=l...  2.56 us
    ppermute x1, waiting for transfers between devices, body(): there = lax.ppermute(here, 'expert', other_core)  2.05 us
    ppermute x1, waiting for transfers between devices, body(): taken = lax.ppermute(given, 'expert', other_core)  1.84 us
  transfers between devices with their start and end apart: 3, of which 3 were waited for; matrix products, arithmetic and copies ran while one was open for 0% of the time, Pallas kernels for 0%

profile of v2, /device:TPU:0, one launch (start us, length us, event | category | flops | bytes accessed | tf_op | source)
XLA Modules:
  0.0 67.6 jit_solution(3495684310370173103)
XLA Ops:
  0.0 0.0 copy-start
  0.0 0.9 %copy.11 = s32[64,8]{1,0:T(8,128)S(1)} copy(s32[64,8]{0,1:T(8,128)} %param.7) | data formatting | bytes 4096 | tf_op args[1]
  0.9 0.1 eq.46
  0.9 0.1 eq.41
  1.0 0.6 reduce-window.6
  1.7 0.2 slice_reduce_fusion
  1.9 0.2 reduce-window.9
  2.1 0.1 add_bitcast_fusion
  2.2 0.1 select_n.12
  2.3 0.1 copy.13
  2.4 0.0 copy-done
  2.4 0.2 convolution_convert_fusion.1
  2.6 0.1 broadcast_in_dim.9
  2.8 23.4 %all_to_all.10 = bf16[8,40,896]{2,1,0:T(8,128)(2,1)S(1)} all-to-all(bf16[8,40,896]{2,1,0:T(8,128)(2,1)S(1)} %bitcast.23), channel_id=1, replica_groups={{0,2,4,6,8,10,12,14},{1,3,5,7,9,11,13,15},{16,18,20,22,24,26,28,30},{17..., dimensions={0} | all-to-all | bytes 1146880 | tf_op jit(solution)/shard_map/all_to_all | solution.py:63
  26.2 0.3 reshape.72
  26.4 0.1 collective-permute-start
  26.6 2.1 %collective-permute-done = bf16[8,40,896]{2,1,0:T(8,128)(2,1)} collective-permute-done((bf16[8,40,896]{2,1,0:T(8,128)(2,1)S(1)}, bf16[8,40,896]{2,1,0:T(8,128)(2,1)}, u32[]{:S(2)}, u32[]{:S(2)}) %collective-permute-start) | collective-permute-done | bytes 573472 | tf_op jit(solution)/shard_map/ppermute | solution.py:66
  28.6 1.3 %reshape.73 = bf16[40,7168]{1,0:T(8,128)(2,1)S(1)} reshape(bf16[8,40,896]{2,1,0:T(8,128)(2,1)} %collective-permute-done) | data formatting | bytes 1146880 | tf_op jit(solution)/shard_map/reshape | solution.py:68
  30.0 2.8 %fusion.11 = f32[80,256]{1,0:T(8,128)S(1)} fusion(bf16[80,7168]{1,0:T(8,128)(2,1)S(1)} %constant_dynamic-update-slice_fusion, bf16[7168,256]{1,0:T(8,128)(2,1)} %param.9), kind=kOutput, calls=%fused_computation.32 | convolution fusion | flops 293601280 | bytes 4898816 | tf_op jit(solution)/shard_map/dot_general | solution.py:37
  32.8 6.7 %fusion.1 = f32[80,7168]{1,0:T(8,128)} fusion(bf16[256,7168]{1,0:T(8,128)(2,1)} %param.11, f32[80,256]{1,0:T(8,128)S(1)} %fusion.11, bf16[80,7168]{1,0:T(8,128)(2,1)S(1)} %constant_dynamic-update-slice_fusion, bf16[7168,256]{1,0:T(8,128)(2,1)} %param.10), kind=kOutput, calls=%fused_computation.7 | convolution fusion | flops 587325440 | bytes 10862592 | tf_op jit(solution)/shard_map/dot_general | solution.py:40
  39.5 1.3 %slice.25 = bf16[40,7168]{1,0:T(8,128)(2,1)S(1)} slice(f32[80,7168]{1,0:T(8,128)} %fusion.1), slice={[40:80], [0:7168]} | slice | bytes 1146880 | tf_op jit(solution)/shard_map/slice | solution.py:70
  40.8 0.0 copy-start.1
  40.8 0.2 collective-permute-start.1
  41.0 1.8 %collective-permute-done.1 = bf16[40,7168]{1,0:T(8,128)(2,1)S(1)} collective-permute-done((bf16[40,7168]{1,0:T(8,128)(2,1)S(1)}, bf16[40,7168]{1,0:T(8,128)(2,1)S(1)}, u32[]{:S(2)}, u32[]{:S(2)}) %collective-permute-start.1) | collective-permute-done | bytes 573472 | tf_op jit(solution)/shard_map/ppermute | solution.py:71
  42.9 1.4 %fusion = bf16[40,7168]{1,0:T(8,128)(2,1)S(1)} fusion(f32[80,7168]{1,0:T(8,128)} %fusion.1, bf16[40,7168]{1,0:T(8,128)(2,1)S(1)} %collective-permute-done.1), kind=kLoop, calls=%fused_computation.4 | loop fusion | flops 860160 | bytes 2293760 | tf_op jit(solution)/shard_map/convert_element_type | solution.py:72
  44.2 1.1 %reshape.74 = bf16[8,40,896]{2,1,0:T(8,128)(2,1)} reshape(bf16[40,7168]{1,0:T(8,128)(2,1)S(1)} %fusion) | data formatting | bytes 1146880 | tf_op jit(solution)/shard_map/reshape | solution.py:74
  45.3 3.5 %all-to-all-start.1 = ((bf16[8,40,896]{2,1,0:T(8,128)(2,1)}), bf16[8,40,896]{2,1,0:T(8,128)(2,1)S(1)}, u32[]{:S(2)}, u32[]{:S(2)}) async-start(bf16[8,40,896]{2,1,0:T(8,128)(2,1)} %reshape.74), calls=%async_computation.1 | async-start | bytes 1146880 | tf_op jit(solution)/shard_map/all_to_all | solution.py:73
  48.8 0.0 copy-done.1
  48.9 16.0 %all-to-all-done.1 = bf16[8,40,896]{2,1,0:T(8,128)(2,1)S(1)} async-done(((bf16[8,40,896]{2,1,0:T(8,128)(2,1)}), bf16[8,40,896]{2,1,0:T(8,128)(2,1)S(1)}, u32[]{:S(2)}, u32[]{:S(2)}) %all-to-all-start.1) | async-done | bytes 573472 | tf_op jit(solution)/shard_map/all_to_all | solution.py:73
  64.9 0.1 convert_reduce_fusion
  65.0 2.6 %convolution_convert_fusion = bf16[64,7168]{1,0:T(8,128)(2,1)} fusion(f32[64,10]{0,1:T(8,128)S(1)} %select_reduce_fusion, f32[10,7168]{1,0:T(8,128)S(1)} %reshape.77), kind=kOutput, calls=%fused_computation | convolution fusion | flops 55508992 | bytes 1206784 | tf_op jit(solution)/shard_map/dot_general | solution.py:84
  (11 shorter events, 0.3 us)
Async XLA Ops:
  0.0 2.4 %copy-start = (bf16[64,7168]{1,0:T(8,128)(2,1)S(1)}, bf16[64,7168]{1,0:T(8,128)(2,1)}, u32[]{:S(2)}) copy-start(bf16[64,7168]{1,0:T(8,128)(2,1)} %param.6) | copy-start | bytes 2752516
  26.4 2.2 %collective-permute-start = (bf16[8,40,896]{2,1,0:T(8,128)(2,1)S(1)}, bf16[8,40,896]{2,1,0:T(8,128)(2,1)}, u32[]{:S(2)}, u32[]{:S(2)}) collective-permute-start(bf16[8,40,896]{2,1,0:T(8,128)(2,1)S(1)} %all_to_all.10), channel_id=1, source_target_pairs={{0,1},{1,0},{2,3},{3,2},{4,5},{5,4},{6,7},{7,6},{8,9},{9,8},{10,11... | collective-permute-start | bytes 1720328 | tf_op jit(solution)/shard_map/ppermute | solution.py:66
  40.8 8.0 %copy-start.1 = (f32[64,8]{0,1:T(8,128)S(1)}, f32[64,8]{0,1:T(8,128)}, u32[]{:S(2)}) copy-start(f32[64,8]{0,1:T(8,128)} %param.8) | copy-start | bytes 6148
  40.8 2.0 %collective-permute-start.1 = (bf16[40,7168]{1,0:T(8,128)(2,1)S(1)}, bf16[40,7168]{1,0:T(8,128)(2,1)S(1)}, u32[]{:S(2)}, u32[]{:S(2)}) collective-permute-start(bf16[40,7168]{1,0:T(8,128)(2,1)S(1)} %slice.25), channel_id=1, source_target_pairs={{0,1},{1,0},{2,3},{3,2},{4,5},{5,4},{6,7},{7,6},{8,9},{9,8},{10,11... | collective-permute-start | bytes 1720328 | tf_op jit(solution)/shard_map/ppermute | solution.py:71
  45.3 19.6 %all-to-all-start.1 = ((bf16[8,40,896]{2,1,0:T(8,128)(2,1)}), bf16[8,40,896]{2,1,0:T(8,128)(2,1)S(1)}, u32[]{:S(2)}, u32[]{:S(2)}) async-start(bf16[8,40,896]{2,1,0:T(8,128)(2,1)} %reshape.74), calls=%async_computation.1 | async-start | bytes 1146880 | tf_op jit(solution)/shard_map/all_to_all | solution.py:73

commit v3 on v2

--- a/solution.py
+++ b/solution.py
@@ -10,10 +10,11 @@
 route_scale = 2.5
 
 
-def route_tables(expert_ids, route_logits, in_flight, capacity):
+def route_tables(expert_ids, route_logits, mine, in_flight, capacity):
     count_of_rows, pick_count = expert_ids.shape
     flat_ids = expert_ids.reshape(count_of_rows * pick_count)
     labels = jnp.arange(in_flight, dtype=jnp.int32)
+    flat_ids = jnp.where(flat_ids < in_flight, (flat_ids - mine) % in_flight, in_flight)
     hit_table = (flat_ids[:, None] == labels[None, :]).astype(jnp.int32)
     earlier = jnp.cumsum(hit_table, axis=0) - hit_table
     slot_index = jnp.sum(earlier * hit_table, axis=1)
@@ -44,46 +45,58 @@
 SEGMENTS = 8
 
 
+def gather_team(block, devices, chips):
+    blocks = [block]
+    for m in range(1, chips):
+        pairs = [(i, i ^ (m * CORES)) for i in range(devices)]
+        blocks.append(lax.ppermute(block, "expert", pairs))
+    return blocks
+
+
 def body(tokens, expert_ids, route_logits, w_gate, w_up, w_down):
     devices = lax.axis_size("expert")
     teams = devices // SPLIT
     chips = SPLIT // CORES
     features = tokens.shape[1]
     wide = features // SEGMENTS
-    same_core = [[i for i in range(devices) if i % CORES == c] for c in range(CORES)]
-    other_core = [(i, i + 1 - 2 * (i % CORES)) for i in range(devices)]
-    device_assignment, expert_weight = route_tables(expert_ids, route_logits, teams, CAP)
+    tall = CAP * SEGMENTS
+    other_core = [(i, i ^ 1) for i in range(devices)]
+    mine = lax.axis_index("expert") // SPLIT
+    device_assignment, expert_weight = route_tables(expert_ids, route_logits, mine, teams, CAP)
     buffer = jnp.dot(device_assignment, tokens, preferred_element_type=jnp.float32).astype(
         jnp.bfloat16
     )
-    packed = buffer.reshape(teams, CAP * SEGMENTS, wide)
-    outbound = jnp.broadcast_to(
-        packed[:, None], (teams, chips, CAP * SEGMENTS, wide)
-    ).reshape(teams * chips, CAP * SEGMENTS, wide)
-    here = lax.all_to_all(
-        outbound, "expert", split_axis=0, concat_axis=0, axis_index_groups=same_core, tiled=True
-    )
-    there = lax.ppermute(here, "expert", other_core)
+    packed = buffer.reshape(teams, tall, wide)
+    blocks = []
+    for k in range(teams):
+        block = packed[k]
+        if k > 0:
+            pairs = [(i, (i + k * SPLIT) % devices) for i in range(devices)]
+            block = lax.ppermute(block, "expert", pairs)
+        blocks.append(jnp.stack(gather_team(block, devices, chips)))
+    swapped = [lax.ppermute(b, "expert", other_core) for b in blocks]
     count = teams * chips * CAP
-    rows = jnp.concatenate([here.reshape(count, features), there.reshape(count, features)], axis=0)
+    rows = jnp.concatenate(blocks + swapped, axis=0).reshape(2 * count, features)
     produced = expert_rows(rows, w_gate, w_up, w_down)
     kept, given = produced[:count], produced[count:].astype(jnp.bfloat16)
-    taken = lax.ppermute(given, "expert", other_core)
-    part = (kept + taken.astype(jnp.float32)).astype(jnp.bfloat16)
-    returned = lax.all_to_all(
-        part.reshape(teams * chips, CAP * SEGMENTS, wide),
-        "expert",
-        split_axis=0,
-        concat_axis=0,
-        axis_index_groups=same_core,
-        tiled=True,
-    )
-    summed = jnp.sum(
-        returned.astype(jnp.float32).reshape(teams, chips, CAP * SEGMENTS, wide), axis=1
-    )
+    kept = kept.reshape(teams, chips, tall, wide)
+    given = given.reshape(teams, chips, tall, wide)
+    summed = [None] * teams
+    for k in reversed(range(teams)):
+        part = kept[k] + lax.ppermute(given[k], "expert", other_core).astype(jnp.float32)
+        total = part[0]
+        for m in range(1, chips):
+            pairs = [(i, i ^ (m * CORES)) for i in range(devices)]
+            total = total + lax.ppermute(
+                part[m].astype(jnp.bfloat16), "expert", pairs
+            ).astype(jnp.float32)
+        if k > 0:
+            pairs = [(i, (i - k * SPLIT) % devices) for i in range(devices)]
+            total = lax.ppermute(total.astype(jnp.bfloat16), "expert", pairs).astype(jnp.float32)
+        summed[k] = total
     blended = jnp.dot(
         expert_weight,
-        summed.reshape(teams * CAP, features),
+        jnp.stack(summed).reshape(teams * CAP, features),
         precision=lax.Precision.HIGHEST,
         preferred_element_type=jnp.float32,
     )

time: 68 us -> 59.6 us (0.88)
  blocking collectives: 23.4 us -> 0 us
  starting transfers between devices: 3.82 us -> 22.4 us
  waiting for transfers between devices: 19.8 us -> 10.1 us
  local copies, waits for them, and re-layouts: 5.64 us -> 9.48 us
  other arithmetic: 2.46 us -> 4.39 us
    all_to_all x1 -> x0, blocking collectives: 23.4 us -> none  [body(): lax.all_to_all(outbound, 'expert', split_axis=0, concat_axis=0, axis_inde...]
    ppermute x2 -> x18, starting transfers between devices: 0.28 us -> 22.4 us  [the longest x6 8.44 us: gather_team(): blocks.append(lax.ppermute(block, 'expert', pairs))]
    all_to_all x1 -> x0, waiting for transfers between devices: 16 us -> none  [body(): lax.all_to_all(part.reshape(teams * chips, CAP * SEGMENTS, wide), 'expert...]
    ppermute x2 -> x18, waiting for transfers between devices: 3.89 us -> 10.1 us  [the longest x6 4.83 us: gather_team(): blocks.append(lax.ppermute(block, 'expert', pairs))]
    squeeze x0 -> x6, local copies, waits for them, and re-layouts: none -> 4.33 us  [the longest x2 2.77 us: body(): given[k]]
    all_to_all x1 -> x0, starting transfers between devices: 3.54 us -> none  [body(): lax.all_to_all(part.reshape(teams * chips, CAP * SEGMENTS, wide), 'expert...]
    reshape x4 -> x2, local copies, waits for them, and re-layouts: 2.7 us -> 0.62 us  [the longest x1 0.57 us: body(): jnp.concatenate(blocks + swapped, axis=0).reshape(2 * count, features)]
    slice x2 -> x5, local copies, waits for them, and re-layouts: 1.53 us -> 3.55 us  [the longest x1 2.02 us: body(): given[k]]
  transfers between devices with their start and end apart: 3 -> 18, of which waited for: 3 -> 8; matrix products, arithmetic and copies ran while one was open for 0% -> 8% of each run, Pallas kernels for 0% -> 0%
where the time goes in v3:
time: 59.6 us; the launch traced here: 59.3 us
  starting transfers between devices  22.4 us (38%)
  matrix products  12.6 us (21%)
  waiting for transfers between devices  10.1 us (17%)
  local copies, waits for them, and re-layouts  9.48 us (16%)
  other arithmetic  4.39 us (7%)
    ppermute x6, starting transfers between devices, gather_team(): blocks.append(lax.ppermute(block, 'expert', pairs))  8.44 us
    ppermute x6, starting transfers between devices, body(): lax.ppermute(part[m].astype(jnp.bfloat16), 'expert', pairs)  7.11 us
    dot_general x1, matrix products, expert_rows(): return jnp.dot(hidden, down_rows, preferred_element_type=jnp.float32)  7.04 us
    ppermute x6, waiting for transfers between devices, gather_team(): blocks.append(lax.ppermute(block, 'expert', pairs))  4.83 us
    ppermute x1, starting transfers between devices, body(): lax.ppermute(total.astype(jnp.bfloat16), 'expert', pairs)  3.21 us
    ppermute x1, starting transfers between devices, body(): block = lax.ppermute(block, 'expert', pairs)  2.97 us
    dot_general x1, matrix products, expert_rows(): gate_act = jnp.dot(rows_in, gate_cols, preferred_element_type=jnp.float32)  2.79 us
    squeeze x2, local copies, waits for them, and re-layouts, body(): given[k]  2.77 us
  transfers between devices with their start and end apart: 18, of which 8 were waited for; matrix products, arithmetic and copies ran while one was open for 8% of the time, Pallas kernels for 0%

profile of v3, /device:TPU:0, one launch (start us, length us, event | category | flops | bytes accessed | tf_op | source)
XLA Modules:
  0.0 59.3 jit_solution(1004522907119750541)
XLA Ops:
  0.0 0.8 %broadcast_compare_fusion = pred[64,8]{0,1:T(8,128)(4,1)S(1)} fusion(s32[64,8]{0,1:T(8,128)} %param.7), kind=kLoop, calls=%fused_computation.66 | loop fusion | flops 512 | bytes 2560 | tf_op jit(solution)/shard_map/lt | solution.py:17
  0.8 0.1 copy.13
  0.9 0.1 lt.34
  1.0 0.1 lt.31
  1.1 0.7 %broadcast_subtract_fusion = s32[64,8]{0,1:T(8,128)S(1)} fusion(s32[64,8]{0,1:T(8,128)} %param.7, s32[]{:T(128)S(6)} %select_n.39), kind=kLoop, calls=%fused_computation.65 | loop fusion | flops 512 | bytes 4100 | tf_op jit(solution)/shard_map/sub | solution.py:17
  1.9 0.1 sub.28
  2.0 0.1 sub.27
  2.1 0.6 %reduce-window.6 = s32[2,4,128]{2,1,0:T(4,128)S(1)} reduce-window(s32[2,4,128]{2,1,0:T(4,128)S(1)} %fusion.13, s32[]{:T(128)} %constant.45.clone.1), window={size=1x1x128 pad=0_0x0_0x127_0}, to_apply=%region_2.3 | reduce-window | flops 130048 | bytes 8196 | tf_op jit(solution)/shard_map/reduce-window
  2.7 0.2 slice_reduce_fusion
  2.9 0.2 reduce-window.9
  3.5 0.2 convolution_convert_fusion.1
  3.7 0.1 squeeze.30
  3.9 4.0 %collective-permute-start.2 = (bf16[40,896]{1,0:T(8,128)(2,1)S(1)}, bf16[40,896]{1,0:T(8,128)(2,1)S(1)}, u32[]{:S(2)}, u32[]{:S(2)}) collective-permute-start(bf16[40,896]{1,0:T(8,128)(2,1)S(1)} %squeeze.30), channel_id=1, source_target_pairs={{0,6},{1,7},{2,4},{3,5},{4,2},{5,3},{6,0},{7,1},{8,14},{9,15},{10,... | collective-permute-start | bytes 215048 | tf_op jit(solution)/shard_map/ppermute | solution.py:52
  7.9 0.4 collective-permute-start.1
  8.4 0.2 collective-permute-start
  8.5 0.1 squeeze.31
  8.7 3.0 %collective-permute-start.3 = (bf16[40,896]{1,0:T(8,128)(2,1)S(1)}, bf16[40,896]{1,0:T(8,128)(2,1)S(1)}, u32[]{:S(2)}, u32[]{:S(2)}) collective-permute-start(bf16[40,896]{1,0:T(8,128)(2,1)S(1)} %squeeze.31), channel_id=1, source_target_pairs={{0,8},{1,9},{2,10},{3,11},{4,12},{5,13},{6,14},{7,15},{8,0},{9,1},... | collective-permute-start | bytes 215048 | tf_op jit(solution)/shard_map/ppermute | solution.py:75
  11.6 0.1 slice.72
  11.8 0.6 %select_reduce_fusion = f32[64,10]{0,1:T(8,128)} fusion(f32[64,8]{0,1:T(8,128)S(1)} %multiply_divide_fusion, s32[64,8]{0,1:T(8,128)S(1)} %copy.17), kind=kLoop, calls=%fused_computation.28 | loop fusion | flops 14720 | bytes 6656 | tf_op jit(solution)/shard_map/reduce_sum | solution.py:30
  12.4 0.6 collective-permute-done.1
  13.1 1.4 %collective-permute-done.3 = bf16[40,896]{1,0:T(8,128)(2,1)S(1)} collective-permute-done((bf16[40,896]{1,0:T(8,128)(2,1)S(1)}, bf16[40,896]{1,0:T(8,128)(2,1)S(1)}, u32[]{:S(2)}, u32[]{:S(2)}) %collective-permute-start.3) | collective-permute-done | bytes 71712 | tf_op jit(solution)/shard_map/ppermute | solution.py:75
  14.6 2.2 %collective-permute-start.6 = (bf16[40,896]{1,0:T(8,128)(2,1)S(1)}, bf16[40,896]{1,0:T(8,128)(2,1)S(1)}, u32[]{:S(2)}, u32[]{:S(2)}) collective-permute-start(bf16[40,896]{1,0:T(8,128)(2,1)S(1)} %collective-permute-done.3), channel_id=1, source_target_pairs={{0,6},{1,7},{2,4},{3,5},{4,2},{5,3},{6,0},{7,1},{8,14},{9,15},{10,... | collective-permute-start | bytes 215048 | tf_op jit(solution)/shard_map/ppermute | solution.py:52
  16.8 1.5 %collective-permute-start.5 = (bf16[40,896]{1,0:T(8,128)(2,1)S(1)}, bf16[40,896]{1,0:T(8,128)(2,1)S(1)}, u32[]{:S(2)}, u32[]{:S(2)}) collective-permute-start(bf16[40,896]{1,0:T(8,128)(2,1)S(1)} %collective-permute-done.3), channel_id=1, source_target_pairs={{0,4},{1,5},{2,6},{3,7},{4,0},{5,1},{6,2},{7,3},{8,12},{9,13},{10,... | collective-permute-start | bytes 215048 | tf_op jit(solution)/shard_map/ppermute | solution.py:52
  18.4 1.6 %collective-permute-done.6 = bf16[40,896]{1,0:T(8,128)(2,1)S(1)} collective-permute-done((bf16[40,896]{1,0:T(8,128)(2,1)S(1)}, bf16[40,896]{1,0:T(8,128)(2,1)S(1)}, u32[]{:S(2)}, u32[]{:S(2)}) %collective-permute-start.6) | collective-permute-done | bytes 71712 | tf_op jit(solution)/shard_map/ppermute | solution.py:52
  20.0 1.4 %collective-permute-done.5 = bf16[40,896]{1,0:T(8,128)(2,1)S(1)} collective-permute-done((bf16[40,896]{1,0:T(8,128)(2,1)S(1)}, bf16[40,896]{1,0:T(8,128)(2,1)S(1)}, u32[]{:S(2)}, u32[]{:S(2)}) %collective-permute-start.5) | collective-permute-done | bytes 71712 | tf_op jit(solution)/shard_map/ppermute | solution.py:52
  21.4 1.3 %collective-permute-done.4 = bf16[40,896]{1,0:T(8,128)(2,1)S(1)} collective-permute-done((bf16[40,896]{1,0:T(8,128)(2,1)S(1)}, bf16[40,896]{1,0:T(8,128)(2,1)S(1)}, u32[]{:S(2)}, u32[]{:S(2)}) %collective-permute-start.4) | collective-permute-done | bytes 71712 | tf_op jit(solution)/shard_map/ppermute | solution.py:52
  22.9 1.4 %collective-permute-done.8 = bf16[4,40,896]{2,1,0:T(8,128)(2,1)S(1)} collective-permute-done((bf16[4,40,896]{2,1,0:T(8,128)(2,1)S(1)}, bf16[4,40,896]{2,1,0:T(8,128)(2,1)S(1)}, u32[]{:S(2)}, u32[]{:S(2)}) %collective-permute-start.8) | collective-permute-done | bytes 286752 | tf_op jit(solution)/shard_map/ppermute | solution.py:77
  24.4 0.6 reshape.107
  24.9 2.8 %fusion.28 = f32[80,256]{1,0:T(8,128)S(1)} fusion(bf16[80,7168]{1,0:T(8,128)(2,1)S(1)} %reshape.107, bf16[7168,256]{1,0:T(8,128)(2,1)} %param.9), kind=kOutput, calls=%fused_computation.76 | convolution fusion | flops 293601280 | bytes 4898816 | tf_op jit(solution)/shard_map/dot_general | solution.py:38
  27.7 7.0 %fusion.25 = (bf16[80,7168]{1,0:T(8,128)(2,1)}, f32[80,7168]{1,0:T(8,128)}) fusion(bf16[256,7168]{1,0:T(8,128)(2,1)} %param.11, f32[80,256]{1,0:T(8,128)S(1)} %fusion.28, bf16[80,7168]{1,0:T(8,128)(2,1)S(1)} %reshape.107, bf16[7168,256]{1,0:T(8,128)(2,1)} %param.10), kind=kOutput, calls=%fused_computation.74 | convolution fusion | flops 587898880 | bytes 12009472 | tf_op jit(solution)/shard_map/dot_general | solution.py:41
  34.8 2.0 %fusion.23 = (bf16[20,7168]{1,0:T(8,128)(2,1)}, bf16[20,7168]{1,0:T(8,128)(2,1)S(1)}) fusion(bf16[80,7168]{1,0:T(8,128)(2,1)} %get-tuple-element.24), kind=kLoop, calls=%fused_computation.72 | loop fusion | bytes 1146880 | tf_op jit(solution)/shard_map/slice | solution.py:86
  36.8 1.9 %squeeze.33 = bf16[4,40,896]{2,1,0:T(8,128)(2,1)} reshape(bf16[20,7168]{1,0:T(8,128)(2,1)} %get-tuple-element.14) | data formatting | bytes 573440 | tf_op jit(solution)/shard_map/squeeze | solution.py:86
  38.7 0.9 %squeeze.36 = bf16[4,40,896]{2,1,0:T(8,128)(2,1)} reshape(bf16[20,7168]{1,0:T(8,128)(2,1)S(1)} %get-tuple-element.15) | data formatting | bytes 573440 | tf_op jit(solution)/shard_map/squeeze | solution.py:86
  39.6 0.1 collective-permute-start.13
  39.7 0.4 collective-permute-start.9
  40.1 1.2 %fusion.22 = (f32[20,7168]{1,0:T(8,128)}, f32[20,7168]{1,0:T(8,128)}) fusion(f32[80,7168]{1,0:T(8,128)S(1)} %copy-done.1), kind=kLoop, calls=%fused_computation.71 | loop fusion | bytes 2293760 | tf_op jit(solution)/shard_map/slice | solution.py:86
  41.3 1.3 %squeeze.32 = f32[4,40,896]{2,1,0:T(8,128)S(1)} reshape(f32[20,7168]{1,0:T(8,128)} %get-tuple-element.12) | data formatting | bytes 1146880 | tf_op jit(solution)/shard_map/squeeze | solution.py:86
  42.7 1.0 %fusion.21 = (bf16[4,40,896]{2,1,0:T(8,128)(2,1)S(1)}, f32[4,40,896]{2,1,0:T(8,128)S(1)}) fusion(f32[4,40,896]{2,1,0:T(8,128)S(1)} %squeeze.35, bf16[4,40,896]{2,1,0:T(8,128)(2,1)} %collective-permute-done.13), kind=kLoop, calls=%fused_computation.70 | loop fusion | flops 430080 | bytes 1720320 | tf_op jit(solution)/shard_map/convert.3
  43.7 0.3 collective-permute-start.14
  44.0 1.8 %collective-permute-start.16 = (bf16[40,896]{1,0:T(8,128)(2,1)S(1)}, bf16[40,896]{1,0:T(8,128)(2,1)S(1)}, u32[]{:S(2)}, u32[]{:S(2)}) collective-permute-start(bf16[40,896]{1,0:T(8,128)(2,1)S(1)} %get-tuple-element.20), channel_id=1, source_target_pairs={{0,6},{1,7},{2,4},{3,5},{4,2},{5,3},{6,0},{7,1},{8,14},{9,15},{10,... | collective-permute-start | bytes 215048 | tf_op jit(solution)/shard_map/ppermute | solution.py:90
  45.8 1.5 %collective-permute-start.15 = (bf16[40,896]{1,0:T(8,128)(2,1)S(1)}, bf16[40,896]{1,0:T(8,128)(2,1)S(1)}, u32[]{:S(2)}, u32[]{:S(2)}) collective-permute-start(bf16[40,896]{1,0:T(8,128)(2,1)S(1)} %get-tuple-element.21), channel_id=1, source_target_pairs={{0,4},{1,5},{2,6},{3,7},{4,0},{5,1},{6,2},{7,3},{8,12},{9,13},{10,... | collective-permute-start | bytes 215048 | tf_op jit(solution)/shard_map/ppermute | solution.py:90
  47.4 0.3 collective-permute-start.10
  47.6 1.8 %collective-permute-start.12 = (bf16[40,896]{1,0:T(8,128)(2,1)S(1)}, bf16[40,896]{1,0:T(8,128)(2,1)S(1)}, u32[]{:S(2)}, u32[]{:S(2)}) collective-permute-start(bf16[40,896]{1,0:T(8,128)(2,1)S(1)} %get-tuple-element.17), channel_id=1, source_target_pairs={{0,6},{1,7},{2,4},{3,5},{4,2},{5,3},{6,0},{7,1},{8,14},{9,15},{10,... | collective-permute-start | bytes 215048 | tf_op jit(solution)/shard_map/ppermute | solution.py:90
  49.4 1.5 %collective-permute-start.11 = (bf16[40,896]{1,0:T(8,128)(2,1)S(1)}, bf16[40,896]{1,0:T(8,128)(2,1)S(1)}, u32[]{:S(2)}, u32[]{:S(2)}) collective-permute-start(bf16[40,896]{1,0:T(8,128)(2,1)S(1)} %get-tuple-element.18), channel_id=1, source_target_pairs={{0,4},{1,5},{2,6},{3,7},{4,0},{5,1},{6,2},{7,3},{8,12},{9,13},{10,... | collective-permute-start | bytes 215048 | tf_op jit(solution)/shard_map/ppermute | solution.py:90
  51.0 3.2 %collective-permute-start.17 = (bf16[40,896]{1,0:T(8,128)(2,1)S(1)}, bf16[40,896]{1,0:T(8,128)(2,1)S(1)}, u32[]{:S(2)}, u32[]{:S(2)}) collective-permute-start(bf16[40,896]{1,0:T(8,128)(2,1)S(1)} %fusion.3), channel_id=1, source_target_pairs={{0,8},{1,9},{2,10},{3,11},{4,12},{5,13},{6,14},{7,15},{8,0},{9,1},... | collective-permute-start | bytes 215048 | tf_op jit(solution)/shard_map/ppermute | solution.py:95
  54.2 0.5 collective-permute-done.11
  54.8 1.8 %collective-permute-done.17 = bf16[40,896]{1,0:T(8,128)(2,1)S(1)} collective-permute-done((bf16[40,896]{1,0:T(8,128)(2,1)S(1)}, bf16[40,896]{1,0:T(8,128)(2,1)S(1)}, u32[]{:S(2)}, u32[]{:S(2)}) %collective-permute-start.17) | collective-permute-done | bytes 71712 | tf_op jit(solution)/shard_map/ppermute | solution.py:95
  56.7 2.6 %convolution_convert_fusion = bf16[64,7168]{1,0:T(8,128)(2,1)} fusion(f32[64,10]{0,1:T(8,128)S(1)} %copy-done.3, f32[10,7168]{1,0:T(8,128)S(1)} %reshape.108), kind=kOutput, calls=%fused_computation | convolution fusion | flops 55508992 | bytes 1206784 | tf_op jit(solution)/shard_map/dot_general | solution.py:97
  (57 shorter events, 1.4 us)
Async XLA Ops:
  0.0 3.4 %copy-start = (bf16[64,7168]{1,0:T(8,128)(2,1)S(1)}, bf16[64,7168]{1,0:T(8,128)(2,1)}, u32[]{:S(2)}) copy-start(bf16[64,7168]{1,0:T(8,128)(2,1)} %param.6) | copy-start | bytes 2752516
  3.2 8.6 %copy-start.4 = (f32[64,8]{0,1:T(8,128)S(1)}, f32[64,8]{0,1:T(8,128)}, u32[]{:S(2)}) copy-start(f32[64,8]{0,1:T(8,128)} %param.8) | copy-start | bytes 6148
  3.9 8.6 %collective-permute-start.2 = (bf16[40,896]{1,0:T(8,128)(2,1)S(1)}, bf16[40,896]{1,0:T(8,128)(2,1)S(1)}, u32[]{:S(2)}, u32[]{:S(2)}) collective-permute-start(bf16[40,896]{1,0:T(8,128)(2,1)S(1)} %squeeze.30), channel_id=1, source_target_pairs={{0,6},{1,7},{2,4},{3,5},{4,2},{5,3},{6,0},{7,1},{8,14},{9,15},{10,... | collective-permute-start | bytes 215048 | tf_op jit(solution)/shard_map/ppermute | solution.py:52
  7.9 5.1 %collective-permute-start.1 = (bf16[40,896]{1,0:T(8,128)(2,1)S(1)}, bf16[40,896]{1,0:T(8,128)(2,1)S(1)}, u32[]{:S(2)}, u32[]{:S(2)}) collective-permute-start(bf16[40,896]{1,0:T(8,128)(2,1)S(1)} %squeeze.30), channel_id=1, source_target_pairs={{0,4},{1,5},{2,6},{3,7},{4,0},{5,1},{6,2},{7,3},{8,12},{9,13},{10,... | collective-permute-start | bytes 215048 | tf_op jit(solution)/shard_map/ppermute | solution.py:52
  8.4 4.7 %collective-permute-start = (bf16[40,896]{1,0:T(8,128)(2,1)S(1)}, bf16[40,896]{1,0:T(8,128)(2,1)S(1)}, u32[]{:S(2)}, u32[]{:S(2)}) collective-permute-start(bf16[40,896]{1,0:T(8,128)(2,1)S(1)} %squeeze.30), channel_id=1, source_target_pairs={{0,2},{1,3},{2,0},{3,1},{4,6},{5,7},{6,4},{7,5},{8,10},{9,11},{10,... | collective-permute-start | bytes 215048 | tf_op jit(solution)/shard_map/ppermute | solution.py:52
  8.7 5.9 %collective-permute-start.3 = (bf16[40,896]{1,0:T(8,128)(2,1)S(1)}, bf16[40,896]{1,0:T(8,128)(2,1)S(1)}, u32[]{:S(2)}, u32[]{:S(2)}) collective-permute-start(bf16[40,896]{1,0:T(8,128)(2,1)S(1)} %squeeze.31), channel_id=1, source_target_pairs={{0,8},{1,9},{2,10},{3,11},{4,12},{5,13},{6,14},{7,15},{8,0},{9,1},... | collective-permute-start | bytes 215048 | tf_op jit(solution)/shard_map/ppermute | solution.py:75
  13.1 9.8 %collective-permute-start.7 = (bf16[4,40,896]{2,1,0:T(8,128)(2,1)S(1)}, bf16[4,40,896]{2,1,0:T(8,128)(2,1)S(1)}, u32[]{:S(2)}, u32[]{:S(2)}) collective-permute-start(bf16[4,40,896]{2,1,0:T(8,128)(2,1)S(1)} %pad_maximum_fusion), channel_id=1, source_target_pairs={{0,1},{1,0},{2,3},{3,2},{4,5},{5,4},{6,7},{7,6},{8,9},{9,8},{10,11... | collective-permute-start | bytes 860168 | tf_op jit(solution)/shard_map/ppermute | solution.py:77
  14.6 5.5 %collective-permute-start.6 = (bf16[40,896]{1,0:T(8,128)(2,1)S(1)}, bf16[40,896]{1,0:T(8,128)(2,1)S(1)}, u32[]{:S(2)}, u32[]{:S(2)}) collective-permute-start(bf16[40,896]{1,0:T(8,128)(2,1)S(1)} %collective-permute-done.3), channel_id=1, source_target_pairs={{0,6},{1,7},{2,4},{3,5},{4,2},{5,3},{6,0},{7,1},{8,14},{9,15},{10,... | collective-permute-start | bytes 215048 | tf_op jit(solution)/shard_map/ppermute | solution.py:52
  16.8 4.6 %collective-permute-start.5 = (bf16[40,896]{1,0:T(8,128)(2,1)S(1)}, bf16[40,896]{1,0:T(8,128)(2,1)S(1)}, u32[]{:S(2)}, u32[]{:S(2)}) collective-permute-start(bf16[40,896]{1,0:T(8,128)(2,1)S(1)} %collective-permute-done.3), channel_id=1, source_target_pairs={{0,4},{1,5},{2,6},{3,7},{4,0},{5,1},{6,2},{7,3},{8,12},{9,13},{10,... | collective-permute-start | bytes 215048 | tf_op jit(solution)/shard_map/ppermute | solution.py:52
  18.3 4.3 %collective-permute-start.4 = (bf16[40,896]{1,0:T(8,128)(2,1)S(1)}, bf16[40,896]{1,0:T(8,128)(2,1)S(1)}, u32[]{:S(2)}, u32[]{:S(2)}) collective-permute-start(bf16[40,896]{1,0:T(8,128)(2,1)S(1)} %collective-permute-done.3), channel_id=1, source_target_pairs={{0,2},{1,3},{2,0},{3,1},{4,6},{5,7},{6,4},{7,5},{8,10},{9,11},{10,... | collective-permute-start | bytes 215048 | tf_op jit(solution)/shard_map/ppermute | solution.py:52
  22.7 1.6 %collective-permute-start.8 = (bf16[4,40,896]{2,1,0:T(8,128)(2,1)S(1)}, bf16[4,40,896]{2,1,0:T(8,128)(2,1)S(1)}, u32[]{:S(2)}, u32[]{:S(2)}) collective-permute-start(bf16[4,40,896]{2,1,0:T(8,128)(2,1)S(1)} %pad_maximum_fusion.1), channel_id=1, source_target_pairs={{0,1},{1,0},{2,3},{3,2},{4,5},{5,4},{6,7},{7,6},{8,9},{9,8},{10,11... | collective-permute-start | bytes 860168 | tf_op jit(solution)/shard_map/ppermute | solution.py:77
  34.8 5.3 %copy-start.1 = (f32[80,7168]{1,0:T(8,128)S(1)}, f32[80,7168]{1,0:T(8,128)}, u32[]{:S(2)}) copy-start(f32[80,7168]{1,0:T(8,128)} %get-tuple-element.25) | copy-start | bytes 6881284
  39.6 3.1 %collective-permute-start.13 = (bf16[4,40,896]{2,1,0:T(8,128)(2,1)}, bf16[4,40,896]{2,1,0:T(8,128)(2,1)}, u32[]{:S(2)}, u32[]{:S(2)}) collective-permute-start(bf16[4,40,896]{2,1,0:T(8,128)(2,1)} %squeeze.36), channel_id=1, source_target_pairs={{0,1},{1,0},{2,3},{3,2},{4,5},{5,4},{6,7},{7,6},{8,9},{9,8},{10,11... | collective-permute-start | bytes 860168 | tf_op jit(solution)/shard_map/ppermute | solution.py:86
  39.7 7.6 %collective-permute-start.9 = (bf16[4,40,896]{2,1,0:T(8,128)(2,1)}, bf16[4,40,896]{2,1,0:T(8,128)(2,1)S(1)}, u32[]{:S(2)}, u32[]{:S(2)}) collective-permute-start(bf16[4,40,896]{2,1,0:T(8,128)(2,1)} %squeeze.33), channel_id=1, source_target_pairs={{0,1},{1,0},{2,3},{3,2},{4,5},{5,4},{6,7},{7,6},{8,9},{9,8},{10,11... | collective-permute-start | bytes 860168 | tf_op jit(solution)/shard_map/ppermute | solution.py:86
  41.3 1.3 %copy-start.2 = (f32[20,7168]{1,0:T(8,128)S(1)}, f32[20,7168]{1,0:T(8,128)}, u32[]{:S(2)}) copy-start(f32[20,7168]{1,0:T(8,128)} %get-tuple-element.13) | copy-start | bytes 1720324
  43.7 5.7 %collective-permute-start.14 = (bf16[40,896]{1,0:T(8,128)(2,1)S(1)}, bf16[40,896]{1,0:T(8,128)(2,1)S(1)}, u32[]{:S(2)}, u32[]{:S(2)}) collective-permute-start(bf16[40,896]{1,0:T(8,128)(2,1)S(1)} %get-tuple-element.19), channel_id=1, source_target_pairs={{0,2},{1,3},{2,0},{3,1},{4,6},{5,7},{6,4},{7,5},{8,10},{9,11},{10,... | collective-permute-start | bytes 215048 | tf_op jit(solution)/shard_map/ppermute | solution.py:90
  44.0 6.9 %collective-permute-start.16 = (bf16[40,896]{1,0:T(8,128)(2,1)S(1)}, bf16[40,896]{1,0:T(8,128)(2,1)S(1)}, u32[]{:S(2)}, u32[]{:S(2)}) collective-permute-start(bf16[40,896]{1,0:T(8,128)(2,1)S(1)} %get-tuple-element.20), channel_id=1, source_target_pairs={{0,6},{1,7},{2,4},{3,5},{4,2},{5,3},{6,0},{7,1},{8,14},{9,15},{10,... | collective-permute-start | bytes 215048 | tf_op jit(solution)/shard_map/ppermute | solution.py:90
  45.8 5.2 %collective-permute-start.15 = (bf16[40,896]{1,0:T(8,128)(2,1)S(1)}, bf16[40,896]{1,0:T(8,128)(2,1)S(1)}, u32[]{:S(2)}, u32[]{:S(2)}) collective-permute-start(bf16[40,896]{1,0:T(8,128)(2,1)S(1)} %get-tuple-element.21), channel_id=1, source_target_pairs={{0,4},{1,5},{2,6},{3,7},{4,0},{5,1},{6,2},{7,3},{8,12},{9,13},{10,... | collective-permute-start | bytes 215048 | tf_op jit(solution)/shard_map/ppermute | solution.py:90
  47.4 6.8 %collective-permute-start.10 = (bf16[40,896]{1,0:T(8,128)(2,1)S(1)}, bf16[40,896]{1,0:T(8,128)(2,1)S(1)}, u32[]{:S(2)}, u32[]{:S(2)}) collective-permute-start(bf16[40,896]{1,0:T(8,128)(2,1)S(1)} %get-tuple-element.16), channel_id=1, source_target_pairs={{0,2},{1,3},{2,0},{3,1},{4,6},{5,7},{6,4},{7,5},{8,10},{9,11},{10,... | collective-permute-start | bytes 215048 | tf_op jit(solution)/shard_map/ppermute | solution.py:90
  47.6 6.6 %collective-permute-start.12 = (bf16[40,896]{1,0:T(8,128)(2,1)S(1)}, bf16[40,896]{1,0:T(8,128)(2,1)S(1)}, u32[]{:S(2)}, u32[]{:S(2)}) collective-permute-start(bf16[40,896]{1,0:T(8,128)(2,1)S(1)} %get-tuple-element.17), channel_id=1, source_target_pairs={{0,6},{1,7},{2,4},{3,5},{4,2},{5,3},{6,0},{7,1},{8,14},{9,15},{10,... | collective-permute-start | bytes 215048 | tf_op jit(solution)/shard_map/ppermute | solution.py:90
  49.4 5.3 %collective-permute-start.11 = (bf16[40,896]{1,0:T(8,128)(2,1)S(1)}, bf16[40,896]{1,0:T(8,128)(2,1)S(1)}, u32[]{:S(2)}, u32[]{:S(2)}) collective-permute-start(bf16[40,896]{1,0:T(8,128)(2,1)S(1)} %get-tuple-element.18), channel_id=1, source_target_pairs={{0,4},{1,5},{2,6},{3,7},{4,0},{5,1},{6,2},{7,3},{8,12},{9,13},{10,... | collective-permute-start | bytes 215048 | tf_op jit(solution)/shard_map/ppermute | solution.py:90
  51.0 5.7 %copy-start.3 = (f32[64,10]{0,1:T(8,128)S(1)}, f32[64,10]{0,1:T(8,128)}, u32[]{:S(2)}) copy-start(f32[64,10]{0,1:T(8,128)} %select_reduce_fusion) | copy-start | bytes 7684
  51.0 5.6 %collective-permute-start.17 = (bf16[40,896]{1,0:T(8,128)(2,1)S(1)}, bf16[40,896]{1,0:T(8,128)(2,1)S(1)}, u32[]{:S(2)}, u32[]{:S(2)}) collective-permute-start(bf16[40,896]{1,0:T(8,128)(2,1)S(1)} %fusion.3), channel_id=1, source_target_pairs={{0,8},{1,9},{2,10},{3,11},{4,12},{5,13},{6,14},{7,15},{8,0},{9,1},... | collective-permute-start | bytes 215048 | tf_op jit(solution)/shard_map/ppermute | solution.py:95

commit v4 on v3

v4 whole, which is shorter than its diff:
```python
import functools

import jax
import jax.numpy as jnp
from jax import lax
from jax.experimental import pallas as pl
from jax.experimental.pallas import tpu as pltpu
from jax.sharding import PartitionSpec as P

SPLIT = 8
CAP = 5
CORES = 2
SEGMENTS = 8

route_scale = 2.5

VMEM = pl.BlockSpec(memory_space=pltpu.VMEM)
MIB = 1024 * 1024


def hits(ids, mine, teams):
    count = ids.shape[1]
    row = lax.broadcasted_iota(jnp.int32, (8 * pl.cdiv(teams, 8), count), 0)
    wanted = lax.rem(mine + row, teams)
    hit = jnp.zeros(row.shape, jnp.int32)
    for j in range(ids.shape[0]):
        hit = hit + jnp.where(ids[j : j + 1, :] == wanted, 1, 0)
    hit = jnp.where(row < teams, hit, 0).astype(jnp.float32)
    before = lax.broadcasted_iota(jnp.int32, (count, count), 0)
    after = lax.broadcasted_iota(jnp.int32, (count, count), 1)
    earlier = jnp.where(before < after, 1.0, 0.0).astype(jnp.bfloat16)
    slot = jnp.dot(hit.astype(jnp.bfloat16), earlier, preferred_element_type=jnp.float32)
    return hit, jnp.where(hit > 0, slot, -1.0)


def pack_kernel(teams, ids_ref, tokens_ref, *out_refs):
    mine = lax.axis_index("expert") // SPLIT
    _, slot = hits(ids_ref[...], mine, teams)
    count, features = tokens_ref.shape
    wide = features // SEGMENTS
    tall = CAP * SEGMENTS
    stacked = jnp.concatenate(
        [tokens_ref[:, s * wide : (s + 1) * wide] for s in range(SEGMENTS)], axis=0
    )
    shape = (tall, SEGMENTS * count)
    row = lax.broadcasted_iota(jnp.int32, shape, 0)
    column = lax.broadcasted_iota(jnp.int32, shape, 1)
    same = (row // CAP) == (column // count)
    place = lax.rem(row, CAP).astype(jnp.float32)
    picks = []
    for k in range(teams):
        slots = jnp.concatenate([slot[k : k + 1, :]] * SEGMENTS, axis=1)
        picks.append(jnp.where(same & (slots == place), 1.0, 0.0))
    packed = jnp.dot(
        jnp.concatenate(picks, axis=0).astype(jnp.bfloat16),
        stacked,
        preferred_element_type=jnp.float32,
    )
    for k in range(teams):
        out_refs[k][...] = packed[k * tall : (k + 1) * tall].astype(jnp.bfloat16)


def pack_rows(ids, tokens, teams):
    wide = tokens.shape[1] // SEGMENTS
    block = jax.ShapeDtypeStruct((CAP * SEGMENTS, wide), jnp.bfloat16)
    return pl.pallas_call(
        functools.partial(pack_kernel, teams),
        out_shape=[block] * teams,
        in_specs=[VMEM, VMEM],
        out_specs=[VMEM] * teams,
        name="pack_rows",
    )(ids, tokens)


def weight_kernel(teams, ids_ref, logits_ref, high_ref, low_ref):
    mine = lax.axis_index("expert") // SPLIT
    ids = ids_ref[...]
    hit, slot = hits(ids, mine, teams)
    count = ids.shape[1]
    lifted = jax.nn.sigmoid(logits_ref[...])
    gates = route_scale * lifted / jnp.sum(lifted, axis=0, keepdims=True)
    row = lax.broadcasted_iota(jnp.int32, hit.shape, 0)
    wanted = lax.rem(mine + row, teams)
    gate = jnp.zeros(hit.shape, jnp.float32)
    for j in range(ids.shape[0]):
        gate = gate + jnp.where(ids[j : j + 1, :] == wanted, gates[j : j + 1, :], 0.0)
    slot = jnp.transpose(slot)
    gate = jnp.transpose(gate)
    tall = CAP * SEGMENTS
    shape = (SEGMENTS * count, tall)
    down = lax.broadcasted_iota(jnp.int32, shape, 0)
    across = lax.broadcasted_iota(jnp.int32, shape, 1)
    same = (down // count) == (across // CAP)
    place = lax.rem(across, CAP).astype(jnp.float32)
    for k in range(teams):
        slots = jnp.concatenate([slot[:, k : k + 1]] * SEGMENTS, axis=0)
        factor = jnp.concatenate([gate[:, k : k + 1]] * SEGMENTS, axis=0)
        full = jnp.where(same & (slots == place), factor, 0.0)
        high = full.astype(jnp.bfloat16)
        high_ref[k] = high
        low_ref[k] = (full - high.astype(jnp.float32)).astype(jnp.bfloat16)


def blend_weights(ids, logits, teams):
    shape = (teams, SEGMENTS * ids.shape[1], CAP * SEGMENTS)
    out = jax.ShapeDtypeStruct(shape, jnp.bfloat16)
    return pl.pallas_call(
        functools.partial(weight_kernel, teams),
        out_shape=[out, out],
        in_specs=[VMEM, VMEM],
        out_specs=[VMEM, VMEM],
        name="blend_weights",
    )(ids, logits)


def down_rows(hidden, down_ref, out_ref):
    features = out_ref.shape[1]
    step = features // SEGMENTS
    for s in range(SEGMENTS):
        columns = slice(s * step, (s + 1) * step)
        out_ref[:, columns] = jnp.dot(
            hidden, down_ref[:, columns], preferred_element_type=jnp.float32
        ).astype(out_ref.dtype)


def expert_kernel(rows_ref, gate_ref, up_ref, down_ref, given_ref, hidden_ref):
    count, features = rows_ref.shape
    units = gate_ref.shape[1]
    step = features // 7

    def add_chunk(i, sums):
        columns = pl.ds(pl.multiple_of(i * step, step), step)
        rows = rows_ref[:, columns]
        return tuple(
            total + jnp.dot(rows, ref[columns, :], preferred_element_type=jnp.float32)
            for total, ref in zip(sums, (gate_ref, up_ref))
        )

    zero = jnp.zeros((count, units), jnp.float32)
    gate_act, up_act = lax.fori_loop(0, 7, add_chunk, (zero, zero))
    hidden = (jax.nn.silu(gate_act) * up_act).astype(jnp.bfloat16)
    half = count // 2
    hidden_ref[...] = hidden[:half]
    down_rows(hidden[half:], down_ref, given_ref)


def expert_half(rows, w_gate, w_up, w_down):
    count, features = rows.shape
    units = w_gate.shape[1]
    return pl.pallas_call(
        expert_kernel,
        out_shape=[
            jax.ShapeDtypeStruct((count // 2, features), jnp.bfloat16),
            jax.ShapeDtypeStruct((count // 2, units), jnp.bfloat16),
        ],
        in_specs=[VMEM] * 4,
        out_specs=[VMEM] * 2,
        compiler_params=pltpu.CompilerParams(vmem_limit_bytes=40 * MIB),
        cost_estimate=pl.CostEstimate(
            flops=5 * count * units * features,
            bytes_accessed=6 * features * units,
            transcendentals=count * units,
        ),
        name="expert_half",
    )(rows, w_gate, w_up, w_down)


def kept_kernel(hidden_ref, down_ref, kept_ref):
    down_rows(hidden_ref[...], down_ref, kept_ref)


def kept_half(hidden, w_down):
    count, units = hidden.shape
    features = w_down.shape[1]
    return pl.pallas_call(
        kept_kernel,
        out_shape=jax.ShapeDtypeStruct((count, features), jnp.float32),
        in_specs=[VMEM] * 2,
        out_specs=VMEM,
        compiler_params=pltpu.CompilerParams(vmem_limit_bytes=24 * MIB),
        cost_estimate=pl.CostEstimate(
            flops=2 * count * units * features,
            bytes_accessed=2 * features * units,
            transcendentals=0,
        ),
        name="kept_half",
    )(hidden, w_down)


def repack_kernel(chips, kept_ref, taken_ref, *out_refs):
    features = kept_ref.shape[1]
    wide = features // SEGMENTS
    for b, out_ref in enumerate(out_refs):
        for s in range(SEGMENTS):
            columns = slice(s * wide, (s + 1) * wide)
            rows = slice(b * CAP, (b + 1) * CAP)
            part = kept_ref[rows, columns] + taken_ref[rows, columns].astype(jnp.float32)
            out_ref[s * CAP : (s + 1) * CAP, :] = part.astype(out_ref.dtype)


def repack(kept, taken, teams, chips):
    count, features = kept.shape
    shape = (CAP * SEGMENTS, features // SEGMENTS)
    outs = [
        jax.ShapeDtypeStruct(shape, jnp.bfloat16 if m else jnp.float32)
        for k in range(teams)
        for m in range(chips)
    ]
    return pl.pallas_call(
        functools.partial(repack_kernel, chips),
        out_shape=outs,
        in_specs=[VMEM] * 2,
        out_specs=[VMEM] * len(outs),
        name="repack",
    )(kept, taken)


def sum_kernel(*refs):
    total = refs[0][...]
    for ref in refs[1:-1]:
        total = total + ref[...].astype(jnp.float32)
    refs[-1][...] = total.astype(refs[-1].dtype)


def sum_blocks(blocks):
    return pl.pallas_call(
        sum_kernel,
        out_shape=jax.ShapeDtypeStruct(blocks[0].shape, jnp.bfloat16),
        in_specs=[VMEM] * len(blocks),
        out_specs=VMEM,
        name="sum_blocks",
    )(*blocks)


def blend_kernel(chips, high_ref, low_ref, *refs):
    out_ref = refs[-1]
    teams = high_ref.shape[0]
    count, features = out_ref.shape
    wide = features // SEGMENTS
    own = refs[0][...]
    for ref in refs[1:chips]:
        own = own + ref[...].astype(jnp.float32)
    own_high = own.astype(jnp.bfloat16)
    own_low = (own - own_high.astype(jnp.float32)).astype(jnp.bfloat16)
    dot = functools.partial(jnp.dot, preferred_element_type=jnp.float32)
    total = dot(high_ref[0], own_high) + dot(high_ref[0], own_low) + dot(low_ref[0], own_high)
    for k in range(1, teams):
        rows = refs[chips + k - 1][...]
        total = total + dot(high_ref[k], rows) + dot(low_ref[k], rows)
    for s in range(SEGMENTS):
        out_ref[:, s * wide : (s + 1) * wide] = total[s * count : (s + 1) * count].astype(
            jnp.bfloat16
        )


def blend(high, low, own_blocks, other_blocks, count):
    chips = len(own_blocks)
    features = own_blocks[0].shape[1] * SEGMENTS
    return pl.pallas_call(
        functools.partial(blend_kernel, chips),
        out_shape=jax.ShapeDtypeStruct((count, features), jnp.bfloat16),
        in_specs=[VMEM] * (2 + chips + len(other_blocks)),
        out_specs=VMEM,
        compiler_params=pltpu.CompilerParams(vmem_limit_bytes=40 * MIB),
        name="blend",
    )(high, low, *own_blocks, *other_blocks)


def body(tokens, expert_ids, route_logits, w_gate, w_up, w_down):
    devices = lax.axis_size("expert")
    teams = devices // SPLIT
    chips = SPLIT // CORES
    features = tokens.shape[1]
    other_core = [(i, i ^ 1) for i in range(devices)]
    other_chip = [[(i, i ^ (m * CORES)) for i in range(devices)] for m in range(chips)]
    ids = expert_ids.T
    packed = pack_rows(ids, tokens, teams)
    high, low = blend_weights(ids, route_logits.T, teams)
    blocks = []
    for k in range(teams):
        block = packed[k]
        if k > 0:
            pairs = [(i, (i + k * SPLIT) % devices) for i in range(devices)]
            block = lax.ppermute(block, "expert", pairs)
        team = [block]
        for m in range(1, chips):
            team.append(lax.ppermute(block, "expert", other_chip[m]))
        blocks.append(jnp.stack(team))
    swapped = [lax.ppermute(b, "expert", other_core) for b in blocks]
    count = teams * chips * CAP
    both = jnp.concatenate(blocks + swapped, axis=0)
    wide = features // SEGMENTS
    both = both.reshape(2 * teams * chips, SEGMENTS, CAP, wide)
    rows = jnp.transpose(both, (0, 2, 1, 3)).reshape(2 * count, features)
    given, hidden = expert_half(rows, w_gate, w_up, w_down)
    taken = lax.ppermute(given, "expert", other_core)
    kept = kept_half(hidden, w_down)
    parts = repack(kept, taken, teams, chips)
    others = []
    own = None
    for k in reversed(range(teams)):
        team = [parts[k * chips]]
        for m in range(1, chips):
            team.append(lax.ppermute(parts[k * chips + m], "expert", other_chip[m]))
        if k > 0:
            pairs = [(i, (i - k * SPLIT) % devices) for i in range(devices)]
            others.insert(0, lax.ppermute(sum_blocks(team), "expert", pairs))
        else:
            own = team
    return blend(high, low, own, others, tokens.shape[0])


def solution(mesh):
    placed = (
        P(("groups", "expert"), None),
        P(("groups", "expert"), None),
        P(("groups", "expert"), None),
        P(None, "expert"),
        P(None, "expert"),
        P("expert", None),
    )
    return jax.shard_map(
        body, mesh=mesh, in_specs=placed, out_specs=P(("groups", "expert"), None), check_vma=False
    )
```

time: 59.6 us -> 58.1 us (0.975)
  Pallas kernels: 0 us -> 14.1 us
  matrix products: 12.6 us -> 0 us
  local copies, waits for them, and re-layouts: 9.48 us -> 14.1 us
  other arithmetic: 4.39 us -> 0.98 us
  waiting for transfers between devices: 10.1 us -> 7.4 us
  starting transfers between devices: 22.4 us -> 20.8 us
    pallas_call x0 -> x7, Pallas kernels: none -> 14.1 us  [the longest x1 2.82 us: expert_half(): pl.pallas_call(expert_kernel, out_shape=[jax.ShapeDtypeStruct((count // 2...]
    dot_general x4 -> x0, matrix products: 12.6 us -> none  [the longest x1 7.04 us: expert_rows(): return jnp.dot(hidden, down_rows, preferred_element_type=jnp.float32)]
    unnamed x19 -> x25, local copies, waits for them, and re-layouts: 0.2 us -> 11.1 us
    squeeze x6 -> x0, local copies, waits for them, and re-layouts: 4.33 us -> none  [the longest x2 2.77 us: body(): given[k]]
    slice x5 -> x0, local copies, waits for them, and re-layouts: 3.55 us -> none  [the longest x1 2.02 us: body(): given[k]]
    ppermute x15 -> x14, starting transfers between devices: 19.3 us -> 16.7 us  [the longest x6 6.98 us: body(): team.append(lax.ppermute(block, 'expert', other_chip[m]))]
    concatenate x1 -> x9, local copies, waits for them, and re-layouts: 0.03 us -> 2.59 us  [body(): both = jnp.concatenate(blocks + swapped, axis=0)]
    ppermute x15 -> x14, waiting for transfers between devices: 7.22 us -> 6.02 us  [the longest x6 2.62 us: body(): team.append(lax.ppermute(block, 'expert', other_chip[m]))]
  transfers between devices with their start and end apart: 18 -> 17, of which waited for: 8 -> 9; matrix products, arithmetic and copies ran while one was open for 8% -> 2% of each run, Pallas kernels for 0% -> 7%
where the time goes in v4:
time: 58.1 us; the launch traced here: 57.7 us
  starting transfers between devices  20.8 us (36%)
  Pallas kernels  14.1 us (24%)
  local copies, waits for them, and re-layouts  14.1 us (24%)
  waiting for transfers between devices  7.4 us (13%)
  other arithmetic  0.98 us (2%)
    unnamed x25, local copies, waits for them, and re-layouts  11.1 us
    ppermute x6, starting transfers between devices, body(): team.append(lax.ppermute(block, 'expert', other_chip[m]))  6.98 us
    ppermute x6, starting transfers between devices, body(): team.append(lax.ppermute(parts[k * chips + m], 'expert', other_chip[m]))  6.98 us
    ppermute x1, starting transfers between devices, body(): block = lax.ppermute(block, 'expert', pairs)  4.04 us
    pallas_call x1, Pallas kernels, expert_half(): pl.pallas_call(expert_kernel, out_shape=[jax.ShapeDtypeStruct((count // 2...  2.82 us
    ppermute x6, waiting for transfers between devices, body(): team.append(lax.ppermute(block, 'expert', other_chip[m]))  2.62 us
    concatenate x9, local copies, waits for them, and re-layouts, body(): both = jnp.concatenate(blocks + swapped, axis=0)  2.59 us
    pallas_call x1, Pallas kernels, repack(): pl.pallas_call(functools.partial(repack_kernel, chips), out_shape=outs, i...  2.52 us
  transfers between devices with their start and end apart: 17, of which 9 were waited for; matrix products, arithmetic and copies ran while one was open for 2% of the time, Pallas kernels for 7%

profile of v4, /device:TPU:0, one launch (start us, length us, event | category | flops | bytes accessed | tf_op | source)
XLA Modules:
  0.0 57.7 jit_solution(17339326090122758038)
XLA Ops:
  0.0 2.3 %pack_rows.1 = (bf16[40,896]{1,0:T(8,128)(2,1)}, bf16[40,896]{1,0:T(8,128)(2,1)}) custom-call(s32[8,64]{1,0:T(8,128)} %bitcast.29, bf16[64,7168]{1,0:T(8,128)(2,1)} %tokens_ref.1), custom_call_target="tpu_custom_call" | custom-call | tf_op jit(solution)/shard_map/pack_rows/pallas_call | solution.py:66
  2.3 4.0 %collective-permute-start.3 = (bf16[40,896]{1,0:T(8,128)(2,1)}, bf16[40,896]{1,0:T(8,128)(2,1)S(1)}, u32[]{:S(2)}, u32[]{:S(2)}) collective-permute-start(bf16[40,896]{1,0:T(8,128)(2,1)} %get-tuple-element.22), channel_id=1, source_target_pairs={{0,8},{1,9},{2,10},{3,11},{4,12},{5,13},{6,14},{7,15},{8,0},{9,1},... | collective-permute-start | bytes 215048 | tf_op jit(solution)/shard_map/ppermute | solution.py:284
  6.4 1.5 %collective-permute-start = (bf16[40,896]{1,0:T(8,128)(2,1)}, bf16[40,896]{1,0:T(8,128)(2,1)S(1)}, u32[]{:S(2)}, u32[]{:S(2)}) collective-permute-start(bf16[40,896]{1,0:T(8,128)(2,1)} %get-tuple-element.21), channel_id=1, source_target_pairs={{0,2},{1,3},{2,0},{3,1},{4,6},{5,7},{6,4},{7,5},{8,10},{9,11},{10,... | collective-permute-start | bytes 215048 | tf_op jit(solution)/shard_map/ppermute | solution.py:287
  7.9 1.6 %collective-permute-start.1 = (bf16[40,896]{1,0:T(8,128)(2,1)}, bf16[40,896]{1,0:T(8,128)(2,1)S(1)}, u32[]{:S(2)}, u32[]{:S(2)}) collective-permute-start(bf16[40,896]{1,0:T(8,128)(2,1)} %get-tuple-element.21), channel_id=1, source_target_pairs={{0,4},{1,5},{2,6},{3,7},{4,0},{5,1},{6,2},{7,3},{8,12},{9,13},{10,... | collective-permute-start | bytes 215048 | tf_op jit(solution)/shard_map/ppermute | solution.py:287
  9.5 0.4 collective-permute-start.2
  9.9 0.3 collective-permute-done.3
  10.1 2.3 %collective-permute-start.6 = (bf16[40,896]{1,0:T(8,128)(2,1)S(1)}, bf16[40,896]{1,0:T(8,128)(2,1)S(1)}, u32[]{:S(2)}, u32[]{:S(2)}) collective-permute-start(bf16[40,896]{1,0:T(8,128)(2,1)S(1)} %collective-permute-done.3), channel_id=1, source_target_pairs={{0,6},{1,7},{2,4},{3,5},{4,2},{5,3},{6,0},{7,1},{8,14},{9,15},{10,... | collective-permute-start | bytes 215048 | tf_op jit(solution)/shard_map/ppermute | solution.py:287
  12.4 0.5 collective-permute-start.4
  12.9 0.7 %collective-permute-start.5 = (bf16[40,896]{1,0:T(8,128)(2,1)S(1)}, bf16[40,896]{1,0:T(8,128)(2,1)S(1)}, u32[]{:S(2)}, u32[]{:S(2)}) collective-permute-start(bf16[40,896]{1,0:T(8,128)(2,1)S(1)} %collective-permute-done.3), channel_id=1, source_target_pairs={{0,4},{1,5},{2,6},{3,7},{4,0},{5,1},{6,2},{7,3},{8,12},{9,13},{10,... | collective-permute-start | bytes 215048 | tf_op jit(solution)/shard_map/ppermute | solution.py:287
  13.6 1.4 %collective-permute-done.2 = bf16[40,896]{1,0:T(8,128)(2,1)S(1)} collective-permute-done((bf16[40,896]{1,0:T(8,128)(2,1)}, bf16[40,896]{1,0:T(8,128)(2,1)S(1)}, u32[]{:S(2)}, u32[]{:S(2)}) %collective-permute-start.2) | collective-permute-done | bytes 71712 | tf_op jit(solution)/shard_map/ppermute | solution.py:287
  15.0 0.9 %pad_maximum_fusion = bf16[4,40,896]{2,1,0:T(8,128)(2,1)S(1)} fusion(bf16[1,40,896]{2,1,0:T(8,128)(2,1)S(1)} %bitcast.25, bf16[1,40,896]{2,1,0:T(8,128)(2,1)S(1)} %bitcast.24, bf16[1,40,896]{2,1,0:T(8,128)(2,1)S(1)} %bitcast.23, bf16[1,40,896]{2,1,0:T(8,128)(2,1)} %bitcast.22), kind=kLoop, calls=%fused_computation | loop fusion | flops 430080 | bytes 573440 | tf_op jit(solution)/shard_map/stack | solution.py:288
  15.9 0.1 collective-permute-start.7
  16.0 0.3 collective-permute-done.6
  16.3 0.8 %collective-permute-done.4 = bf16[40,896]{1,0:T(8,128)(2,1)S(1)} collective-permute-done((bf16[40,896]{1,0:T(8,128)(2,1)S(1)}, bf16[40,896]{1,0:T(8,128)(2,1)S(1)}, u32[]{:S(2)}, u32[]{:S(2)}) %collective-permute-start.4) | collective-permute-done | bytes 71712 | tf_op jit(solution)/shard_map/ppermute | solution.py:287
  17.0 0.2 collective-permute-done.5
  17.3 0.1 collective-permute-start.8
  17.7 0.1 copy.17
  17.8 1.1 %collective-permute-done.8 = bf16[4,40,896]{2,1,0:T(8,128)(2,1)S(1)} collective-permute-done((bf16[4,40,896]{2,1,0:T(8,128)(2,1)S(1)}, bf16[4,40,896]{2,1,0:T(8,128)(2,1)S(1)}, u32[]{:S(2)}, u32[]{:S(2)}) %collective-permute-start.8) | collective-permute-done | bytes 286752 | tf_op jit(solution)/shard_map/ppermute | solution.py:289
  18.9 0.1 copy.18
  19.0 2.3 %concatenate.35 = bf16[16,8,5,896]{3,0,2,1:T(8,128)(2,1)S(1)} concatenate(bf16[1,8,5,896]{3,0,2,1:T(2,128)(2,1)S(1)} %concatenate.36, bf16[1,8,5,896]{3,0,2,1:T(2,128)(2,1)S(1)} %concatenate.37, bf16[1,8,5,896]{3,0,2,1:T(2,128)(2,1)S(1)} %concatenate.38, bf16[1,8,5,896]{3,0,2,1:T(2,128)(2,1)S(1)} %concatenate.39, bf16[1,8,5,896]{3,0,2,1:T(2,128)(2,1)S(1)} %concatenate.40, ...), dimensions={0} | concatenate | bytes 2293760 | tf_op jit(solution)/shard_map/concatenate | solution.py:291
  21.4 0.2 copy.27
  21.6 0.2 copy.28
  21.8 1.6 %copy-done = bf16[256,7168]{1,0:T(8,128)(2,1)S(1)} copy-done((bf16[256,7168]{1,0:T(8,128)(2,1)S(1)}, bf16[256,7168]{1,0:T(8,128)(2,1)}, u32[]{:S(2)}) %copy-start) | copy-done | bytes 3670040
  23.4 2.0 %copy-done.2 = bf16[7168,256]{1,0:T(8,128)(2,1)S(1)} copy-done((bf16[7168,256]{1,0:T(8,128)(2,1)S(1)}, bf16[7168,256]{1,0:T(8,128)(2,1)}, u32[]{:S(2)}) %copy-start.2) | copy-done | bytes 3670040
  25.5 2.0 %copy-done.3 = bf16[7168,256]{1,0:T(8,128)(2,1)S(1)} copy-done((bf16[7168,256]{1,0:T(8,128)(2,1)S(1)}, bf16[7168,256]{1,0:T(8,128)(2,1)}, u32[]{:S(2)}) %copy-start.3) | copy-done | bytes 3670040
  27.5 2.8 %expert_half.1 = (bf16[40,7168]{1,0:T(8,128)(2,1)S(1)}, bf16[40,256]{1,0:T(8,128)(2,1)S(1)}) custom-call(bf16[80,7168]{1,0:T(8,128)(2,1)S(1)} %bitcast.16, bf16[7168,256]{1,0:T(8,128)(2,1)S(1)} %copy-done.2, bf16[7168,256]{1,0:T(8,128)(2,1)S(1)} %copy-done.3, bf16[256,7168]{1,0:T(8,128)(2,1)S(1)} %copy-done), custom_call_target="tpu_custom_call" | custom-call | flops 734003200 | bytes 11010048 | tf_op jit(solution)/shard_map/expert_half/pallas_call | solution.py:150
  30.3 0.2 collective-permute-start.9
  30.5 0.6 %kept_half.1.kept_ref = f32[40,7168]{1,0:T(8,128)S(1)} custom-call(bf16[40,256]{1,0:T(8,128)(2,1)S(1)} %get-tuple-element.23.hidden_ref, bf16[256,7168]{1,0:T(8,128)(2,1)S(1)} %copy-done), custom_call_target="tpu_custom_call" | custom-call | flops 146800640 | bytes 3670016 | tf_op jit(solution)/shard_map/kept_half/pallas_call | solution.py:175
  31.2 1.0 %copy-done.1 = f32[40,7168]{1,0:T(8,128)} copy-done((f32[40,7168]{1,0:T(8,128)}, f32[40,7168]{1,0:T(8,128)S(1)}, u32[]{:S(2)}) %copy-start.1) | copy-done | bytes 1146904
  32.2 0.2 collective-permute-done.9.taken_ref
  32.4 0.8 %copy-done.7 = bf16[40,7168]{1,0:T(8,128)(2,1)} copy-done((bf16[40,7168]{1,0:T(8,128)(2,1)}, bf16[40,7168]{1,0:T(8,128)(2,1)S(1)}, u32[]{:S(2)}) %copy-start.7) | copy-done | bytes 573464
  33.2 2.5 %repack.1 = (f32[40,896]{1,0:T(8,128)}, bf16[40,896]{1,0:T(8,128)(2,1)}, bf16[40,896]{1,0:T(8,128)(2,1)}, bf16[40,896]{1,0:T(8,128)(2,1)}, f32[40,896]{1,0:T(8,1...) custom-call(f32[40,7168]{1,0:T(8,128)} %copy-done.1, bf16[40,7168]{1,0:T(8,128)(2,1)} %copy-done.7), custom_call_target="tpu_custom_call" | custom-call | tf_op jit(solution)/shard_map/repack/pallas_call | solution.py:209
  35.7 1.5 %collective-permute-start.13 = (bf16[40,896]{1,0:T(8,128)(2,1)}, bf16[40,896]{1,0:T(8,128)(2,1)S(1)}, u32[]{:S(2)}, u32[]{:S(2)}) collective-permute-start(bf16[40,896]{1,0:T(8,128)(2,1)} %get-tuple-element.30), channel_id=1, source_target_pairs={{0,2},{1,3},{2,0},{3,1},{4,6},{5,7},{6,4},{7,5},{8,10},{9,11},{10,... | collective-permute-start | bytes 215048 | tf_op jit(solution)/shard_map/ppermute | solution.py:304
  37.2 0.8 %collective-permute-start.14 = (bf16[40,896]{1,0:T(8,128)(2,1)}, bf16[40,896]{1,0:T(8,128)(2,1)S(1)}, u32[]{:S(2)}, u32[]{:S(2)}) collective-permute-start(bf16[40,896]{1,0:T(8,128)(2,1)} %get-tuple-element.31), channel_id=1, source_target_pairs={{0,4},{1,5},{2,6},{3,7},{4,0},{5,1},{6,2},{7,3},{8,12},{9,13},{10,... | collective-permute-start | bytes 215048 | tf_op jit(solution)/shard_map/ppermute | solution.py:304
  38.1 1.1 %collective-permute-start.15 = (bf16[40,896]{1,0:T(8,128)(2,1)}, bf16[40,896]{1,0:T(8,128)(2,1)S(1)}, u32[]{:S(2)}, u32[]{:S(2)}) collective-permute-start(bf16[40,896]{1,0:T(8,128)(2,1)} %get-tuple-element.32), channel_id=1, source_target_pairs={{0,6},{1,7},{2,4},{3,5},{4,2},{5,3},{6,0},{7,1},{8,14},{9,15},{10,... | collective-permute-start | bytes 215048 | tf_op jit(solution)/shard_map/ppermute | solution.py:304
  39.2 1.5 %collective-permute-start.10 = (bf16[40,896]{1,0:T(8,128)(2,1)}, bf16[40,896]{1,0:T(8,128)(2,1)S(1)}, u32[]{:S(2)}, u32[]{:S(2)}) collective-permute-start(bf16[40,896]{1,0:T(8,128)(2,1)} %get-tuple-element.26), channel_id=1, source_target_pairs={{0,2},{1,3},{2,0},{3,1},{4,6},{5,7},{6,4},{7,5},{8,10},{9,11},{10,... | collective-permute-start | bytes 215048 | tf_op jit(solution)/shard_map/ppermute | solution.py:304
  40.7 0.8 %collective-permute-start.11 = (bf16[40,896]{1,0:T(8,128)(2,1)}, bf16[40,896]{1,0:T(8,128)(2,1)S(1)}, u32[]{:S(2)}, u32[]{:S(2)}) collective-permute-start(bf16[40,896]{1,0:T(8,128)(2,1)} %get-tuple-element.27), channel_id=1, source_target_pairs={{0,4},{1,5},{2,6},{3,7},{4,0},{5,1},{6,2},{7,3},{8,12},{9,13},{10,... | collective-permute-start | bytes 215048 | tf_op jit(solution)/shard_map/ppermute | solution.py:304
  41.6 1.1 %collective-permute-start.12 = (bf16[40,896]{1,0:T(8,128)(2,1)}, bf16[40,896]{1,0:T(8,128)(2,1)S(1)}, u32[]{:S(2)}, u32[]{:S(2)}) collective-permute-start(bf16[40,896]{1,0:T(8,128)(2,1)} %get-tuple-element.28), channel_id=1, source_target_pairs={{0,6},{1,7},{2,4},{3,5},{4,2},{5,3},{6,0},{7,1},{8,14},{9,15},{10,... | collective-permute-start | bytes 215048 | tf_op jit(solution)/shard_map/ppermute | solution.py:304
  42.7 1.4 %collective-permute-done.15.refs_3_ = bf16[40,896]{1,0:T(8,128)(2,1)S(1)} collective-permute-done((bf16[40,896]{1,0:T(8,128)(2,1)}, bf16[40,896]{1,0:T(8,128)(2,1)S(1)}, u32[]{:S(2)}, u32[]{:S(2)}) %collective-permute-start.15) | collective-permute-done | bytes 71712 | tf_op jit(solution)/shard_map/ppermute | solution.py:304
  44.1 0.6 %copy-done.11 = bf16[40,896]{1,0:T(8,128)(2,1)} copy-done((bf16[40,896]{1,0:T(8,128)(2,1)}, bf16[40,896]{1,0:T(8,128)(2,1)S(1)}, u32[]{:S(2)}) %copy-start.11) | copy-done | bytes 71704
  44.7 1.7 %sum_blocks.1 = bf16[40,896]{1,0:T(8,128)(2,1)} custom-call(f32[40,896]{1,0:T(8,128)} %get-tuple-element.29.refs_0_, bf16[40,896]{1,0:T(8,128)(2,1)} %copy-done.9, bf16[40,896]{1,0:T(8,128)(2,1)} %copy-done.10, bf16[40,896]{1,0:T(8,128)(2,1)} %copy-done.11), custom_call_target="tpu_custom_call" | custom-call | tf_op jit(solution)/shard_map/sum_blocks/pallas_call | solution.py:226
  46.4 2.5 %collective-permute-start.16 = (bf16[40,896]{1,0:T(8,128)(2,1)}, bf16[40,896]{1,0:T(8,128)(2,1)S(1)}, u32[]{:S(2)}, u32[]{:S(2)}) collective-permute-start(bf16[40,896]{1,0:T(8,128)(2,1)} %sum_blocks.1), channel_id=1, source_target_pairs={{0,8},{1,9},{2,10},{3,11},{4,12},{5,13},{6,14},{7,15},{8,0},{9,1},... | collective-permute-start | bytes 215048 | tf_op jit(solution)/shard_map/ppermute | solution.py:307
  48.9 1.9 %blend_weights.1 = (bf16[2,512,40]{2,1,0:T(8,128)(2,1)}, bf16[2,512,40]{2,1,0:T(8,128)(2,1)}) custom-call(s32[8,64]{1,0:T(8,128)} %bitcast.30, f32[8,64]{1,0:T(8,128)} %bitcast.31), custom_call_target="tpu_custom_call" | custom-call | tf_op jit(solution)/shard_map/blend_weights/pallas_call | solution.py:107
  50.8 1.8 %collective-permute-done.16.refs_4_ = bf16[40,896]{1,0:T(8,128)(2,1)S(1)} collective-permute-done((bf16[40,896]{1,0:T(8,128)(2,1)}, bf16[40,896]{1,0:T(8,128)(2,1)S(1)}, u32[]{:S(2)}, u32[]{:S(2)}) %collective-permute-start.16) | collective-permute-done | bytes 71712 | tf_op jit(solution)/shard_map/ppermute | solution.py:307
  52.6 0.9 %copy-done.4 = bf16[2,512,40]{2,1,0:T(8,128)(2,1)S(1)} copy-done((bf16[2,512,40]{2,1,0:T(8,128)(2,1)S(1)}, bf16[2,512,40]{2,1,0:T(8,128)(2,1)}, u32[]{:S(2)}) %copy-start.4) | copy-done | bytes 81944
  53.5 0.9 %copy-done.5 = bf16[2,512,40]{2,1,0:T(8,128)(2,1)S(1)} copy-done((bf16[2,512,40]{2,1,0:T(8,128)(2,1)S(1)}, bf16[2,512,40]{2,1,0:T(8,128)(2,1)}, u32[]{:S(2)}) %copy-start.5) | copy-done | bytes 81944
  54.5 0.9 %copy-done.6 = f32[40,896]{1,0:T(8,128)S(1)} copy-done((f32[40,896]{1,0:T(8,128)S(1)}, f32[40,896]{1,0:T(8,128)}, u32[]{:S(2)}) %copy-start.6) | copy-done | bytes 143384
  55.4 2.3 %blend.1 = bf16[64,7168]{1,0:T(8,128)(2,1)} custom-call(bf16[2,512,40]{2,1,0:T(8,128)(2,1)S(1)} %copy-done.4, bf16[2,512,40]{2,1,0:T(8,128)(2,1)S(1)} %copy-done.5, f32[40,896]{1,0:T(8,128)S(1)} %copy-done.6, bf16[40,896]{1,0:T(8,128)(2,1)S(1)} %collective-permute-done.10.refs_1_, bf16[40,896]{1,0:T(8,128)(2,1)S(1)} %collective-permute-done.11.refs_2_, ...), custom_call_target="tpu_custom_call" | custom-call | tf_op jit(solution)/shard_map/blend/pallas_call | solution.py:259
  (32 shorter events, 0.3 us)
Async XLA Ops:
  2.3 15.0 %copy-start.8 = (bf16[40,896]{1,0:T(8,128)(2,1)S(1)}, bf16[40,896]{1,0:T(8,128)(2,1)}, u32[]{:S(2)}) copy-start(bf16[40,896]{1,0:T(8,128)(2,1)} %get-tuple-element.21) | copy-start | bytes 215044
  2.3 7.8 %collective-permute-start.3 = (bf16[40,896]{1,0:T(8,128)(2,1)}, bf16[40,896]{1,0:T(8,128)(2,1)S(1)}, u32[]{:S(2)}, u32[]{:S(2)}) collective-permute-start(bf16[40,896]{1,0:T(8,128)(2,1)} %get-tuple-element.22), channel_id=1, source_target_pairs={{0,8},{1,9},{2,10},{3,11},{4,12},{5,13},{6,14},{7,15},{8,0},{9,1},... | collective-permute-start | bytes 215048 | tf_op jit(solution)/shard_map/ppermute | solution.py:284
  6.4 6.5 %collective-permute-start = (bf16[40,896]{1,0:T(8,128)(2,1)}, bf16[40,896]{1,0:T(8,128)(2,1)S(1)}, u32[]{:S(2)}, u32[]{:S(2)}) collective-permute-start(bf16[40,896]{1,0:T(8,128)(2,1)} %get-tuple-element.21), channel_id=1, source_target_pairs={{0,2},{1,3},{2,0},{3,1},{4,6},{5,7},{6,4},{7,5},{8,10},{9,11},{10,... | collective-permute-start | bytes 215048 | tf_op jit(solution)/shard_map/ppermute | solution.py:287
  7.9 5.7 %collective-permute-start.1 = (bf16[40,896]{1,0:T(8,128)(2,1)}, bf16[40,896]{1,0:T(8,128)(2,1)S(1)}, u32[]{:S(2)}, u32[]{:S(2)}) collective-permute-start(bf16[40,896]{1,0:T(8,128)(2,1)} %get-tuple-element.21), channel_id=1, source_target_pairs={{0,4},{1,5},{2,6},{3,7},{4,0},{5,1},{6,2},{7,3},{8,12},{9,13},{10,... | collective-permute-start | bytes 215048 | tf_op jit(solution)/shard_map/ppermute | solution.py:287
  9.5 5.5 %collective-permute-start.2 = (bf16[40,896]{1,0:T(8,128)(2,1)}, bf16[40,896]{1,0:T(8,128)(2,1)S(1)}, u32[]{:S(2)}, u32[]{:S(2)}) collective-permute-start(bf16[40,896]{1,0:T(8,128)(2,1)} %get-tuple-element.21), channel_id=1, source_target_pairs={{0,6},{1,7},{2,4},{3,5},{4,2},{5,3},{6,0},{7,1},{8,14},{9,15},{10,... | collective-permute-start | bytes 215048 | tf_op jit(solution)/shard_map/ppermute | solution.py:287
  10.1 6.2 %collective-permute-start.6 = (bf16[40,896]{1,0:T(8,128)(2,1)S(1)}, bf16[40,896]{1,0:T(8,128)(2,1)S(1)}, u32[]{:S(2)}, u32[]{:S(2)}) collective-permute-start(bf16[40,896]{1,0:T(8,128)(2,1)S(1)} %collective-permute-done.3), channel_id=1, source_target_pairs={{0,6},{1,7},{2,4},{3,5},{4,2},{5,3},{6,0},{7,1},{8,14},{9,15},{10,... | collective-permute-start | bytes 215048 | tf_op jit(solution)/shard_map/ppermute | solution.py:287
  12.4 4.6 %collective-permute-start.4 = (bf16[40,896]{1,0:T(8,128)(2,1)S(1)}, bf16[40,896]{1,0:T(8,128)(2,1)S(1)}, u32[]{:S(2)}, u32[]{:S(2)}) collective-permute-start(bf16[40,896]{1,0:T(8,128)(2,1)S(1)} %collective-permute-done.3), channel_id=1, source_target_pairs={{0,2},{1,3},{2,0},{3,1},{4,6},{5,7},{6,4},{7,5},{8,10},{9,11},{10,... | collective-permute-start | bytes 215048 | tf_op jit(solution)/shard_map/ppermute | solution.py:287
  12.9 4.3 %collective-permute-start.5 = (bf16[40,896]{1,0:T(8,128)(2,1)S(1)}, bf16[40,896]{1,0:T(8,128)(2,1)S(1)}, u32[]{:S(2)}, u32[]{:S(2)}) collective-permute-start(bf16[40,896]{1,0:T(8,128)(2,1)S(1)} %collective-permute-done.3), channel_id=1, source_target_pairs={{0,4},{1,5},{2,6},{3,7},{4,0},{5,1},{6,2},{7,3},{8,12},{9,13},{10,... | collective-permute-start | bytes 215048 | tf_op jit(solution)/shard_map/ppermute | solution.py:287
  15.9 1.7 %collective-permute-start.7 = (bf16[4,40,896]{2,1,0:T(8,128)(2,1)S(1)}, bf16[4,40,896]{2,1,0:T(8,128)(2,1)S(1)}, u32[]{:S(2)}, u32[]{:S(2)}) collective-permute-start(bf16[4,40,896]{2,1,0:T(8,128)(2,1)S(1)} %pad_maximum_fusion), channel_id=1, source_target_pairs={{0,1},{1,0},{2,3},{3,2},{4,5},{5,4},{6,7},{7,6},{8,9},{9,8},{10,11... | collective-permute-start | bytes 860168 | tf_op jit(solution)/shard_map/ppermute | solution.py:289
  17.3 1.6 %collective-permute-start.8 = (bf16[4,40,896]{2,1,0:T(8,128)(2,1)S(1)}, bf16[4,40,896]{2,1,0:T(8,128)(2,1)S(1)}, u32[]{:S(2)}, u32[]{:S(2)}) collective-permute-start(bf16[4,40,896]{2,1,0:T(8,128)(2,1)S(1)} %pad_maximum_fusion.1), channel_id=1, source_target_pairs={{0,1},{1,0},{2,3},{3,2},{4,5},{5,4},{6,7},{7,6},{8,9},{9,8},{10,11... | collective-permute-start | bytes 860168 | tf_op jit(solution)/shard_map/ppermute | solution.py:289
  21.4 2.0 %copy-start = (bf16[256,7168]{1,0:T(8,128)(2,1)S(1)}, bf16[256,7168]{1,0:T(8,128)(2,1)}, u32[]{:S(2)}) copy-start(bf16[256,7168]{1,0:T(8,128)(2,1)} %down_ref.3) | copy-start | bytes 11010052
  23.4 2.0 %copy-start.2 = (bf16[7168,256]{1,0:T(8,128)(2,1)S(1)}, bf16[7168,256]{1,0:T(8,128)(2,1)}, u32[]{:S(2)}) copy-start(bf16[7168,256]{1,0:T(8,128)(2,1)} %gate_ref.1) | copy-start | bytes 11010052
  25.5 2.0 %copy-start.3 = (bf16[7168,256]{1,0:T(8,128)(2,1)S(1)}, bf16[7168,256]{1,0:T(8,128)(2,1)}, u32[]{:S(2)}) copy-start(bf16[7168,256]{1,0:T(8,128)(2,1)} %up_ref.1) | copy-start | bytes 11010052
  30.3 2.0 %collective-permute-start.9 = (bf16[40,7168]{1,0:T(8,128)(2,1)S(1)}, bf16[40,7168]{1,0:T(8,128)(2,1)S(1)}, u32[]{:S(2)}, u32[]{:S(2)}) collective-permute-start(bf16[40,7168]{1,0:T(8,128)(2,1)S(1)} %get-tuple-element.24), channel_id=1, source_target_pairs={{0,1},{1,0},{2,3},{3,2},{4,5},{5,4},{6,7},{7,6},{8,9},{9,8},{10,11... | collective-permute-start | bytes 1720328 | tf_op jit(solution)/shard_map/ppermute | solution.py:296
  31.2 1.0 %copy-start.1 = (f32[40,7168]{1,0:T(8,128)}, f32[40,7168]{1,0:T(8,128)S(1)}, u32[]{:S(2)}) copy-start(f32[40,7168]{1,0:T(8,128)S(1)} %kept_half.1.kept_ref) | copy-start | bytes 3440644
  32.4 0.8 %copy-start.7 = (bf16[40,7168]{1,0:T(8,128)(2,1)}, bf16[40,7168]{1,0:T(8,128)(2,1)S(1)}, u32[]{:S(2)}) copy-start(bf16[40,7168]{1,0:T(8,128)(2,1)S(1)} %collective-permute-done.9.taken_ref) | copy-start | bytes 1720324
  35.7 5.8 %collective-permute-start.13 = (bf16[40,896]{1,0:T(8,128)(2,1)}, bf16[40,896]{1,0:T(8,128)(2,1)S(1)}, u32[]{:S(2)}, u32[]{:S(2)}) collective-permute-start(bf16[40,896]{1,0:T(8,128)(2,1)} %get-tuple-element.30), channel_id=1, source_target_pairs={{0,2},{1,3},{2,0},{3,1},{4,6},{5,7},{6,4},{7,5},{8,10},{9,11},{10,... | collective-permute-start | bytes 215048 | tf_op jit(solution)/shard_map/ppermute | solution.py:304
  37.2 5.5 %collective-permute-start.14 = (bf16[40,896]{1,0:T(8,128)(2,1)}, bf16[40,896]{1,0:T(8,128)(2,1)S(1)}, u32[]{:S(2)}, u32[]{:S(2)}) collective-permute-start(bf16[40,896]{1,0:T(8,128)(2,1)} %get-tuple-element.31), channel_id=1, source_target_pairs={{0,4},{1,5},{2,6},{3,7},{4,0},{5,1},{6,2},{7,3},{8,12},{9,13},{10,... | collective-permute-start | bytes 215048 | tf_op jit(solution)/shard_map/ppermute | solution.py:304
  38.1 6.0 %collective-permute-start.15 = (bf16[40,896]{1,0:T(8,128)(2,1)}, bf16[40,896]{1,0:T(8,128)(2,1)S(1)}, u32[]{:S(2)}, u32[]{:S(2)}) collective-permute-start(bf16[40,896]{1,0:T(8,128)(2,1)} %get-tuple-element.32), channel_id=1, source_target_pairs={{0,6},{1,7},{2,4},{3,5},{4,2},{5,3},{6,0},{7,1},{8,14},{9,15},{10,... | collective-permute-start | bytes 215048 | tf_op jit(solution)/shard_map/ppermute | solution.py:304
  39.2 11.6 %collective-permute-start.10 = (bf16[40,896]{1,0:T(8,128)(2,1)}, bf16[40,896]{1,0:T(8,128)(2,1)S(1)}, u32[]{:S(2)}, u32[]{:S(2)}) collective-permute-start(bf16[40,896]{1,0:T(8,128)(2,1)} %get-tuple-element.26), channel_id=1, source_target_pairs={{0,2},{1,3},{2,0},{3,1},{4,6},{5,7},{6,4},{7,5},{8,10},{9,11},{10,... | collective-permute-start | bytes 215048 | tf_op jit(solution)/shard_map/ppermute | solution.py:304
  40.7 10.1 %collective-permute-start.11 = (bf16[40,896]{1,0:T(8,128)(2,1)}, bf16[40,896]{1,0:T(8,128)(2,1)S(1)}, u32[]{:S(2)}, u32[]{:S(2)}) collective-permute-start(bf16[40,896]{1,0:T(8,128)(2,1)} %get-tuple-element.27), channel_id=1, source_target_pairs={{0,4},{1,5},{2,6},{3,7},{4,0},{5,1},{6,2},{7,3},{8,12},{9,13},{10,... | collective-permute-start | bytes 215048 | tf_op jit(solution)/shard_map/ppermute | solution.py:304
  41.6 2.5 %copy-start.9 = (bf16[40,896]{1,0:T(8,128)(2,1)}, bf16[40,896]{1,0:T(8,128)(2,1)S(1)}, u32[]{:S(2)}) copy-start(bf16[40,896]{1,0:T(8,128)(2,1)S(1)} %collective-permute-done.13.refs_1_) | copy-start | bytes 215044
  41.6 9.2 %collective-permute-start.12 = (bf16[40,896]{1,0:T(8,128)(2,1)}, bf16[40,896]{1,0:T(8,128)(2,1)S(1)}, u32[]{:S(2)}, u32[]{:S(2)}) collective-permute-start(bf16[40,896]{1,0:T(8,128)(2,1)} %get-tuple-element.28), channel_id=1, source_target_pairs={{0,6},{1,7},{2,4},{3,5},{4,2},{5,3},{6,0},{7,1},{8,14},{9,15},{10,... | collective-permute-start | bytes 215048 | tf_op jit(solution)/shard_map/ppermute | solution.py:304
  42.7 1.4 %copy-start.10 = (bf16[40,896]{1,0:T(8,128)(2,1)}, bf16[40,896]{1,0:T(8,128)(2,1)S(1)}, u32[]{:S(2)}) copy-start(bf16[40,896]{1,0:T(8,128)(2,1)S(1)} %collective-permute-done.14.refs_2_) | copy-start | bytes 215044
  44.1 0.6 %copy-start.11 = (bf16[40,896]{1,0:T(8,128)(2,1)}, bf16[40,896]{1,0:T(8,128)(2,1)S(1)}, u32[]{:S(2)}) copy-start(bf16[40,896]{1,0:T(8,128)(2,1)S(1)} %collective-permute-done.15.refs_3_) | copy-start | bytes 215044
  46.4 6.2 %collective-permute-start.16 = (bf16[40,896]{1,0:T(8,128)(2,1)}, bf16[40,896]{1,0:T(8,128)(2,1)S(1)}, u32[]{:S(2)}, u32[]{:S(2)}) collective-permute-start(bf16[40,896]{1,0:T(8,128)(2,1)} %sum_blocks.1), channel_id=1, source_target_pairs={{0,8},{1,9},{2,10},{3,11},{4,12},{5,13},{6,14},{7,15},{8,0},{9,1},... | collective-permute-start | bytes 215048 | tf_op jit(solution)/shard_map/ppermute | solution.py:307
  52.6 1.0 %copy-start.4 = (bf16[2,512,40]{2,1,0:T(8,128)(2,1)S(1)}, bf16[2,512,40]{2,1,0:T(8,128)(2,1)}, u32[]{:S(2)}) copy-start(bf16[2,512,40]{2,1,0:T(8,128)(2,1)} %get-tuple-element.19.high_ref) | copy-start | bytes 245764
  53.5 0.9 %copy-start.5 = (bf16[2,512,40]{2,1,0:T(8,128)(2,1)S(1)}, bf16[2,512,40]{2,1,0:T(8,128)(2,1)}, u32[]{:S(2)}) copy-start(bf16[2,512,40]{2,1,0:T(8,128)(2,1)} %get-tuple-element.20.low_ref) | copy-start | bytes 245764
  54.5 0.9 %copy-start.6 = (f32[40,896]{1,0:T(8,128)S(1)}, f32[40,896]{1,0:T(8,128)}, u32[]{:S(2)}) copy-start(f32[40,896]{1,0:T(8,128)} %get-tuple-element.25.refs_0_) | copy-start | bytes 430084

commit v5 on v4

v5 whole, which is shorter than its diff:
```python
import functools

import jax
import jax.numpy as jnp
from jax import lax
from jax.experimental import pallas as pl
from jax.experimental.pallas import tpu as pltpu
from jax.sharding import PartitionSpec as P

SPLIT = 8
CAP = 5
CORES = 2
SEGMENTS = 8

route_scale = 2.5

VMEM = pl.BlockSpec(memory_space=pltpu.VMEM)
MIB = 1024 * 1024


def hits(ids, mine, teams):
    count = ids.shape[1]
    row = lax.broadcasted_iota(jnp.int32, (8 * pl.cdiv(teams, 8), count), 0)
    wanted = lax.rem(mine + row, teams)
    hit = jnp.zeros(row.shape, jnp.int32)
    for j in range(ids.shape[0]):
        hit = hit + jnp.where(ids[j : j + 1, :] == wanted, 1, 0)
    hit = jnp.where(row < teams, hit, 0).astype(jnp.float32)
    before = lax.broadcasted_iota(jnp.int32, (count, count), 0)
    after = lax.broadcasted_iota(jnp.int32, (count, count), 1)
    earlier = jnp.where(before < after, 1.0, 0.0).astype(jnp.bfloat16)
    slot = jnp.dot(hit.astype(jnp.bfloat16), earlier, preferred_element_type=jnp.float32)
    return hit, jnp.where(hit > 0, slot, -1.0)


def fifth(shape, axis):
    at = lax.broadcasted_iota(jnp.int32, shape, axis)
    segment = jnp.zeros(shape, jnp.int32)
    for s in range(1, SEGMENTS):
        segment = segment + jnp.where(at >= s * CAP, 1, 0)
    return segment, (at - CAP * segment).astype(jnp.float32)


def params(mib):
    return pltpu.CompilerParams(vmem_limit_bytes=mib * MIB)


def pack_kernel(teams, ids_ref, tokens_ref, *out_refs):
    mine = lax.axis_index("expert") // SPLIT
    _, slot = hits(ids_ref[...], mine, teams)
    count, features = tokens_ref.shape
    wide = features // SEGMENTS
    tall = CAP * SEGMENTS
    stacked = jnp.concatenate(
        [tokens_ref[:, s * wide : (s + 1) * wide] for s in range(SEGMENTS)], axis=0
    )
    segment, place = fifth((tall, 1), 0)
    column = lax.broadcasted_iota(jnp.int32, (1, SEGMENTS * count), 1)
    same = segment == column // count
    picks = []
    for k in range(teams):
        slots = jnp.concatenate([slot[k : k + 1, :]] * SEGMENTS, axis=1)
        picks.append(jnp.where(same & (slots == place), 1.0, 0.0))
    packed = jnp.dot(
        jnp.concatenate(picks, axis=0).astype(jnp.bfloat16),
        stacked,
        preferred_element_type=jnp.float32,
    )
    for k in range(teams):
        out_refs[k][...] = packed[k * tall : (k + 1) * tall].astype(jnp.bfloat16)


def pack_rows(ids, tokens, teams):
    wide = tokens.shape[1] // SEGMENTS
    block = jax.ShapeDtypeStruct((CAP * SEGMENTS, wide), jnp.bfloat16)
    return pl.pallas_call(
        functools.partial(pack_kernel, teams),
        out_shape=[block] * teams,
        in_specs=[VMEM, VMEM],
        out_specs=[VMEM] * teams,
        compiler_params=params(8),
        name="pack_rows",
    )(ids, tokens)


def weight_kernel(teams, ids_ref, logits_ref, out_ref):
    mine = lax.axis_index("expert") // SPLIT
    ids = ids_ref[...]
    hit, slot = hits(ids, mine, teams)
    count = ids.shape[1]
    lifted = jax.nn.sigmoid(logits_ref[...])
    gates = route_scale * lifted / jnp.sum(lifted, axis=0, keepdims=True)
    row = lax.broadcasted_iota(jnp.int32, hit.shape, 0)
    wanted = lax.rem(mine + row, teams)
    gate = jnp.zeros(hit.shape, jnp.float32)
    for j in range(ids.shape[0]):
        gate = gate + jnp.where(ids[j : j + 1, :] == wanted, gates[j : j + 1, :], 0.0)
    slot = jnp.transpose(slot)
    gate = jnp.transpose(gate)
    tall = CAP * SEGMENTS
    depth = out_ref.shape[1]
    column = lax.broadcasted_iota(jnp.int32, (1, depth), 1)
    part = jnp.zeros((1, depth), jnp.int32)
    for g in range(1, depth // tall):
        part = part + jnp.where(column >= g * tall, 1, 0)
    column = column - tall * part
    segment = jnp.zeros((1, depth), jnp.int32)
    for s in range(1, SEGMENTS):
        segment = segment + jnp.where(column >= s * CAP, 1, 0)
    place = (column - CAP * segment).astype(jnp.float32)
    team = jnp.where(part < 3, 0, (part - 1) >> 1)
    low = jnp.where(part < 3, part >> 1, (part - 3) & 1) == 1
    for s in range(SEGMENTS):
        full = jnp.zeros((count, depth), jnp.float32)
        for k in range(teams):
            chosen = (team == k) & (segment == s) & (slot[:, k : k + 1] == place)
            full = full + jnp.where(chosen, gate[:, k : k + 1], 0.0)
        high = full.astype(jnp.bfloat16).astype(jnp.float32)
        out_ref[s * count : (s + 1) * count, :] = jnp.where(low, full - high, high).astype(
            jnp.bfloat16
        )


def blend_weights(ids, logits, teams):
    shape = (SEGMENTS * ids.shape[1], CAP * SEGMENTS * (1 + 2 * teams))
    return pl.pallas_call(
        functools.partial(weight_kernel, teams),
        out_shape=jax.ShapeDtypeStruct(shape, jnp.bfloat16),
        in_specs=[VMEM, VMEM],
        out_specs=VMEM,
        compiler_params=params(4 + teams),
        name="blend_weights",
    )(ids, logits)


def join_kernel(*refs):
    tall = refs[0].shape[0]
    for i, ref in enumerate(refs[:-1]):
        refs[-1][i * tall : (i + 1) * tall, :] = ref[...]


def join(blocks):
    tall, wide = blocks[0].shape
    return pl.pallas_call(
        join_kernel,
        out_shape=jax.ShapeDtypeStruct((tall * len(blocks), wide), blocks[0].dtype),
        in_specs=[VMEM] * len(blocks),
        out_specs=VMEM,
        compiler_params=params(4),
        name="join",
    )(*blocks)


def packed_down(hidden, down_ref, out_ref, flat):
    count, wide = flat.shape[1:]
    tall = CAP * SEGMENTS
    for s in range(SEGMENTS):
        slot = flat.at[s % 2]
        slot[...] = jnp.dot(
            hidden, down_ref[:, s * wide : (s + 1) * wide], preferred_element_type=jnp.float32
        )
        for b in range(count // CAP):
            start = b * tall + s * CAP
            out_ref[start : start + CAP, :] = slot[b * CAP : (b + 1) * CAP, :]


def expert_kernel(own, *refs):
    blocks, joined = refs[:own], refs[own : own + own // (SPLIT // CORES)]
    gate_ref, up_ref, down_ref, given_ref, hidden_ref, packed, flat, out = refs[-8:]
    tall = CAP * SEGMENTS
    wide = packed.shape[1]
    units = gate_ref.shape[1]
    for b, ref in enumerate(blocks):
        packed[b * tall : (b + 1) * tall, :] = ref[...].astype(jnp.float32)
    start = own * tall
    for ref in joined:
        packed[start : start + ref.shape[0], :] = ref[...].astype(jnp.float32)
        start += ref.shape[0]
    count = 2 * own * CAP
    gate_act = jnp.zeros((count, units), jnp.float32)
    up_act = jnp.zeros((count, units), jnp.float32)
    for s in range(SEGMENTS):
        slot = flat.at[s % 2]
        for b in range(2 * own):
            start = b * tall + s * CAP
            slot[b * CAP : (b + 1) * CAP, :] = packed[start : start + CAP, :]
        rows = slot[...].astype(jnp.bfloat16)
        columns = slice(s * wide, (s + 1) * wide)
        gate_act += jnp.dot(rows, gate_ref[columns, :], preferred_element_type=jnp.float32)
        up_act += jnp.dot(rows, up_ref[columns, :], preferred_element_type=jnp.float32)
    hidden = (jax.nn.silu(gate_act) * up_act).astype(jnp.bfloat16)
    half = count // 2
    hidden_ref[...] = hidden[:half]
    packed_down(hidden[half:], down_ref, out, flat.at[:, :half, :])
    given_ref[...] = out[...].astype(jnp.bfloat16)


def expert_half(blocks, joined, w_gate, w_up, w_down):
    own = len(blocks)
    tall, wide = blocks[0].shape
    features, units = w_gate.shape
    rows = 2 * own * CAP
    return pl.pallas_call(
        functools.partial(expert_kernel, own),
        out_shape=[
            jax.ShapeDtypeStruct((own * tall, wide), jnp.bfloat16),
            jax.ShapeDtypeStruct((own * CAP, units), jnp.bfloat16),
        ],
        in_specs=[VMEM] * (own + len(joined) + 3),
        out_specs=[VMEM] * 2,
        scratch_shapes=[
            pltpu.VMEM((2 * own * tall, wide), jnp.float32),
            pltpu.VMEM((2, rows, wide), jnp.float32),
            pltpu.VMEM((own * tall, wide), jnp.float32),
        ],
        compiler_params=params(16 + own),
        cost_estimate=pl.CostEstimate(
            flops=5 * rows * units * features,
            bytes_accessed=6 * features * units,
            transcendentals=rows * units,
        ),
        name="expert_half",
    )(*blocks, *joined, w_gate, w_up, w_down)


def kept_kernel(hidden_ref, down_ref, kept_ref, flat):
    packed_down(hidden_ref[...], down_ref, kept_ref, flat)


def kept_half(hidden, w_down):
    count, units = hidden.shape
    features = w_down.shape[1]
    wide = features // SEGMENTS
    return pl.pallas_call(
        kept_kernel,
        out_shape=jax.ShapeDtypeStruct((count * SEGMENTS, wide), jnp.float32),
        in_specs=[VMEM] * 2,
        out_specs=VMEM,
        scratch_shapes=[pltpu.VMEM((2, count, wide), jnp.float32)],
        compiler_params=params(8 + count // 10),
        cost_estimate=pl.CostEstimate(
            flops=2 * count * units * features,
            bytes_accessed=2 * features * units,
            transcendentals=0,
        ),
        name="kept_half",
    )(hidden, w_down)


def add_kernel(kept_ref, taken_ref, *out_refs):
    tall = out_refs[0].shape[0]
    for b, out_ref in enumerate(out_refs):
        rows = slice(b * tall, (b + 1) * tall)
        total = kept_ref[rows, :] + taken_ref[rows, :].astype(jnp.float32)
        out_ref[...] = total.astype(out_ref.dtype)


def add_cores(kept, taken, teams, chips):
    shape = (CAP * SEGMENTS, kept.shape[1])
    outs = [
        jax.ShapeDtypeStruct(shape, jnp.bfloat16 if m else jnp.float32)
        for k in range(teams)
        for m in range(chips)
    ]
    return pl.pallas_call(
        add_kernel,
        out_shape=outs,
        in_specs=[VMEM] * 2,
        out_specs=[VMEM] * len(outs),
        compiler_params=params(4 + 4 * teams),
        name="add_cores",
    )(kept, taken)


def sum_kernel(*refs):
    total = refs[0][...]
    for ref in refs[1:-1]:
        total = total + ref[...].astype(jnp.float32)
    refs[-1][...] = total.astype(refs[-1].dtype)


def sum_blocks(blocks):
    return pl.pallas_call(
        sum_kernel,
        out_shape=jax.ShapeDtypeStruct(blocks[0].shape, jnp.bfloat16),
        in_specs=[VMEM] * len(blocks),
        out_specs=VMEM,
        compiler_params=params(4),
        name="sum_blocks",
    )(*blocks)


def blend_kernel(chips, weight_ref, *refs):
    out_ref = refs[-1]
    count, features = out_ref.shape
    wide = features // SEGMENTS
    own = refs[0][...]
    for ref in refs[1:chips]:
        own = own + ref[...].astype(jnp.float32)
    high = own.astype(jnp.bfloat16).astype(jnp.float32)
    terms = [high, own - high, high]
    for ref in refs[chips:-1]:
        terms += [ref[...].astype(jnp.float32)] * 2
    rows = jnp.concatenate(terms, axis=0).astype(jnp.bfloat16)
    total = jnp.dot(weight_ref[...], rows, preferred_element_type=jnp.float32)
    for s in range(SEGMENTS):
        out_ref[:, s * wide : (s + 1) * wide] = total[s * count : (s + 1) * count].astype(
            jnp.bfloat16
        )


def blend(weights, own_blocks, other_blocks, count):
    chips = len(own_blocks)
    features = own_blocks[0].shape[1] * SEGMENTS
    return pl.pallas_call(
        functools.partial(blend_kernel, chips),
        out_shape=jax.ShapeDtypeStruct((count, features), jnp.bfloat16),
        in_specs=[VMEM] * (1 + chips + len(other_blocks)),
        out_specs=VMEM,
        compiler_params=params(16),
        name="blend",
    )(weights, *own_blocks, *other_blocks)


def body(tokens, expert_ids, route_logits, w_gate, w_up, w_down):
    devices = lax.axis_size("expert")
    teams = devices // SPLIT
    chips = SPLIT // CORES
    other_core = [(i, i ^ 1) for i in range(devices)]
    other_chip = [[(i, i ^ (m * CORES)) for i in range(devices)] for m in range(chips)]
    ids = expert_ids.T
    packed = pack_rows(ids, tokens, teams)
    ids, logits, packed = lax.optimization_barrier((ids, route_logits.T, packed))
    weights = blend_weights(ids, logits, teams)
    arrived = [packed[0]]
    for k in range(1, teams):
        pairs = [(i, (i + k * SPLIT) % devices) for i in range(devices)]
        arrived.append(lax.ppermute(packed[k], "expert", pairs))
    *arrived[1:], weights = lax.optimization_barrier((*arrived[1:], weights))
    blocks, swapped = [], []
    for block in arrived:
        team = [block]
        for m in range(1, chips):
            team.append(lax.ppermute(block, "expert", other_chip[m]))
        blocks += team
        swapped.append(lax.ppermute(join(team), "expert", other_core))
    given, hidden = expert_half(blocks, swapped, w_gate, w_up, w_down)
    taken = lax.ppermute(given, "expert", other_core)
    kept = kept_half(hidden, w_down)
    parts = add_cores(kept, taken, teams, chips)
    others = []
    for k in range(1, teams):
        team = [parts[k * chips]]
        for m in range(1, chips):
            team.append(lax.ppermute(parts[k * chips + m], "expert", other_chip[m]))
        pairs = [(i, (i - k * SPLIT) % devices) for i in range(devices)]
        total, parts = lax.optimization_barrier((sum_blocks(team), parts))
        others.append(lax.ppermute(total, "expert", pairs))
    own = [parts[0]]
    for m in range(1, chips):
        own.append(lax.ppermute(parts[m], "expert", other_chip[m]))
    return blend(weights, own, others, tokens.shape[0])


def solution(mesh):
    placed = (
        P(("groups", "expert"), None),
        P(("groups", "expert"), None),
        P(("groups", "expert"), None),
        P(None, "expert"),
        P(None, "expert"),
        P("expert", None),
    )
    return jax.shard_map(
        body, mesh=mesh, in_specs=placed, out_specs=P(("groups", "expert"), None), check_vma=False
    )
```

time: 58.1 us -> 48.8 us (0.84)
  Pallas kernels: 14.1 us -> 5.68 us
  waiting for transfers between devices: 7.4 us -> 13.8 us
  local copies, waits for them, and re-layouts: 14.1 us -> 8.67 us
  other arithmetic: 0.98 us -> 0 us
    pallas_call x4 -> x6, Pallas kernels: 7.86 us -> 3.79 us  [the longest x1 2.51 us: expert_half(): pl.pallas_call(functools.partial(expert_kernel, own), out_shape=[jax.Shap...]
    ppermute x6 -> x3, starting transfers between devices: 6.98 us -> 3.55 us  [body(): team.append(lax.ppermute(parts[k * chips + m], 'expert', other_chip[m]))]
    ppermute x4 -> x7, starting transfers between devices: 6.69 us -> 9.47 us  [the longest x1 4.1 us: body(): arrived.append(lax.ppermute(packed[k], 'expert', pairs))]
    concatenate x9 -> x0, local copies, waits for them, and re-layouts: 2.59 us -> none  [body(): both = jnp.concatenate(blocks + swapped, axis=0)]
    unnamed x25 -> x12, local copies, waits for them, and re-layouts: 11.1 us -> 8.67 us
    ppermute x6 -> x3, waiting for transfers between devices: 1.4 us -> 3.84 us  [body(): team.append(lax.ppermute(parts[k * chips + m], 'expert', other_chip[m]))]
    ppermute x4 -> x7, waiting for transfers between devices: 3.18 us -> 5.11 us  [the longest x3 2.28 us: body(): own.append(lax.ppermute(parts[m], 'expert', other_chip[m]))]
    pallas_call x1, Pallas kernels: 2.32 us -> 0.47 us  [pack_rows(): pl.pallas_call(functools.partial(pack_kernel, teams), out_shape=[block] *...]
  transfers between devices with their start and end apart: 17 -> 17, of which waited for: 9 -> 11; matrix products, arithmetic and copies ran while one was open for 2% -> 0% of each run, Pallas kernels for 7% -> 2%
where the time goes in v5:
time: 48.8 us; the launch traced here: 48.5 us
  starting transfers between devices  20.3 us (42%)
  waiting for transfers between devices  13.8 us (28%)
  local copies, waits for them, and re-layouts  8.67 us (18%)
  Pallas kernels  5.68 us (12%)
    unnamed x12, local copies, waits for them, and re-layouts  8.67 us
    ppermute x6, starting transfers between devices, body(): team.append(lax.ppermute(block, 'expert', other_chip[m]))  7.04 us
    ppermute x1, starting transfers between devices, body(): arrived.append(lax.ppermute(packed[k], 'expert', pairs))  4.1 us
    ppermute x3, waiting for transfers between devices, body(): team.append(lax.ppermute(parts[k * chips + m], 'expert', other_chip[m]))  3.84 us
    ppermute x6, waiting for transfers between devices, body(): team.append(lax.ppermute(block, 'expert', other_chip[m]))  3.72 us
    ppermute x3, starting transfers between devices, body(): team.append(lax.ppermute(parts[k * chips + m], 'expert', other_chip[m]))  3.55 us
    ppermute x3, starting transfers between devices, body(): own.append(lax.ppermute(parts[m], 'expert', other_chip[m]))  3.55 us
    pallas_call x1, Pallas kernels, expert_half(): pl.pallas_call(functools.partial(expert_kernel, own), out_shape=[jax.Shap...  2.51 us
  transfers between devices with their start and end apart: 17, of which 11 were waited for; matrix products, arithmetic and copies ran while one was open for 0% of the time, Pallas kernels for 2%

profile of v5, /device:TPU:0, one launch (start us, length us, event | category | flops | bytes accessed | tf_op | source)
XLA Modules:
  0.0 48.5 jit_solution(6486452634796843322)
XLA Ops:
  0.0 0.0 copy-start.3
  0.0 1.2 %copy-done.3 = bf16[64,7168]{1,0:T(8,128)(2,1)S(1)} copy-done((bf16[64,7168]{1,0:T(8,128)(2,1)S(1)}, bf16[64,7168]{1,0:T(8,128)(2,1)}, u32[]{:S(2)}) %copy-start.3) | copy-done | bytes 917528
  1.2 0.0 copy-start.4
  1.2 0.7 %copy-done.4 = s32[64,8]{0,1:T(8,128)S(1)} copy-done((s32[64,8]{0,1:T(8,128)S(1)}, s32[64,8]{0,1:T(8,128)}, u32[]{:S(2)}) %copy-start.4) | copy-done | bytes 2072
  1.9 0.5 pack_rows.1
  2.3 4.1 %collective-permute-start = (bf16[40,896]{1,0:T(8,128)(2,1)S(1)}, bf16[40,896]{1,0:T(8,128)(2,1)S(1)}, u32[]{:S(2)}, u32[]{:S(2)}) collective-permute-start(bf16[40,896]{1,0:T(8,128)(2,1)S(1)} %get-tuple-element.30), channel_id=1, source_target_pairs={{0,8},{1,9},{2,10},{3,11},{4,12},{5,13},{6,14},{7,15},{8,0},{9,1},... | collective-permute-start | bytes 215048 | tf_op jit(solution)/shard_map/ppermute | solution.py:338
  6.4 2.5 %collective-permute-start.3 = (bf16[40,896]{1,0:T(8,128)(2,1)S(1)}, bf16[40,896]{1,0:T(8,128)(2,1)S(1)}, u32[]{:S(2)}, u32[]{:S(2)}) collective-permute-start(bf16[40,896]{1,0:T(8,128)(2,1)S(1)} %get-tuple-element.34.refs_0_), channel_id=1, source_target_pairs={{0,6},{1,7},{2,4},{3,5},{4,2},{5,3},{6,0},{7,1},{8,14},{9,15},{10,... | collective-permute-start | bytes 215048 | tf_op jit(solution)/shard_map/ppermute | solution.py:344
  9.0 0.4 collective-permute-start.2
  9.4 0.5 %collective-permute-start.1 = (bf16[40,896]{1,0:T(8,128)(2,1)S(1)}, bf16[40,896]{1,0:T(8,128)(2,1)S(1)}, u32[]{:S(2)}, u32[]{:S(2)}) collective-permute-start(bf16[40,896]{1,0:T(8,128)(2,1)S(1)} %get-tuple-element.34.refs_0_), channel_id=1, source_target_pairs={{0,2},{1,3},{2,0},{3,1},{4,6},{5,7},{6,4},{7,5},{8,10},{9,11},{10,... | collective-permute-start | bytes 215048 | tf_op jit(solution)/shard_map/ppermute | solution.py:344
  9.9 0.7 %copy-done.5 = f32[64,8]{0,1:T(8,128)S(1)} copy-done((f32[64,8]{0,1:T(8,128)S(1)}, f32[64,8]{0,1:T(8,128)}, u32[]{:S(2)}) %copy-start.5) | copy-done | bytes 2072
  10.6 0.4 blend_weights.1.weight_ref
  11.1 0.0 collective-permute-done.refs_0_.refs_4_
  11.1 2.6 %collective-permute-start.6 = (bf16[40,896]{1,0:T(8,128)(2,1)S(1)}, bf16[40,896]{1,0:T(8,128)(2,1)S(1)}, u32[]{:S(2)}, u32[]{:S(2)}) collective-permute-start(bf16[40,896]{1,0:T(8,128)(2,1)S(1)} %collective-permute-done.refs_0_.refs_4_), channel_id=1, source_target_pairs={{0,6},{1,7},{2,4},{3,5},{4,2},{5,3},{6,0},{7,1},{8,14},{9,15},{10,... | collective-permute-start | bytes 215048 | tf_op jit(solution)/shard_map/ppermute | solution.py:344
  13.7 0.4 collective-permute-start.5
  14.1 0.0 collective-permute-done.3.refs_3_
  14.1 0.5 %collective-permute-start.4 = (bf16[40,896]{1,0:T(8,128)(2,1)S(1)}, bf16[40,896]{1,0:T(8,128)(2,1)S(1)}, u32[]{:S(2)}, u32[]{:S(2)}) collective-permute-start(bf16[40,896]{1,0:T(8,128)(2,1)S(1)} %collective-permute-done.refs_0_.refs_4_), channel_id=1, source_target_pairs={{0,2},{1,3},{2,0},{3,1},{4,6},{5,7},{6,4},{7,5},{8,10},{9,11},{10,... | collective-permute-start | bytes 215048 | tf_op jit(solution)/shard_map/ppermute | solution.py:344
  14.6 0.0 collective-permute-done.2.refs_2_
  14.6 0.0 collective-permute-done.1.refs_1_
  14.7 0.1 collective-permute-start.7
  14.7 1.7 %collective-permute-done.6.refs_3_.refs_7_ = bf16[40,896]{1,0:T(8,128)(2,1)S(1)} collective-permute-done((bf16[40,896]{1,0:T(8,128)(2,1)S(1)}, bf16[40,896]{1,0:T(8,128)(2,1)S(1)}, u32[]{:S(2)}, u32[]{:S(2)}) %collective-permute-start.6) | collective-permute-done | bytes 71712 | tf_op jit(solution)/shard_map/ppermute | solution.py:344
  16.4 1.6 %collective-permute-done.5.refs_2_.refs_6_ = bf16[40,896]{1,0:T(8,128)(2,1)S(1)} collective-permute-done((bf16[40,896]{1,0:T(8,128)(2,1)S(1)}, bf16[40,896]{1,0:T(8,128)(2,1)S(1)}, u32[]{:S(2)}, u32[]{:S(2)}) %collective-permute-start.5) | collective-permute-done | bytes 71712 | tf_op jit(solution)/shard_map/ppermute | solution.py:344
  18.0 0.5 collective-permute-done.4.refs_1_.refs_5_
  18.5 0.1 collective-permute-start.8
  18.6 0.0 collective-permute-done.7.refs_8_
  18.6 1.5 %collective-permute-done.8.refs_9_ = bf16[160,896]{1,0:T(8,128)(2,1)S(1)} collective-permute-done((bf16[160,896]{1,0:T(8,128)(2,1)S(1)}, bf16[160,896]{1,0:T(8,128)(2,1)S(1)}, u32[]{:S(2)}, u32[]{:S(2)}) %collective-permute-start.8) | collective-permute-done | bytes 286752 | tf_op jit(solution)/shard_map/ppermute | solution.py:346
  20.1 2.0 %copy-done = bf16[256,7168]{1,0:T(8,128)(2,1)S(1)} copy-done((bf16[256,7168]{1,0:T(8,128)(2,1)S(1)}, bf16[256,7168]{1,0:T(8,128)(2,1)}, u32[]{:S(2)}) %copy-start) | copy-done | bytes 3670040
  22.2 2.0 %copy-done.1 = bf16[7168,256]{1,0:T(8,128)(2,1)S(1)} copy-done((bf16[7168,256]{1,0:T(8,128)(2,1)S(1)}, bf16[7168,256]{1,0:T(8,128)(2,1)}, u32[]{:S(2)}) %copy-start.1) | copy-done | bytes 3670040
  24.2 2.0 %copy-done.2 = bf16[7168,256]{1,0:T(8,128)(2,1)S(1)} copy-done((bf16[7168,256]{1,0:T(8,128)(2,1)S(1)}, bf16[7168,256]{1,0:T(8,128)(2,1)}, u32[]{:S(2)}) %copy-start.2) | copy-done | bytes 3670040
  26.2 2.5 %expert_half.1 = (bf16[320,896]{1,0:T(8,128)(2,1)S(1)}, bf16[40,256]{1,0:T(8,128)(2,1)S(1)}) custom-call(bf16[40,896]{1,0:T(8,128)(2,1)S(1)} %get-tuple-element.34.refs_0_, bf16[40,896]{1,0:T(8,128)(2,1)S(1)} %collective-permute-done.1.refs_1_, bf16[40,896]{1,0:T(8,128)(2,1)S(1)} %collective-permute-done.2.refs_2_, ...), custom_call_target="tpu_custom_call" | custom-call | flops 734003200 | bytes 11010048 | tf_op jit(solution)/shard_map/expert_half/pallas_call | solution.py:203
  28.7 0.2 collective-permute-start.9
  28.9 0.7 %kept_half.1.kept_ref = f32[320,896]{1,0:T(8,128)S(1)} custom-call(bf16[40,256]{1,0:T(8,128)(2,1)S(1)} %get-tuple-element.36.hidden_ref, bf16[256,7168]{1,0:T(8,128)(2,1)S(1)} %copy-done), custom_call_target="tpu_custom_call" | custom-call | flops 146800640 | bytes 3670016 | tf_op jit(solution)/shard_map/kept_half/pallas_call | solution.py:234
  29.7 1.1 %collective-permute-done.9.taken_ref = bf16[320,896]{1,0:T(8,128)(2,1)S(1)} collective-permute-done((bf16[320,896]{1,0:T(8,128)(2,1)S(1)}, bf16[320,896]{1,0:T(8,128)(2,1)S(1)}, u32[]{:S(2)}, u32[]{:S(2)}) %collective-permute-start.9) | collective-permute-done | bytes 573472 | tf_op jit(solution)/shard_map/ppermute | solution.py:348
  30.8 0.1 add_cores.1
  30.9 0.6 %collective-permute-start.10 = (bf16[40,896]{1,0:T(8,128)(2,1)S(1)}, bf16[40,896]{1,0:T(8,128)(2,1)S(1)}, u32[]{:S(2)}, u32[]{:S(2)}) collective-permute-start(bf16[40,896]{1,0:T(8,128)(2,1)S(1)} %get-tuple-element.39), channel_id=1, source_target_pairs={{0,2},{1,3},{2,0},{3,1},{4,6},{5,7},{6,4},{7,5},{8,10},{9,11},{10,... | collective-permute-start | bytes 215048 | tf_op jit(solution)/shard_map/ppermute | solution.py:355
  31.5 1.6 %collective-permute-start.11 = (bf16[40,896]{1,0:T(8,128)(2,1)S(1)}, bf16[40,896]{1,0:T(8,128)(2,1)S(1)}, u32[]{:S(2)}, u32[]{:S(2)}) collective-permute-start(bf16[40,896]{1,0:T(8,128)(2,1)S(1)} %get-tuple-element.40), channel_id=1, source_target_pairs={{0,4},{1,5},{2,6},{3,7},{4,0},{5,1},{6,2},{7,3},{8,12},{9,13},{10,... | collective-permute-start | bytes 215048 | tf_op jit(solution)/shard_map/ppermute | solution.py:355
  33.0 1.4 %collective-permute-start.12 = (bf16[40,896]{1,0:T(8,128)(2,1)S(1)}, bf16[40,896]{1,0:T(8,128)(2,1)S(1)}, u32[]{:S(2)}, u32[]{:S(2)}) collective-permute-start(bf16[40,896]{1,0:T(8,128)(2,1)S(1)} %get-tuple-element.41), channel_id=1, source_target_pairs={{0,6},{1,7},{2,4},{3,5},{4,2},{5,3},{6,0},{7,1},{8,14},{9,15},{10,... | collective-permute-start | bytes 215048 | tf_op jit(solution)/shard_map/ppermute | solution.py:355
  34.4 0.8 %collective-permute-done.10.refs_1_ = bf16[40,896]{1,0:T(8,128)(2,1)S(1)} collective-permute-done((bf16[40,896]{1,0:T(8,128)(2,1)S(1)}, bf16[40,896]{1,0:T(8,128)(2,1)S(1)}, u32[]{:S(2)}, u32[]{:S(2)}) %collective-permute-start.10) | collective-permute-done | bytes 71712 | tf_op jit(solution)/shard_map/ppermute | solution.py:355
  35.3 0.5 %collective-permute-done.11.refs_2_ = bf16[40,896]{1,0:T(8,128)(2,1)S(1)} collective-permute-done((bf16[40,896]{1,0:T(8,128)(2,1)S(1)}, bf16[40,896]{1,0:T(8,128)(2,1)S(1)}, u32[]{:S(2)}, u32[]{:S(2)}) %collective-permute-start.11) | collective-permute-done | bytes 71712 | tf_op jit(solution)/shard_map/ppermute | solution.py:355
  35.8 2.5 %collective-permute-done.12.refs_3_ = bf16[40,896]{1,0:T(8,128)(2,1)S(1)} collective-permute-done((bf16[40,896]{1,0:T(8,128)(2,1)S(1)}, bf16[40,896]{1,0:T(8,128)(2,1)S(1)}, u32[]{:S(2)}, u32[]{:S(2)}) %collective-permute-start.12) | collective-permute-done | bytes 71712 | tf_op jit(solution)/shard_map/ppermute | solution.py:355
  38.3 1.6 %collective-permute-start.13 = (bf16[40,896]{1,0:T(8,128)(2,1)S(1)}, bf16[40,896]{1,0:T(8,128)(2,1)S(1)}, u32[]{:S(2)}, u32[]{:S(2)}) collective-permute-start(bf16[40,896]{1,0:T(8,128)(2,1)S(1)} %get-tuple-element.47), channel_id=1, source_target_pairs={{0,2},{1,3},{2,0},{3,1},{4,6},{5,7},{6,4},{7,5},{8,10},{9,11},{10,... | collective-permute-start | bytes 215048 | tf_op jit(solution)/shard_map/ppermute | solution.py:361
  39.9 0.6 %collective-permute-start.14 = (bf16[40,896]{1,0:T(8,128)(2,1)S(1)}, bf16[40,896]{1,0:T(8,128)(2,1)S(1)}, u32[]{:S(2)}, u32[]{:S(2)}) collective-permute-start(bf16[40,896]{1,0:T(8,128)(2,1)S(1)} %get-tuple-element.48), channel_id=1, source_target_pairs={{0,4},{1,5},{2,6},{3,7},{4,0},{5,1},{6,2},{7,3},{8,12},{9,13},{10,... | collective-permute-start | bytes 215048 | tf_op jit(solution)/shard_map/ppermute | solution.py:361
  40.5 1.4 %collective-permute-start.15 = (bf16[40,896]{1,0:T(8,128)(2,1)S(1)}, bf16[40,896]{1,0:T(8,128)(2,1)S(1)}, u32[]{:S(2)}, u32[]{:S(2)}) collective-permute-start(bf16[40,896]{1,0:T(8,128)(2,1)S(1)} %get-tuple-element.49), channel_id=1, source_target_pairs={{0,6},{1,7},{2,4},{3,5},{4,2},{5,3},{6,0},{7,1},{8,14},{9,15},{10,... | collective-permute-start | bytes 215048 | tf_op jit(solution)/shard_map/ppermute | solution.py:361
  41.9 1.7 %collective-permute-start.16 = (bf16[40,896]{1,0:T(8,128)(2,1)S(1)}, bf16[40,896]{1,0:T(8,128)(2,1)S(1)}, u32[]{:S(2)}, u32[]{:S(2)}) collective-permute-start(bf16[40,896]{1,0:T(8,128)(2,1)S(1)} %sum_blocks.1), channel_id=1, source_target_pairs={{0,8},{1,9},{2,10},{3,11},{4,12},{5,13},{6,14},{7,15},{8,0},{9,1},... | collective-permute-start | bytes 215048 | tf_op jit(solution)/shard_map/ppermute | solution.py:358
  43.6 0.0 collective-permute-done.13.refs_1_
  43.6 1.1 %collective-permute-done.14.refs_2_ = bf16[40,896]{1,0:T(8,128)(2,1)S(1)} collective-permute-done((bf16[40,896]{1,0:T(8,128)(2,1)S(1)}, bf16[40,896]{1,0:T(8,128)(2,1)S(1)}, u32[]{:S(2)}, u32[]{:S(2)}) %collective-permute-start.14) | collective-permute-done | bytes 71712 | tf_op jit(solution)/shard_map/ppermute | solution.py:361
  44.6 1.2 %collective-permute-done.15.refs_3_ = bf16[40,896]{1,0:T(8,128)(2,1)S(1)} collective-permute-done((bf16[40,896]{1,0:T(8,128)(2,1)S(1)}, bf16[40,896]{1,0:T(8,128)(2,1)S(1)}, u32[]{:S(2)}, u32[]{:S(2)}) %collective-permute-start.15) | collective-permute-done | bytes 71712 | tf_op jit(solution)/shard_map/ppermute | solution.py:361
  45.8 1.3 %collective-permute-done.16.refs_4_ = bf16[40,896]{1,0:T(8,128)(2,1)S(1)} collective-permute-done((bf16[40,896]{1,0:T(8,128)(2,1)S(1)}, bf16[40,896]{1,0:T(8,128)(2,1)S(1)}, u32[]{:S(2)}, u32[]{:S(2)}) %collective-permute-start.16) | collective-permute-done | bytes 71712 | tf_op jit(solution)/shard_map/ppermute | solution.py:358
  47.1 1.4 %blend.1 = bf16[64,7168]{1,0:T(8,128)(2,1)} custom-call(bf16[512,200]{1,0:T(8,128)(2,1)S(1)} %blend_weights.1.weight_ref, f32[40,896]{1,0:T(8,128)S(1)} %get-tuple-element.46.refs_0_, bf16[40,896]{1,0:T(8,128)(2,1)S(1)} %collective-permute-done.13.refs_1_, bf16[40,896]{1,0:T(8,128)(2,1)S(1)} %collective-permute-done.14.refs_2_, ...), custom_call_target="tpu_custom_call" | custom-call | tf_op jit(solution)/shard_map/blend/pallas_call | solution.py:315
  (7 shorter events, 0.1 us)
Async XLA Ops:
  0.0 1.2 %copy-start.3 = (bf16[64,7168]{1,0:T(8,128)(2,1)S(1)}, bf16[64,7168]{1,0:T(8,128)(2,1)}, u32[]{:S(2)}) copy-start(bf16[64,7168]{1,0:T(8,128)(2,1)} %tokens_ref.1) | copy-start | bytes 2752516
  1.2 0.7 %copy-start.4 = (s32[64,8]{0,1:T(8,128)S(1)}, s32[64,8]{0,1:T(8,128)}, u32[]{:S(2)}) copy-start(s32[64,8]{0,1:T(8,128)} %param.7) | copy-start | bytes 6148
  2.3 8.7 %collective-permute-start = (bf16[40,896]{1,0:T(8,128)(2,1)S(1)}, bf16[40,896]{1,0:T(8,128)(2,1)S(1)}, u32[]{:S(2)}, u32[]{:S(2)}) collective-permute-start(bf16[40,896]{1,0:T(8,128)(2,1)S(1)} %get-tuple-element.30), channel_id=1, source_target_pairs={{0,8},{1,9},{2,10},{3,11},{4,12},{5,13},{6,14},{7,15},{8,0},{9,1},... | collective-permute-start | bytes 215048 | tf_op jit(solution)/shard_map/ppermute | solution.py:338
  6.4 7.7 %collective-permute-start.3 = (bf16[40,896]{1,0:T(8,128)(2,1)S(1)}, bf16[40,896]{1,0:T(8,128)(2,1)S(1)}, u32[]{:S(2)}, u32[]{:S(2)}) collective-permute-start(bf16[40,896]{1,0:T(8,128)(2,1)S(1)} %get-tuple-element.34.refs_0_), channel_id=1, source_target_pairs={{0,6},{1,7},{2,4},{3,5},{4,2},{5,3},{6,0},{7,1},{8,14},{9,15},{10,... | collective-permute-start | bytes 215048 | tf_op jit(solution)/shard_map/ppermute | solution.py:344
  9.0 5.7 %collective-permute-start.2 = (bf16[40,896]{1,0:T(8,128)(2,1)S(1)}, bf16[40,896]{1,0:T(8,128)(2,1)S(1)}, u32[]{:S(2)}, u32[]{:S(2)}) collective-permute-start(bf16[40,896]{1,0:T(8,128)(2,1)S(1)} %get-tuple-element.34.refs_0_), channel_id=1, source_target_pairs={{0,4},{1,5},{2,6},{3,7},{4,0},{5,1},{6,2},{7,3},{8,12},{9,13},{10,... | collective-permute-start | bytes 215048 | tf_op jit(solution)/shard_map/ppermute | solution.py:344
  9.4 5.2 %collective-permute-start.1 = (bf16[40,896]{1,0:T(8,128)(2,1)S(1)}, bf16[40,896]{1,0:T(8,128)(2,1)S(1)}, u32[]{:S(2)}, u32[]{:S(2)}) collective-permute-start(bf16[40,896]{1,0:T(8,128)(2,1)S(1)} %get-tuple-element.34.refs_0_), channel_id=1, source_target_pairs={{0,2},{1,3},{2,0},{3,1},{4,6},{5,7},{6,4},{7,5},{8,10},{9,11},{10,... | collective-permute-start | bytes 215048 | tf_op jit(solution)/shard_map/ppermute | solution.py:344
  9.9 0.7 %copy-start.5 = (f32[64,8]{0,1:T(8,128)S(1)}, f32[64,8]{0,1:T(8,128)}, u32[]{:S(2)}) copy-start(f32[64,8]{0,1:T(8,128)} %param.8) | copy-start | bytes 6148
  11.1 5.3 %collective-permute-start.6 = (bf16[40,896]{1,0:T(8,128)(2,1)S(1)}, bf16[40,896]{1,0:T(8,128)(2,1)S(1)}, u32[]{:S(2)}, u32[]{:S(2)}) collective-permute-start(bf16[40,896]{1,0:T(8,128)(2,1)S(1)} %collective-permute-done.refs_0_.refs_4_), channel_id=1, source_target_pairs={{0,6},{1,7},{2,4},{3,5},{4,2},{5,3},{6,0},{7,1},{8,14},{9,15},{10,... | collective-permute-start | bytes 215048 | tf_op jit(solution)/shard_map/ppermute | solution.py:344
  13.7 4.3 %collective-permute-start.5 = (bf16[40,896]{1,0:T(8,128)(2,1)S(1)}, bf16[40,896]{1,0:T(8,128)(2,1)S(1)}, u32[]{:S(2)}, u32[]{:S(2)}) collective-permute-start(bf16[40,896]{1,0:T(8,128)(2,1)S(1)} %collective-permute-done.refs_0_.refs_4_), channel_id=1, source_target_pairs={{0,4},{1,5},{2,6},{3,7},{4,0},{5,1},{6,2},{7,3},{8,12},{9,13},{10,... | collective-permute-start | bytes 215048 | tf_op jit(solution)/shard_map/ppermute | solution.py:344
  14.1 4.3 %collective-permute-start.4 = (bf16[40,896]{1,0:T(8,128)(2,1)S(1)}, bf16[40,896]{1,0:T(8,128)(2,1)S(1)}, u32[]{:S(2)}, u32[]{:S(2)}) collective-permute-start(bf16[40,896]{1,0:T(8,128)(2,1)S(1)} %collective-permute-done.refs_0_.refs_4_), channel_id=1, source_target_pairs={{0,2},{1,3},{2,0},{3,1},{4,6},{5,7},{6,4},{7,5},{8,10},{9,11},{10,... | collective-permute-start | bytes 215048 | tf_op jit(solution)/shard_map/ppermute | solution.py:344
  14.7 3.9 %collective-permute-start.7 = (bf16[160,896]{1,0:T(8,128)(2,1)S(1)}, bf16[160,896]{1,0:T(8,128)(2,1)S(1)}, u32[]{:S(2)}, u32[]{:S(2)}) collective-permute-start(bf16[160,896]{1,0:T(8,128)(2,1)S(1)} %join.2), channel_id=1, source_target_pairs={{0,1},{1,0},{2,3},{3,2},{4,5},{5,4},{6,7},{7,6},{8,9},{9,8},{10,11... | collective-permute-start | bytes 860168 | tf_op jit(solution)/shard_map/ppermute | solution.py:346
  18.5 1.6 %collective-permute-start.8 = (bf16[160,896]{1,0:T(8,128)(2,1)S(1)}, bf16[160,896]{1,0:T(8,128)(2,1)S(1)}, u32[]{:S(2)}, u32[]{:S(2)}) collective-permute-start(bf16[160,896]{1,0:T(8,128)(2,1)S(1)} %join.3), channel_id=1, source_target_pairs={{0,1},{1,0},{2,3},{3,2},{4,5},{5,4},{6,7},{7,6},{8,9},{9,8},{10,11... | collective-permute-start | bytes 860168 | tf_op jit(solution)/shard_map/ppermute | solution.py:346
  20.1 2.0 %copy-start = (bf16[256,7168]{1,0:T(8,128)(2,1)S(1)}, bf16[256,7168]{1,0:T(8,128)(2,1)}, u32[]{:S(2)}) copy-start(bf16[256,7168]{1,0:T(8,128)(2,1)} %down_ref.1) | copy-start | bytes 11010052
  22.2 2.0 %copy-start.1 = (bf16[7168,256]{1,0:T(8,128)(2,1)S(1)}, bf16[7168,256]{1,0:T(8,128)(2,1)}, u32[]{:S(2)}) copy-start(bf16[7168,256]{1,0:T(8,128)(2,1)} %refs_10_.1) | copy-start | bytes 11010052
  24.2 2.0 %copy-start.2 = (bf16[7168,256]{1,0:T(8,128)(2,1)S(1)}, bf16[7168,256]{1,0:T(8,128)(2,1)}, u32[]{:S(2)}) copy-start(bf16[7168,256]{1,0:T(8,128)(2,1)} %refs_11_.1) | copy-start | bytes 11010052
  28.7 2.0 %collective-permute-start.9 = (bf16[320,896]{1,0:T(8,128)(2,1)S(1)}, bf16[320,896]{1,0:T(8,128)(2,1)S(1)}, u32[]{:S(2)}, u32[]{:S(2)}) collective-permute-start(bf16[320,896]{1,0:T(8,128)(2,1)S(1)} %get-tuple-element.37), channel_id=1, source_target_pairs={{0,1},{1,0},{2,3},{3,2},{4,5},{5,4},{6,7},{7,6},{8,9},{9,8},{10,11... | collective-permute-start | bytes 1720328 | tf_op jit(solution)/shard_map/ppermute | solution.py:348
  30.9 4.4 %collective-permute-start.10 = (bf16[40,896]{1,0:T(8,128)(2,1)S(1)}, bf16[40,896]{1,0:T(8,128)(2,1)S(1)}, u32[]{:S(2)}, u32[]{:S(2)}) collective-permute-start(bf16[40,896]{1,0:T(8,128)(2,1)S(1)} %get-tuple-element.39), channel_id=1, source_target_pairs={{0,2},{1,3},{2,0},{3,1},{4,6},{5,7},{6,4},{7,5},{8,10},{9,11},{10,... | collective-permute-start | bytes 215048 | tf_op jit(solution)/shard_map/ppermute | solution.py:355
  31.5 4.3 %collective-permute-start.11 = (bf16[40,896]{1,0:T(8,128)(2,1)S(1)}, bf16[40,896]{1,0:T(8,128)(2,1)S(1)}, u32[]{:S(2)}, u32[]{:S(2)}) collective-permute-start(bf16[40,896]{1,0:T(8,128)(2,1)S(1)} %get-tuple-element.40), channel_id=1, source_target_pairs={{0,4},{1,5},{2,6},{3,7},{4,0},{5,1},{6,2},{7,3},{8,12},{9,13},{10,... | collective-permute-start | bytes 215048 | tf_op jit(solution)/shard_map/ppermute | solution.py:355
  33.0 5.2 %collective-permute-start.12 = (bf16[40,896]{1,0:T(8,128)(2,1)S(1)}, bf16[40,896]{1,0:T(8,128)(2,1)S(1)}, u32[]{:S(2)}, u32[]{:S(2)}) collective-permute-start(bf16[40,896]{1,0:T(8,128)(2,1)S(1)} %get-tuple-element.41), channel_id=1, source_target_pairs={{0,6},{1,7},{2,4},{3,5},{4,2},{5,3},{6,0},{7,1},{8,14},{9,15},{10,... | collective-permute-start | bytes 215048 | tf_op jit(solution)/shard_map/ppermute | solution.py:355
  38.3 5.2 %collective-permute-start.13 = (bf16[40,896]{1,0:T(8,128)(2,1)S(1)}, bf16[40,896]{1,0:T(8,128)(2,1)S(1)}, u32[]{:S(2)}, u32[]{:S(2)}) collective-permute-start(bf16[40,896]{1,0:T(8,128)(2,1)S(1)} %get-tuple-element.47), channel_id=1, source_target_pairs={{0,2},{1,3},{2,0},{3,1},{4,6},{5,7},{6,4},{7,5},{8,10},{9,11},{10,... | collective-permute-start | bytes 215048 | tf_op jit(solution)/shard_map/ppermute | solution.py:361
  39.9 4.7 %collective-permute-start.14 = (bf16[40,896]{1,0:T(8,128)(2,1)S(1)}, bf16[40,896]{1,0:T(8,128)(2,1)S(1)}, u32[]{:S(2)}, u32[]{:S(2)}) collective-permute-start(bf16[40,896]{1,0:T(8,128)(2,1)S(1)} %get-tuple-element.48), channel_id=1, source_target_pairs={{0,4},{1,5},{2,6},{3,7},{4,0},{5,1},{6,2},{7,3},{8,12},{9,13},{10,... | collective-permute-start | bytes 215048 | tf_op jit(solution)/shard_map/ppermute | solution.py:361
  40.5 5.4 %collective-permute-start.15 = (bf16[40,896]{1,0:T(8,128)(2,1)S(1)}, bf16[40,896]{1,0:T(8,128)(2,1)S(1)}, u32[]{:S(2)}, u32[]{:S(2)}) collective-permute-start(bf16[40,896]{1,0:T(8,128)(2,1)S(1)} %get-tuple-element.49), channel_id=1, source_target_pairs={{0,6},{1,7},{2,4},{3,5},{4,2},{5,3},{6,0},{7,1},{8,14},{9,15},{10,... | collective-permute-start | bytes 215048 | tf_op jit(solution)/shard_map/ppermute | solution.py:361
  41.9 5.2 %collective-permute-start.16 = (bf16[40,896]{1,0:T(8,128)(2,1)S(1)}, bf16[40,896]{1,0:T(8,128)(2,1)S(1)}, u32[]{:S(2)}, u32[]{:S(2)}) collective-permute-start(bf16[40,896]{1,0:T(8,128)(2,1)S(1)} %sum_blocks.1), channel_id=1, source_target_pairs={{0,8},{1,9},{2,10},{3,11},{4,12},{5,13},{6,14},{7,15},{8,0},{9,1},... | collective-permute-start | bytes 215048 | tf_op jit(solution)/shard_map/ppermute | solution.py:358

commit v6 on v5

--- a/solution.py
+++ b/solution.py
@@ -15,6 +15,7 @@
 route_scale = 2.5
 
 VMEM = pl.BlockSpec(memory_space=pltpu.VMEM)
+HBM = pl.BlockSpec(memory_space=pltpu.HBM)
 MIB = 1024 * 1024
 
 
@@ -42,18 +43,46 @@
 
 
 def params(mib):
-    return pltpu.CompilerParams(vmem_limit_bytes=mib * MIB)
-
-
-def pack_kernel(teams, ids_ref, tokens_ref, *out_refs):
+    return pltpu.CompilerParams(vmem_limit_bytes=int(mib * MIB))
+
+
+def bring(source, target, semaphores, parts):
+    step = source.shape[0] // parts
+    copies = []
+    for i in range(parts):
+        rows = pl.ds(i * step, step)
+        copies.append(pltpu.make_async_copy(source.at[rows], target.at[rows], semaphores.at[i]))
+        copies[-1].start()
+    return copies
+
+
+def wait_all(copies):
+    for copy in copies:
+        copy.wait()
+
+
+def pack_kernel(teams, ids_hbm, logits_hbm, tokens_hbm, *refs):
+    *out_refs, table_ref, ids_ref, logits_ref, tokens_ref, ids_sem, logits_sem, tokens_sem = refs
+    ids_copy = bring(ids_hbm, ids_ref, ids_sem, 1)
+    tokens_copy = bring(tokens_hbm, tokens_ref, tokens_sem, 4)
+    logits_copy = bring(logits_hbm, logits_ref, logits_sem, 1)
+    wait_all(ids_copy)
     mine = lax.axis_index("expert") // SPLIT
-    _, slot = hits(ids_ref[...], mine, teams)
+    ids = ids_ref[...]
+    hit, slot = hits(ids, mine, teams)
+    wait_all(logits_copy)
+    lifted = jax.nn.sigmoid(logits_ref[...])
+    gates = route_scale * lifted / jnp.sum(lifted, axis=0, keepdims=True)
+    row = lax.broadcasted_iota(jnp.int32, hit.shape, 0)
+    wanted = lax.rem(mine + row, teams)
+    gate = jnp.zeros(hit.shape, jnp.float32)
+    for j in range(ids.shape[0]):
+        gate = gate + jnp.where(ids[j : j + 1, :] == wanted, gates[j : j + 1, :], 0.0)
+    table_ref[: hit.shape[0], :] = slot
+    table_ref[hit.shape[0] :, :] = gate
     count, features = tokens_ref.shape
     wide = features // SEGMENTS
     tall = CAP * SEGMENTS
-    stacked = jnp.concatenate(
-        [tokens_ref[:, s * wide : (s + 1) * wide] for s in range(SEGMENTS)], axis=0
-    )
     segment, place = fifth((tall, 1), 0)
     column = lax.broadcasted_iota(jnp.int32, (1, SEGMENTS * count), 1)
     same = segment == column // count
@@ -61,6 +90,10 @@
     for k in range(teams):
         slots = jnp.concatenate([slot[k : k + 1, :]] * SEGMENTS, axis=1)
         picks.append(jnp.where(same & (slots == place), 1.0, 0.0))
+    wait_all(tokens_copy)
+    stacked = jnp.concatenate(
+        [tokens_ref[:, s * wide : (s + 1) * wide] for s in range(SEGMENTS)], axis=0
+    )
     packed = jnp.dot(
         jnp.concatenate(picks, axis=0).astype(jnp.bfloat16),
         stacked,
@@ -70,33 +103,46 @@
         out_refs[k][...] = packed[k * tall : (k + 1) * tall].astype(jnp.bfloat16)
 
 
-def pack_rows(ids, tokens, teams):
+def pack_rows(ids, logits, tokens, teams):
     wide = tokens.shape[1] // SEGMENTS
     block = jax.ShapeDtypeStruct((CAP * SEGMENTS, wide), jnp.bfloat16)
-    return pl.pallas_call(
+    table = jax.ShapeDtypeStruct((16 * pl.cdiv(teams, 8), ids.shape[1]), jnp.float32)
+    *packed, table = pl.pallas_call(
         functools.partial(pack_kernel, teams),
-        out_shape=[block] * teams,
-        in_specs=[VMEM, VMEM],
-        out_specs=[VMEM] * teams,
-        compiler_params=params(8),
+        out_shape=[block] * teams + [table],
+        in_specs=[HBM] * 3,
+        out_specs=[VMEM] * (teams + 1),
+        scratch_shapes=[
+            pltpu.VMEM(ids.shape, ids.dtype),
+            pltpu.VMEM(logits.shape, logits.dtype),
+            pltpu.VMEM(tokens.shape, tokens.dtype),
+            pltpu.SemaphoreType.DMA((1,)),
+            pltpu.SemaphoreType.DMA((1,)),
+            pltpu.SemaphoreType.DMA((4,)),
+        ],
         name="pack_rows",
-    )(ids, tokens)
-
-
-def weight_kernel(teams, ids_ref, logits_ref, out_ref):
-    mine = lax.axis_index("expert") // SPLIT
-    ids = ids_ref[...]
-    hit, slot = hits(ids, mine, teams)
-    count = ids.shape[1]
-    lifted = jax.nn.sigmoid(logits_ref[...])
-    gates = route_scale * lifted / jnp.sum(lifted, axis=0, keepdims=True)
-    row = lax.broadcasted_iota(jnp.int32, hit.shape, 0)
-    wanted = lax.rem(mine + row, teams)
-    gate = jnp.zeros(hit.shape, jnp.float32)
-    for j in range(ids.shape[0]):
-        gate = gate + jnp.where(ids[j : j + 1, :] == wanted, gates[j : j + 1, :], 0.0)
-    slot = jnp.transpose(slot)
-    gate = jnp.transpose(gate)
+    )(ids, logits, tokens)
+    return packed, table
+
+
+PARTS = 4
+
+
+def load_kernel(teams, *refs):
+    table_ref, *weights = refs[:4]
+    out_ref, *held = refs[4:8]
+    sem = refs[8]
+    copies = []
+    for i, (source, target) in enumerate(zip(weights, held)):
+        copies += bring(source, target, sem.at[pl.ds(i * PARTS, PARTS)], PARTS)
+    blend_matrix(teams, table_ref, out_ref)
+    wait_all(copies)
+
+
+def blend_matrix(teams, table_ref, out_ref):
+    rows, count = table_ref.shape
+    slot = jnp.transpose(table_ref[: rows // 2, :])
+    gate = jnp.transpose(table_ref[rows // 2 :, :])
     tall = CAP * SEGMENTS
     depth = out_ref.shape[1]
     column = lax.broadcasted_iota(jnp.int32, (1, depth), 1)
@@ -121,16 +167,21 @@
         )
 
 
-def blend_weights(ids, logits, teams):
-    shape = (SEGMENTS * ids.shape[1], CAP * SEGMENTS * (1 + 2 * teams))
-    return pl.pallas_call(
-        functools.partial(weight_kernel, teams),
-        out_shape=jax.ShapeDtypeStruct(shape, jnp.bfloat16),
-        in_specs=[VMEM, VMEM],
-        out_specs=VMEM,
-        compiler_params=params(4 + teams),
-        name="blend_weights",
-    )(ids, logits)
+def load(table, weights, teams):
+    shape = (SEGMENTS * table.shape[1], CAP * SEGMENTS * (1 + 2 * teams))
+    return pl.pallas_call(
+        functools.partial(load_kernel, teams),
+        out_shape=[jax.ShapeDtypeStruct(shape, jnp.bfloat16)]
+        + [jax.ShapeDtypeStruct(w.shape, w.dtype) for w in weights],
+        in_specs=[VMEM] + [HBM] * len(weights),
+        out_specs=[VMEM] * (1 + len(weights)),
+        scratch_shapes=[pltpu.SemaphoreType.DMA((PARTS * len(weights),))],
+        compiler_params=params(41),
+        cost_estimate=pl.CostEstimate(
+            flops=0, bytes_accessed=2 * sum(2 * w.size for w in weights), transcendentals=0
+        ),
+        name="load",
+    )(table, *weights)
 
 
 def join_kernel(*refs):
@@ -291,7 +342,7 @@
 
 
 def blend_kernel(chips, weight_ref, *refs):
-    out_ref = refs[-1]
+    *refs, out_hbm, out_ref, sem = refs
     count, features = out_ref.shape
     wide = features // SEGMENTS
     own = refs[0][...]
@@ -299,14 +350,20 @@
         own = own + ref[...].astype(jnp.float32)
     high = own.astype(jnp.bfloat16).astype(jnp.float32)
     terms = [high, own - high, high]
-    for ref in refs[chips:-1]:
+    for ref in refs[chips:]:
         terms += [ref[...].astype(jnp.float32)] * 2
     rows = jnp.concatenate(terms, axis=0).astype(jnp.bfloat16)
-    total = jnp.dot(weight_ref[...], rows, preferred_element_type=jnp.float32)
+    copies = []
     for s in range(SEGMENTS):
-        out_ref[:, s * wide : (s + 1) * wide] = total[s * count : (s + 1) * count].astype(
-            jnp.bfloat16
+        columns = pl.ds(s * wide, wide)
+        out_ref[:, columns] = jnp.dot(
+            weight_ref[s * count : (s + 1) * count, :], rows, preferred_element_type=jnp.float32
+        ).astype(jnp.bfloat16)
+        copies.append(
+            pltpu.make_async_copy(out_ref.at[:, columns], out_hbm.at[:, columns], sem.at[s])
         )
+        copies[-1].start()
+    wait_all(copies)
 
 
 def blend(weights, own_blocks, other_blocks, count):
@@ -316,7 +373,11 @@
         functools.partial(blend_kernel, chips),
         out_shape=jax.ShapeDtypeStruct((count, features), jnp.bfloat16),
         in_specs=[VMEM] * (1 + chips + len(other_blocks)),
-        out_specs=VMEM,
+        out_specs=HBM,
+        scratch_shapes=[
+            pltpu.VMEM((count, features), jnp.bfloat16),
+            pltpu.SemaphoreType.DMA((SEGMENTS,)),
+        ],
         compiler_params=params(16),
         name="blend",
     )(weights, *own_blocks, *other_blocks)
@@ -328,22 +389,25 @@
     chips = SPLIT // CORES
     other_core = [(i, i ^ 1) for i in range(devices)]
     other_chip = [[(i, i ^ (m * CORES)) for i in range(devices)] for m in range(chips)]
-    ids = expert_ids.T
-    packed = pack_rows(ids, tokens, teams)
-    ids, logits, packed = lax.optimization_barrier((ids, route_logits.T, packed))
-    weights = blend_weights(ids, logits, teams)
-    arrived = [packed[0]]
-    for k in range(1, teams):
-        pairs = [(i, (i + k * SPLIT) % devices) for i in range(devices)]
-        arrived.append(lax.ppermute(packed[k], "expert", pairs))
-    *arrived[1:], weights = lax.optimization_barrier((*arrived[1:], weights))
+    packed, table = pack_rows(expert_ids.T, route_logits.T, tokens, teams)
     blocks, swapped = [], []
-    for block in arrived:
+    for k in range(teams):
+        block = packed[k]
+        if k > 0:
+            pairs = [(i, (i + k * SPLIT) % devices) for i in range(devices)]
+            block = lax.ppermute(block, "expert", pairs)
         team = [block]
         for m in range(1, chips):
             team.append(lax.ppermute(block, "expert", other_chip[m]))
+        if k == teams - 1:
+            start = (table, w_gate, w_up, w_down)
+            start, swapped = lax.optimization_barrier((start, swapped))
+            held = load(start[0], start[1:], teams)
+            team, (weights, w_gate, w_up, w_down) = lax.optimization_barrier((team, held))
         blocks += team
-        swapped.append(lax.ppermute(join(team), "expert", other_core))
+        joined = join(team)
+        swapped.append(joined)
+    swapped = [lax.ppermute(joined, "expert", other_core) for joined in swapped]
     given, hidden = expert_half(blocks, swapped, w_gate, w_up, w_down)
     taken = lax.ppermute(given, "expert", other_core)
     kept = kept_half(hidden, w_down)
@@ -354,8 +418,7 @@
         for m in range(1, chips):
             team.append(lax.ppermute(parts[k * chips + m], "expert", other_chip[m]))
         pairs = [(i, (i - k * SPLIT) % devices) for i in range(devices)]
-        total, parts = lax.optimization_barrier((sum_blocks(team), parts))
-        others.append(lax.ppermute(total, "expert", pairs))
+        others.append(lax.ppermute(sum_blocks(team), "expert", pairs))
     own = [parts[0]]
     for m in range(1, chips):
         own.append(lax.ppermute(parts[m], "expert", other_chip[m]))

time: 48.8 us -> 43.6 us (0.89)
  local copies, waits for them, and re-layouts: 8.67 us -> 1.58 us
  Pallas kernels: 5.68 us -> 11.6 us
  waiting for transfers between devices: 13.8 us -> 8 us
  starting transfers between devices: 20.3 us -> 22.1 us
    unnamed x12 -> x6, local copies, waits for them, and re-layouts: 8.67 us -> 1.58 us
    pallas_call x1, Pallas kernels: 0.43 us -> 4.25 us  [load(): pl.pallas_call(functools.partial(load_kernel, teams), out_shape=[jax.Shap...]
    ppermute x3, waiting for transfers between devices: 3.84 us -> 0.83 us  [body(): team.append(lax.ppermute(parts[k * chips + m], 'expert', other_chip[m]))]
    ppermute x6, waiting for transfers between devices: 3.72 us -> 1.14 us  [body(): team.append(lax.ppermute(block, 'expert', other_chip[m]))]
    ppermute x4, waiting for transfers between devices: 2.84 us -> 4.71 us  [the longest x1 3.52 us: body(): others.append(lax.ppermute(sum_blocks(team), 'expert', pairs))]
    pallas_call x1, Pallas kernels: 0.47 us -> 2.28 us  [pack_rows(): pl.pallas_call(functools.partial(pack_kernel, teams), out_shape=[block] *...]
    ppermute x3, waiting for transfers between devices: 2.28 us -> 0.48 us  [body(): own.append(lax.ppermute(parts[m], 'expert', other_chip[m]))]
    ppermute x4, starting transfers between devices: 5.92 us -> 6.8 us  [the longest x1 4.1 us: body(): block = lax.ppermute(block, 'expert', pairs)]
  transfers between devices with their start and end apart: 17 -> 17, of which waited for: 11 -> 7; matrix products, arithmetic and copies ran while one was open for 0% -> 0% of each run, Pallas kernels for 2% -> 12%
where the time goes in v6:
time: 43.6 us; the launch traced here: 43.4 us
  starting transfers between devices  22.1 us (51%)
  Pallas kernels  11.6 us (27%)
  waiting for transfers between devices  8 us (18%)
  local copies, waits for them, and re-layouts  1.58 us (4%)
    ppermute x6, starting transfers between devices, body(): team.append(lax.ppermute(block, 'expert', other_chip[m]))  7.82 us
    pallas_call x1, Pallas kernels, load(): pl.pallas_call(functools.partial(load_kernel, teams), out_shape=[jax.Shap...  4.25 us
    ppermute x1, starting transfers between devices, body(): block = lax.ppermute(block, 'expert', pairs)  4.1 us
    ppermute x3, starting transfers between devices, body(): team.append(lax.ppermute(parts[k * chips + m], 'expert', other_chip[m]))  3.57 us
    ppermute x1, waiting for transfers between devices, body(): others.append(lax.ppermute(sum_blocks(team), 'expert', pairs))  3.52 us
    ppermute x3, starting transfers between devices, body(): own.append(lax.ppermute(parts[m], 'expert', other_chip[m]))  3.49 us
    pallas_call x1, Pallas kernels, expert_half(): pl.pallas_call(functools.partial(expert_kernel, own), out_shape=[jax.Shap...  2.63 us
    pallas_call x1, Pallas kernels, pack_rows(): pl.pallas_call(functools.partial(pack_kernel, teams), out_shape=[block] *...  2.28 us
  transfers between devices with their start and end apart: 17, of which 7 were waited for; matrix products, arithmetic and copies ran while one was open for 0% of the time, Pallas kernels for 12%

profile of v6, /device:TPU:0, one launch (start us, length us, event | category | flops | bytes accessed | tf_op | source)
XLA Modules:
  0.0 43.4 jit_solution(5124731729772674274)
XLA Ops:
  0.0 2.3 %pack_rows.1 = (bf16[40,896]{1,0:T(8,128)(2,1)}, bf16[40,896]{1,0:T(8,128)(2,1)}, f32[16,64]{1,0:T(8,128)}) custom-call(s32[8,64]{1,0:T(8,128)} %bitcast.2, f32[8,64]{1,0:T(8,128)} %bitcast.3, bf16[64,7168]{1,0:T(8,128)(2,1)} %tokens_hbm.1), custom_call_target="tpu_custom_call" | custom-call | tf_op jit(solution)/shard_map/pack_rows/pallas_call | solution.py:110
  2.3 4.1 %collective-permute-start = (bf16[40,896]{1,0:T(8,128)(2,1)}, bf16[40,896]{1,0:T(8,128)(2,1)S(1)}, u32[]{:S(2)}, u32[]{:S(2)}) collective-permute-start(bf16[40,896]{1,0:T(8,128)(2,1)} %get-tuple-element.35), channel_id=1, source_target_pairs={{0,8},{1,9},{2,10},{3,11},{4,12},{5,13},{6,14},{7,15},{8,0},{9,1},... | collective-permute-start | bytes 215048 | tf_op jit(solution)/shard_map/ppermute | solution.py:398
  6.4 2.5 %collective-permute-start.6 = (bf16[40,896]{1,0:T(8,128)(2,1)}, bf16[40,896]{1,0:T(8,128)(2,1)S(1)}, u32[]{:S(2)}, u32[]{:S(2)}) collective-permute-start(bf16[40,896]{1,0:T(8,128)(2,1)} %get-tuple-element.37.refs_0_), channel_id=1, source_target_pairs={{0,6},{1,7},{2,4},{3,5},{4,2},{5,3},{6,0},{7,1},{8,14},{9,15},{10,... | collective-permute-start | bytes 215048 | tf_op jit(solution)/shard_map/ppermute | solution.py:401
  8.9 0.4 %collective-permute-start.5 = (bf16[40,896]{1,0:T(8,128)(2,1)}, bf16[40,896]{1,0:T(8,128)(2,1)S(1)}, u32[]{:S(2)}, u32[]{:S(2)}) collective-permute-start(bf16[40,896]{1,0:T(8,128)(2,1)} %get-tuple-element.37.refs_0_), channel_id=1, source_target_pairs={{0,4},{1,5},{2,6},{3,7},{4,0},{5,1},{6,2},{7,3},{8,12},{9,13},{10,... | collective-permute-start | bytes 215048 | tf_op jit(solution)/shard_map/ppermute | solution.py:401
  9.4 0.5 %collective-permute-start.4 = (bf16[40,896]{1,0:T(8,128)(2,1)}, bf16[40,896]{1,0:T(8,128)(2,1)S(1)}, u32[]{:S(2)}, u32[]{:S(2)}) collective-permute-start(bf16[40,896]{1,0:T(8,128)(2,1)} %get-tuple-element.37.refs_0_), channel_id=1, source_target_pairs={{0,2},{1,3},{2,0},{3,1},{4,6},{5,7},{6,4},{7,5},{8,10},{9,11},{10,... | collective-permute-start | bytes 215048 | tf_op jit(solution)/shard_map/ppermute | solution.py:401
  9.9 0.0 collective-permute-done.refs_0_.refs_4_
  9.9 2.7 %collective-permute-start.3 = (bf16[40,896]{1,0:T(8,128)(2,1)S(1)}, bf16[40,896]{1,0:T(8,128)(2,1)S(1)}, u32[]{:S(2)}, u32[]{:S(2)}) collective-permute-start(bf16[40,896]{1,0:T(8,128)(2,1)S(1)} %collective-permute-done.refs_0_.refs_4_), channel_id=1, source_target_pairs={{0,6},{1,7},{2,4},{3,5},{4,2},{5,3},{6,0},{7,1},{8,14},{9,15},{10,... | collective-permute-start | bytes 215048 | tf_op jit(solution)/shard_map/ppermute | solution.py:401
  12.6 0.7 %collective-permute-start.2 = (bf16[40,896]{1,0:T(8,128)(2,1)S(1)}, bf16[40,896]{1,0:T(8,128)(2,1)S(1)}, u32[]{:S(2)}, u32[]{:S(2)}) collective-permute-start(bf16[40,896]{1,0:T(8,128)(2,1)S(1)} %collective-permute-done.refs_0_.refs_4_), channel_id=1, source_target_pairs={{0,4},{1,5},{2,6},{3,7},{4,0},{5,1},{6,2},{7,3},{8,12},{9,13},{10,... | collective-permute-start | bytes 215048 | tf_op jit(solution)/shard_map/ppermute | solution.py:401
  13.3 0.0 collective-permute-done.6.refs_3_
  13.3 1.0 %collective-permute-start.1 = (bf16[40,896]{1,0:T(8,128)(2,1)S(1)}, bf16[40,896]{1,0:T(8,128)(2,1)S(1)}, u32[]{:S(2)}, u32[]{:S(2)}) collective-permute-start(bf16[40,896]{1,0:T(8,128)(2,1)S(1)} %collective-permute-done.refs_0_.refs_4_), channel_id=1, source_target_pairs={{0,2},{1,3},{2,0},{3,1},{4,6},{5,7},{6,4},{7,5},{8,10},{9,11},{10,... | collective-permute-start | bytes 215048 | tf_op jit(solution)/shard_map/ppermute | solution.py:401
  14.2 0.1 collective-permute-done.5.refs_2_
  14.3 1.0 %collective-permute-done.4.refs_1_ = bf16[40,896]{1,0:T(8,128)(2,1)S(1)} collective-permute-done((bf16[40,896]{1,0:T(8,128)(2,1)}, bf16[40,896]{1,0:T(8,128)(2,1)S(1)}, u32[]{:S(2)}, u32[]{:S(2)}) %collective-permute-start.4) | collective-permute-done | bytes 71712 | tf_op jit(solution)/shard_map/ppermute | solution.py:401
  15.3 0.0 copy-start
  15.3 0.9 %copy-done = bf16[40,896]{1,0:T(8,128)(2,1)S(1)} copy-done((bf16[40,896]{1,0:T(8,128)(2,1)S(1)}, bf16[40,896]{1,0:T(8,128)(2,1)}, u32[]{:S(2)}) %copy-start) | copy-done | bytes 71704
  16.3 0.0 copy-start.1
  16.3 0.1 collective-permute-start.7
  16.3 0.0 copy-start.2
  16.4 0.7 %copy-done.2 = f32[16,64]{1,0:T(8,128)S(1)} copy-done((f32[16,64]{1,0:T(8,128)S(1)}, f32[16,64]{1,0:T(8,128)}, u32[]{:S(2)}) %copy-start.2) | copy-done | bytes 4120
  17.0 4.2 %load.1 = (bf16[512,200]{1,0:T(8,128)(2,1)S(1)}, bf16[7168,256]{1,0:T(8,128)(2,1)S(1)}, bf16[7168,256]{1,0:T(8,128)(2,1)S(1)}, bf16[256,7168]{1,0:T(8,128)(2,1)S(1)}) custom-call(f32[16,64]{1,0:T(8,128)S(1)} %copy-done.2, bf16[7168,256]{1,0:T(8,128)(2,1)} %refs_1_, bf16[7168,256]{1,0:T(8,128)(2,1)} %refs_2_, bf16[256,7168]{1,0:T(8,128)(2,1)} %refs_3_), custom_call_target="tpu_custom_call" | custom-call | bytes 22020096 | tf_op jit(solution)/shard_map/load/pallas_call | solution.py:172
  21.3 0.0 collective-permute-done.3.refs_3_.refs_7_
  21.3 0.0 collective-permute-done.2.refs_2_.refs_6_
  21.3 0.0 collective-permute-done.1.refs_1_.refs_5_
  21.4 0.6 %collective-permute-start.8 = (bf16[160,896]{1,0:T(8,128)(2,1)S(1)}, bf16[160,896]{1,0:T(8,128)(2,1)S(1)}, u32[]{:S(2)}, u32[]{:S(2)}) collective-permute-start(bf16[160,896]{1,0:T(8,128)(2,1)S(1)} %join.3), channel_id=1, source_target_pairs={{0,1},{1,0},{2,3},{3,2},{4,5},{5,4},{6,7},{7,6},{8,9},{9,8},{10,11... | collective-permute-start | bytes 860168 | tf_op jit(solution)/shard_map/ppermute | solution.py:410
  21.9 0.0 collective-permute-done.7.refs_8_
  21.9 1.2 %collective-permute-done.8.refs_9_ = bf16[160,896]{1,0:T(8,128)(2,1)S(1)} collective-permute-done((bf16[160,896]{1,0:T(8,128)(2,1)S(1)}, bf16[160,896]{1,0:T(8,128)(2,1)S(1)}, u32[]{:S(2)}, u32[]{:S(2)}) %collective-permute-start.8) | collective-permute-done | bytes 286752 | tf_op jit(solution)/shard_map/ppermute | solution.py:410
  23.1 0.0 copy-done.1
  23.1 2.6 %expert_half.1 = (bf16[320,896]{1,0:T(8,128)(2,1)S(1)}, bf16[40,256]{1,0:T(8,128)(2,1)S(1)}) custom-call(bf16[40,896]{1,0:T(8,128)(2,1)S(1)} %copy-done.1, bf16[40,896]{1,0:T(8,128)(2,1)S(1)} %collective-permute-done.4.refs_1_, bf16[40,896]{1,0:T(8,128)(2,1)S(1)} %collective-permute-done.5.refs_2_, bf16[40,896]{1,0:T(8,128)(2,1)S(1)} %collective-permute-done.6.refs_3_, ...), custom_call_target="tpu_custom_call" | custom-call | flops 734003200 | bytes 11010048 | tf_op jit(solution)/shard_map/expert_half/pallas_call | solution.py:254
  25.8 0.4 %collective-permute-start.9 = (bf16[320,896]{1,0:T(8,128)(2,1)S(1)}, bf16[320,896]{1,0:T(8,128)(2,1)S(1)}, u32[]{:S(2)}, u32[]{:S(2)}) collective-permute-start(bf16[320,896]{1,0:T(8,128)(2,1)S(1)} %get-tuple-element.56), channel_id=1, source_target_pairs={{0,1},{1,0},{2,3},{3,2},{4,5},{5,4},{6,7},{7,6},{8,9},{9,8},{10,11... | collective-permute-start | bytes 1720328 | tf_op jit(solution)/shard_map/ppermute | solution.py:412
  26.2 0.8 %kept_half.1.kept_ref = f32[320,896]{1,0:T(8,128)S(1)} custom-call(bf16[40,256]{1,0:T(8,128)(2,1)S(1)} %get-tuple-element.55.hidden_ref, bf16[256,7168]{1,0:T(8,128)(2,1)S(1)} %get-tuple-element.54.refs_12_.down_ref), custom_call_target="tpu_custom_call" | custom-call | flops 146800640 | bytes 3670016 | tf_op jit(solution)/shard_map/kept_half/pallas_call | solution.py:285
  27.0 0.8 %collective-permute-done.9.taken_ref = bf16[320,896]{1,0:T(8,128)(2,1)S(1)} collective-permute-done((bf16[320,896]{1,0:T(8,128)(2,1)S(1)}, bf16[320,896]{1,0:T(8,128)(2,1)S(1)}, u32[]{:S(2)}, u32[]{:S(2)}) %collective-permute-start.9) | collective-permute-done | bytes 573472 | tf_op jit(solution)/shard_map/ppermute | solution.py:412
  27.8 0.1 add_cores.1
  27.9 0.7 %collective-permute-start.13 = (bf16[40,896]{1,0:T(8,128)(2,1)S(1)}, bf16[40,896]{1,0:T(8,128)(2,1)S(1)}, u32[]{:S(2)}, u32[]{:S(2)}) collective-permute-start(bf16[40,896]{1,0:T(8,128)(2,1)S(1)} %get-tuple-element.62), channel_id=1, source_target_pairs={{0,2},{1,3},{2,0},{3,1},{4,6},{5,7},{6,4},{7,5},{8,10},{9,11},{10,... | collective-permute-start | bytes 215048 | tf_op jit(solution)/shard_map/ppermute | solution.py:419
  28.6 1.0 %collective-permute-start.14 = (bf16[40,896]{1,0:T(8,128)(2,1)S(1)}, bf16[40,896]{1,0:T(8,128)(2,1)S(1)}, u32[]{:S(2)}, u32[]{:S(2)}) collective-permute-start(bf16[40,896]{1,0:T(8,128)(2,1)S(1)} %get-tuple-element.63), channel_id=1, source_target_pairs={{0,4},{1,5},{2,6},{3,7},{4,0},{5,1},{6,2},{7,3},{8,12},{9,13},{10,... | collective-permute-start | bytes 215048 | tf_op jit(solution)/shard_map/ppermute | solution.py:419
  29.6 2.0 %collective-permute-start.15 = (bf16[40,896]{1,0:T(8,128)(2,1)S(1)}, bf16[40,896]{1,0:T(8,128)(2,1)S(1)}, u32[]{:S(2)}, u32[]{:S(2)}) collective-permute-start(bf16[40,896]{1,0:T(8,128)(2,1)S(1)} %get-tuple-element.64), channel_id=1, source_target_pairs={{0,6},{1,7},{2,4},{3,5},{4,2},{5,3},{6,0},{7,1},{8,14},{9,15},{10,... | collective-permute-start | bytes 215048 | tf_op jit(solution)/shard_map/ppermute | solution.py:419
  31.5 0.6 %collective-permute-start.10 = (bf16[40,896]{1,0:T(8,128)(2,1)S(1)}, bf16[40,896]{1,0:T(8,128)(2,1)S(1)}, u32[]{:S(2)}, u32[]{:S(2)}) collective-permute-start(bf16[40,896]{1,0:T(8,128)(2,1)S(1)} %get-tuple-element.58), channel_id=1, source_target_pairs={{0,2},{1,3},{2,0},{3,1},{4,6},{5,7},{6,4},{7,5},{8,10},{9,11},{10,... | collective-permute-start | bytes 215048 | tf_op jit(solution)/shard_map/ppermute | solution.py:424
  32.1 1.0 %collective-permute-start.11 = (bf16[40,896]{1,0:T(8,128)(2,1)S(1)}, bf16[40,896]{1,0:T(8,128)(2,1)S(1)}, u32[]{:S(2)}, u32[]{:S(2)}) collective-permute-start(bf16[40,896]{1,0:T(8,128)(2,1)S(1)} %get-tuple-element.59), channel_id=1, source_target_pairs={{0,4},{1,5},{2,6},{3,7},{4,0},{5,1},{6,2},{7,3},{8,12},{9,13},{10,... | collective-permute-start | bytes 215048 | tf_op jit(solution)/shard_map/ppermute | solution.py:424
  33.0 0.0 collective-permute-done.13.refs_1_
  33.1 2.0 %collective-permute-start.12 = (bf16[40,896]{1,0:T(8,128)(2,1)S(1)}, bf16[40,896]{1,0:T(8,128)(2,1)S(1)}, u32[]{:S(2)}, u32[]{:S(2)}) collective-permute-start(bf16[40,896]{1,0:T(8,128)(2,1)S(1)} %get-tuple-element.60), channel_id=1, source_target_pairs={{0,6},{1,7},{2,4},{3,5},{4,2},{5,3},{6,0},{7,1},{8,14},{9,15},{10,... | collective-permute-start | bytes 215048 | tf_op jit(solution)/shard_map/ppermute | solution.py:424
  35.0 0.0 collective-permute-done.14.refs_2_
  35.0 0.8 %collective-permute-done.15.refs_3_ = bf16[40,896]{1,0:T(8,128)(2,1)S(1)} collective-permute-done((bf16[40,896]{1,0:T(8,128)(2,1)S(1)}, bf16[40,896]{1,0:T(8,128)(2,1)S(1)}, u32[]{:S(2)}, u32[]{:S(2)}) %collective-permute-start.15) | collective-permute-done | bytes 71712 | tf_op jit(solution)/shard_map/ppermute | solution.py:419
  35.9 2.1 %collective-permute-start.16 = (bf16[40,896]{1,0:T(8,128)(2,1)S(1)}, bf16[40,896]{1,0:T(8,128)(2,1)S(1)}, u32[]{:S(2)}, u32[]{:S(2)}) collective-permute-start(bf16[40,896]{1,0:T(8,128)(2,1)S(1)} %sum_blocks.1), channel_id=1, source_target_pairs={{0,8},{1,9},{2,10},{3,11},{4,12},{5,13},{6,14},{7,15},{8,0},{9,1},... | collective-permute-start | bytes 215048 | tf_op jit(solution)/shard_map/ppermute | solution.py:421
  37.9 0.0 collective-permute-done.10.refs_1_
  37.9 0.0 collective-permute-done.11.refs_2_
  37.9 0.5 %collective-permute-done.12.refs_3_ = bf16[40,896]{1,0:T(8,128)(2,1)S(1)} collective-permute-done((bf16[40,896]{1,0:T(8,128)(2,1)S(1)}, bf16[40,896]{1,0:T(8,128)(2,1)S(1)}, u32[]{:S(2)}, u32[]{:S(2)}) %collective-permute-start.12) | collective-permute-done | bytes 71712 | tf_op jit(solution)/shard_map/ppermute | solution.py:424
  38.4 3.5 %collective-permute-done.16.refs_4_ = bf16[40,896]{1,0:T(8,128)(2,1)S(1)} collective-permute-done((bf16[40,896]{1,0:T(8,128)(2,1)S(1)}, bf16[40,896]{1,0:T(8,128)(2,1)S(1)}, u32[]{:S(2)}, u32[]{:S(2)}) %collective-permute-start.16) | collective-permute-done | bytes 71712 | tf_op jit(solution)/shard_map/ppermute | solution.py:421
  41.9 1.5 %blend.1 = bf16[64,7168]{1,0:T(8,128)(2,1)} custom-call(bf16[512,200]{1,0:T(8,128)(2,1)S(1)} %get-tuple-element.46.weight_ref, f32[40,896]{1,0:T(8,128)S(1)} %get-tuple-element.57.refs_0_, bf16[40,896]{1,0:T(8,128)(2,1)S(1)} %collective-permute-done.10.refs_1_, bf16[40,896]{1,0:T(8,128)(2,1)S(1)} %collective-permute-done.11.refs_2_, ...), custom_call_target="tpu_custom_call" | custom-call | tf_op jit(solution)/shard_map/blend/pallas_call | solution.py:372
  (3 shorter events, 0.1 us)
Async XLA Ops:
  2.3 7.6 %collective-permute-start = (bf16[40,896]{1,0:T(8,128)(2,1)}, bf16[40,896]{1,0:T(8,128)(2,1)S(1)}, u32[]{:S(2)}, u32[]{:S(2)}) collective-permute-start(bf16[40,896]{1,0:T(8,128)(2,1)} %get-tuple-element.35), channel_id=1, source_target_pairs={{0,8},{1,9},{2,10},{3,11},{4,12},{5,13},{6,14},{7,15},{8,0},{9,1},... | collective-permute-start | bytes 215048 | tf_op jit(solution)/shard_map/ppermute | solution.py:398
  6.4 6.9 %collective-permute-start.6 = (bf16[40,896]{1,0:T(8,128)(2,1)}, bf16[40,896]{1,0:T(8,128)(2,1)S(1)}, u32[]{:S(2)}, u32[]{:S(2)}) collective-permute-start(bf16[40,896]{1,0:T(8,128)(2,1)} %get-tuple-element.37.refs_0_), channel_id=1, source_target_pairs={{0,6},{1,7},{2,4},{3,5},{4,2},{5,3},{6,0},{7,1},{8,14},{9,15},{10,... | collective-permute-start | bytes 215048 | tf_op jit(solution)/shard_map/ppermute | solution.py:401
  8.9 5.4 %collective-permute-start.5 = (bf16[40,896]{1,0:T(8,128)(2,1)}, bf16[40,896]{1,0:T(8,128)(2,1)S(1)}, u32[]{:S(2)}, u32[]{:S(2)}) collective-permute-start(bf16[40,896]{1,0:T(8,128)(2,1)} %get-tuple-element.37.refs_0_), channel_id=1, source_target_pairs={{0,4},{1,5},{2,6},{3,7},{4,0},{5,1},{6,2},{7,3},{8,12},{9,13},{10,... | collective-permute-start | bytes 215048 | tf_op jit(solution)/shard_map/ppermute | solution.py:401
  9.4 6.0 %collective-permute-start.4 = (bf16[40,896]{1,0:T(8,128)(2,1)}, bf16[40,896]{1,0:T(8,128)(2,1)S(1)}, u32[]{:S(2)}, u32[]{:S(2)}) collective-permute-start(bf16[40,896]{1,0:T(8,128)(2,1)} %get-tuple-element.37.refs_0_), channel_id=1, source_target_pairs={{0,2},{1,3},{2,0},{3,1},{4,6},{5,7},{6,4},{7,5},{8,10},{9,11},{10,... | collective-permute-start | bytes 215048 | tf_op jit(solution)/shard_map/ppermute | solution.py:401
  9.9 11.4 %collective-permute-start.3 = (bf16[40,896]{1,0:T(8,128)(2,1)S(1)}, bf16[40,896]{1,0:T(8,128)(2,1)S(1)}, u32[]{:S(2)}, u32[]{:S(2)}) collective-permute-start(bf16[40,896]{1,0:T(8,128)(2,1)S(1)} %collective-permute-done.refs_0_.refs_4_), channel_id=1, source_target_pairs={{0,6},{1,7},{2,4},{3,5},{4,2},{5,3},{6,0},{7,1},{8,14},{9,15},{10,... | collective-permute-start | bytes 215048 | tf_op jit(solution)/shard_map/ppermute | solution.py:401
  12.6 8.8 %collective-permute-start.2 = (bf16[40,896]{1,0:T(8,128)(2,1)S(1)}, bf16[40,896]{1,0:T(8,128)(2,1)S(1)}, u32[]{:S(2)}, u32[]{:S(2)}) collective-permute-start(bf16[40,896]{1,0:T(8,128)(2,1)S(1)} %collective-permute-done.refs_0_.refs_4_), channel_id=1, source_target_pairs={{0,4},{1,5},{2,6},{3,7},{4,0},{5,1},{6,2},{7,3},{8,12},{9,13},{10,... | collective-permute-start | bytes 215048 | tf_op jit(solution)/shard_map/ppermute | solution.py:401
  13.3 8.1 %collective-permute-start.1 = (bf16[40,896]{1,0:T(8,128)(2,1)S(1)}, bf16[40,896]{1,0:T(8,128)(2,1)S(1)}, u32[]{:S(2)}, u32[]{:S(2)}) collective-permute-start(bf16[40,896]{1,0:T(8,128)(2,1)S(1)} %collective-permute-done.refs_0_.refs_4_), channel_id=1, source_target_pairs={{0,2},{1,3},{2,0},{3,1},{4,6},{5,7},{6,4},{7,5},{8,10},{9,11},{10,... | collective-permute-start | bytes 215048 | tf_op jit(solution)/shard_map/ppermute | solution.py:401
  15.3 0.9 %copy-start = (bf16[40,896]{1,0:T(8,128)(2,1)S(1)}, bf16[40,896]{1,0:T(8,128)(2,1)}, u32[]{:S(2)}) copy-start(bf16[40,896]{1,0:T(8,128)(2,1)} %get-tuple-element.37.refs_0_) | copy-start | bytes 215044
  16.3 6.9 %copy-start.1 = (bf16[40,896]{1,0:T(8,128)(2,1)S(1)}, bf16[40,896]{1,0:T(8,128)(2,1)}, u32[]{:S(2)}) copy-start(bf16[40,896]{1,0:T(8,128)(2,1)} %get-tuple-element.37.refs_0_) | copy-start | bytes 215044
  16.3 5.7 %collective-permute-start.7 = (bf16[160,896]{1,0:T(8,128)(2,1)S(1)}, bf16[160,896]{1,0:T(8,128)(2,1)S(1)}, u32[]{:S(2)}, u32[]{:S(2)}) collective-permute-start(bf16[160,896]{1,0:T(8,128)(2,1)S(1)} %join.2), channel_id=1, source_target_pairs={{0,1},{1,0},{2,3},{3,2},{4,5},{5,4},{6,7},{7,6},{8,9},{9,8},{10,11... | collective-permute-start | bytes 860168 | tf_op jit(solution)/shard_map/ppermute | solution.py:410
  16.3 0.7 %copy-start.2 = (f32[16,64]{1,0:T(8,128)S(1)}, f32[16,64]{1,0:T(8,128)}, u32[]{:S(2)}) copy-start(f32[16,64]{1,0:T(8,128)} %get-tuple-element.38.refs_0_) | copy-start | bytes 12292
  21.4 1.8 %collective-permute-start.8 = (bf16[160,896]{1,0:T(8,128)(2,1)S(1)}, bf16[160,896]{1,0:T(8,128)(2,1)S(1)}, u32[]{:S(2)}, u32[]{:S(2)}) collective-permute-start(bf16[160,896]{1,0:T(8,128)(2,1)S(1)} %join.3), channel_id=1, source_target_pairs={{0,1},{1,0},{2,3},{3,2},{4,5},{5,4},{6,7},{7,6},{8,9},{9,8},{10,11... | collective-permute-start | bytes 860168 | tf_op jit(solution)/shard_map/ppermute | solution.py:410
  25.8 2.0 %collective-permute-start.9 = (bf16[320,896]{1,0:T(8,128)(2,1)S(1)}, bf16[320,896]{1,0:T(8,128)(2,1)S(1)}, u32[]{:S(2)}, u32[]{:S(2)}) collective-permute-start(bf16[320,896]{1,0:T(8,128)(2,1)S(1)} %get-tuple-element.56), channel_id=1, source_target_pairs={{0,1},{1,0},{2,3},{3,2},{4,5},{5,4},{6,7},{7,6},{8,9},{9,8},{10,11... | collective-permute-start | bytes 1720328 | tf_op jit(solution)/shard_map/ppermute | solution.py:412
  27.9 5.1 %collective-permute-start.13 = (bf16[40,896]{1,0:T(8,128)(2,1)S(1)}, bf16[40,896]{1,0:T(8,128)(2,1)S(1)}, u32[]{:S(2)}, u32[]{:S(2)}) collective-permute-start(bf16[40,896]{1,0:T(8,128)(2,1)S(1)} %get-tuple-element.62), channel_id=1, source_target_pairs={{0,2},{1,3},{2,0},{3,1},{4,6},{5,7},{6,4},{7,5},{8,10},{9,11},{10,... | collective-permute-start | bytes 215048 | tf_op jit(solution)/shard_map/ppermute | solution.py:419
  28.6 6.4 %collective-permute-start.14 = (bf16[40,896]{1,0:T(8,128)(2,1)S(1)}, bf16[40,896]{1,0:T(8,128)(2,1)S(1)}, u32[]{:S(2)}, u32[]{:S(2)}) collective-permute-start(bf16[40,896]{1,0:T(8,128)(2,1)S(1)} %get-tuple-element.63), channel_id=1, source_target_pairs={{0,4},{1,5},{2,6},{3,7},{4,0},{5,1},{6,2},{7,3},{8,12},{9,13},{10,... | collective-permute-start | bytes 215048 | tf_op jit(solution)/shard_map/ppermute | solution.py:419
  29.6 6.3 %collective-permute-start.15 = (bf16[40,896]{1,0:T(8,128)(2,1)S(1)}, bf16[40,896]{1,0:T(8,128)(2,1)S(1)}, u32[]{:S(2)}, u32[]{:S(2)}) collective-permute-start(bf16[40,896]{1,0:T(8,128)(2,1)S(1)} %get-tuple-element.64), channel_id=1, source_target_pairs={{0,6},{1,7},{2,4},{3,5},{4,2},{5,3},{6,0},{7,1},{8,14},{9,15},{10,... | collective-permute-start | bytes 215048 | tf_op jit(solution)/shard_map/ppermute | solution.py:419
  31.5 6.4 %collective-permute-start.10 = (bf16[40,896]{1,0:T(8,128)(2,1)S(1)}, bf16[40,896]{1,0:T(8,128)(2,1)S(1)}, u32[]{:S(2)}, u32[]{:S(2)}) collective-permute-start(bf16[40,896]{1,0:T(8,128)(2,1)S(1)} %get-tuple-element.58), channel_id=1, source_target_pairs={{0,2},{1,3},{2,0},{3,1},{4,6},{5,7},{6,4},{7,5},{8,10},{9,11},{10,... | collective-permute-start | bytes 215048 | tf_op jit(solution)/shard_map/ppermute | solution.py:424
  32.1 5.9 %collective-permute-start.11 = (bf16[40,896]{1,0:T(8,128)(2,1)S(1)}, bf16[40,896]{1,0:T(8,128)(2,1)S(1)}, u32[]{:S(2)}, u32[]{:S(2)}) collective-permute-start(bf16[40,896]{1,0:T(8,128)(2,1)S(1)} %get-tuple-element.59), channel_id=1, source_target_pairs={{0,4},{1,5},{2,6},{3,7},{4,0},{5,1},{6,2},{7,3},{8,12},{9,13},{10,... | collective-permute-start | bytes 215048 | tf_op jit(solution)/shard_map/ppermute | solution.py:424
  33.1 5.4 %collective-permute-start.12 = (bf16[40,896]{1,0:T(8,128)(2,1)S(1)}, bf16[40,896]{1,0:T(8,128)(2,1)S(1)}, u32[]{:S(2)}, u32[]{:S(2)}) collective-permute-start(bf16[40,896]{1,0:T(8,128)(2,1)S(1)} %get-tuple-element.60), channel_id=1, source_target_pairs={{0,6},{1,7},{2,4},{3,5},{4,2},{5,3},{6,0},{7,1},{8,14},{9,15},{10,... | collective-permute-start | bytes 215048 | tf_op jit(solution)/shard_map/ppermute | solution.py:424
  35.9 6.1 %collective-permute-start.16 = (bf16[40,896]{1,0:T(8,128)(2,1)S(1)}, bf16[40,896]{1,0:T(8,128)(2,1)S(1)}, u32[]{:S(2)}, u32[]{:S(2)}) collective-permute-start(bf16[40,896]{1,0:T(8,128)(2,1)S(1)} %sum_blocks.1), channel_id=1, source_target_pairs={{0,8},{1,9},{2,10},{3,11},{4,12},{5,13},{6,14},{7,15},{8,0},{9,1},... | collective-permute-start | bytes 215048 | tf_op jit(solution)/shard_map/ppermute | solution.py:421

commit v7 on v6

--- a/solution.py
+++ b/solution.py
@@ -61,17 +61,13 @@
         copy.wait()
 
 
-def pack_kernel(teams, ids_hbm, logits_hbm, tokens_hbm, *refs):
-    *out_refs, table_ref, ids_ref, logits_ref, tokens_ref, ids_sem, logits_sem, tokens_sem = refs
-    ids_copy = bring(ids_hbm, ids_ref, ids_sem, 1)
-    tokens_copy = bring(tokens_hbm, tokens_ref, tokens_sem, 4)
-    logits_copy = bring(logits_hbm, logits_ref, logits_sem, 1)
-    wait_all(ids_copy)
+def pack_kernel(teams, routes_ref, tokens_ref, *refs):
+    *out_refs, table_ref = refs
     mine = lax.axis_index("expert") // SPLIT
-    ids = ids_ref[...]
+    picks = routes_ref.shape[0] // 2
+    ids = routes_ref[:picks, :].astype(jnp.int32)
     hit, slot = hits(ids, mine, teams)
-    wait_all(logits_copy)
-    lifted = jax.nn.sigmoid(logits_ref[...])
+    lifted = jax.nn.sigmoid(routes_ref[picks:, :])
     gates = route_scale * lifted / jnp.sum(lifted, axis=0, keepdims=True)
     row = lax.broadcasted_iota(jnp.int32, hit.shape, 0)
     wanted = lax.rem(mine + row, teams)
@@ -90,7 +86,6 @@
     for k in range(teams):
         slots = jnp.concatenate([slot[k : k + 1, :]] * SEGMENTS, axis=1)
         picks.append(jnp.where(same & (slots == place), 1.0, 0.0))
-    wait_all(tokens_copy)
     stacked = jnp.concatenate(
         [tokens_ref[:, s * wide : (s + 1) * wide] for s in range(SEGMENTS)], axis=0
     )
@@ -103,43 +98,22 @@
         out_refs[k][...] = packed[k * tall : (k + 1) * tall].astype(jnp.bfloat16)
 
 
-def pack_rows(ids, logits, tokens, teams):
+def pack_rows(routes, tokens, teams):
     wide = tokens.shape[1] // SEGMENTS
     block = jax.ShapeDtypeStruct((CAP * SEGMENTS, wide), jnp.bfloat16)
-    table = jax.ShapeDtypeStruct((16 * pl.cdiv(teams, 8), ids.shape[1]), jnp.float32)
+    table = jax.ShapeDtypeStruct((16 * pl.cdiv(teams, 8), routes.shape[1]), jnp.float32)
     *packed, table = pl.pallas_call(
         functools.partial(pack_kernel, teams),
         out_shape=[block] * teams + [table],
-        in_specs=[HBM] * 3,
+        in_specs=[VMEM] * 2,
         out_specs=[VMEM] * (teams + 1),
-        scratch_shapes=[
-            pltpu.VMEM(ids.shape, ids.dtype),
-            pltpu.VMEM(logits.shape, logits.dtype),
-            pltpu.VMEM(tokens.shape, tokens.dtype),
-            pltpu.SemaphoreType.DMA((1,)),
-            pltpu.SemaphoreType.DMA((1,)),
-            pltpu.SemaphoreType.DMA((4,)),
-        ],
+        compiler_params=params(8),
         name="pack_rows",
-    )(ids, logits, tokens)
+    )(routes, tokens)
     return packed, table
 
 
-PARTS = 4
-
-
-def load_kernel(teams, *refs):
-    table_ref, *weights = refs[:4]
-    out_ref, *held = refs[4:8]
-    sem = refs[8]
-    copies = []
-    for i, (source, target) in enumerate(zip(weights, held)):
-        copies += bring(source, target, sem.at[pl.ds(i * PARTS, PARTS)], PARTS)
-    blend_matrix(teams, table_ref, out_ref)
-    wait_all(copies)
-
-
-def blend_matrix(teams, table_ref, out_ref):
+def weight_kernel(teams, table_ref, out_ref):
     rows, count = table_ref.shape
     slot = jnp.transpose(table_ref[: rows // 2, :])
     gate = jnp.transpose(table_ref[rows // 2 :, :])
@@ -167,21 +141,17 @@
         )
 
 
-def load(table, weights, teams):
+def blend_weights(table, teams):
     shape = (SEGMENTS * table.shape[1], CAP * SEGMENTS * (1 + 2 * teams))
     return pl.pallas_call(
-        functools.partial(load_kernel, teams),
-        out_shape=[jax.ShapeDtypeStruct(shape, jnp.bfloat16)]
-        + [jax.ShapeDtypeStruct(w.shape, w.dtype) for w in weights],
-        in_specs=[VMEM] + [HBM] * len(weights),
-        out_specs=[VMEM] * (1 + len(weights)),
-        scratch_shapes=[pltpu.SemaphoreType.DMA((PARTS * len(weights),))],
-        compiler_params=params(41),
-        cost_estimate=pl.CostEstimate(
-            flops=0, bytes_accessed=2 * sum(2 * w.size for w in weights), transcendentals=0
-        ),
-        name="load",
-    )(table, *weights)
+        functools.partial(weight_kernel, teams),
+        out_shape=jax.ShapeDtypeStruct(shape, jnp.bfloat16),
+        in_specs=[VMEM],
+        out_specs=VMEM,
+        compiler_params=params(4 + teams),
+        cost_estimate=pl.CostEstimate(flops=6 * 10**9, bytes_accessed=8 * MIB, transcendentals=0),
+        name="blend_weights",
+    )(table)
 
 
 def join_kernel(*refs):
@@ -341,6 +311,22 @@
     )(*blocks)
 
 
+def settle_kernel(block_ref, out_ref):
+    out_ref[...] = block_ref[...].astype(jnp.float32)
+
+
+def settle(block):
+    return pl.pallas_call(
+        settle_kernel,
+        out_shape=jax.ShapeDtypeStruct(block.shape, jnp.float32),
+        in_specs=[VMEM],
+        out_specs=VMEM,
+        compiler_params=params(4),
+        cost_estimate=pl.CostEstimate(flops=0, bytes_accessed=16 * MIB, transcendentals=0),
+        name="settle",
+    )(block)
+
+
 def blend_kernel(chips, weight_ref, *refs):
     *refs, out_hbm, out_ref, sem = refs
     count, features = out_ref.shape
@@ -351,7 +337,7 @@
     high = own.astype(jnp.bfloat16).astype(jnp.float32)
     terms = [high, own - high, high]
     for ref in refs[chips:]:
-        terms += [ref[...].astype(jnp.float32)] * 2
+        terms += [ref[...]] * 2
     rows = jnp.concatenate(terms, axis=0).astype(jnp.bfloat16)
     copies = []
     for s in range(SEGMENTS):
@@ -389,25 +375,29 @@
     chips = SPLIT // CORES
     other_core = [(i, i ^ 1) for i in range(devices)]
     other_chip = [[(i, i ^ (m * CORES)) for i in range(devices)] for m in range(chips)]
-    packed, table = pack_rows(expert_ids.T, route_logits.T, tokens, teams)
-    blocks, swapped = [], []
+    routes = jnp.concatenate([expert_ids.T.astype(jnp.float32), route_logits.T], axis=0)
+    packed, table = pack_rows(routes, tokens, teams)
+    crowds = []
     for k in range(teams):
         block = packed[k]
         if k > 0:
             pairs = [(i, (i + k * SPLIT) % devices) for i in range(devices)]
             block = lax.ppermute(block, "expert", pairs)
+        if k == teams - 1:
+            block, table = lax.optimization_barrier((block, table))
+            weights = blend_weights(table, teams)
         team = [block]
         for m in range(1, chips):
             team.append(lax.ppermute(block, "expert", other_chip[m]))
-        if k == teams - 1:
-            start = (table, w_gate, w_up, w_down)
-            start, swapped = lax.optimization_barrier((start, swapped))
-            held = load(start[0], start[1:], teams)
-            team, (weights, w_gate, w_up, w_down) = lax.optimization_barrier((team, held))
+        crowds.append(team)
+    crowds[0], weights = lax.optimization_barrier((crowds[0], weights))
+    blocks, joined = [], []
+    for team in crowds:
+        if joined:
+            team, joined = lax.optimization_barrier((team, joined))
         blocks += team
-        joined = join(team)
-        swapped.append(joined)
-    swapped = [lax.ppermute(joined, "expert", other_core) for joined in swapped]
+        joined.append(join(team))
+    swapped = [lax.ppermute(j, "expert", other_core) for j in joined]
     given, hidden = expert_half(blocks, swapped, w_gate, w_up, w_down)
     taken = lax.ppermute(given, "expert", other_core)
     kept = kept_half(hidden, w_down)
@@ -418,7 +408,8 @@
         for m in range(1, chips):
             team.append(lax.ppermute(parts[k * chips + m], "expert", other_chip[m]))
         pairs = [(i, (i - k * SPLIT) % devices) for i in range(devices)]
-        others.append(lax.ppermute(sum_blocks(team), "expert", pairs))
+        total, parts = lax.optimization_barrier((sum_blocks(team), parts))
+        others.append(settle(lax.ppermute(total, "expert", pairs)))
     own = [parts[0]]
     for m in range(1, chips):
         own.append(lax.ppermute(parts[m], "expert", other_chip[m]))

time: 43.6 us -> 43.9 us (level)
  Pallas kernels: 11.6 us -> 5.7 us
  waiting for transfers between devices: 8 us -> 13.2 us
  other arithmetic: 0 us -> 1.38 us
    pallas_call x1 -> x2, Pallas kernels: 4.25 us -> 0.32 us  [the longest x1 0.3 us: blend_weights(): pl.pallas_call(functools.partial(weight_kernel, teams), out_shape=jax.Sha...]
    ppermute x3, waiting for transfers between devices: 0.83 us -> 3.84 us  [body(): team.append(lax.ppermute(parts[k * chips + m], 'expert', other_chip[m]))]
    ppermute x3, waiting for transfers between devices: 4.71 us -> 2.68 us  [the longest x2 1.47 us: body(): swapped = [lax.ppermute(j, 'expert', other_core) for j in joined]]
    ppermute x6, waiting for transfers between devices: 1.14 us -> 3.1 us  [body(): team.append(lax.ppermute(block, 'expert', other_chip[m]))]
    ppermute x3, waiting for transfers between devices: 0.48 us -> 2.42 us  [body(): own.append(lax.ppermute(parts[m], 'expert', other_chip[m]))]
    pallas_call x1, Pallas kernels: 2.28 us -> 0.47 us  [pack_rows(): pl.pallas_call(functools.partial(pack_kernel, teams), out_shape=[block] *...]
    concatenate x0 -> x1, other arithmetic: none -> 0.69 us  [body(): jnp.concatenate([expert_ids.T.astype(jnp.float32), route_logits.T], axis=0)]
    convert_element_type x0 -> x1, other arithmetic: none -> 0.69 us  [body(): expert_ids.T.astype(jnp.float32)]
  transfers between devices with their start and end apart: 17 -> 17, of which waited for: 7 -> 13; matrix products, arithmetic and copies ran while one was open for 0% -> 0% of each run, Pallas kernels for 12% -> 2%
where the time goes in v7:
time: 43.9 us; the launch traced here: 43.7 us
  starting transfers between devices  22.2 us (51%)
  waiting for transfers between devices  13.2 us (30%)
  Pallas kernels  5.7 us (13%)
  other arithmetic  1.38 us (3%)
  local copies, waits for them, and re-layouts  1.19 us (3%)
    ppermute x6, starting transfers between devices, body(): team.append(lax.ppermute(block, 'expert', other_chip[m]))  7.53 us
    ppermute x1, starting transfers between devices, body(): block = lax.ppermute(block, 'expert', pairs)  4.1 us
    ppermute x3, waiting for transfers between devices, body(): team.append(lax.ppermute(parts[k * chips + m], 'expert', other_chip[m]))  3.84 us
    ppermute x3, starting transfers between devices, body(): team.append(lax.ppermute(parts[k * chips + m], 'expert', other_chip[m]))  3.55 us
    ppermute x3, starting transfers between devices, body(): own.append(lax.ppermute(parts[m], 'expert', other_chip[m]))  3.47 us
    ppermute x6, waiting for transfers between devices, body(): team.append(lax.ppermute(block, 'expert', other_chip[m]))  3.1 us
    ppermute x1, starting transfers between devices, body(): others.append(settle(lax.ppermute(total, 'expert', pairs)))  2.78 us
    pallas_call x1, Pallas kernels, expert_half(): pl.pallas_call(functools.partial(expert_kernel, own), out_shape=[jax.Shap...  2.5 us
  transfers between devices with their start and end apart: 17, of which 13 were waited for; matrix products, arithmetic and copies ran while one was open for 0% of the time, Pallas kernels for 2%

profile of v7, /device:TPU:0, one launch (start us, length us, event | category | flops | bytes accessed | tf_op | source)
XLA Modules:
  0.0 43.7 jit_solution(16733451560848263469)
XLA Ops:
  0.0 0.7 %convert_bitcast_fusion = f32[8,64]{1,0:T(8,128)S(1)} fusion(s32[64,8]{0,1:T(8,128)} %param.7), kind=kLoop, calls=%fused_computation.1 | loop fusion | flops 512 | bytes 4096 | tf_op jit(solution)/shard_map/convert_element_type | solution.py:378
  0.7 0.7 %pad_maximum_fusion.routes_ref = f32[16,64]{1,0:T(8,128)S(1)} fusion(f32[8,64]{1,0:T(8,128)} %bitcast.3, f32[8,64]{1,0:T(8,128)S(1)} %convert_bitcast_fusion), kind=kLoop, calls=%fused_computation | loop fusion | flops 1024 | bytes 8192 | tf_op jit(solution)/shard_map/concatenate | solution.py:378
  1.4 0.0 copy-start.3
  1.4 1.2 %copy-done.3 = bf16[64,7168]{1,0:T(8,128)(2,1)S(1)} copy-done((bf16[64,7168]{1,0:T(8,128)(2,1)S(1)}, bf16[64,7168]{1,0:T(8,128)(2,1)}, u32[]{:S(2)}) %copy-start.3) | copy-done | bytes 917528
  2.6 0.5 %pack_rows.1 = (bf16[40,896]{1,0:T(8,128)(2,1)S(1)}, bf16[40,896]{1,0:T(8,128)(2,1)S(1)}, f32[16,64]{1,0:T(8,128)S(1)}) custom-call(f32[16,64]{1,0:T(8,128)S(1)} %pad_maximum_fusion.routes_ref, bf16[64,7168]{1,0:T(8,128)(2,1)S(1)} %copy-done.3), custom_call_target="tpu_custom_call" | custom-call | tf_op jit(solution)/shard_map/pack_rows/pallas_call | solution.py:105
  3.0 4.1 %collective-permute-start.3 = (bf16[40,896]{1,0:T(8,128)(2,1)S(1)}, bf16[40,896]{1,0:T(8,128)(2,1)S(1)}, u32[]{:S(2)}, u32[]{:S(2)}) collective-permute-start(bf16[40,896]{1,0:T(8,128)(2,1)S(1)} %get-tuple-element.36), channel_id=1, source_target_pairs={{0,8},{1,9},{2,10},{3,11},{4,12},{5,13},{6,14},{7,15},{8,0},{9,1},... | collective-permute-start | bytes 215048 | tf_op jit(solution)/shard_map/ppermute | solution.py:385
  7.1 2.5 %collective-permute-start.2 = (bf16[40,896]{1,0:T(8,128)(2,1)S(1)}, bf16[40,896]{1,0:T(8,128)(2,1)S(1)}, u32[]{:S(2)}, u32[]{:S(2)}) collective-permute-start(bf16[40,896]{1,0:T(8,128)(2,1)S(1)} %get-tuple-element.40.refs_0_), channel_id=1, source_target_pairs={{0,6},{1,7},{2,4},{3,5},{4,2},{5,3},{6,0},{7,1},{8,14},{9,15},{10,... | collective-permute-start | bytes 215048 | tf_op jit(solution)/shard_map/ppermute | solution.py:391
  9.7 0.4 %collective-permute-start.1 = (bf16[40,896]{1,0:T(8,128)(2,1)S(1)}, bf16[40,896]{1,0:T(8,128)(2,1)S(1)}, u32[]{:S(2)}, u32[]{:S(2)}) collective-permute-start(bf16[40,896]{1,0:T(8,128)(2,1)S(1)} %get-tuple-element.40.refs_0_), channel_id=1, source_target_pairs={{0,4},{1,5},{2,6},{3,7},{4,0},{5,1},{6,2},{7,3},{8,12},{9,13},{10,... | collective-permute-start | bytes 215048 | tf_op jit(solution)/shard_map/ppermute | solution.py:391
  10.1 0.5 %collective-permute-start = (bf16[40,896]{1,0:T(8,128)(2,1)S(1)}, bf16[40,896]{1,0:T(8,128)(2,1)S(1)}, u32[]{:S(2)}, u32[]{:S(2)}) collective-permute-start(bf16[40,896]{1,0:T(8,128)(2,1)S(1)} %get-tuple-element.40.refs_0_), channel_id=1, source_target_pairs={{0,2},{1,3},{2,0},{3,1},{4,6},{5,7},{6,4},{7,5},{8,10},{9,11},{10,... | collective-permute-start | bytes 215048 | tf_op jit(solution)/shard_map/ppermute | solution.py:391
  10.6 0.0 collective-permute-done.3.refs_0_.refs_4_
  10.6 0.0 copy-start
  10.6 2.6 %collective-permute-start.6 = (bf16[40,896]{1,0:T(8,128)(2,1)S(1)}, bf16[40,896]{1,0:T(8,128)(2,1)S(1)}, u32[]{:S(2)}, u32[]{:S(2)}) collective-permute-start(bf16[40,896]{1,0:T(8,128)(2,1)S(1)} %collective-permute-done.3.refs_0_.refs_4_), channel_id=1, source_target_pairs={{0,6},{1,7},{2,4},{3,5},{4,2},{5,3},{6,0},{7,1},{8,14},{9,15},{10,... | collective-permute-start | bytes 215048 | tf_op jit(solution)/shard_map/ppermute | solution.py:391
  13.2 0.6 %collective-permute-start.5 = (bf16[40,896]{1,0:T(8,128)(2,1)S(1)}, bf16[40,896]{1,0:T(8,128)(2,1)S(1)}, u32[]{:S(2)}, u32[]{:S(2)}) collective-permute-start(bf16[40,896]{1,0:T(8,128)(2,1)S(1)} %collective-permute-done.3.refs_0_.refs_4_), channel_id=1, source_target_pairs={{0,4},{1,5},{2,6},{3,7},{4,0},{5,1},{6,2},{7,3},{8,12},{9,13},{10,... | collective-permute-start | bytes 215048 | tf_op jit(solution)/shard_map/ppermute | solution.py:391
  13.8 0.0 collective-permute-done.2.refs_3_
  13.8 0.9 %collective-permute-start.4 = (bf16[40,896]{1,0:T(8,128)(2,1)S(1)}, bf16[40,896]{1,0:T(8,128)(2,1)S(1)}, u32[]{:S(2)}, u32[]{:S(2)}) collective-permute-start(bf16[40,896]{1,0:T(8,128)(2,1)S(1)} %collective-permute-done.3.refs_0_.refs_4_), channel_id=1, source_target_pairs={{0,2},{1,3},{2,0},{3,1},{4,6},{5,7},{6,4},{7,5},{8,10},{9,11},{10,... | collective-permute-start | bytes 215048 | tf_op jit(solution)/shard_map/ppermute | solution.py:391
  14.7 0.3 blend_weights.1.weight_ref
  15.0 0.0 collective-permute-done.1.refs_2_
  15.0 0.6 %collective-permute-done.refs_1_ = bf16[40,896]{1,0:T(8,128)(2,1)S(1)} collective-permute-done((bf16[40,896]{1,0:T(8,128)(2,1)S(1)}, bf16[40,896]{1,0:T(8,128)(2,1)S(1)}, u32[]{:S(2)}, u32[]{:S(2)}) %collective-permute-start) | collective-permute-done | bytes 71712 | tf_op jit(solution)/shard_map/ppermute | solution.py:391
  15.6 0.8 %collective-permute-done.6.refs_3_.refs_7_ = bf16[40,896]{1,0:T(8,128)(2,1)S(1)} collective-permute-done((bf16[40,896]{1,0:T(8,128)(2,1)S(1)}, bf16[40,896]{1,0:T(8,128)(2,1)S(1)}, u32[]{:S(2)}, u32[]{:S(2)}) %collective-permute-start.6) | collective-permute-done | bytes 71712 | tf_op jit(solution)/shard_map/ppermute | solution.py:391
  16.4 1.2 %collective-permute-done.5.refs_2_.refs_6_ = bf16[40,896]{1,0:T(8,128)(2,1)S(1)} collective-permute-done((bf16[40,896]{1,0:T(8,128)(2,1)S(1)}, bf16[40,896]{1,0:T(8,128)(2,1)S(1)}, u32[]{:S(2)}, u32[]{:S(2)}) %collective-permute-start.5) | collective-permute-done | bytes 71712 | tf_op jit(solution)/shard_map/ppermute | solution.py:391
  17.6 0.6 %collective-permute-done.4.refs_1_.refs_5_ = bf16[40,896]{1,0:T(8,128)(2,1)S(1)} collective-permute-done((bf16[40,896]{1,0:T(8,128)(2,1)S(1)}, bf16[40,896]{1,0:T(8,128)(2,1)S(1)}, u32[]{:S(2)}, u32[]{:S(2)}) %collective-permute-start.4) | collective-permute-done | bytes 71712 | tf_op jit(solution)/shard_map/ppermute | solution.py:391
  18.2 0.1 collective-permute-start.8
  18.2 0.5 %collective-permute-start.7 = (bf16[160,896]{1,0:T(8,128)(2,1)S(1)}, bf16[160,896]{1,0:T(8,128)(2,1)S(1)}, u32[]{:S(2)}, u32[]{:S(2)}) collective-permute-start(bf16[160,896]{1,0:T(8,128)(2,1)S(1)} %join.2), channel_id=1, source_target_pairs={{0,1},{1,0},{2,3},{3,2},{4,5},{5,4},{6,7},{7,6},{8,9},{9,8},{10,11... | collective-permute-start | bytes 860168 | tf_op jit(solution)/shard_map/ppermute | solution.py:400
  18.7 1.1 %collective-permute-done.8.refs_9_ = bf16[160,896]{1,0:T(8,128)(2,1)S(1)} collective-permute-done((bf16[160,896]{1,0:T(8,128)(2,1)S(1)}, bf16[160,896]{1,0:T(8,128)(2,1)S(1)}, u32[]{:S(2)}, u32[]{:S(2)}) %collective-permute-start.8) | collective-permute-done | bytes 286752 | tf_op jit(solution)/shard_map/ppermute | solution.py:400
  19.8 0.4 collective-permute-done.7.refs_8_
  20.2 0.0 copy-done
  20.2 0.0 copy-done.1
  20.2 0.0 copy-done.2
  20.2 2.5 %expert_half.1 = (bf16[320,896]{1,0:T(8,128)(2,1)S(1)}, bf16[40,256]{1,0:T(8,128)(2,1)S(1)}) custom-call(bf16[40,896]{1,0:T(8,128)(2,1)S(1)} %get-tuple-element.40.refs_0_, bf16[40,896]{1,0:T(8,128)(2,1)S(1)} %collective-permute-done.refs_1_, bf16[40,896]{1,0:T(8,128)(2,1)S(1)} %collective-permute-done.1.refs_2_, ...), custom_call_target="tpu_custom_call" | custom-call | flops 734003200 | bytes 11010048 | tf_op jit(solution)/shard_map/expert_half/pallas_call | solution.py:224
  22.7 0.2 collective-permute-start.9
  22.9 0.7 %kept_half.1.kept_ref = f32[320,896]{1,0:T(8,128)S(1)} custom-call(bf16[40,256]{1,0:T(8,128)(2,1)S(1)} %get-tuple-element.50.hidden_ref, bf16[256,7168]{1,0:T(8,128)(2,1)S(1)} %copy-done), custom_call_target="tpu_custom_call" | custom-call | flops 146800640 | bytes 3670016 | tf_op jit(solution)/shard_map/kept_half/pallas_call | solution.py:255
  23.6 1.1 %collective-permute-done.9.taken_ref = bf16[320,896]{1,0:T(8,128)(2,1)S(1)} collective-permute-done((bf16[320,896]{1,0:T(8,128)(2,1)S(1)}, bf16[320,896]{1,0:T(8,128)(2,1)S(1)}, u32[]{:S(2)}, u32[]{:S(2)}) %collective-permute-start.9) | collective-permute-done | bytes 573472 | tf_op jit(solution)/shard_map/ppermute | solution.py:402
  24.8 0.1 add_cores.1
  24.9 1.0 %collective-permute-start.10 = (bf16[40,896]{1,0:T(8,128)(2,1)S(1)}, bf16[40,896]{1,0:T(8,128)(2,1)S(1)}, u32[]{:S(2)}, u32[]{:S(2)}) collective-permute-start(bf16[40,896]{1,0:T(8,128)(2,1)S(1)} %get-tuple-element.53), channel_id=1, source_target_pairs={{0,2},{1,3},{2,0},{3,1},{4,6},{5,7},{6,4},{7,5},{8,10},{9,11},{10,... | collective-permute-start | bytes 215048 | tf_op jit(solution)/shard_map/ppermute | solution.py:409
  25.9 1.1 %collective-permute-start.11 = (bf16[40,896]{1,0:T(8,128)(2,1)S(1)}, bf16[40,896]{1,0:T(8,128)(2,1)S(1)}, u32[]{:S(2)}, u32[]{:S(2)}) collective-permute-start(bf16[40,896]{1,0:T(8,128)(2,1)S(1)} %get-tuple-element.54), channel_id=1, source_target_pairs={{0,4},{1,5},{2,6},{3,7},{4,0},{5,1},{6,2},{7,3},{8,12},{9,13},{10,... | collective-permute-start | bytes 215048 | tf_op jit(solution)/shard_map/ppermute | solution.py:409
  26.9 1.5 %collective-permute-start.12 = (bf16[40,896]{1,0:T(8,128)(2,1)S(1)}, bf16[40,896]{1,0:T(8,128)(2,1)S(1)}, u32[]{:S(2)}, u32[]{:S(2)}) collective-permute-start(bf16[40,896]{1,0:T(8,128)(2,1)S(1)} %get-tuple-element.55), channel_id=1, source_target_pairs={{0,6},{1,7},{2,4},{3,5},{4,2},{5,3},{6,0},{7,1},{8,14},{9,15},{10,... | collective-permute-start | bytes 215048 | tf_op jit(solution)/shard_map/ppermute | solution.py:409
  28.5 0.8 %collective-permute-done.10.refs_1_ = bf16[40,896]{1,0:T(8,128)(2,1)S(1)} collective-permute-done((bf16[40,896]{1,0:T(8,128)(2,1)S(1)}, bf16[40,896]{1,0:T(8,128)(2,1)S(1)}, u32[]{:S(2)}, u32[]{:S(2)}) %collective-permute-start.10) | collective-permute-done | bytes 71712 | tf_op jit(solution)/shard_map/ppermute | solution.py:409
  29.3 1.1 %collective-permute-done.11.refs_2_ = bf16[40,896]{1,0:T(8,128)(2,1)S(1)} collective-permute-done((bf16[40,896]{1,0:T(8,128)(2,1)S(1)}, bf16[40,896]{1,0:T(8,128)(2,1)S(1)}, u32[]{:S(2)}, u32[]{:S(2)}) %collective-permute-start.11) | collective-permute-done | bytes 71712 | tf_op jit(solution)/shard_map/ppermute | solution.py:409
  30.4 1.9 %collective-permute-done.12.refs_3_ = bf16[40,896]{1,0:T(8,128)(2,1)S(1)} collective-permute-done((bf16[40,896]{1,0:T(8,128)(2,1)S(1)}, bf16[40,896]{1,0:T(8,128)(2,1)S(1)}, u32[]{:S(2)}, u32[]{:S(2)}) %collective-permute-start.12) | collective-permute-done | bytes 71712 | tf_op jit(solution)/shard_map/ppermute | solution.py:409
  32.3 1.5 %collective-permute-start.13 = (bf16[40,896]{1,0:T(8,128)(2,1)S(1)}, bf16[40,896]{1,0:T(8,128)(2,1)S(1)}, u32[]{:S(2)}, u32[]{:S(2)}) collective-permute-start(bf16[40,896]{1,0:T(8,128)(2,1)S(1)} %get-tuple-element.61), channel_id=1, source_target_pairs={{0,2},{1,3},{2,0},{3,1},{4,6},{5,7},{6,4},{7,5},{8,10},{9,11},{10,... | collective-permute-start | bytes 215048 | tf_op jit(solution)/shard_map/ppermute | solution.py:415
  33.8 2.8 %collective-permute-start.16 = (bf16[40,896]{1,0:T(8,128)(2,1)S(1)}, bf16[40,896]{1,0:T(8,128)(2,1)S(1)}, u32[]{:S(2)}, u32[]{:S(2)}) collective-permute-start(bf16[40,896]{1,0:T(8,128)(2,1)S(1)} %sum_blocks.1), channel_id=1, source_target_pairs={{0,8},{1,9},{2,10},{3,11},{4,12},{5,13},{6,14},{7,15},{8,0},{9,1},... | collective-permute-start | bytes 215048 | tf_op jit(solution)/shard_map/ppermute | solution.py:412
  36.6 0.4 collective-permute-start.14
  37.0 1.6 %collective-permute-start.15 = (bf16[40,896]{1,0:T(8,128)(2,1)S(1)}, bf16[40,896]{1,0:T(8,128)(2,1)S(1)}, u32[]{:S(2)}, u32[]{:S(2)}) collective-permute-start(bf16[40,896]{1,0:T(8,128)(2,1)S(1)} %get-tuple-element.63), channel_id=1, source_target_pairs={{0,6},{1,7},{2,4},{3,5},{4,2},{5,3},{6,0},{7,1},{8,14},{9,15},{10,... | collective-permute-start | bytes 215048 | tf_op jit(solution)/shard_map/ppermute | solution.py:415
  38.6 1.2 %collective-permute-done.16.block_ref = bf16[40,896]{1,0:T(8,128)(2,1)S(1)} collective-permute-done((bf16[40,896]{1,0:T(8,128)(2,1)S(1)}, bf16[40,896]{1,0:T(8,128)(2,1)S(1)}, u32[]{:S(2)}, u32[]{:S(2)}) %collective-permute-start.16) | collective-permute-done | bytes 71712 | tf_op jit(solution)/shard_map/ppermute | solution.py:412
  39.8 0.0 collective-permute-done.13.refs_1_
  39.8 1.1 %collective-permute-done.14.refs_2_ = bf16[40,896]{1,0:T(8,128)(2,1)S(1)} collective-permute-done((bf16[40,896]{1,0:T(8,128)(2,1)S(1)}, bf16[40,896]{1,0:T(8,128)(2,1)S(1)}, u32[]{:S(2)}, u32[]{:S(2)}) %collective-permute-start.14) | collective-permute-done | bytes 71712 | tf_op jit(solution)/shard_map/ppermute | solution.py:415
  40.9 1.3 %collective-permute-done.15.refs_3_ = bf16[40,896]{1,0:T(8,128)(2,1)S(1)} collective-permute-done((bf16[40,896]{1,0:T(8,128)(2,1)S(1)}, bf16[40,896]{1,0:T(8,128)(2,1)S(1)}, u32[]{:S(2)}, u32[]{:S(2)}) %collective-permute-start.15) | collective-permute-done | bytes 71712 | tf_op jit(solution)/shard_map/ppermute | solution.py:415
  42.2 1.5 %blend.1 = bf16[64,7168]{1,0:T(8,128)(2,1)} custom-call(bf16[512,200]{1,0:T(8,128)(2,1)S(1)} %blend_weights.1.weight_ref, f32[40,896]{1,0:T(8,128)S(1)} %get-tuple-element.60.refs_0_, bf16[40,896]{1,0:T(8,128)(2,1)S(1)} %collective-permute-done.13.refs_1_, bf16[40,896]{1,0:T(8,128)(2,1)S(1)} %collective-permute-done.14.refs_2_, ...), custom_call_target="tpu_custom_call" | custom-call | tf_op jit(solution)/shard_map/blend/pallas_call | solution.py:358
  (6 shorter events, 0.1 us)
Async XLA Ops:
  1.4 1.2 %copy-start.3 = (bf16[64,7168]{1,0:T(8,128)(2,1)S(1)}, bf16[64,7168]{1,0:T(8,128)(2,1)}, u32[]{:S(2)}) copy-start(bf16[64,7168]{1,0:T(8,128)(2,1)} %tokens_ref.1) | copy-start | bytes 2752516
  3.0 7.6 %collective-permute-start.3 = (bf16[40,896]{1,0:T(8,128)(2,1)S(1)}, bf16[40,896]{1,0:T(8,128)(2,1)S(1)}, u32[]{:S(2)}, u32[]{:S(2)}) collective-permute-start(bf16[40,896]{1,0:T(8,128)(2,1)S(1)} %get-tuple-element.36), channel_id=1, source_target_pairs={{0,8},{1,9},{2,10},{3,11},{4,12},{5,13},{6,14},{7,15},{8,0},{9,1},... | collective-permute-start | bytes 215048 | tf_op jit(solution)/shard_map/ppermute | solution.py:385
  7.1 6.7 %collective-permute-start.2 = (bf16[40,896]{1,0:T(8,128)(2,1)S(1)}, bf16[40,896]{1,0:T(8,128)(2,1)S(1)}, u32[]{:S(2)}, u32[]{:S(2)}) collective-permute-start(bf16[40,896]{1,0:T(8,128)(2,1)S(1)} %get-tuple-element.40.refs_0_), channel_id=1, source_target_pairs={{0,6},{1,7},{2,4},{3,5},{4,2},{5,3},{6,0},{7,1},{8,14},{9,15},{10,... | collective-permute-start | bytes 215048 | tf_op jit(solution)/shard_map/ppermute | solution.py:391
  9.7 5.3 %collective-permute-start.1 = (bf16[40,896]{1,0:T(8,128)(2,1)S(1)}, bf16[40,896]{1,0:T(8,128)(2,1)S(1)}, u32[]{:S(2)}, u32[]{:S(2)}) collective-permute-start(bf16[40,896]{1,0:T(8,128)(2,1)S(1)} %get-tuple-element.40.refs_0_), channel_id=1, source_target_pairs={{0,4},{1,5},{2,6},{3,7},{4,0},{5,1},{6,2},{7,3},{8,12},{9,13},{10,... | collective-permute-start | bytes 215048 | tf_op jit(solution)/shard_map/ppermute | solution.py:391
  10.1 5.4 %collective-permute-start = (bf16[40,896]{1,0:T(8,128)(2,1)S(1)}, bf16[40,896]{1,0:T(8,128)(2,1)S(1)}, u32[]{:S(2)}, u32[]{:S(2)}) collective-permute-start(bf16[40,896]{1,0:T(8,128)(2,1)S(1)} %get-tuple-element.40.refs_0_), channel_id=1, source_target_pairs={{0,2},{1,3},{2,0},{3,1},{4,6},{5,7},{6,4},{7,5},{8,10},{9,11},{10,... | collective-permute-start | bytes 215048 | tf_op jit(solution)/shard_map/ppermute | solution.py:391
  10.6 9.6 %copy-start = (bf16[256,7168]{1,0:T(8,128)(2,1)S(1)}, bf16[256,7168]{1,0:T(8,128)(2,1)}, u32[]{:S(2)}) copy-start(bf16[256,7168]{1,0:T(8,128)(2,1)} %down_ref.1) | copy-start | bytes 11010052
  10.6 9.6 %copy-start.1 = (bf16[7168,256]{1,0:T(8,128)(2,1)S(1)}, bf16[7168,256]{1,0:T(8,128)(2,1)}, u32[]{:S(2)}) copy-start(bf16[7168,256]{1,0:T(8,128)(2,1)} %refs_10_.1) | copy-start | bytes 11010052
  10.6 9.6 %copy-start.2 = (bf16[7168,256]{1,0:T(8,128)(2,1)S(1)}, bf16[7168,256]{1,0:T(8,128)(2,1)}, u32[]{:S(2)}) copy-start(bf16[7168,256]{1,0:T(8,128)(2,1)} %refs_11_.1) | copy-start | bytes 11010052
  10.6 5.8 %collective-permute-start.6 = (bf16[40,896]{1,0:T(8,128)(2,1)S(1)}, bf16[40,896]{1,0:T(8,128)(2,1)S(1)}, u32[]{:S(2)}, u32[]{:S(2)}) collective-permute-start(bf16[40,896]{1,0:T(8,128)(2,1)S(1)} %collective-permute-done.3.refs_0_.refs_4_), channel_id=1, source_target_pairs={{0,6},{1,7},{2,4},{3,5},{4,2},{5,3},{6,0},{7,1},{8,14},{9,15},{10,... | collective-permute-start | bytes 215048 | tf_op jit(solution)/shard_map/ppermute | solution.py:391
  13.2 4.3 %collective-permute-start.5 = (bf16[40,896]{1,0:T(8,128)(2,1)S(1)}, bf16[40,896]{1,0:T(8,128)(2,1)S(1)}, u32[]{:S(2)}, u32[]{:S(2)}) collective-permute-start(bf16[40,896]{1,0:T(8,128)(2,1)S(1)} %collective-permute-done.3.refs_0_.refs_4_), channel_id=1, source_target_pairs={{0,4},{1,5},{2,6},{3,7},{4,0},{5,1},{6,2},{7,3},{8,12},{9,13},{10,... | collective-permute-start | bytes 215048 | tf_op jit(solution)/shard_map/ppermute | solution.py:391
  13.8 4.3 %collective-permute-start.4 = (bf16[40,896]{1,0:T(8,128)(2,1)S(1)}, bf16[40,896]{1,0:T(8,128)(2,1)S(1)}, u32[]{:S(2)}, u32[]{:S(2)}) collective-permute-start(bf16[40,896]{1,0:T(8,128)(2,1)S(1)} %collective-permute-done.3.refs_0_.refs_4_), channel_id=1, source_target_pairs={{0,2},{1,3},{2,0},{3,1},{4,6},{5,7},{6,4},{7,5},{8,10},{9,11},{10,... | collective-permute-start | bytes 215048 | tf_op jit(solution)/shard_map/ppermute | solution.py:391
  18.2 1.6 %collective-permute-start.8 = (bf16[160,896]{1,0:T(8,128)(2,1)S(1)}, bf16[160,896]{1,0:T(8,128)(2,1)S(1)}, u32[]{:S(2)}, u32[]{:S(2)}) collective-permute-start(bf16[160,896]{1,0:T(8,128)(2,1)S(1)} %join.3), channel_id=1, source_target_pairs={{0,1},{1,0},{2,3},{3,2},{4,5},{5,4},{6,7},{7,6},{8,9},{9,8},{10,11... | collective-permute-start | bytes 860168 | tf_op jit(solution)/shard_map/ppermute | solution.py:400
  18.2 2.0 %collective-permute-start.7 = (bf16[160,896]{1,0:T(8,128)(2,1)S(1)}, bf16[160,896]{1,0:T(8,128)(2,1)S(1)}, u32[]{:S(2)}, u32[]{:S(2)}) collective-permute-start(bf16[160,896]{1,0:T(8,128)(2,1)S(1)} %join.2), channel_id=1, source_target_pairs={{0,1},{1,0},{2,3},{3,2},{4,5},{5,4},{6,7},{7,6},{8,9},{9,8},{10,11... | collective-permute-start | bytes 860168 | tf_op jit(solution)/shard_map/ppermute | solution.py:400
  22.7 2.0 %collective-permute-start.9 = (bf16[320,896]{1,0:T(8,128)(2,1)S(1)}, bf16[320,896]{1,0:T(8,128)(2,1)S(1)}, u32[]{:S(2)}, u32[]{:S(2)}) collective-permute-start(bf16[320,896]{1,0:T(8,128)(2,1)S(1)} %get-tuple-element.51), channel_id=1, source_target_pairs={{0,1},{1,0},{2,3},{3,2},{4,5},{5,4},{6,7},{7,6},{8,9},{9,8},{10,11... | collective-permute-start | bytes 1720328 | tf_op jit(solution)/shard_map/ppermute | solution.py:402
  24.9 4.4 %collective-permute-start.10 = (bf16[40,896]{1,0:T(8,128)(2,1)S(1)}, bf16[40,896]{1,0:T(8,128)(2,1)S(1)}, u32[]{:S(2)}, u32[]{:S(2)}) collective-permute-start(bf16[40,896]{1,0:T(8,128)(2,1)S(1)} %get-tuple-element.53), channel_id=1, source_target_pairs={{0,2},{1,3},{2,0},{3,1},{4,6},{5,7},{6,4},{7,5},{8,10},{9,11},{10,... | collective-permute-start | bytes 215048 | tf_op jit(solution)/shard_map/ppermute | solution.py:409
  25.9 4.5 %collective-permute-start.11 = (bf16[40,896]{1,0:T(8,128)(2,1)S(1)}, bf16[40,896]{1,0:T(8,128)(2,1)S(1)}, u32[]{:S(2)}, u32[]{:S(2)}) collective-permute-start(bf16[40,896]{1,0:T(8,128)(2,1)S(1)} %get-tuple-element.54), channel_id=1, source_target_pairs={{0,4},{1,5},{2,6},{3,7},{4,0},{5,1},{6,2},{7,3},{8,12},{9,13},{10,... | collective-permute-start | bytes 215048 | tf_op jit(solution)/shard_map/ppermute | solution.py:409
  26.9 5.4 %collective-permute-start.12 = (bf16[40,896]{1,0:T(8,128)(2,1)S(1)}, bf16[40,896]{1,0:T(8,128)(2,1)S(1)}, u32[]{:S(2)}, u32[]{:S(2)}) collective-permute-start(bf16[40,896]{1,0:T(8,128)(2,1)S(1)} %get-tuple-element.55), channel_id=1, source_target_pairs={{0,6},{1,7},{2,4},{3,5},{4,2},{5,3},{6,0},{7,1},{8,14},{9,15},{10,... | collective-permute-start | bytes 215048 | tf_op jit(solution)/shard_map/ppermute | solution.py:409
  32.3 7.5 %collective-permute-start.13 = (bf16[40,896]{1,0:T(8,128)(2,1)S(1)}, bf16[40,896]{1,0:T(8,128)(2,1)S(1)}, u32[]{:S(2)}, u32[]{:S(2)}) collective-permute-start(bf16[40,896]{1,0:T(8,128)(2,1)S(1)} %get-tuple-element.61), channel_id=1, source_target_pairs={{0,2},{1,3},{2,0},{3,1},{4,6},{5,7},{6,4},{7,5},{8,10},{9,11},{10,... | collective-permute-start | bytes 215048 | tf_op jit(solution)/shard_map/ppermute | solution.py:415
  33.8 6.0 %collective-permute-start.16 = (bf16[40,896]{1,0:T(8,128)(2,1)S(1)}, bf16[40,896]{1,0:T(8,128)(2,1)S(1)}, u32[]{:S(2)}, u32[]{:S(2)}) collective-permute-start(bf16[40,896]{1,0:T(8,128)(2,1)S(1)} %sum_blocks.1), channel_id=1, source_target_pairs={{0,8},{1,9},{2,10},{3,11},{4,12},{5,13},{6,14},{7,15},{8,0},{9,1},... | collective-permute-start | bytes 215048 | tf_op jit(solution)/shard_map/ppermute | solution.py:412
  36.6 4.3 %collective-permute-start.14 = (bf16[40,896]{1,0:T(8,128)(2,1)S(1)}, bf16[40,896]{1,0:T(8,128)(2,1)S(1)}, u32[]{:S(2)}, u32[]{:S(2)}) collective-permute-start(bf16[40,896]{1,0:T(8,128)(2,1)S(1)} %get-tuple-element.62), channel_id=1, source_target_pairs={{0,4},{1,5},{2,6},{3,7},{4,0},{5,1},{6,2},{7,3},{8,12},{9,13},{10,... | collective-permute-start | bytes 215048 | tf_op jit(solution)/shard_map/ppermute | solution.py:415
  37.0 5.2 %collective-permute-start.15 = (bf16[40,896]{1,0:T(8,128)(2,1)S(1)}, bf16[40,896]{1,0:T(8,128)(2,1)S(1)}, u32[]{:S(2)}, u32[]{:S(2)}) collective-permute-start(bf16[40,896]{1,0:T(8,128)(2,1)S(1)} %get-tuple-element.63), channel_id=1, source_target_pairs={{0,6},{1,7},{2,4},{3,5},{4,2},{5,3},{6,0},{7,1},{8,14},{9,15},{10,... | collective-permute-start | bytes 215048 | tf_op jit(solution)/shard_map/ppermute | solution.py:415

commit v8 on v7

--- a/solution.py
+++ b/solution.py
@@ -61,13 +61,17 @@
         copy.wait()
 
 
-def pack_kernel(teams, routes_ref, tokens_ref, *refs):
-    *out_refs, table_ref = refs
+def pack_kernel(teams, ids_hbm, logits_hbm, tokens_hbm, *refs):
+    *out_refs, table_ref, ids_ref, logits_ref, tokens_ref, ids_sem, logits_sem, tokens_sem = refs
+    ids_copy = bring(ids_hbm, ids_ref, ids_sem, 1)
+    tokens_copy = bring(tokens_hbm, tokens_ref, tokens_sem, 4)
+    logits_copy = bring(logits_hbm, logits_ref, logits_sem, 1)
+    wait_all(ids_copy)
     mine = lax.axis_index("expert") // SPLIT
-    picks = routes_ref.shape[0] // 2
-    ids = routes_ref[:picks, :].astype(jnp.int32)
+    ids = ids_ref[...]
     hit, slot = hits(ids, mine, teams)
-    lifted = jax.nn.sigmoid(routes_ref[picks:, :])
+    wait_all(logits_copy)
+    lifted = jax.nn.sigmoid(logits_ref[...])
     gates = route_scale * lifted / jnp.sum(lifted, axis=0, keepdims=True)
     row = lax.broadcasted_iota(jnp.int32, hit.shape, 0)
     wanted = lax.rem(mine + row, teams)
@@ -86,6 +90,7 @@
     for k in range(teams):
         slots = jnp.concatenate([slot[k : k + 1, :]] * SEGMENTS, axis=1)
         picks.append(jnp.where(same & (slots == place), 1.0, 0.0))
+    wait_all(tokens_copy)
     stacked = jnp.concatenate(
         [tokens_ref[:, s * wide : (s + 1) * wide] for s in range(SEGMENTS)], axis=0
     )
@@ -98,18 +103,25 @@
         out_refs[k][...] = packed[k * tall : (k + 1) * tall].astype(jnp.bfloat16)
 
 
-def pack_rows(routes, tokens, teams):
+def pack_rows(ids, logits, tokens, teams):
     wide = tokens.shape[1] // SEGMENTS
     block = jax.ShapeDtypeStruct((CAP * SEGMENTS, wide), jnp.bfloat16)
-    table = jax.ShapeDtypeStruct((16 * pl.cdiv(teams, 8), routes.shape[1]), jnp.float32)
+    table = jax.ShapeDtypeStruct((16 * pl.cdiv(teams, 8), ids.shape[1]), jnp.float32)
     *packed, table = pl.pallas_call(
         functools.partial(pack_kernel, teams),
         out_shape=[block] * teams + [table],
-        in_specs=[VMEM] * 2,
+        in_specs=[HBM] * 3,
         out_specs=[VMEM] * (teams + 1),
-        compiler_params=params(8),
+        scratch_shapes=[
+            pltpu.VMEM(ids.shape, ids.dtype),
+            pltpu.VMEM(logits.shape, logits.dtype),
+            pltpu.VMEM(tokens.shape, tokens.dtype),
+            pltpu.SemaphoreType.DMA((1,)),
+            pltpu.SemaphoreType.DMA((1,)),
+            pltpu.SemaphoreType.DMA((4,)),
+        ],
         name="pack_rows",
-    )(routes, tokens)
+    )(ids, logits, tokens)
     return packed, table
 
 
@@ -311,22 +323,6 @@
     )(*blocks)
 
 
-def settle_kernel(block_ref, out_ref):
-    out_ref[...] = block_ref[...].astype(jnp.float32)
-
-
-def settle(block):
-    return pl.pallas_call(
-        settle_kernel,
-        out_shape=jax.ShapeDtypeStruct(block.shape, jnp.float32),
-        in_specs=[VMEM],
-        out_specs=VMEM,
-        compiler_params=params(4),
-        cost_estimate=pl.CostEstimate(flops=0, bytes_accessed=16 * MIB, transcendentals=0),
-        name="settle",
-    )(block)
-
-
 def blend_kernel(chips, weight_ref, *refs):
     *refs, out_hbm, out_ref, sem = refs
     count, features = out_ref.shape
@@ -337,7 +333,7 @@
     high = own.astype(jnp.bfloat16).astype(jnp.float32)
     terms = [high, own - high, high]
     for ref in refs[chips:]:
-        terms += [ref[...]] * 2
+        terms += [ref[...].astype(jnp.float32)] * 2
     rows = jnp.concatenate(terms, axis=0).astype(jnp.bfloat16)
     copies = []
     for s in range(SEGMENTS):
@@ -375,8 +371,7 @@
     chips = SPLIT // CORES
     other_core = [(i, i ^ 1) for i in range(devices)]
     other_chip = [[(i, i ^ (m * CORES)) for i in range(devices)] for m in range(chips)]
-    routes = jnp.concatenate([expert_ids.T.astype(jnp.float32), route_logits.T], axis=0)
-    packed, table = pack_rows(routes, tokens, teams)
+    packed, table = pack_rows(expert_ids.T, route_logits.T, tokens, teams)
     crowds = []
     for k in range(teams):
         block = packed[k]
@@ -408,8 +403,7 @@
         for m in range(1, chips):
             team.append(lax.ppermute(parts[k * chips + m], "expert", other_chip[m]))
         pairs = [(i, (i - k * SPLIT) % devices) for i in range(devices)]
-        total, parts = lax.optimization_barrier((sum_blocks(team), parts))
-        others.append(settle(lax.ppermute(total, "expert", pairs)))
+        others.append(lax.ppermute(sum_blocks(team), "expert", pairs))
     own = [parts[0]]
     for m in range(1, chips):
         own.append(lax.ppermute(parts[m], "expert", other_chip[m]))

time: 43.9 us -> 40 us (0.911)
  waiting for transfers between devices: 13.2 us -> 8.84 us
  Pallas kernels: 5.7 us -> 7.49 us
  other arithmetic: 1.38 us -> 0 us
  starting transfers between devices: 22.2 us -> 22.7 us
  local copies, waits for them, and re-layouts: 1.19 us -> 0.71 us
    ppermute x3, waiting for transfers between devices: 3.84 us -> 0.76 us  [body(): team.append(lax.ppermute(parts[k * chips + m], 'expert', other_chip[m]))]
    ppermute x3, waiting for transfers between devices: 2.42 us -> 0.51 us  [body(): own.append(lax.ppermute(parts[m], 'expert', other_chip[m]))]
    pallas_call x1, Pallas kernels: 0.47 us -> 2.28 us  [pack_rows(): pl.pallas_call(functools.partial(pack_kernel, teams), out_shape=[block] *...]
    ppermute x1, waiting for transfers between devices: 1.21 us -> 2.56 us  [body(): others.append(lax.ppermute(sum_blocks(team), 'expert', pairs))]
    ppermute x6, waiting for transfers between devices: 3.1 us -> 2.39 us  [body(): team.append(lax.ppermute(block, 'expert', other_chip[m]))]
    concatenate x1 -> x0, other arithmetic: 0.69 us -> none  [body(): jnp.concatenate([expert_ids.T.astype(jnp.float32), route_logits.T], axis=0)]
    convert_element_type x1 -> x0, other arithmetic: 0.69 us -> none  [body(): expert_ids.T.astype(jnp.float32)]
    unnamed x8 -> x10, local copies, waits for them, and re-layouts: 1.19 us -> 0.71 us
  transfers between devices with their start and end apart: 17 -> 17, of which waited for: 13 -> 9; matrix products, arithmetic and copies ran while one was open for 0% -> 0% of each run, Pallas kernels for 2% -> 3%
where the time goes in v8:
time: 40 us; the launch traced here: 39.8 us
  starting transfers between devices  22.7 us (57%)
  waiting for transfers between devices  8.84 us (22%)
  Pallas kernels  7.49 us (19%)
  local copies, waits for them, and re-layouts  0.71 us (2%)
    ppermute x6, starting transfers between devices, body(): team.append(lax.ppermute(block, 'expert', other_chip[m]))  7.79 us
    ppermute x1, starting transfers between devices, body(): block = lax.ppermute(block, 'expert', pairs)  4.1 us
    ppermute x3, starting transfers between devices, body(): team.append(lax.ppermute(parts[k * chips + m], 'expert', other_chip[m]))  3.55 us
    ppermute x3, starting transfers between devices, body(): own.append(lax.ppermute(parts[m], 'expert', other_chip[m]))  3.49 us
    ppermute x1, starting transfers between devices, body(): others.append(lax.ppermute(sum_blocks(team), 'expert', pairs))  3 us
    ppermute x1, waiting for transfers between devices, body(): others.append(lax.ppermute(sum_blocks(team), 'expert', pairs))  2.56 us
    pallas_call x1, Pallas kernels, expert_half(): pl.pallas_call(functools.partial(expert_kernel, own), out_shape=[jax.Shap...  2.5 us
    ppermute x6, waiting for transfers between devices, body(): team.append(lax.ppermute(block, 'expert', other_chip[m]))  2.39 us
  transfers between devices with their start and end apart: 17, of which 9 were waited for; matrix products, arithmetic and copies ran while one was open for 0% of the time, Pallas kernels for 3%

profile of v8, /device:TPU:0, one launch (start us, length us, event | category | flops | bytes accessed | tf_op | source)
XLA Modules:
  0.0 39.8 jit_solution(167778082097989096)
XLA Ops:
  0.0 2.3 %pack_rows.1 = (bf16[40,896]{1,0:T(8,128)(2,1)}, bf16[40,896]{1,0:T(8,128)(2,1)}, f32[16,64]{1,0:T(8,128)}) custom-call(s32[8,64]{1,0:T(8,128)} %bitcast.2, f32[8,64]{1,0:T(8,128)} %bitcast.3, bf16[64,7168]{1,0:T(8,128)(2,1)} %tokens_hbm.1), custom_call_target="tpu_custom_call" | custom-call | tf_op jit(solution)/shard_map/pack_rows/pallas_call | solution.py:110
  2.3 4.1 %collective-permute-start.3 = (bf16[40,896]{1,0:T(8,128)(2,1)}, bf16[40,896]{1,0:T(8,128)(2,1)S(1)}, u32[]{:S(2)}, u32[]{:S(2)}) collective-permute-start(bf16[40,896]{1,0:T(8,128)(2,1)} %get-tuple-element.31), channel_id=1, source_target_pairs={{0,8},{1,9},{2,10},{3,11},{4,12},{5,13},{6,14},{7,15},{8,0},{9,1},... | collective-permute-start | bytes 215048 | tf_op jit(solution)/shard_map/ppermute | solution.py:380
  6.4 2.5 %collective-permute-start.2 = (bf16[40,896]{1,0:T(8,128)(2,1)}, bf16[40,896]{1,0:T(8,128)(2,1)S(1)}, u32[]{:S(2)}, u32[]{:S(2)}) collective-permute-start(bf16[40,896]{1,0:T(8,128)(2,1)} %get-tuple-element.35.refs_0_), channel_id=1, source_target_pairs={{0,6},{1,7},{2,4},{3,5},{4,2},{5,3},{6,0},{7,1},{8,14},{9,15},{10,... | collective-permute-start | bytes 215048 | tf_op jit(solution)/shard_map/ppermute | solution.py:386
  8.9 0.4 %collective-permute-start.1 = (bf16[40,896]{1,0:T(8,128)(2,1)}, bf16[40,896]{1,0:T(8,128)(2,1)S(1)}, u32[]{:S(2)}, u32[]{:S(2)}) collective-permute-start(bf16[40,896]{1,0:T(8,128)(2,1)} %get-tuple-element.35.refs_0_), channel_id=1, source_target_pairs={{0,4},{1,5},{2,6},{3,7},{4,0},{5,1},{6,2},{7,3},{8,12},{9,13},{10,... | collective-permute-start | bytes 215048 | tf_op jit(solution)/shard_map/ppermute | solution.py:386
  9.4 0.5 %collective-permute-start = (bf16[40,896]{1,0:T(8,128)(2,1)}, bf16[40,896]{1,0:T(8,128)(2,1)S(1)}, u32[]{:S(2)}, u32[]{:S(2)}) collective-permute-start(bf16[40,896]{1,0:T(8,128)(2,1)} %get-tuple-element.35.refs_0_), channel_id=1, source_target_pairs={{0,2},{1,3},{2,0},{3,1},{4,6},{5,7},{6,4},{7,5},{8,10},{9,11},{10,... | collective-permute-start | bytes 215048 | tf_op jit(solution)/shard_map/ppermute | solution.py:386
  9.9 0.0 collective-permute-done.3.refs_0_.refs_4_
  9.9 0.0 copy-start.3
  9.9 0.0 copy-start
  9.9 0.0 copy-start.2
  9.9 2.7 %collective-permute-start.6 = (bf16[40,896]{1,0:T(8,128)(2,1)S(1)}, bf16[40,896]{1,0:T(8,128)(2,1)S(1)}, u32[]{:S(2)}, u32[]{:S(2)}) collective-permute-start(bf16[40,896]{1,0:T(8,128)(2,1)S(1)} %collective-permute-done.3.refs_0_.refs_4_), channel_id=1, source_target_pairs={{0,6},{1,7},{2,4},{3,5},{4,2},{5,3},{6,0},{7,1},{8,14},{9,15},{10,... | collective-permute-start | bytes 215048 | tf_op jit(solution)/shard_map/ppermute | solution.py:386
  12.6 0.7 %collective-permute-start.5 = (bf16[40,896]{1,0:T(8,128)(2,1)S(1)}, bf16[40,896]{1,0:T(8,128)(2,1)S(1)}, u32[]{:S(2)}, u32[]{:S(2)}) collective-permute-start(bf16[40,896]{1,0:T(8,128)(2,1)S(1)} %collective-permute-done.3.refs_0_.refs_4_), channel_id=1, source_target_pairs={{0,4},{1,5},{2,6},{3,7},{4,0},{5,1},{6,2},{7,3},{8,12},{9,13},{10,... | collective-permute-start | bytes 215048 | tf_op jit(solution)/shard_map/ppermute | solution.py:386
  13.3 0.0 collective-permute-done.2.refs_3_
  13.3 0.9 %collective-permute-start.4 = (bf16[40,896]{1,0:T(8,128)(2,1)S(1)}, bf16[40,896]{1,0:T(8,128)(2,1)S(1)}, u32[]{:S(2)}, u32[]{:S(2)}) collective-permute-start(bf16[40,896]{1,0:T(8,128)(2,1)S(1)} %collective-permute-done.3.refs_0_.refs_4_), channel_id=1, source_target_pairs={{0,2},{1,3},{2,0},{3,1},{4,6},{5,7},{6,4},{7,5},{8,10},{9,11},{10,... | collective-permute-start | bytes 215048 | tf_op jit(solution)/shard_map/ppermute | solution.py:386
  14.2 0.7 %copy-done.4 = f32[16,64]{1,0:T(8,128)S(1)} copy-done((f32[16,64]{1,0:T(8,128)S(1)}, f32[16,64]{1,0:T(8,128)}, u32[]{:S(2)}) %copy-start.4) | copy-done | bytes 4120
  14.9 0.3 blend_weights.1.weight_ref
  15.2 0.0 collective-permute-done.1.refs_2_
  15.2 0.0 collective-permute-done.refs_1_
  15.3 0.0 copy-done.3
  15.3 0.6 %collective-permute-done.6.refs_3_.refs_7_ = bf16[40,896]{1,0:T(8,128)(2,1)S(1)} collective-permute-done((bf16[40,896]{1,0:T(8,128)(2,1)S(1)}, bf16[40,896]{1,0:T(8,128)(2,1)S(1)}, u32[]{:S(2)}, u32[]{:S(2)}) %collective-permute-start.6) | collective-permute-done | bytes 71712 | tf_op jit(solution)/shard_map/ppermute | solution.py:386
  15.9 1.1 %collective-permute-done.5.refs_2_.refs_6_ = bf16[40,896]{1,0:T(8,128)(2,1)S(1)} collective-permute-done((bf16[40,896]{1,0:T(8,128)(2,1)S(1)}, bf16[40,896]{1,0:T(8,128)(2,1)S(1)}, u32[]{:S(2)}, u32[]{:S(2)}) %collective-permute-start.5) | collective-permute-done | bytes 71712 | tf_op jit(solution)/shard_map/ppermute | solution.py:386
  17.0 0.7 %collective-permute-done.4.refs_1_.refs_5_ = bf16[40,896]{1,0:T(8,128)(2,1)S(1)} collective-permute-done((bf16[40,896]{1,0:T(8,128)(2,1)S(1)}, bf16[40,896]{1,0:T(8,128)(2,1)S(1)}, u32[]{:S(2)}, u32[]{:S(2)}) %collective-permute-start.4) | collective-permute-done | bytes 71712 | tf_op jit(solution)/shard_map/ppermute | solution.py:386
  17.7 0.1 collective-permute-start.8
  17.8 0.5 %collective-permute-start.7 = (bf16[160,896]{1,0:T(8,128)(2,1)S(1)}, bf16[160,896]{1,0:T(8,128)(2,1)S(1)}, u32[]{:S(2)}, u32[]{:S(2)}) collective-permute-start(bf16[160,896]{1,0:T(8,128)(2,1)S(1)} %join.2), channel_id=1, source_target_pairs={{0,1},{1,0},{2,3},{3,2},{4,5},{5,4},{6,7},{7,6},{8,9},{9,8},{10,11... | collective-permute-start | bytes 860168 | tf_op jit(solution)/shard_map/ppermute | solution.py:395
  18.3 1.1 %collective-permute-done.8.refs_9_ = bf16[160,896]{1,0:T(8,128)(2,1)S(1)} collective-permute-done((bf16[160,896]{1,0:T(8,128)(2,1)S(1)}, bf16[160,896]{1,0:T(8,128)(2,1)S(1)}, u32[]{:S(2)}, u32[]{:S(2)}) %collective-permute-start.8) | collective-permute-done | bytes 286752 | tf_op jit(solution)/shard_map/ppermute | solution.py:395
  19.3 0.4 %collective-permute-done.7.refs_8_ = bf16[160,896]{1,0:T(8,128)(2,1)S(1)} collective-permute-done((bf16[160,896]{1,0:T(8,128)(2,1)S(1)}, bf16[160,896]{1,0:T(8,128)(2,1)S(1)}, u32[]{:S(2)}, u32[]{:S(2)}) %collective-permute-start.7) | collective-permute-done | bytes 286752 | tf_op jit(solution)/shard_map/ppermute | solution.py:395
  19.7 0.0 copy-done
  19.7 0.0 copy-done.1
  19.7 0.0 copy-done.2
  19.7 2.5 %expert_half.1 = (bf16[320,896]{1,0:T(8,128)(2,1)S(1)}, bf16[40,256]{1,0:T(8,128)(2,1)S(1)}) custom-call(bf16[40,896]{1,0:T(8,128)(2,1)S(1)} %copy-done.3, bf16[40,896]{1,0:T(8,128)(2,1)S(1)} %collective-permute-done.refs_1_, bf16[40,896]{1,0:T(8,128)(2,1)S(1)} %collective-permute-done.1.refs_2_, bf16[40,896]{1,0:T(8,128)(2,1)S(1)} %collective-permute-done.2.refs_3_, ...), custom_call_target="tpu_custom_call" | custom-call | flops 734003200 | bytes 11010048 | tf_op jit(solution)/shard_map/expert_half/pallas_call | solution.py:236
  22.2 0.2 collective-permute-start.9
  22.4 0.7 %kept_half.1.kept_ref = f32[320,896]{1,0:T(8,128)S(1)} custom-call(bf16[40,256]{1,0:T(8,128)(2,1)S(1)} %get-tuple-element.45.hidden_ref, bf16[256,7168]{1,0:T(8,128)(2,1)S(1)} %copy-done), custom_call_target="tpu_custom_call" | custom-call | flops 146800640 | bytes 3670016 | tf_op jit(solution)/shard_map/kept_half/pallas_call | solution.py:267
  23.2 1.1 %collective-permute-done.9.taken_ref = bf16[320,896]{1,0:T(8,128)(2,1)S(1)} collective-permute-done((bf16[320,896]{1,0:T(8,128)(2,1)S(1)}, bf16[320,896]{1,0:T(8,128)(2,1)S(1)}, u32[]{:S(2)}, u32[]{:S(2)}) %collective-permute-start.9) | collective-permute-done | bytes 573472 | tf_op jit(solution)/shard_map/ppermute | solution.py:397
  24.3 0.1 add_cores.1
  24.4 1.0 %collective-permute-start.13 = (bf16[40,896]{1,0:T(8,128)(2,1)S(1)}, bf16[40,896]{1,0:T(8,128)(2,1)S(1)}, u32[]{:S(2)}, u32[]{:S(2)}) collective-permute-start(bf16[40,896]{1,0:T(8,128)(2,1)S(1)} %get-tuple-element.52), channel_id=1, source_target_pairs={{0,2},{1,3},{2,0},{3,1},{4,6},{5,7},{6,4},{7,5},{8,10},{9,11},{10,... | collective-permute-start | bytes 215048 | tf_op jit(solution)/shard_map/ppermute | solution.py:404
  25.4 0.9 %collective-permute-start.14 = (bf16[40,896]{1,0:T(8,128)(2,1)S(1)}, bf16[40,896]{1,0:T(8,128)(2,1)S(1)}, u32[]{:S(2)}, u32[]{:S(2)}) collective-permute-start(bf16[40,896]{1,0:T(8,128)(2,1)S(1)} %get-tuple-element.53), channel_id=1, source_target_pairs={{0,4},{1,5},{2,6},{3,7},{4,0},{5,1},{6,2},{7,3},{8,12},{9,13},{10,... | collective-permute-start | bytes 215048 | tf_op jit(solution)/shard_map/ppermute | solution.py:404
  26.3 1.7 %collective-permute-start.15 = (bf16[40,896]{1,0:T(8,128)(2,1)S(1)}, bf16[40,896]{1,0:T(8,128)(2,1)S(1)}, u32[]{:S(2)}, u32[]{:S(2)}) collective-permute-start(bf16[40,896]{1,0:T(8,128)(2,1)S(1)} %get-tuple-element.54), channel_id=1, source_target_pairs={{0,6},{1,7},{2,4},{3,5},{4,2},{5,3},{6,0},{7,1},{8,14},{9,15},{10,... | collective-permute-start | bytes 215048 | tf_op jit(solution)/shard_map/ppermute | solution.py:404
  28.0 0.9 %collective-permute-start.10 = (bf16[40,896]{1,0:T(8,128)(2,1)S(1)}, bf16[40,896]{1,0:T(8,128)(2,1)S(1)}, u32[]{:S(2)}, u32[]{:S(2)}) collective-permute-start(bf16[40,896]{1,0:T(8,128)(2,1)S(1)} %get-tuple-element.48), channel_id=1, source_target_pairs={{0,2},{1,3},{2,0},{3,1},{4,6},{5,7},{6,4},{7,5},{8,10},{9,11},{10,... | collective-permute-start | bytes 215048 | tf_op jit(solution)/shard_map/ppermute | solution.py:409
  28.9 0.9 %collective-permute-start.11 = (bf16[40,896]{1,0:T(8,128)(2,1)S(1)}, bf16[40,896]{1,0:T(8,128)(2,1)S(1)}, u32[]{:S(2)}, u32[]{:S(2)}) collective-permute-start(bf16[40,896]{1,0:T(8,128)(2,1)S(1)} %get-tuple-element.49), channel_id=1, source_target_pairs={{0,4},{1,5},{2,6},{3,7},{4,0},{5,1},{6,2},{7,3},{8,12},{9,13},{10,... | collective-permute-start | bytes 215048 | tf_op jit(solution)/shard_map/ppermute | solution.py:409
  29.8 0.0 collective-permute-done.13.refs_1_
  29.8 1.7 %collective-permute-start.12 = (bf16[40,896]{1,0:T(8,128)(2,1)S(1)}, bf16[40,896]{1,0:T(8,128)(2,1)S(1)}, u32[]{:S(2)}, u32[]{:S(2)}) collective-permute-start(bf16[40,896]{1,0:T(8,128)(2,1)S(1)} %get-tuple-element.50), channel_id=1, source_target_pairs={{0,6},{1,7},{2,4},{3,5},{4,2},{5,3},{6,0},{7,1},{8,14},{9,15},{10,... | collective-permute-start | bytes 215048 | tf_op jit(solution)/shard_map/ppermute | solution.py:409
  31.5 0.0 collective-permute-done.14.refs_2_
  31.5 0.8 %collective-permute-done.15.refs_3_ = bf16[40,896]{1,0:T(8,128)(2,1)S(1)} collective-permute-done((bf16[40,896]{1,0:T(8,128)(2,1)S(1)}, bf16[40,896]{1,0:T(8,128)(2,1)S(1)}, u32[]{:S(2)}, u32[]{:S(2)}) %collective-permute-start.15) | collective-permute-done | bytes 71712 | tf_op jit(solution)/shard_map/ppermute | solution.py:404
  32.3 3.0 %collective-permute-start.16 = (bf16[40,896]{1,0:T(8,128)(2,1)S(1)}, bf16[40,896]{1,0:T(8,128)(2,1)S(1)}, u32[]{:S(2)}, u32[]{:S(2)}) collective-permute-start(bf16[40,896]{1,0:T(8,128)(2,1)S(1)} %sum_blocks.1), channel_id=1, source_target_pairs={{0,8},{1,9},{2,10},{3,11},{4,12},{5,13},{6,14},{7,15},{8,0},{9,1},... | collective-permute-start | bytes 215048 | tf_op jit(solution)/shard_map/ppermute | solution.py:406
  35.3 0.0 collective-permute-done.10.refs_1_
  35.3 0.0 collective-permute-done.11.refs_2_
  35.3 0.5 %collective-permute-done.12.refs_3_ = bf16[40,896]{1,0:T(8,128)(2,1)S(1)} collective-permute-done((bf16[40,896]{1,0:T(8,128)(2,1)S(1)}, bf16[40,896]{1,0:T(8,128)(2,1)S(1)}, u32[]{:S(2)}, u32[]{:S(2)}) %collective-permute-start.12) | collective-permute-done | bytes 71712 | tf_op jit(solution)/shard_map/ppermute | solution.py:409
  35.8 2.6 %collective-permute-done.16.refs_4_ = bf16[40,896]{1,0:T(8,128)(2,1)S(1)} collective-permute-done((bf16[40,896]{1,0:T(8,128)(2,1)S(1)}, bf16[40,896]{1,0:T(8,128)(2,1)S(1)}, u32[]{:S(2)}, u32[]{:S(2)}) %collective-permute-start.16) | collective-permute-done | bytes 71712 | tf_op jit(solution)/shard_map/ppermute | solution.py:406
  38.4 1.5 %blend.1 = bf16[64,7168]{1,0:T(8,128)(2,1)} custom-call(bf16[512,200]{1,0:T(8,128)(2,1)S(1)} %blend_weights.1.weight_ref, f32[40,896]{1,0:T(8,128)S(1)} %get-tuple-element.47.refs_0_, bf16[40,896]{1,0:T(8,128)(2,1)S(1)} %collective-permute-done.10.refs_1_, bf16[40,896]{1,0:T(8,128)(2,1)S(1)} %collective-permute-done.11.refs_2_, ...), custom_call_target="tpu_custom_call" | custom-call | tf_op jit(solution)/shard_map/blend/pallas_call | solution.py:354
  (5 shorter events, 0.1 us)
Async XLA Ops:
  2.3 7.6 %collective-permute-start.3 = (bf16[40,896]{1,0:T(8,128)(2,1)}, bf16[40,896]{1,0:T(8,128)(2,1)S(1)}, u32[]{:S(2)}, u32[]{:S(2)}) collective-permute-start(bf16[40,896]{1,0:T(8,128)(2,1)} %get-tuple-element.31), channel_id=1, source_target_pairs={{0,8},{1,9},{2,10},{3,11},{4,12},{5,13},{6,14},{7,15},{8,0},{9,1},... | collective-permute-start | bytes 215048 | tf_op jit(solution)/shard_map/ppermute | solution.py:380
  6.4 6.9 %collective-permute-start.2 = (bf16[40,896]{1,0:T(8,128)(2,1)}, bf16[40,896]{1,0:T(8,128)(2,1)S(1)}, u32[]{:S(2)}, u32[]{:S(2)}) collective-permute-start(bf16[40,896]{1,0:T(8,128)(2,1)} %get-tuple-element.35.refs_0_), channel_id=1, source_target_pairs={{0,6},{1,7},{2,4},{3,5},{4,2},{5,3},{6,0},{7,1},{8,14},{9,15},{10,... | collective-permute-start | bytes 215048 | tf_op jit(solution)/shard_map/ppermute | solution.py:386
  8.9 6.3 %collective-permute-start.1 = (bf16[40,896]{1,0:T(8,128)(2,1)}, bf16[40,896]{1,0:T(8,128)(2,1)S(1)}, u32[]{:S(2)}, u32[]{:S(2)}) collective-permute-start(bf16[40,896]{1,0:T(8,128)(2,1)} %get-tuple-element.35.refs_0_), channel_id=1, source_target_pairs={{0,4},{1,5},{2,6},{3,7},{4,0},{5,1},{6,2},{7,3},{8,12},{9,13},{10,... | collective-permute-start | bytes 215048 | tf_op jit(solution)/shard_map/ppermute | solution.py:386
  9.4 5.9 %collective-permute-start = (bf16[40,896]{1,0:T(8,128)(2,1)}, bf16[40,896]{1,0:T(8,128)(2,1)S(1)}, u32[]{:S(2)}, u32[]{:S(2)}) collective-permute-start(bf16[40,896]{1,0:T(8,128)(2,1)} %get-tuple-element.35.refs_0_), channel_id=1, source_target_pairs={{0,2},{1,3},{2,0},{3,1},{4,6},{5,7},{6,4},{7,5},{8,10},{9,11},{10,... | collective-permute-start | bytes 215048 | tf_op jit(solution)/shard_map/ppermute | solution.py:386
  9.9 5.4 %copy-start.3 = (bf16[40,896]{1,0:T(8,128)(2,1)S(1)}, bf16[40,896]{1,0:T(8,128)(2,1)}, u32[]{:S(2)}) copy-start(bf16[40,896]{1,0:T(8,128)(2,1)} %get-tuple-element.35.refs_0_) | copy-start | bytes 215044
  9.9 9.9 %copy-start = (bf16[256,7168]{1,0:T(8,128)(2,1)S(1)}, bf16[256,7168]{1,0:T(8,128)(2,1)}, u32[]{:S(2)}) copy-start(bf16[256,7168]{1,0:T(8,128)(2,1)} %down_ref.1) | copy-start | bytes 11010052
  9.9 9.9 %copy-start.1 = (bf16[7168,256]{1,0:T(8,128)(2,1)S(1)}, bf16[7168,256]{1,0:T(8,128)(2,1)}, u32[]{:S(2)}) copy-start(bf16[7168,256]{1,0:T(8,128)(2,1)} %refs_10_.1) | copy-start | bytes 11010052
  9.9 9.8 %copy-start.2 = (bf16[7168,256]{1,0:T(8,128)(2,1)S(1)}, bf16[7168,256]{1,0:T(8,128)(2,1)}, u32[]{:S(2)}) copy-start(bf16[7168,256]{1,0:T(8,128)(2,1)} %refs_11_.1) | copy-start | bytes 11010052
  9.9 6.0 %collective-permute-start.6 = (bf16[40,896]{1,0:T(8,128)(2,1)S(1)}, bf16[40,896]{1,0:T(8,128)(2,1)S(1)}, u32[]{:S(2)}, u32[]{:S(2)}) collective-permute-start(bf16[40,896]{1,0:T(8,128)(2,1)S(1)} %collective-permute-done.3.refs_0_.refs_4_), channel_id=1, source_target_pairs={{0,6},{1,7},{2,4},{3,5},{4,2},{5,3},{6,0},{7,1},{8,14},{9,15},{10,... | collective-permute-start | bytes 215048 | tf_op jit(solution)/shard_map/ppermute | solution.py:386
  12.6 4.3 %collective-permute-start.5 = (bf16[40,896]{1,0:T(8,128)(2,1)S(1)}, bf16[40,896]{1,0:T(8,128)(2,1)S(1)}, u32[]{:S(2)}, u32[]{:S(2)}) collective-permute-start(bf16[40,896]{1,0:T(8,128)(2,1)S(1)} %collective-permute-done.3.refs_0_.refs_4_), channel_id=1, source_target_pairs={{0,4},{1,5},{2,6},{3,7},{4,0},{5,1},{6,2},{7,3},{8,12},{9,13},{10,... | collective-permute-start | bytes 215048 | tf_op jit(solution)/shard_map/ppermute | solution.py:386
  13.3 4.3 %collective-permute-start.4 = (bf16[40,896]{1,0:T(8,128)(2,1)S(1)}, bf16[40,896]{1,0:T(8,128)(2,1)S(1)}, u32[]{:S(2)}, u32[]{:S(2)}) collective-permute-start(bf16[40,896]{1,0:T(8,128)(2,1)S(1)} %collective-permute-done.3.refs_0_.refs_4_), channel_id=1, source_target_pairs={{0,2},{1,3},{2,0},{3,1},{4,6},{5,7},{6,4},{7,5},{8,10},{9,11},{10,... | collective-permute-start | bytes 215048 | tf_op jit(solution)/shard_map/ppermute | solution.py:386
  14.2 0.7 %copy-start.4 = (f32[16,64]{1,0:T(8,128)S(1)}, f32[16,64]{1,0:T(8,128)}, u32[]{:S(2)}) copy-start(f32[16,64]{1,0:T(8,128)} %get-tuple-element.33.table_ref) | copy-start | bytes 12292
  17.7 1.6 %collective-permute-start.8 = (bf16[160,896]{1,0:T(8,128)(2,1)S(1)}, bf16[160,896]{1,0:T(8,128)(2,1)S(1)}, u32[]{:S(2)}, u32[]{:S(2)}) collective-permute-start(bf16[160,896]{1,0:T(8,128)(2,1)S(1)} %join.3), channel_id=1, source_target_pairs={{0,1},{1,0},{2,3},{3,2},{4,5},{5,4},{6,7},{7,6},{8,9},{9,8},{10,11... | collective-permute-start | bytes 860168 | tf_op jit(solution)/shard_map/ppermute | solution.py:395
  17.8 2.0 %collective-permute-start.7 = (bf16[160,896]{1,0:T(8,128)(2,1)S(1)}, bf16[160,896]{1,0:T(8,128)(2,1)S(1)}, u32[]{:S(2)}, u32[]{:S(2)}) collective-permute-start(bf16[160,896]{1,0:T(8,128)(2,1)S(1)} %join.2), channel_id=1, source_target_pairs={{0,1},{1,0},{2,3},{3,2},{4,5},{5,4},{6,7},{7,6},{8,9},{9,8},{10,11... | collective-permute-start | bytes 860168 | tf_op jit(solution)/shard_map/ppermute | solution.py:395
  22.2 2.0 %collective-permute-start.9 = (bf16[320,896]{1,0:T(8,128)(2,1)S(1)}, bf16[320,896]{1,0:T(8,128)(2,1)S(1)}, u32[]{:S(2)}, u32[]{:S(2)}) collective-permute-start(bf16[320,896]{1,0:T(8,128)(2,1)S(1)} %get-tuple-element.46), channel_id=1, source_target_pairs={{0,1},{1,0},{2,3},{3,2},{4,5},{5,4},{6,7},{7,6},{8,9},{9,8},{10,11... | collective-permute-start | bytes 1720328 | tf_op jit(solution)/shard_map/ppermute | solution.py:397
  24.4 5.4 %collective-permute-start.13 = (bf16[40,896]{1,0:T(8,128)(2,1)S(1)}, bf16[40,896]{1,0:T(8,128)(2,1)S(1)}, u32[]{:S(2)}, u32[]{:S(2)}) collective-permute-start(bf16[40,896]{1,0:T(8,128)(2,1)S(1)} %get-tuple-element.52), channel_id=1, source_target_pairs={{0,2},{1,3},{2,0},{3,1},{4,6},{5,7},{6,4},{7,5},{8,10},{9,11},{10,... | collective-permute-start | bytes 215048 | tf_op jit(solution)/shard_map/ppermute | solution.py:404
  25.4 6.1 %collective-permute-start.14 = (bf16[40,896]{1,0:T(8,128)(2,1)S(1)}, bf16[40,896]{1,0:T(8,128)(2,1)S(1)}, u32[]{:S(2)}, u32[]{:S(2)}) collective-permute-start(bf16[40,896]{1,0:T(8,128)(2,1)S(1)} %get-tuple-element.53), channel_id=1, source_target_pairs={{0,4},{1,5},{2,6},{3,7},{4,0},{5,1},{6,2},{7,3},{8,12},{9,13},{10,... | collective-permute-start | bytes 215048 | tf_op jit(solution)/shard_map/ppermute | solution.py:404
  26.3 5.9 %collective-permute-start.15 = (bf16[40,896]{1,0:T(8,128)(2,1)S(1)}, bf16[40,896]{1,0:T(8,128)(2,1)S(1)}, u32[]{:S(2)}, u32[]{:S(2)}) collective-permute-start(bf16[40,896]{1,0:T(8,128)(2,1)S(1)} %get-tuple-element.54), channel_id=1, source_target_pairs={{0,6},{1,7},{2,4},{3,5},{4,2},{5,3},{6,0},{7,1},{8,14},{9,15},{10,... | collective-permute-start | bytes 215048 | tf_op jit(solution)/shard_map/ppermute | solution.py:404
  28.0 7.3 %collective-permute-start.10 = (bf16[40,896]{1,0:T(8,128)(2,1)S(1)}, bf16[40,896]{1,0:T(8,128)(2,1)S(1)}, u32[]{:S(2)}, u32[]{:S(2)}) collective-permute-start(bf16[40,896]{1,0:T(8,128)(2,1)S(1)} %get-tuple-element.48), channel_id=1, source_target_pairs={{0,2},{1,3},{2,0},{3,1},{4,6},{5,7},{6,4},{7,5},{8,10},{9,11},{10,... | collective-permute-start | bytes 215048 | tf_op jit(solution)/shard_map/ppermute | solution.py:409
  28.9 6.4 %collective-permute-start.11 = (bf16[40,896]{1,0:T(8,128)(2,1)S(1)}, bf16[40,896]{1,0:T(8,128)(2,1)S(1)}, u32[]{:S(2)}, u32[]{:S(2)}) collective-permute-start(bf16[40,896]{1,0:T(8,128)(2,1)S(1)} %get-tuple-element.49), channel_id=1, source_target_pairs={{0,4},{1,5},{2,6},{3,7},{4,0},{5,1},{6,2},{7,3},{8,12},{9,13},{10,... | collective-permute-start | bytes 215048 | tf_op jit(solution)/shard_map/ppermute | solution.py:409
  29.8 6.0 %collective-permute-start.12 = (bf16[40,896]{1,0:T(8,128)(2,1)S(1)}, bf16[40,896]{1,0:T(8,128)(2,1)S(1)}, u32[]{:S(2)}, u32[]{:S(2)}) collective-permute-start(bf16[40,896]{1,0:T(8,128)(2,1)S(1)} %get-tuple-element.50), channel_id=1, source_target_pairs={{0,6},{1,7},{2,4},{3,5},{4,2},{5,3},{6,0},{7,1},{8,14},{9,15},{10,... | collective-permute-start | bytes 215048 | tf_op jit(solution)/shard_map/ppermute | solution.py:409
  32.3 6.1 %collective-permute-start.16 = (bf16[40,896]{1,0:T(8,128)(2,1)S(1)}, bf16[40,896]{1,0:T(8,128)(2,1)S(1)}, u32[]{:S(2)}, u32[]{:S(2)}) collective-permute-start(bf16[40,896]{1,0:T(8,128)(2,1)S(1)} %sum_blocks.1), channel_id=1, source_target_pairs={{0,8},{1,9},{2,10},{3,11},{4,12},{5,13},{6,14},{7,15},{8,0},{9,1},... | collective-permute-start | bytes 215048 | tf_op jit(solution)/shard_map/ppermute | solution.py:406

commit v9 on v8

--- a/solution.py
+++ b/solution.py
@@ -166,6 +166,24 @@
     )(table)
 
 
+def spread_kernel(block_ref, out_ref):
+    tall = block_ref.shape[0]
+    for q in range(out_ref.shape[0] // tall):
+        out_ref[q * tall : (q + 1) * tall, :] = block_ref[...]
+
+
+def spread(block, copies):
+    tall, wide = block.shape
+    return pl.pallas_call(
+        spread_kernel,
+        out_shape=jax.ShapeDtypeStruct((tall * copies, wide), block.dtype),
+        in_specs=[VMEM],
+        out_specs=VMEM,
+        compiler_params=params(4),
+        name="spread",
+    )(block)
+
+
 def join_kernel(*refs):
     tall = refs[0].shape[0]
     for i, ref in enumerate(refs[:-1]):
@@ -198,15 +216,13 @@
 
 
 def expert_kernel(own, *refs):
-    blocks, joined = refs[:own], refs[own : own + own // (SPLIT // CORES)]
+    pieces = refs[:-8]
     gate_ref, up_ref, down_ref, given_ref, hidden_ref, packed, flat, out = refs[-8:]
     tall = CAP * SEGMENTS
     wide = packed.shape[1]
     units = gate_ref.shape[1]
-    for b, ref in enumerate(blocks):
-        packed[b * tall : (b + 1) * tall, :] = ref[...].astype(jnp.float32)
-    start = own * tall
-    for ref in joined:
+    start = 0
+    for ref in pieces:
         packed[start : start + ref.shape[0], :] = ref[...].astype(jnp.float32)
         start += ref.shape[0]
     count = 2 * own * CAP
@@ -228,9 +244,8 @@
     given_ref[...] = out[...].astype(jnp.bfloat16)
 
 
-def expert_half(blocks, joined, w_gate, w_up, w_down):
-    own = len(blocks)
-    tall, wide = blocks[0].shape
+def expert_half(pieces, own, w_gate, w_up, w_down):
+    tall, wide = CAP * SEGMENTS, pieces[0].shape[1]
     features, units = w_gate.shape
     rows = 2 * own * CAP
     return pl.pallas_call(
@@ -239,7 +254,7 @@
             jax.ShapeDtypeStruct((own * tall, wide), jnp.bfloat16),
             jax.ShapeDtypeStruct((own * CAP, units), jnp.bfloat16),
         ],
-        in_specs=[VMEM] * (own + len(joined) + 3),
+        in_specs=[VMEM] * (len(pieces) + 3),
         out_specs=[VMEM] * 2,
         scratch_shapes=[
             pltpu.VMEM((2 * own * tall, wide), jnp.float32),
@@ -253,7 +268,7 @@
             transcendentals=rows * units,
         ),
         name="expert_half",
-    )(*blocks, *joined, w_gate, w_up, w_down)
+    )(*pieces, w_gate, w_up, w_down)
 
 
 def kept_kernel(hidden_ref, down_ref, kept_ref, flat):
@@ -281,20 +296,19 @@
 
 
 def add_kernel(kept_ref, taken_ref, *out_refs):
-    tall = out_refs[0].shape[0]
-    for b, out_ref in enumerate(out_refs):
-        rows = slice(b * tall, (b + 1) * tall)
+    start = 0
+    for out_ref in out_refs:
+        rows = slice(start, start + out_ref.shape[0])
         total = kept_ref[rows, :] + taken_ref[rows, :].astype(jnp.float32)
         out_ref[...] = total.astype(out_ref.dtype)
+        start += out_ref.shape[0]
 
 
 def add_cores(kept, taken, teams, chips):
-    shape = (CAP * SEGMENTS, kept.shape[1])
-    outs = [
-        jax.ShapeDtypeStruct(shape, jnp.bfloat16 if m else jnp.float32)
-        for k in range(teams)
-        for m in range(chips)
-    ]
+    tall, wide = CAP * SEGMENTS, kept.shape[1]
+    outs = [jax.ShapeDtypeStruct((tall, wide), jnp.float32)]
+    outs += [jax.ShapeDtypeStruct((tall, wide), jnp.bfloat16)] * (chips - 1)
+    outs += [jax.ShapeDtypeStruct((chips * tall, wide), jnp.bfloat16)] * (teams - 1)
     return pl.pallas_call(
         add_kernel,
         out_shape=outs,
@@ -305,22 +319,23 @@
     )(kept, taken)
 
 
-def sum_kernel(*refs):
-    total = refs[0][...]
-    for ref in refs[1:-1]:
-        total = total + ref[...].astype(jnp.float32)
-    refs[-1][...] = total.astype(refs[-1].dtype)
-
-
-def sum_blocks(blocks):
+def sum_kernel(terms_ref, out_ref):
+    tall = out_ref.shape[0]
+    total = terms_ref[:tall, :].astype(jnp.float32)
+    for q in range(1, terms_ref.shape[0] // tall):
+        total = total + terms_ref[q * tall : (q + 1) * tall, :].astype(jnp.float32)
+    out_ref[...] = total.astype(out_ref.dtype)
+
+
+def sum_blocks(terms, chips):
     return pl.pallas_call(
         sum_kernel,
-        out_shape=jax.ShapeDtypeStruct(blocks[0].shape, jnp.bfloat16),
-        in_specs=[VMEM] * len(blocks),
+        out_shape=jax.ShapeDtypeStruct((terms.shape[0] // chips, terms.shape[1]), jnp.bfloat16),
+        in_specs=[VMEM],
         out_specs=VMEM,
         compiler_params=params(4),
         name="sum_blocks",
-    )(*blocks)
+    )(terms)
 
 
 def blend_kernel(chips, weight_ref, *refs):
@@ -370,40 +385,52 @@
     teams = devices // SPLIT
     chips = SPLIT // CORES
     other_core = [(i, i ^ 1) for i in range(devices)]
+    same_core = [
+        [t * SPLIT + q * CORES + c for q in range(chips)] for t in range(teams) for c in range(CORES)
+    ]
     other_chip = [[(i, i ^ (m * CORES)) for i in range(devices)] for m in range(chips)]
     packed, table = pack_rows(expert_ids.T, route_logits.T, tokens, teams)
+    own = [packed[0]]
+    for m in range(1, chips):
+        own.append(lax.ppermute(packed[0], "expert", other_chip[m]))
     crowds = []
-    for k in range(teams):
-        block = packed[k]
-        if k > 0:
-            pairs = [(i, (i + k * SPLIT) % devices) for i in range(devices)]
-            block = lax.ppermute(block, "expert", pairs)
+    for k in range(1, teams):
+        pairs = [(i, (i + k * SPLIT) % devices) for i in range(devices)]
+        block = lax.ppermute(packed[k], "expert", pairs)
         if k == teams - 1:
             block, table = lax.optimization_barrier((block, table))
             weights = blend_weights(table, teams)
-        team = [block]
-        for m in range(1, chips):
-            team.append(lax.ppermute(block, "expert", other_chip[m]))
-        crowds.append(team)
-    crowds[0], weights = lax.optimization_barrier((crowds[0], weights))
-    blocks, joined = [], []
-    for team in crowds:
-        if joined:
-            team, joined = lax.optimization_barrier((team, joined))
-        blocks += team
-        joined.append(join(team))
-    swapped = [lax.ppermute(j, "expert", other_core) for j in joined]
-    given, hidden = expert_half(blocks, swapped, w_gate, w_up, w_down)
+        crowds.append(
+            lax.all_to_all(
+                spread(block, chips),
+                "expert",
+                split_axis=0,
+                concat_axis=0,
+                axis_index_groups=same_core,
+                tiled=True,
+            )
+        )
+    own, weights = lax.optimization_barrier((own, weights))
+    crowds, joined = lax.optimization_barrier((crowds, join(own)))
+    swapped = [lax.ppermute(piece, "expert", other_core) for piece in (joined, *crowds)]
+    given, hidden = expert_half(
+        [*own, *crowds, *swapped], teams * chips, w_gate, w_up, w_down
+    )
     taken = lax.ppermute(given, "expert", other_core)
     kept = kept_half(hidden, w_down)
     parts = add_cores(kept, taken, teams, chips)
     others = []
     for k in range(1, teams):
-        team = [parts[k * chips]]
-        for m in range(1, chips):
-            team.append(lax.ppermute(parts[k * chips + m], "expert", other_chip[m]))
+        terms = lax.all_to_all(
+            parts[chips + k - 1],
+            "expert",
+            split_axis=0,
+            concat_axis=0,
+            axis_index_groups=same_core,
+            tiled=True,
+        )
         pairs = [(i, (i - k * SPLIT) % devices) for i in range(devices)]
-        others.append(lax.ppermute(sum_blocks(team), "expert", pairs))
+        others.append(lax.ppermute(sum_blocks(terms, chips), "expert", pairs))
     own = [parts[0]]
     for m in range(1, chips):
         own.append(lax.ppermute(parts[m], "expert", other_chip[m]))

time: 40 us -> 52.5 us (1.31)
  local copies, waits for them, and re-layouts: 0.71 us -> 7.35 us
  waiting for transfers between devices: 8.84 us -> 13.2 us
  Pallas kernels: 7.49 us -> 9.09 us
    ppermute x13 -> x7, starting transfers between devices: 19 us -> 11.1 us  [the longest x1 4.1 us: body(): block = lax.ppermute(packed[k], 'expert', pairs)]
    all_to_all x0 -> x2, starting transfers between devices: none -> 7.4 us  [the longest x1 3.94 us: body(): lax.all_to_all(spread(block, chips), 'expert', split_axis=0, concat_axis=...]
    all_to_all x0 -> x2, waiting for transfers between devices: none -> 7.05 us  [the longest x1 3.83 us: body(): lax.all_to_all(spread(block, chips), 'expert', split_axis=0, concat_axis=...]
    unnamed x10, local copies, waits for them, and re-layouts: 0.71 us -> 7.35 us
    ppermute x13 -> x7, waiting for transfers between devices: 7.2 us -> 4.94 us  [the longest x1 3.46 us: body(): others.append(lax.ppermute(sum_blocks(terms, chips), 'expert', pairs))]
    pallas_call x1 -> x2, Pallas kernels: 0.04 us -> 0.77 us  [the longest x1 0.73 us: spread(): pl.pallas_call(spread_kernel, out_shape=jax.ShapeDtypeStruct((tall * copi...]
    pallas_call x1, Pallas kernels: 0.13 us -> 0.81 us  [add_cores(): pl.pallas_call(add_kernel, out_shape=outs, in_specs=[VMEM] * 2, out_specs...]
  transfers between devices with their start and end apart: 17 -> 13, of which waited for: 9 -> 7; matrix products, arithmetic and copies ran while one was open for 0% -> 0% of each run, Pallas kernels for 3% -> 4%
where the time goes in v9:
time: 52.5 us; the launch traced here: 52 us
  starting transfers between devices  22.2 us (42%)
  waiting for transfers between devices  13.2 us (25%)
  Pallas kernels  9.09 us (17%)
  local copies, waits for them, and re-layouts  7.35 us (14%)
    unnamed x10, local copies, waits for them, and re-layouts  7.35 us
    ppermute x1, starting transfers between devices, body(): block = lax.ppermute(packed[k], 'expert', pairs)  4.1 us
    all_to_all x1, starting transfers between devices, body(): lax.all_to_all(spread(block, chips), 'expert', split_axis=0, concat_axis=...  3.94 us
    all_to_all x1, waiting for transfers between devices, body(): lax.all_to_all(spread(block, chips), 'expert', split_axis=0, concat_axis=...  3.83 us
    ppermute x3, starting transfers between devices, body(): own.append(lax.ppermute(parts[m], 'expert', other_chip[m]))  3.55 us
    ppermute x3, starting transfers between devices, body(): own.append(lax.ppermute(packed[0], 'expert', other_chip[m]))  3.49 us
    ppermute x1, waiting for transfers between devices, body(): others.append(lax.ppermute(sum_blocks(terms, chips), 'expert', pairs))  3.46 us
    all_to_all x1, starting transfers between devices, body(): lax.all_to_all(parts[chips + k - 1], 'expert', split_axis=0, concat_axis=...  3.45 us
  transfers between devices with their start and end apart: 13, of which 7 were waited for; matrix products, arithmetic and copies ran while one was open for 0% of the time, Pallas kernels for 4%

profile of v9, /device:TPU:0, one launch (start us, length us, event | category | flops | bytes accessed | tf_op | source)
XLA Modules:
  0.0 52.0 jit_solution(9132182471019008225)
XLA Ops:
  0.0 2.3 %pack_rows.1 = (bf16[40,896]{1,0:T(8,128)(2,1)}, bf16[40,896]{1,0:T(8,128)(2,1)}, f32[16,64]{1,0:T(8,128)}) custom-call(s32[8,64]{1,0:T(8,128)} %bitcast.9, f32[8,64]{1,0:T(8,128)} %bitcast.10, bf16[64,7168]{1,0:T(8,128)(2,1)} %tokens_hbm.1), custom_call_target="tpu_custom_call" | custom-call | tf_op jit(solution)/shard_map/pack_rows/pallas_call | solution.py:110
  2.3 4.1 %collective-permute-start.3 = (bf16[40,896]{1,0:T(8,128)(2,1)}, bf16[40,896]{1,0:T(8,128)(2,1)S(1)}, u32[]{:S(2)}, u32[]{:S(2)}) collective-permute-start(bf16[40,896]{1,0:T(8,128)(2,1)} %get-tuple-element.25), channel_id=1, source_target_pairs={{0,8},{1,9},{2,10},{3,11},{4,12},{5,13},{6,14},{7,15},{8,0},{9,1},... | collective-permute-start | bytes 215048 | tf_op jit(solution)/shard_map/ppermute | solution.py:399
  6.4 2.5 %collective-permute-start.2 = (bf16[40,896]{1,0:T(8,128)(2,1)}, bf16[40,896]{1,0:T(8,128)(2,1)S(1)}, u32[]{:S(2)}, u32[]{:S(2)}) collective-permute-start(bf16[40,896]{1,0:T(8,128)(2,1)} %get-tuple-element.29.refs_0_), channel_id=1, source_target_pairs={{0,6},{1,7},{2,4},{3,5},{4,2},{5,3},{6,0},{7,1},{8,14},{9,15},{10,... | collective-permute-start | bytes 215048 | tf_op jit(solution)/shard_map/ppermute | solution.py:395
  8.9 0.4 collective-permute-start.1
  9.4 0.5 collective-permute-start
  9.9 0.0 collective-permute-done.3.block_ref
  9.9 0.7 %spread.1 = bf16[160,896]{1,0:T(8,128)(2,1)} custom-call(bf16[40,896]{1,0:T(8,128)(2,1)S(1)} %collective-permute-done.3.block_ref), custom_call_target="tpu_custom_call" | custom-call | tf_op jit(solution)/shard_map/spread/pallas_call | solution.py:177
  10.6 3.9 %all-to-all-start = ((bf16[4,40,896]{2,1,0:T(8,128)(2,1)}), bf16[4,40,896]{2,1,0:T(8,128)(2,1)S(1)}, u32[]{:S(2)}, u32[]{:S(2)}) async-start(bf16[4,40,896]{2,1,0:T(8,128)(2,1)} %bitcast.2), calls=%async_computation | async-start | bytes 573440 | tf_op jit(solution)/shard_map/all_to_all | solution.py:404
  14.6 0.0 copy-start.4
  14.6 0.7 %copy-done.4 = f32[16,64]{1,0:T(8,128)S(1)} copy-done((f32[16,64]{1,0:T(8,128)S(1)}, f32[16,64]{1,0:T(8,128)}, u32[]{:S(2)}) %copy-start.4) | copy-done | bytes 4120
  15.3 0.0 copy-start.3
  15.3 0.3 blend_weights.1.weight_ref
  15.6 0.0 collective-permute-done.2.refs_3_
  15.6 0.0 collective-permute-done.1.refs_2_
  15.6 0.0 collective-permute-done.refs_1_
  15.6 0.5 %copy-done.3 = bf16[40,896]{1,0:T(8,128)(2,1)S(1)} copy-done((bf16[40,896]{1,0:T(8,128)(2,1)S(1)}, bf16[40,896]{1,0:T(8,128)(2,1)}, u32[]{:S(2)}) %copy-start.3) | copy-done | bytes 71704
  16.2 3.8 %all-to-all-done = bf16[4,40,896]{2,1,0:T(8,128)(2,1)S(1)} async-done(((bf16[4,40,896]{2,1,0:T(8,128)(2,1)}), bf16[4,40,896]{2,1,0:T(8,128)(2,1)S(1)}, u32[]{:S(2)}, u32[]{:S(2)}) %all-to-all-start) | async-done | bytes 286752 | tf_op jit(solution)/shard_map/all_to_all | solution.py:404
  20.0 0.0 collective-permute-start.4
  20.0 0.5 collective-permute-start.5
  20.5 1.1 %collective-permute-done.4.refs_5_ = bf16[160,896]{1,0:T(8,128)(2,1)S(1)} collective-permute-done((bf16[160,896]{1,0:T(8,128)(2,1)S(1)}, bf16[160,896]{1,0:T(8,128)(2,1)S(1)}, u32[]{:S(2)}, u32[]{:S(2)}) %collective-permute-start.4) | collective-permute-done | bytes 286752 | tf_op jit(solution)/shard_map/ppermute | solution.py:415
  21.6 0.4 collective-permute-done.5.refs_6_
  22.0 0.0 copy-start
  22.0 2.0 %copy-done = bf16[256,7168]{1,0:T(8,128)(2,1)S(1)} copy-done((bf16[256,7168]{1,0:T(8,128)(2,1)S(1)}, bf16[256,7168]{1,0:T(8,128)(2,1)}, u32[]{:S(2)}) %copy-start) | copy-done | bytes 3670040
  24.0 0.0 copy-start.1
  24.0 2.0 %copy-done.1 = bf16[7168,256]{1,0:T(8,128)(2,1)S(1)} copy-done((bf16[7168,256]{1,0:T(8,128)(2,1)S(1)}, bf16[7168,256]{1,0:T(8,128)(2,1)}, u32[]{:S(2)}) %copy-start.1) | copy-done | bytes 3670040
  26.1 0.0 copy-start.2
  26.1 2.0 %copy-done.2 = bf16[7168,256]{1,0:T(8,128)(2,1)S(1)} copy-done((bf16[7168,256]{1,0:T(8,128)(2,1)S(1)}, bf16[7168,256]{1,0:T(8,128)(2,1)}, u32[]{:S(2)}) %copy-start.2) | copy-done | bytes 3670040
  28.1 2.6 %expert_half.1 = (bf16[320,896]{1,0:T(8,128)(2,1)S(1)}, bf16[40,256]{1,0:T(8,128)(2,1)S(1)}) custom-call(bf16[40,896]{1,0:T(8,128)(2,1)S(1)} %copy-done.3, bf16[40,896]{1,0:T(8,128)(2,1)S(1)} %collective-permute-done.refs_1_, bf16[40,896]{1,0:T(8,128)(2,1)S(1)} %collective-permute-done.1.refs_2_, bf16[40,896]{1,0:T(8,128)(2,1)S(1)} %collective-permute-done.2.refs_3_, ...), custom_call_target="tpu_custom_call" | custom-call | flops 734003200 | bytes 11010048 | tf_op jit(solution)/shard_map/expert_half/pallas_call | solution.py:251
  30.7 0.2 collective-permute-start.6
  31.0 0.8 %kept_half.1.kept_ref = f32[320,896]{1,0:T(8,128)S(1)} custom-call(bf16[40,256]{1,0:T(8,128)(2,1)S(1)} %get-tuple-element.36.hidden_ref, bf16[256,7168]{1,0:T(8,128)(2,1)S(1)} %copy-done), custom_call_target="tpu_custom_call" | custom-call | flops 146800640 | bytes 3670016 | tf_op jit(solution)/shard_map/kept_half/pallas_call | solution.py:282
  31.7 1.1 %collective-permute-done.6.taken_ref = bf16[320,896]{1,0:T(8,128)(2,1)S(1)} collective-permute-done((bf16[320,896]{1,0:T(8,128)(2,1)S(1)}, bf16[320,896]{1,0:T(8,128)(2,1)S(1)}, u32[]{:S(2)}, u32[]{:S(2)}) %collective-permute-start.6) | collective-permute-done | bytes 573472 | tf_op jit(solution)/shard_map/ppermute | solution.py:419
  32.8 0.8 %add_cores.1 = (f32[40,896]{1,0:T(8,128)S(1)}, bf16[40,896]{1,0:T(8,128)(2,1)S(1)}, bf16[40,896]{1,0:T(8,128)(2,1)S(1)}, bf16[40,896]{1,0:T(8,128)(2,1)S(1)}, bf16[160,896]{1,0:T(8,128)(2,1)}) custom-call(f32[320,896]{1,0:T(8,128)S(1)} %kept_half.1.kept_ref, bf16[320,896]{1,0:T(8,128)(2,1)S(1)} %collective-permute-done.6.taken_ref), custom_call_target="tpu_custom_call" | custom-call | tf_op jit(solution)/shard_map/add_cores/pallas_call | solution.py:312
  33.6 3.5 %all-to-all-start.1 = ((bf16[4,40,896]{2,1,0:T(8,128)(2,1)}), bf16[4,40,896]{2,1,0:T(8,128)(2,1)S(1)}, u32[]{:S(2)}, u32[]{:S(2)}) async-start(bf16[4,40,896]{2,1,0:T(8,128)(2,1)} %bitcast.4), calls=%async_computation.1 | async-start | bytes 573440 | tf_op jit(solution)/shard_map/all_to_all | solution.py:424
  37.1 2.0 %collective-permute-start.7 = (bf16[40,896]{1,0:T(8,128)(2,1)S(1)}, bf16[40,896]{1,0:T(8,128)(2,1)S(1)}, u32[]{:S(2)}, u32[]{:S(2)}) collective-permute-start(bf16[40,896]{1,0:T(8,128)(2,1)S(1)} %get-tuple-element.39), channel_id=1, source_target_pairs={{0,2},{1,3},{2,0},{3,1},{4,6},{5,7},{6,4},{7,5},{8,10},{9,11},{10,... | collective-permute-start | bytes 215048 | tf_op jit(solution)/shard_map/ppermute | solution.py:436
  39.1 1.5 %collective-permute-start.8 = (bf16[40,896]{1,0:T(8,128)(2,1)S(1)}, bf16[40,896]{1,0:T(8,128)(2,1)S(1)}, u32[]{:S(2)}, u32[]{:S(2)}) collective-permute-start(bf16[40,896]{1,0:T(8,128)(2,1)S(1)} %get-tuple-element.40), channel_id=1, source_target_pairs={{0,4},{1,5},{2,6},{3,7},{4,0},{5,1},{6,2},{7,3},{8,12},{9,13},{10,... | collective-permute-start | bytes 215048 | tf_op jit(solution)/shard_map/ppermute | solution.py:436
  40.5 0.1 collective-permute-start.9
  40.6 3.2 %all-to-all-done.1 = bf16[4,40,896]{2,1,0:T(8,128)(2,1)S(1)} async-done(((bf16[4,40,896]{2,1,0:T(8,128)(2,1)}), bf16[4,40,896]{2,1,0:T(8,128)(2,1)S(1)}, u32[]{:S(2)}, u32[]{:S(2)}) %all-to-all-start.1) | async-done | bytes 286752 | tf_op jit(solution)/shard_map/all_to_all | solution.py:424
  43.9 3.0 %collective-permute-start.10 = (bf16[40,896]{1,0:T(8,128)(2,1)S(1)}, bf16[40,896]{1,0:T(8,128)(2,1)S(1)}, u32[]{:S(2)}, u32[]{:S(2)}) collective-permute-start(bf16[40,896]{1,0:T(8,128)(2,1)S(1)} %sum_blocks.1), channel_id=1, source_target_pairs={{0,8},{1,9},{2,10},{3,11},{4,12},{5,13},{6,14},{7,15},{8,0},{9,1},... | collective-permute-start | bytes 215048 | tf_op jit(solution)/shard_map/ppermute | solution.py:433
  46.9 0.0 collective-permute-done.7.refs_1_
  46.9 0.0 collective-permute-done.8.refs_2_
  46.9 0.1 collective-permute-done.9.refs_3_
  47.0 3.5 %collective-permute-done.10.refs_4_ = bf16[40,896]{1,0:T(8,128)(2,1)S(1)} collective-permute-done((bf16[40,896]{1,0:T(8,128)(2,1)S(1)}, bf16[40,896]{1,0:T(8,128)(2,1)S(1)}, u32[]{:S(2)}, u32[]{:S(2)}) %collective-permute-start.10) | collective-permute-done | bytes 71712 | tf_op jit(solution)/shard_map/ppermute | solution.py:433
  50.5 1.5 %blend.1 = bf16[64,7168]{1,0:T(8,128)(2,1)} custom-call(bf16[512,200]{1,0:T(8,128)(2,1)S(1)} %blend_weights.1.weight_ref, f32[40,896]{1,0:T(8,128)S(1)} %get-tuple-element.38.refs_0_, bf16[40,896]{1,0:T(8,128)(2,1)S(1)} %collective-permute-done.7.refs_1_, bf16[40,896]{1,0:T(8,128)(2,1)S(1)} %collective-permute-done.8.refs_2_, ...), custom_call_target="tpu_custom_call" | custom-call | tf_op jit(solution)/shard_map/blend/pallas_call | solution.py:369
  (2 shorter events, 0.1 us)
Async XLA Ops:
  2.3 7.6 %collective-permute-start.3 = (bf16[40,896]{1,0:T(8,128)(2,1)}, bf16[40,896]{1,0:T(8,128)(2,1)S(1)}, u32[]{:S(2)}, u32[]{:S(2)}) collective-permute-start(bf16[40,896]{1,0:T(8,128)(2,1)} %get-tuple-element.25), channel_id=1, source_target_pairs={{0,8},{1,9},{2,10},{3,11},{4,12},{5,13},{6,14},{7,15},{8,0},{9,1},... | collective-permute-start | bytes 215048 | tf_op jit(solution)/shard_map/ppermute | solution.py:399
  6.4 9.2 %collective-permute-start.2 = (bf16[40,896]{1,0:T(8,128)(2,1)}, bf16[40,896]{1,0:T(8,128)(2,1)S(1)}, u32[]{:S(2)}, u32[]{:S(2)}) collective-permute-start(bf16[40,896]{1,0:T(8,128)(2,1)} %get-tuple-element.29.refs_0_), channel_id=1, source_target_pairs={{0,6},{1,7},{2,4},{3,5},{4,2},{5,3},{6,0},{7,1},{8,14},{9,15},{10,... | collective-permute-start | bytes 215048 | tf_op jit(solution)/shard_map/ppermute | solution.py:395
  8.9 6.7 %collective-permute-start.1 = (bf16[40,896]{1,0:T(8,128)(2,1)}, bf16[40,896]{1,0:T(8,128)(2,1)S(1)}, u32[]{:S(2)}, u32[]{:S(2)}) collective-permute-start(bf16[40,896]{1,0:T(8,128)(2,1)} %get-tuple-element.29.refs_0_), channel_id=1, source_target_pairs={{0,4},{1,5},{2,6},{3,7},{4,0},{5,1},{6,2},{7,3},{8,12},{9,13},{10,... | collective-permute-start | bytes 215048 | tf_op jit(solution)/shard_map/ppermute | solution.py:395
  9.4 6.2 %collective-permute-start = (bf16[40,896]{1,0:T(8,128)(2,1)}, bf16[40,896]{1,0:T(8,128)(2,1)S(1)}, u32[]{:S(2)}, u32[]{:S(2)}) collective-permute-start(bf16[40,896]{1,0:T(8,128)(2,1)} %get-tuple-element.29.refs_0_), channel_id=1, source_target_pairs={{0,2},{1,3},{2,0},{3,1},{4,6},{5,7},{6,4},{7,5},{8,10},{9,11},{10,... | collective-permute-start | bytes 215048 | tf_op jit(solution)/shard_map/ppermute | solution.py:395
  10.6 9.4 %all-to-all-start = ((bf16[4,40,896]{2,1,0:T(8,128)(2,1)}), bf16[4,40,896]{2,1,0:T(8,128)(2,1)S(1)}, u32[]{:S(2)}, u32[]{:S(2)}) async-start(bf16[4,40,896]{2,1,0:T(8,128)(2,1)} %bitcast.2), calls=%async_computation | async-start | bytes 573440 | tf_op jit(solution)/shard_map/all_to_all | solution.py:404
  14.6 0.7 %copy-start.4 = (f32[16,64]{1,0:T(8,128)S(1)}, f32[16,64]{1,0:T(8,128)}, u32[]{:S(2)}) copy-start(f32[16,64]{1,0:T(8,128)} %get-tuple-element.27.table_ref) | copy-start | bytes 12292
  15.3 0.9 %copy-start.3 = (bf16[40,896]{1,0:T(8,128)(2,1)S(1)}, bf16[40,896]{1,0:T(8,128)(2,1)}, u32[]{:S(2)}) copy-start(bf16[40,896]{1,0:T(8,128)(2,1)} %get-tuple-element.29.refs_0_) | copy-start | bytes 215044
  20.0 1.6 %collective-permute-start.4 = (bf16[160,896]{1,0:T(8,128)(2,1)S(1)}, bf16[160,896]{1,0:T(8,128)(2,1)S(1)}, u32[]{:S(2)}, u32[]{:S(2)}) collective-permute-start(bf16[160,896]{1,0:T(8,128)(2,1)S(1)} %join.1), channel_id=1, source_target_pairs={{0,1},{1,0},{2,3},{3,2},{4,5},{5,4},{6,7},{7,6},{8,9},{9,8},{10,11... | collective-permute-start | bytes 860168 | tf_op jit(solution)/shard_map/ppermute | solution.py:415
  20.0 2.0 %collective-permute-start.5 = (bf16[160,896]{1,0:T(8,128)(2,1)S(1)}, bf16[160,896]{1,0:T(8,128)(2,1)S(1)}, u32[]{:S(2)}, u32[]{:S(2)}) collective-permute-start(bf16[160,896]{1,0:T(8,128)(2,1)S(1)} %bitcast.7), channel_id=1, source_target_pairs={{0,1},{1,0},{2,3},{3,2},{4,5},{5,4},{6,7},{7,6},{8,9},{9,8},{10,11... | collective-permute-start | bytes 860168 | tf_op jit(solution)/shard_map/ppermute | solution.py:415
  22.0 2.0 %copy-start = (bf16[256,7168]{1,0:T(8,128)(2,1)S(1)}, bf16[256,7168]{1,0:T(8,128)(2,1)}, u32[]{:S(2)}) copy-start(bf16[256,7168]{1,0:T(8,128)(2,1)} %down_ref.1) | copy-start | bytes 11010052
  24.0 2.0 %copy-start.1 = (bf16[7168,256]{1,0:T(8,128)(2,1)S(1)}, bf16[7168,256]{1,0:T(8,128)(2,1)}, u32[]{:S(2)}) copy-start(bf16[7168,256]{1,0:T(8,128)(2,1)} %refs_7_.1) | copy-start | bytes 11010052
  26.1 2.0 %copy-start.2 = (bf16[7168,256]{1,0:T(8,128)(2,1)S(1)}, bf16[7168,256]{1,0:T(8,128)(2,1)}, u32[]{:S(2)}) copy-start(bf16[7168,256]{1,0:T(8,128)(2,1)} %refs_8_.1) | copy-start | bytes 11010052
  30.7 2.0 %collective-permute-start.6 = (bf16[320,896]{1,0:T(8,128)(2,1)S(1)}, bf16[320,896]{1,0:T(8,128)(2,1)S(1)}, u32[]{:S(2)}, u32[]{:S(2)}) collective-permute-start(bf16[320,896]{1,0:T(8,128)(2,1)S(1)} %get-tuple-element.37), channel_id=1, source_target_pairs={{0,1},{1,0},{2,3},{3,2},{4,5},{5,4},{6,7},{7,6},{8,9},{9,8},{10,11... | collective-permute-start | bytes 1720328 | tf_op jit(solution)/shard_map/ppermute | solution.py:419
  33.6 10.2 %all-to-all-start.1 = ((bf16[4,40,896]{2,1,0:T(8,128)(2,1)}), bf16[4,40,896]{2,1,0:T(8,128)(2,1)S(1)}, u32[]{:S(2)}, u32[]{:S(2)}) async-start(bf16[4,40,896]{2,1,0:T(8,128)(2,1)} %bitcast.4), calls=%async_computation.1 | async-start | bytes 573440 | tf_op jit(solution)/shard_map/all_to_all | solution.py:424
  37.1 9.8 %collective-permute-start.7 = (bf16[40,896]{1,0:T(8,128)(2,1)S(1)}, bf16[40,896]{1,0:T(8,128)(2,1)S(1)}, u32[]{:S(2)}, u32[]{:S(2)}) collective-permute-start(bf16[40,896]{1,0:T(8,128)(2,1)S(1)} %get-tuple-element.39), channel_id=1, source_target_pairs={{0,2},{1,3},{2,0},{3,1},{4,6},{5,7},{6,4},{7,5},{8,10},{9,11},{10,... | collective-permute-start | bytes 215048 | tf_op jit(solution)/shard_map/ppermute | solution.py:436
  39.1 7.8 %collective-permute-start.8 = (bf16[40,896]{1,0:T(8,128)(2,1)S(1)}, bf16[40,896]{1,0:T(8,128)(2,1)S(1)}, u32[]{:S(2)}, u32[]{:S(2)}) collective-permute-start(bf16[40,896]{1,0:T(8,128)(2,1)S(1)} %get-tuple-element.40), channel_id=1, source_target_pairs={{0,4},{1,5},{2,6},{3,7},{4,0},{5,1},{6,2},{7,3},{8,12},{9,13},{10,... | collective-permute-start | bytes 215048 | tf_op jit(solution)/shard_map/ppermute | solution.py:436
  40.5 6.5 %collective-permute-start.9 = (bf16[40,896]{1,0:T(8,128)(2,1)S(1)}, bf16[40,896]{1,0:T(8,128)(2,1)S(1)}, u32[]{:S(2)}, u32[]{:S(2)}) collective-permute-start(bf16[40,896]{1,0:T(8,128)(2,1)S(1)} %get-tuple-element.41), channel_id=1, source_target_pairs={{0,6},{1,7},{2,4},{3,5},{4,2},{5,3},{6,0},{7,1},{8,14},{9,15},{10,... | collective-permute-start | bytes 215048 | tf_op jit(solution)/shard_map/ppermute | solution.py:436
  43.9 6.6 %collective-permute-start.10 = (bf16[40,896]{1,0:T(8,128)(2,1)S(1)}, bf16[40,896]{1,0:T(8,128)(2,1)S(1)}, u32[]{:S(2)}, u32[]{:S(2)}) collective-permute-start(bf16[40,896]{1,0:T(8,128)(2,1)S(1)} %sum_blocks.1), channel_id=1, source_target_pairs={{0,8},{1,9},{2,10},{3,11},{4,12},{5,13},{6,14},{7,15},{8,0},{9,1},... | collective-permute-start | bytes 215048 | tf_op jit(solution)/shard_map/ppermute | solution.py:433

commit v10 on v8

--- a/solution.py
+++ b/solution.py
@@ -197,16 +197,15 @@
             out_ref[start : start + CAP, :] = slot[b * CAP : (b + 1) * CAP, :]
 
 
-def expert_kernel(own, *refs):
-    blocks, joined = refs[:own], refs[own : own + own // (SPLIT // CORES)]
-    gate_ref, up_ref, down_ref, given_ref, hidden_ref, packed, flat, out = refs[-8:]
+def expert_kernel(own, count_in, *refs):
+    pieces = refs[:count_in]
+    gate_ref, up_ref, down_ref = refs[count_in : count_in + 3]
+    *given_refs, hidden_ref, packed, flat, out = refs[count_in + 3 :]
     tall = CAP * SEGMENTS
     wide = packed.shape[1]
     units = gate_ref.shape[1]
-    for b, ref in enumerate(blocks):
-        packed[b * tall : (b + 1) * tall, :] = ref[...].astype(jnp.float32)
-    start = own * tall
-    for ref in joined:
+    start = 0
+    for ref in pieces:
         packed[start : start + ref.shape[0], :] = ref[...].astype(jnp.float32)
         start += ref.shape[0]
     count = 2 * own * CAP
@@ -225,22 +224,21 @@
     half = count // 2
     hidden_ref[...] = hidden[:half]
     packed_down(hidden[half:], down_ref, out, flat.at[:, :half, :])
-    given_ref[...] = out[...].astype(jnp.bfloat16)
-
-
-def expert_half(blocks, joined, w_gate, w_up, w_down):
-    own = len(blocks)
-    tall, wide = blocks[0].shape
+    for k, given_ref in enumerate(given_refs):
+        rows = given_ref.shape[0]
+        given_ref[...] = out[k * rows : (k + 1) * rows, :].astype(jnp.bfloat16)
+
+
+def expert_half(pieces, own, teams, w_gate, w_up, w_down):
+    tall, wide = CAP * SEGMENTS, pieces[0].shape[1]
     features, units = w_gate.shape
     rows = 2 * own * CAP
     return pl.pallas_call(
-        functools.partial(expert_kernel, own),
-        out_shape=[
-            jax.ShapeDtypeStruct((own * tall, wide), jnp.bfloat16),
-            jax.ShapeDtypeStruct((own * CAP, units), jnp.bfloat16),
-        ],
-        in_specs=[VMEM] * (own + len(joined) + 3),
-        out_specs=[VMEM] * 2,
+        functools.partial(expert_kernel, own, len(pieces)),
+        out_shape=[jax.ShapeDtypeStruct((own // teams * tall, wide), jnp.bfloat16)] * teams
+        + [jax.ShapeDtypeStruct((own * CAP, units), jnp.bfloat16)],
+        in_specs=[VMEM] * (len(pieces) + 3),
+        out_specs=[VMEM] * (teams + 1),
         scratch_shapes=[
             pltpu.VMEM((2 * own * tall, wide), jnp.float32),
             pltpu.VMEM((2, rows, wide), jnp.float32),
@@ -253,7 +251,7 @@
             transcendentals=rows * units,
         ),
         name="expert_half",
-    )(*blocks, *joined, w_gate, w_up, w_down)
+    )(*pieces, w_gate, w_up, w_down)
 
 
 def kept_kernel(hidden_ref, down_ref, kept_ref, flat):
@@ -280,89 +278,168 @@
     )(hidden, w_down)
 
 
-def add_kernel(kept_ref, taken_ref, *out_refs):
-    tall = out_refs[0].shape[0]
-    for b, out_ref in enumerate(out_refs):
-        rows = slice(b * tall, (b + 1) * tall)
-        total = kept_ref[rows, :] + taken_ref[rows, :].astype(jnp.float32)
-        out_ref[...] = total.astype(out_ref.dtype)
-
-
-def add_cores(kept, taken, teams, chips):
-    shape = (CAP * SEGMENTS, kept.shape[1])
-    outs = [
-        jax.ShapeDtypeStruct(shape, jnp.bfloat16 if m else jnp.float32)
-        for k in range(teams)
-        for m in range(chips)
-    ]
-    return pl.pallas_call(
-        add_kernel,
-        out_shape=outs,
-        in_specs=[VMEM] * 2,
+def call(kernel, outs, name, args, mib=4):
+    return pl.pallas_call(
+        kernel,
+        out_shape=[jax.ShapeDtypeStruct(shape, kind) for shape, kind in outs],
+        in_specs=[VMEM] * len(args),
         out_specs=[VMEM] * len(outs),
-        compiler_params=params(4 + 4 * teams),
-        name="add_cores",
-    )(kept, taken)
-
-
-def sum_kernel(*refs):
-    total = refs[0][...]
-    for ref in refs[1:-1]:
-        total = total + ref[...].astype(jnp.float32)
-    refs[-1][...] = total.astype(refs[-1].dtype)
-
-
-def sum_blocks(blocks):
-    return pl.pallas_call(
-        sum_kernel,
-        out_shape=jax.ShapeDtypeStruct(blocks[0].shape, jnp.bfloat16),
-        in_specs=[VMEM] * len(blocks),
-        out_specs=VMEM,
-        compiler_params=params(4),
-        name="sum_blocks",
-    )(*blocks)
-
-
-def blend_kernel(chips, weight_ref, *refs):
+        compiler_params=params(mib),
+        name=name,
+    )(*args)
+
+
+def halves(wide):
+    cut = 128 * pl.cdiv(wide // 128, 2)
+    return slice(0, cut), slice(cut, wide)
+
+
+def halve_kernel(block_ref, *out_refs):
+    for columns, ref in zip(halves(block_ref.shape[1]), out_refs):
+        ref[...] = block_ref[:, columns]
+
+
+def halve(block):
+    outs = []
+    for columns in halves(block.shape[1]):
+        outs.append(((block.shape[0], columns.stop - columns.start), block.dtype))
+    return call(halve_kernel, outs, "halve", [block])
+
+
+def crowd_kernel(left_ref, far_left_ref, right_ref, far_right_ref, out_ref):
+    tall = left_ref.shape[0] // 2
+    left, right = halves(out_ref.shape[1])
+    out_ref[: 2 * tall, left] = left_ref[...]
+    out_ref[2 * tall :, left] = far_left_ref[...]
+    for m, (ref, at) in enumerate(
+        ((right_ref, 0), (far_right_ref, 0), (right_ref, 1), (far_right_ref, 1))
+    ):
+        out_ref[m * tall : (m + 1) * tall, right] = ref[at * tall : (at + 1) * tall, :]
+
+
+def gather_team(block, along):
+    left, right = halve(block)
+    left = join([left, along[1](left)])
+    right = join([right, along[2](right)])
+    far_left, far_right = along[2](left), along[1](right)
+    tall, wide = block.shape
+    return call(
+        crowd_kernel,
+        [((4 * tall, wide), block.dtype)],
+        "crowd",
+        [left, far_left, right, far_right],
+    )[0]
+
+
+def add_own_kernel(kept_ref, taken_ref, near_ref, away_ref):
+    rows = near_ref.shape[0]
+    near_ref[...] = kept_ref[:rows, :] + taken_ref[:rows, :].astype(jnp.float32)
+    total = kept_ref[rows : 2 * rows, :] + taken_ref[rows:, :].astype(jnp.float32)
+    away_ref[...] = total.astype(jnp.bfloat16)
+
+
+def add_own(kept, taken):
+    shape = (taken.shape[0] // 2, taken.shape[1])
+    outs = [(shape, jnp.float32), (shape, jnp.bfloat16)]
+    return call(add_own_kernel, outs, "add_own", [kept, taken], 8)
+
+
+def add_other_kernel(first, kept_ref, taken_ref, *out_refs):
+    tall = taken_ref.shape[0] // 4
+    left, right = halves(taken_ref.shape[1])
+    for columns, near, away, near_ref, away_ref in (
+        (left, (0, 2), (1, 3), out_refs[0], out_refs[1]),
+        (right, (0, 1), (2, 3), out_refs[2], out_refs[3]),
+    ):
+        for blocks, ref in ((near, near_ref), (away, away_ref)):
+            for at, m in enumerate(blocks):
+                total = kept_ref[
+                    first + m * tall : first + (m + 1) * tall, columns
+                ] + taken_ref[m * tall : (m + 1) * tall, columns].astype(jnp.float32)
+                ref[at * tall : (at + 1) * tall, :] = total.astype(ref.dtype)
+
+
+def step_kernel(near_ref, got_ref, here_ref, away_ref):
+    tall = here_ref.shape[0]
+    total = near_ref[...] + got_ref[...].astype(jnp.float32)
+    here_ref[...] = total[:tall]
+    away_ref[...] = total[tall:].astype(jnp.bfloat16)
+
+
+def step(near, got):
+    shape = (near.shape[0] // 2, near.shape[1])
+    return call(step_kernel, [(shape, jnp.float32), (shape, jnp.bfloat16)], "step", [near, got])
+
+
+def last_kernel(left_ref, got_left_ref, right_ref, got_right_ref, out_ref):
+    left, right = halves(out_ref.shape[1])
+    out_ref[:, left] = (left_ref[...] + got_left_ref[...].astype(jnp.float32)).astype(jnp.bfloat16)
+    out_ref[:, right] = (right_ref[...] + got_right_ref[...].astype(jnp.float32)).astype(
+        jnp.bfloat16
+    )
+
+
+def sum_team(kept, taken, k, along, later):
+    rows, wide = taken.shape
+    tall = rows // 4
+    left, right = (columns.stop - columns.start for columns in halves(wide))
+    outs = []
+    for size in (left, right):
+        outs += [((2 * tall, size), jnp.float32), ((2 * tall, size), jnp.bfloat16)]
+    near_left, away_left, near_right, away_right = call(
+        functools.partial(add_other_kernel, k * rows), outs, "add_other", [kept, taken], 8
+    )
+    left, next_left = step(near_left, along[1](away_left))
+    next_left, later = lax.optimization_barrier((next_left, later))
+    right, next_right = step(near_right, along[2](away_right))
+    return call(
+        last_kernel,
+        [((tall, wide), jnp.bfloat16)],
+        "last",
+        [left, along[2](next_left), right, along[1](next_right)],
+    )[0], later
+
+
+def blend_kernel(weight_ref, here_ref, got_ref, *refs):
     *refs, out_hbm, out_ref, sem = refs
     count, features = out_ref.shape
     wide = features // SEGMENTS
-    own = refs[0][...]
-    for ref in refs[1:chips]:
-        own = own + ref[...].astype(jnp.float32)
+    own = here_ref[...] + got_ref[...].astype(jnp.float32)
     high = own.astype(jnp.bfloat16).astype(jnp.float32)
     terms = [high, own - high, high]
-    for ref in refs[chips:]:
+    for ref in refs:
         terms += [ref[...].astype(jnp.float32)] * 2
     rows = jnp.concatenate(terms, axis=0).astype(jnp.bfloat16)
     copies = []
-    for s in range(SEGMENTS):
-        columns = pl.ds(s * wide, wide)
-        out_ref[:, columns] = jnp.dot(
-            weight_ref[s * count : (s + 1) * count, :], rows, preferred_element_type=jnp.float32
-        ).astype(jnp.bfloat16)
-        copies.append(
-            pltpu.make_async_copy(out_ref.at[:, columns], out_hbm.at[:, columns], sem.at[s])
-        )
-        copies[-1].start()
+    for columns in halves(wide):
+        size = columns.stop - columns.start
+        total = jnp.dot(weight_ref[...], rows[:, columns], preferred_element_type=jnp.float32)
+        for s in range(SEGMENTS):
+            part = pl.ds(s * wide + columns.start, size)
+            out_ref[:, part] = total[s * count : (s + 1) * count].astype(jnp.bfloat16)
+            copies.append(
+                pltpu.make_async_copy(
+                    out_ref.at[:, part], out_hbm.at[:, part], sem.at[len(copies)]
+                )
+            )
+            copies[-1].start()
     wait_all(copies)
 
 
-def blend(weights, own_blocks, other_blocks, count):
-    chips = len(own_blocks)
-    features = own_blocks[0].shape[1] * SEGMENTS
-    return pl.pallas_call(
-        functools.partial(blend_kernel, chips),
+def blend(weights, here, got, other_blocks, count):
+    features = here.shape[1] * SEGMENTS
+    return pl.pallas_call(
+        blend_kernel,
         out_shape=jax.ShapeDtypeStruct((count, features), jnp.bfloat16),
-        in_specs=[VMEM] * (1 + chips + len(other_blocks)),
+        in_specs=[VMEM] * (3 + len(other_blocks)),
         out_specs=HBM,
         scratch_shapes=[
             pltpu.VMEM((count, features), jnp.bfloat16),
-            pltpu.SemaphoreType.DMA((SEGMENTS,)),
+            pltpu.SemaphoreType.DMA((2 * SEGMENTS,)),
         ],
         compiler_params=params(16),
         name="blend",
-    )(weights, *own_blocks, *other_blocks)
+    )(weights, here, got, *other_blocks)
 
 
 def body(tokens, expert_ids, route_logits, w_gate, w_up, w_down):
@@ -372,42 +449,32 @@
     other_core = [(i, i ^ 1) for i in range(devices)]
     other_chip = [[(i, i ^ (m * CORES)) for i in range(devices)] for m in range(chips)]
     packed, table = pack_rows(expert_ids.T, route_logits.T, tokens, teams)
+    along = [functools.partial(lax.ppermute, axis_name="expert", perm=p) for p in other_chip]
+    pair = join([packed[0], along[1](packed[0])])
     crowds = []
-    for k in range(teams):
-        block = packed[k]
-        if k > 0:
-            pairs = [(i, (i + k * SPLIT) % devices) for i in range(devices)]
-            block = lax.ppermute(block, "expert", pairs)
+    for k in range(1, teams):
+        pairs = [(i, (i + k * SPLIT) % devices) for i in range(devices)]
+        block = lax.ppermute(packed[k], "expert", pairs)
         if k == teams - 1:
-            block, table = lax.optimization_barrier((block, table))
+            block, table, pair = lax.optimization_barrier((block, table, pair))
             weights = blend_weights(table, teams)
-        team = [block]
-        for m in range(1, chips):
-            team.append(lax.ppermute(block, "expert", other_chip[m]))
-        crowds.append(team)
-    crowds[0], weights = lax.optimization_barrier((crowds[0], weights))
-    blocks, joined = [], []
-    for team in crowds:
-        if joined:
-            team, joined = lax.optimization_barrier((team, joined))
-        blocks += team
-        joined.append(join(team))
-    swapped = [lax.ppermute(j, "expert", other_core) for j in joined]
-    given, hidden = expert_half(blocks, swapped, w_gate, w_up, w_down)
-    taken = lax.ppermute(given, "expert", other_core)
+        crowds.append(gather_team(block, along))
+    own, weights = lax.optimization_barrier((join([pair, along[2](pair)]), weights))
+    own, crowds = lax.optimization_barrier((own, crowds))
+    swapped = [lax.ppermute(piece, "expert", other_core) for piece in (own, *crowds)]
+    *given, hidden = expert_half(
+        [own, *crowds, *swapped], teams * chips, teams, w_gate, w_up, w_down
+    )
+    taken = [lax.ppermute(piece, "expert", other_core) for piece in given]
     kept = kept_half(hidden, w_down)
-    parts = add_cores(kept, taken, teams, chips)
     others = []
     for k in range(1, teams):
-        team = [parts[k * chips]]
-        for m in range(1, chips):
-            team.append(lax.ppermute(parts[k * chips + m], "expert", other_chip[m]))
         pairs = [(i, (i - k * SPLIT) % devices) for i in range(devices)]
-        others.append(lax.ppermute(sum_blocks(team), "expert", pairs))
-    own = [parts[0]]
-    for m in range(1, chips):
-        own.append(lax.ppermute(parts[m], "expert", other_chip[m]))
-    return blend(weights, own, others, tokens.shape[0])
+        total, taken[0] = sum_team(kept, taken[k], k, along, taken[0])
+        others.append(lax.ppermute(total, "expert", pairs))
+    near, away = add_own(kept, taken[0])
+    here, away = step(near, along[2](away))
+    return blend(weights, here, along[1](away), others, tokens.shape[0])
 
 
 def solution(mesh):

time: 40 us -> 52.1 us (1.30)
  waiting for transfers between devices: 8.84 us -> 25.5 us
  starting transfers between devices: 22.7 us -> 17.2 us
  local copies, waits for them, and re-layouts: 0.71 us -> 1.83 us
    ppermute x17 -> x18, waiting for transfers between devices: 8.84 us -> 25.5 us  [the longest x1 4.33 us: sum_team(): right, next_right = step(near_right, along[2](away_right))]
    ppermute x17 -> x18, starting transfers between devices: 22.7 us -> 17.2 us  [the longest x1 3.03 us: body(): pair = join([packed[0], along[1](packed[0])])]
    unnamed x10, local copies, waits for them, and re-layouts: 0.71 us -> 1.83 us
    pallas_call x4 -> x10, Pallas kernels: 4.16 us -> 3.93 us  [the longest x1 2.48 us: expert_half(): pl.pallas_call(functools.partial(expert_kernel, own, len(pieces)), out_sh...]
  transfers between devices with their start and end apart: 17 -> 18, of which waited for: 9 -> 12; matrix products, arithmetic and copies ran while one was open for 0% -> 0% of each run, Pallas kernels for 3% -> 2%
where the time goes in v10:
time: 52.1 us; the launch traced here: 51.9 us
  waiting for transfers between devices  25.5 us (49%)
  starting transfers between devices  17.2 us (33%)
  Pallas kernels  7.28 us (14%)
  local copies, waits for them, and re-layouts  1.83 us (4%)
    ppermute x1, waiting for transfers between devices, sum_team(): right, next_right = step(near_right, along[2](away_right))  4.33 us
    ppermute x1, waiting for transfers between devices, sum_team(): left, next_left = step(near_left, along[1](away_left))  4.15 us
    ppermute x1, waiting for transfers between devices, sum_team(): along[1](next_right)  3.55 us
    ppermute x1, waiting for transfers between devices, body(): others.append(lax.ppermute(total, 'expert', pairs))  3.5 us
    ppermute x1, waiting for transfers between devices, body(): block = lax.ppermute(packed[k], 'expert', pairs)  3.08 us
    ppermute x1, starting transfers between devices, body(): pair = join([packed[0], along[1](packed[0])])  3.03 us
    ppermute x2, waiting for transfers between devices, gather_team(): far_left, far_right = (along[2](left), along[1](right))  2.84 us
    ppermute x1, starting transfers between devices, body(): block = lax.ppermute(packed[k], 'expert', pairs)  2.59 us
  transfers between devices with their start and end apart: 18, of which 12 were waited for; matrix products, arithmetic and copies ran while one was open for 0% of the time, Pallas kernels for 2%

profile of v10, /device:TPU:0, one launch (start us, length us, event | category | flops | bytes accessed | tf_op | source)
XLA Modules:
  0.0 51.9 jit_solution(18402856217218321092)
XLA Ops:
  0.0 2.3 %pack_rows.1 = (bf16[40,896]{1,0:T(8,128)(2,1)}, bf16[40,896]{1,0:T(8,128)(2,1)}, f32[16,64]{1,0:T(8,128)}) custom-call(s32[8,64]{1,0:T(8,128)} %bitcast.2, f32[8,64]{1,0:T(8,128)} %bitcast.3, bf16[64,7168]{1,0:T(8,128)(2,1)} %tokens_hbm.1), custom_call_target="tpu_custom_call" | custom-call | tf_op jit(solution)/shard_map/pack_rows/pallas_call | solution.py:110
  2.3 3.0 %collective-permute-start.1 = (bf16[40,896]{1,0:T(8,128)(2,1)}, bf16[40,896]{1,0:T(8,128)(2,1)S(1)}, u32[]{:S(2)}, u32[]{:S(2)}) collective-permute-start(bf16[40,896]{1,0:T(8,128)(2,1)} %get-tuple-element.36.refs_0_), channel_id=1, source_target_pairs={{0,2},{1,3},{2,0},{3,1},{4,6},{5,7},{6,4},{7,5},{8,10},{9,11},{10,... | collective-permute-start | bytes 215048 | tf_op jit(solution)/shard_map/ppermute | solution.py:453
  5.3 2.6 %collective-permute-start = (bf16[40,896]{1,0:T(8,128)(2,1)}, bf16[40,896]{1,0:T(8,128)(2,1)S(1)}, u32[]{:S(2)}, u32[]{:S(2)}) collective-permute-start(bf16[40,896]{1,0:T(8,128)(2,1)} %get-tuple-element.34), channel_id=1, source_target_pairs={{0,8},{1,9},{2,10},{3,11},{4,12},{5,13},{6,14},{7,15},{8,0},{9,1},... | collective-permute-start | bytes 215048 | tf_op jit(solution)/shard_map/ppermute | solution.py:457
  7.9 0.0 collective-permute-done.1.refs_1_
  7.9 0.9 %copy-done.3 = bf16[40,896]{1,0:T(8,128)(2,1)S(1)} copy-done((bf16[40,896]{1,0:T(8,128)(2,1)S(1)}, bf16[40,896]{1,0:T(8,128)(2,1)}, u32[]{:S(2)}) %copy-start.3) | copy-done | bytes 71704
  8.8 3.1 %collective-permute-done.block_ref = bf16[40,896]{1,0:T(8,128)(2,1)S(1)} collective-permute-done((bf16[40,896]{1,0:T(8,128)(2,1)}, bf16[40,896]{1,0:T(8,128)(2,1)S(1)}, u32[]{:S(2)}, u32[]{:S(2)}) %collective-permute-start) | collective-permute-done | bytes 71712 | tf_op jit(solution)/shard_map/ppermute | solution.py:457
  11.9 0.5 collective-permute-start.3
  12.4 0.5 %collective-permute-start.5 = (bf16[40,384]{1,0:T(8,128)(2,1)S(1)}, bf16[40,384]{1,0:T(8,128)(2,1)S(1)}, u32[]{:S(2)}, u32[]{:S(2)}) collective-permute-start(bf16[40,384]{1,0:T(8,128)(2,1)S(1)} %get-tuple-element.43.refs_0_), channel_id=1, source_target_pairs={{0,4},{1,5},{2,6},{3,7},{4,0},{5,1},{6,2},{7,3},{8,12},{9,13},{10,... | collective-permute-start | bytes 92168 | tf_op jit(solution)/shard_map/ppermute | solution.py:323
  13.0 1.5 %collective-permute-start.2 = (bf16[80,896]{1,0:T(8,128)(2,1)S(1)}, bf16[80,896]{1,0:T(8,128)(2,1)S(1)}, u32[]{:S(2)}, u32[]{:S(2)}) collective-permute-start(bf16[80,896]{1,0:T(8,128)(2,1)S(1)} %join.4.refs_0_), channel_id=1, source_target_pairs={{0,4},{1,5},{2,6},{3,7},{4,0},{5,1},{6,2},{7,3},{8,12},{9,13},{10,... | collective-permute-start | bytes 430088 | tf_op jit(solution)/shard_map/ppermute | solution.py:462
  14.4 1.9 %collective-permute-done.5.refs_1_ = bf16[40,384]{1,0:T(8,128)(2,1)S(1)} collective-permute-done((bf16[40,384]{1,0:T(8,128)(2,1)S(1)}, bf16[40,384]{1,0:T(8,128)(2,1)S(1)}, u32[]{:S(2)}, u32[]{:S(2)}) %collective-permute-start.5) | collective-permute-done | bytes 30752 | tf_op jit(solution)/shard_map/ppermute | solution.py:323
  16.3 1.7 %collective-permute-start.6 = (bf16[80,384]{1,0:T(8,128)(2,1)S(1)}, bf16[80,384]{1,0:T(8,128)(2,1)S(1)}, u32[]{:S(2)}, u32[]{:S(2)}) collective-permute-start(bf16[80,384]{1,0:T(8,128)(2,1)S(1)} %join.7.right_ref), channel_id=1, source_target_pairs={{0,2},{1,3},{2,0},{3,1},{4,6},{5,7},{6,4},{7,5},{8,10},{9,11},{10,... | collective-permute-start | bytes 184328 | tf_op jit(solution)/shard_map/ppermute | solution.py:324
  18.0 0.0 collective-permute-done.3.refs_1_
  18.0 0.0 copy-start
  18.0 0.0 copy-start.1
  18.0 0.0 copy-start.2
  18.1 0.4 collective-permute-start.4
  18.5 0.9 %copy-done.4 = f32[16,64]{1,0:T(8,128)S(1)} copy-done((f32[16,64]{1,0:T(8,128)S(1)}, f32[16,64]{1,0:T(8,128)}, u32[]{:S(2)}) %copy-start.4) | copy-done | bytes 4120
  19.4 0.3 blend_weights.1.weight_ref
  19.7 0.8 %collective-permute-done.6.far_right_ref = bf16[80,384]{1,0:T(8,128)(2,1)S(1)} collective-permute-done((bf16[80,384]{1,0:T(8,128)(2,1)S(1)}, bf16[80,384]{1,0:T(8,128)(2,1)S(1)}, u32[]{:S(2)}, u32[]{:S(2)}) %collective-permute-start.6) | collective-permute-done | bytes 61472 | tf_op jit(solution)/shard_map/ppermute | solution.py:324
  20.5 2.0 %collective-permute-done.4.far_left_ref = bf16[80,512]{1,0:T(8,128)(2,1)S(1)} collective-permute-done((bf16[80,512]{1,0:T(8,128)(2,1)S(1)}, bf16[80,512]{1,0:T(8,128)(2,1)S(1)}, u32[]{:S(2)}, u32[]{:S(2)}) %collective-permute-start.4) | collective-permute-done | bytes 81952 | tf_op jit(solution)/shard_map/ppermute | solution.py:324
  22.6 0.0 collective-permute-done.2.refs_1_
  22.6 0.1 collective-permute-start.7
  22.7 0.5 collective-permute-start.8
  23.2 1.1 %collective-permute-done.7.refs_2_ = bf16[160,896]{1,0:T(8,128)(2,1)S(1)} collective-permute-done((bf16[160,896]{1,0:T(8,128)(2,1)S(1)}, bf16[160,896]{1,0:T(8,128)(2,1)S(1)}, u32[]{:S(2)}, u32[]{:S(2)}) %collective-permute-start.7) | collective-permute-done | bytes 286752 | tf_op jit(solution)/shard_map/ppermute | solution.py:464
  24.3 0.4 collective-permute-done.8.refs_3_
  24.7 2.5 %expert_half.1 = (bf16[160,896]{1,0:T(8,128)(2,1)S(1)}, bf16[160,896]{1,0:T(8,128)(2,1)S(1)}, bf16[40,256]{1,0:T(8,128)(2,1)S(1)}) custom-call(bf16[160,896]{1,0:T(8,128)(2,1)S(1)} %join.5.refs_0_, bf16[160,896]{1,0:T(8,128)(2,1)S(1)} %crowd.1.refs_1_, bf16[160,896]{1,0:T(8,128)(2,1)S(1)} %collective-permute-done.7.refs_2_, ...), custom_call_target="tpu_custom_call" | custom-call | flops 734003200 | bytes 11010048 | tf_op jit(solution)/shard_map/expert_half/pallas_call | solution.py:236
  27.2 0.2 collective-permute-start.9
  27.4 0.4 collective-permute-start.11
  27.7 0.7 %kept_half.1.kept_ref = f32[320,896]{1,0:T(8,128)S(1)} custom-call(bf16[40,256]{1,0:T(8,128)(2,1)S(1)} %get-tuple-element.46.hidden_ref, bf16[256,7168]{1,0:T(8,128)(2,1)S(1)} %copy-done), custom_call_target="tpu_custom_call" | custom-call | flops 146800640 | bytes 3670016 | tf_op jit(solution)/shard_map/kept_half/pallas_call | solution.py:265
  28.5 0.3 collective-permute-done.9.taken_ref
  28.8 0.1 add_other.1
  28.9 0.4 collective-permute-start.10
  29.3 4.1 %collective-permute-done.10.got_ref = bf16[80,512]{1,0:T(8,128)(2,1)S(1)} collective-permute-done((bf16[80,512]{1,0:T(8,128)(2,1)S(1)}, bf16[80,512]{1,0:T(8,128)(2,1)S(1)}, u32[]{:S(2)}, u32[]{:S(2)}) %collective-permute-start.10) | collective-permute-done | bytes 81952 | tf_op jit(solution)/shard_map/ppermute | solution.py:392
  33.4 0.0 collective-permute-done.11.taken_ref
  33.5 0.1 add_own.1
  33.5 0.4 collective-permute-start.12
  34.0 1.7 %collective-permute-start.15 = (bf16[80,384]{1,0:T(8,128)(2,1)S(1)}, bf16[80,384]{1,0:T(8,128)(2,1)S(1)}, u32[]{:S(2)}, u32[]{:S(2)}) collective-permute-start(bf16[80,384]{1,0:T(8,128)(2,1)S(1)} %get-tuple-element.60), channel_id=1, source_target_pairs={{0,4},{1,5},{2,6},{3,7},{4,0},{5,1},{6,2},{7,3},{8,12},{9,13},{10,... | collective-permute-start | bytes 184328 | tf_op jit(solution)/shard_map/ppermute | solution.py:394
  35.6 0.4 collective-permute-start.14
  36.0 4.3 %collective-permute-done.15.got_ref = bf16[80,384]{1,0:T(8,128)(2,1)S(1)} collective-permute-done((bf16[80,384]{1,0:T(8,128)(2,1)S(1)}, bf16[80,384]{1,0:T(8,128)(2,1)S(1)}, u32[]{:S(2)}, u32[]{:S(2)}) %collective-permute-start.15) | collective-permute-done | bytes 61472 | tf_op jit(solution)/shard_map/ppermute | solution.py:394
  40.3 0.4 collective-permute-start.16
  40.7 3.6 %collective-permute-done.16.got_right_ref = bf16[40,384]{1,0:T(8,128)(2,1)S(1)} collective-permute-done((bf16[40,384]{1,0:T(8,128)(2,1)S(1)}, bf16[40,384]{1,0:T(8,128)(2,1)S(1)}, u32[]{:S(2)}, u32[]{:S(2)}) %collective-permute-start.16) | collective-permute-done | bytes 30752 | tf_op jit(solution)/shard_map/ppermute | solution.py:399
  44.3 0.0 collective-permute-done.14.got_left_ref
  44.3 2.0 %collective-permute-start.17 = (bf16[40,896]{1,0:T(8,128)(2,1)S(1)}, bf16[40,896]{1,0:T(8,128)(2,1)S(1)}, u32[]{:S(2)}, u32[]{:S(2)}) collective-permute-start(bf16[40,896]{1,0:T(8,128)(2,1)S(1)} %last.1), channel_id=1, source_target_pairs={{0,8},{1,9},{2,10},{3,11},{4,12},{5,13},{6,14},{7,15},{8,0},{9,1},... | collective-permute-start | bytes 215048 | tf_op jit(solution)/shard_map/ppermute | solution.py:474
  46.3 0.0 collective-permute-done.12.got_ref
  46.3 0.6 %collective-permute-start.13 = (bf16[40,896]{1,0:T(8,128)(2,1)S(1)}, bf16[40,896]{1,0:T(8,128)(2,1)S(1)}, u32[]{:S(2)}, u32[]{:S(2)}) collective-permute-start(bf16[40,896]{1,0:T(8,128)(2,1)S(1)} %get-tuple-element.56), channel_id=1, source_target_pairs={{0,2},{1,3},{2,0},{3,1},{4,6},{5,7},{6,4},{7,5},{8,10},{9,11},{10,... | collective-permute-start | bytes 215048 | tf_op jit(solution)/shard_map/ppermute | solution.py:477
  46.9 3.5 %collective-permute-done.17.refs_0_ = bf16[40,896]{1,0:T(8,128)(2,1)S(1)} collective-permute-done((bf16[40,896]{1,0:T(8,128)(2,1)S(1)}, bf16[40,896]{1,0:T(8,128)(2,1)S(1)}, u32[]{:S(2)}, u32[]{:S(2)}) %collective-permute-start.17) | collective-permute-done | bytes 71712 | tf_op jit(solution)/shard_map/ppermute | solution.py:474
  50.4 0.3 collective-permute-done.13.got_ref
  50.7 1.2 %blend.1 = bf16[64,7168]{1,0:T(8,128)(2,1)} custom-call(bf16[512,200]{1,0:T(8,128)(2,1)S(1)} %blend_weights.1.weight_ref, f32[40,896]{1,0:T(8,128)S(1)} %get-tuple-element.55.here_ref, bf16[40,896]{1,0:T(8,128)(2,1)S(1)} %collective-permute-done.13.got_ref, bf16[40,896]{1,0:T(8,128)(2,1)S(1)} %collective-permute-done.17.refs_0_), custom_call_target="tpu_custom_call" | custom-call | tf_op jit(solution)/shard_map/blend/pallas_call | solution.py:431
  (15 shorter events, 0.2 us)
Async XLA Ops:
  2.3 5.6 %collective-permute-start.1 = (bf16[40,896]{1,0:T(8,128)(2,1)}, bf16[40,896]{1,0:T(8,128)(2,1)S(1)}, u32[]{:S(2)}, u32[]{:S(2)}) collective-permute-start(bf16[40,896]{1,0:T(8,128)(2,1)} %get-tuple-element.36.refs_0_), channel_id=1, source_target_pairs={{0,2},{1,3},{2,0},{3,1},{4,6},{5,7},{6,4},{7,5},{8,10},{9,11},{10,... | collective-permute-start | bytes 215048 | tf_op jit(solution)/shard_map/ppermute | solution.py:453
  5.3 6.6 %collective-permute-start = (bf16[40,896]{1,0:T(8,128)(2,1)}, bf16[40,896]{1,0:T(8,128)(2,1)S(1)}, u32[]{:S(2)}, u32[]{:S(2)}) collective-permute-start(bf16[40,896]{1,0:T(8,128)(2,1)} %get-tuple-element.34), channel_id=1, source_target_pairs={{0,8},{1,9},{2,10},{3,11},{4,12},{5,13},{6,14},{7,15},{8,0},{9,1},... | collective-permute-start | bytes 215048 | tf_op jit(solution)/shard_map/ppermute | solution.py:457
  7.9 0.9 %copy-start.3 = (bf16[40,896]{1,0:T(8,128)(2,1)S(1)}, bf16[40,896]{1,0:T(8,128)(2,1)}, u32[]{:S(2)}) copy-start(bf16[40,896]{1,0:T(8,128)(2,1)} %get-tuple-element.36.refs_0_) | copy-start | bytes 215044
  11.9 6.1 %collective-permute-start.3 = (bf16[40,512]{1,0:T(8,128)(2,1)S(1)}, bf16[40,512]{1,0:T(8,128)(2,1)S(1)}, u32[]{:S(2)}, u32[]{:S(2)}) collective-permute-start(bf16[40,512]{1,0:T(8,128)(2,1)S(1)} %get-tuple-element.42.refs_0_), channel_id=1, source_target_pairs={{0,2},{1,3},{2,0},{3,1},{4,6},{5,7},{6,4},{7,5},{8,10},{9,11},{10,... | collective-permute-start | bytes 122888 | tf_op jit(solution)/shard_map/ppermute | solution.py:322
  12.4 3.9 %collective-permute-start.5 = (bf16[40,384]{1,0:T(8,128)(2,1)S(1)}, bf16[40,384]{1,0:T(8,128)(2,1)S(1)}, u32[]{:S(2)}, u32[]{:S(2)}) collective-permute-start(bf16[40,384]{1,0:T(8,128)(2,1)S(1)} %get-tuple-element.43.refs_0_), channel_id=1, source_target_pairs={{0,4},{1,5},{2,6},{3,7},{4,0},{5,1},{6,2},{7,3},{8,12},{9,13},{10,... | collective-permute-start | bytes 92168 | tf_op jit(solution)/shard_map/ppermute | solution.py:323
  13.0 9.6 %collective-permute-start.2 = (bf16[80,896]{1,0:T(8,128)(2,1)S(1)}, bf16[80,896]{1,0:T(8,128)(2,1)S(1)}, u32[]{:S(2)}, u32[]{:S(2)}) collective-permute-start(bf16[80,896]{1,0:T(8,128)(2,1)S(1)} %join.4.refs_0_), channel_id=1, source_target_pairs={{0,4},{1,5},{2,6},{3,7},{4,0},{5,1},{6,2},{7,3},{8,12},{9,13},{10,... | collective-permute-start | bytes 430088 | tf_op jit(solution)/shard_map/ppermute | solution.py:462
  16.3 4.2 %collective-permute-start.6 = (bf16[80,384]{1,0:T(8,128)(2,1)S(1)}, bf16[80,384]{1,0:T(8,128)(2,1)S(1)}, u32[]{:S(2)}, u32[]{:S(2)}) collective-permute-start(bf16[80,384]{1,0:T(8,128)(2,1)S(1)} %join.7.right_ref), channel_id=1, source_target_pairs={{0,2},{1,3},{2,0},{3,1},{4,6},{5,7},{6,4},{7,5},{8,10},{9,11},{10,... | collective-permute-start | bytes 184328 | tf_op jit(solution)/shard_map/ppermute | solution.py:324
  18.0 6.7 %copy-start = (bf16[256,7168]{1,0:T(8,128)(2,1)S(1)}, bf16[256,7168]{1,0:T(8,128)(2,1)}, u32[]{:S(2)}) copy-start(bf16[256,7168]{1,0:T(8,128)(2,1)} %down_ref.1) | copy-start | bytes 11010052
  18.0 6.7 %copy-start.1 = (bf16[7168,256]{1,0:T(8,128)(2,1)S(1)}, bf16[7168,256]{1,0:T(8,128)(2,1)}, u32[]{:S(2)}) copy-start(bf16[7168,256]{1,0:T(8,128)(2,1)} %refs_4_.1) | copy-start | bytes 11010052
  18.0 6.6 %copy-start.2 = (bf16[7168,256]{1,0:T(8,128)(2,1)S(1)}, bf16[7168,256]{1,0:T(8,128)(2,1)}, u32[]{:S(2)}) copy-start(bf16[7168,256]{1,0:T(8,128)(2,1)} %refs_5_.1) | copy-start | bytes 11010052
  18.1 4.5 %collective-permute-start.4 = (bf16[80,512]{1,0:T(8,128)(2,1)S(1)}, bf16[80,512]{1,0:T(8,128)(2,1)S(1)}, u32[]{:S(2)}, u32[]{:S(2)}) collective-permute-start(bf16[80,512]{1,0:T(8,128)(2,1)S(1)} %join.6.left_ref), channel_id=1, source_target_pairs={{0,4},{1,5},{2,6},{3,7},{4,0},{5,1},{6,2},{7,3},{8,12},{9,13},{10,... | collective-permute-start | bytes 245768 | tf_op jit(solution)/shard_map/ppermute | solution.py:324
  18.5 0.9 %copy-start.4 = (f32[16,64]{1,0:T(8,128)S(1)}, f32[16,64]{1,0:T(8,128)}, u32[]{:S(2)}) copy-start(f32[16,64]{1,0:T(8,128)} %get-tuple-element.38.table_ref) | copy-start | bytes 12292
  22.6 1.6 %collective-permute-start.7 = (bf16[160,896]{1,0:T(8,128)(2,1)S(1)}, bf16[160,896]{1,0:T(8,128)(2,1)S(1)}, u32[]{:S(2)}, u32[]{:S(2)}) collective-permute-start(bf16[160,896]{1,0:T(8,128)(2,1)S(1)} %join.5.refs_0_), channel_id=1, source_target_pairs={{0,1},{1,0},{2,3},{3,2},{4,5},{5,4},{6,7},{7,6},{8,9},{9,8},{10,11... | collective-permute-start | bytes 860168 | tf_op jit(solution)/shard_map/ppermute | solution.py:464
  22.7 2.0 %collective-permute-start.8 = (bf16[160,896]{1,0:T(8,128)(2,1)S(1)}, bf16[160,896]{1,0:T(8,128)(2,1)S(1)}, u32[]{:S(2)}, u32[]{:S(2)}) collective-permute-start(bf16[160,896]{1,0:T(8,128)(2,1)S(1)} %crowd.1.refs_1_), channel_id=1, source_target_pairs={{0,1},{1,0},{2,3},{3,2},{4,5},{5,4},{6,7},{7,6},{8,9},{9,8},{10,11... | collective-permute-start | bytes 860168 | tf_op jit(solution)/shard_map/ppermute | solution.py:464
  27.2 1.6 %collective-permute-start.9 = (bf16[160,896]{1,0:T(8,128)(2,1)S(1)}, bf16[160,896]{1,0:T(8,128)(2,1)S(1)}, u32[]{:S(2)}, u32[]{:S(2)}) collective-permute-start(bf16[160,896]{1,0:T(8,128)(2,1)S(1)} %get-tuple-element.47), channel_id=1, source_target_pairs={{0,1},{1,0},{2,3},{3,2},{4,5},{5,4},{6,7},{7,6},{8,9},{9,8},{10,11... | collective-permute-start | bytes 860168 | tf_op jit(solution)/shard_map/ppermute | solution.py:468
  27.4 6.1 %collective-permute-start.11 = (bf16[160,896]{1,0:T(8,128)(2,1)S(1)}, bf16[160,896]{1,0:T(8,128)(2,1)S(1)}, u32[]{:S(2)}, u32[]{:S(2)}) collective-permute-start(bf16[160,896]{1,0:T(8,128)(2,1)S(1)} %get-tuple-element.51), channel_id=1, source_target_pairs={{0,1},{1,0},{2,3},{3,2},{4,5},{5,4},{6,7},{7,6},{8,9},{9,8},{10,11... | collective-permute-start | bytes 860168 | tf_op jit(solution)/shard_map/ppermute | solution.py:468
  28.9 4.6 %collective-permute-start.10 = (bf16[80,512]{1,0:T(8,128)(2,1)S(1)}, bf16[80,512]{1,0:T(8,128)(2,1)S(1)}, u32[]{:S(2)}, u32[]{:S(2)}) collective-permute-start(bf16[80,512]{1,0:T(8,128)(2,1)S(1)} %get-tuple-element.49), channel_id=1, source_target_pairs={{0,2},{1,3},{2,0},{3,1},{4,6},{5,7},{6,4},{7,5},{8,10},{9,11},{10,... | collective-permute-start | bytes 245768 | tf_op jit(solution)/shard_map/ppermute | solution.py:392
  33.5 12.8 %collective-permute-start.12 = (bf16[80,896]{1,0:T(8,128)(2,1)S(1)}, bf16[80,896]{1,0:T(8,128)(2,1)S(1)}, u32[]{:S(2)}, u32[]{:S(2)}) collective-permute-start(bf16[80,896]{1,0:T(8,128)(2,1)S(1)} %get-tuple-element.54), channel_id=1, source_target_pairs={{0,4},{1,5},{2,6},{3,7},{4,0},{5,1},{6,2},{7,3},{8,12},{9,13},{10,... | collective-permute-start | bytes 430088 | tf_op jit(solution)/shard_map/ppermute | solution.py:476
  34.0 6.4 %collective-permute-start.15 = (bf16[80,384]{1,0:T(8,128)(2,1)S(1)}, bf16[80,384]{1,0:T(8,128)(2,1)S(1)}, u32[]{:S(2)}, u32[]{:S(2)}) collective-permute-start(bf16[80,384]{1,0:T(8,128)(2,1)S(1)} %get-tuple-element.60), channel_id=1, source_target_pairs={{0,4},{1,5},{2,6},{3,7},{4,0},{5,1},{6,2},{7,3},{8,12},{9,13},{10,... | collective-permute-start | bytes 184328 | tf_op jit(solution)/shard_map/ppermute | solution.py:394
  35.6 8.7 %collective-permute-start.14 = (bf16[40,512]{1,0:T(8,128)(2,1)S(1)}, bf16[40,512]{1,0:T(8,128)(2,1)S(1)}, u32[]{:S(2)}, u32[]{:S(2)}) collective-permute-start(bf16[40,512]{1,0:T(8,128)(2,1)S(1)} %get-tuple-element.58), channel_id=1, source_target_pairs={{0,4},{1,5},{2,6},{3,7},{4,0},{5,1},{6,2},{7,3},{8,12},{9,13},{10,... | collective-permute-start | bytes 122888 | tf_op jit(solution)/shard_map/ppermute | solution.py:399
  40.3 4.0 %collective-permute-start.16 = (bf16[40,384]{1,0:T(8,128)(2,1)S(1)}, bf16[40,384]{1,0:T(8,128)(2,1)S(1)}, u32[]{:S(2)}, u32[]{:S(2)}) collective-permute-start(bf16[40,384]{1,0:T(8,128)(2,1)S(1)} %get-tuple-element.62), channel_id=1, source_target_pairs={{0,2},{1,3},{2,0},{3,1},{4,6},{5,7},{6,4},{7,5},{8,10},{9,11},{10,... | collective-permute-start | bytes 92168 | tf_op jit(solution)/shard_map/ppermute | solution.py:399
  44.3 6.1 %collective-permute-start.17 = (bf16[40,896]{1,0:T(8,128)(2,1)S(1)}, bf16[40,896]{1,0:T(8,128)(2,1)S(1)}, u32[]{:S(2)}, u32[]{:S(2)}) collective-permute-start(bf16[40,896]{1,0:T(8,128)(2,1)S(1)} %last.1), channel_id=1, source_target_pairs={{0,8},{1,9},{2,10},{3,11},{4,12},{5,13},{6,14},{7,15},{8,0},{9,1},... | collective-permute-start | bytes 215048 | tf_op jit(solution)/shard_map/ppermute | solution.py:474
  46.3 4.4 %collective-permute-start.13 = (bf16[40,896]{1,0:T(8,128)(2,1)S(1)}, bf16[40,896]{1,0:T(8,128)(2,1)S(1)}, u32[]{:S(2)}, u32[]{:S(2)}) collective-permute-start(bf16[40,896]{1,0:T(8,128)(2,1)S(1)} %get-tuple-element.56), channel_id=1, source_target_pairs={{0,2},{1,3},{2,0},{3,1},{4,6},{5,7},{6,4},{7,5},{8,10},{9,11},{10,... | collective-permute-start | bytes 215048 | tf_op jit(solution)/shard_map/ppermute | solution.py:477

commit v11 on v8

--- a/solution.py
+++ b/solution.py
@@ -197,63 +197,99 @@
             out_ref[start : start + CAP, :] = slot[b * CAP : (b + 1) * CAP, :]
 
 
-def expert_kernel(own, *refs):
-    blocks, joined = refs[:own], refs[own : own + own // (SPLIT // CORES)]
-    gate_ref, up_ref, down_ref, given_ref, hidden_ref, packed, flat, out = refs[-8:]
+def unpack_kernel(own_ref, other_ref, out_ref, packed):
+    tall = CAP * SEGMENTS
+    half = own_ref.shape[0]
+    wide = own_ref.shape[1]
+    packed[:half, :] = own_ref[...].astype(jnp.float32)
+    packed[half:, :] = other_ref[...].astype(jnp.float32)
+    for s in range(SEGMENTS):
+        for b in range(2 * half // tall):
+            start = b * tall + s * CAP
+            out_ref[b * CAP : (b + 1) * CAP, s * wide : (s + 1) * wide] = packed[
+                start : start + CAP, :
+            ]
+
+
+def unpack(own, other):
+    rows, wide = own.shape
+    return pl.pallas_call(
+        unpack_kernel,
+        out_shape=jax.ShapeDtypeStruct((2 * rows // SEGMENTS, wide * SEGMENTS), jnp.float32),
+        in_specs=[VMEM] * 2,
+        out_specs=VMEM,
+        scratch_shapes=[pltpu.VMEM((2 * rows, wide), jnp.float32)],
+        compiler_params=params(6),
+        name="unpack",
+    )(own, other)
+
+
+def expert_kernel(teams, first_ref, *refs):
+    pieces = refs[: 2 * (teams - 1)]
+    gate_ref, up_ref, down_ref = refs[2 * (teams - 1) : 2 * teams + 1]
+    *given_refs, hidden_ref, packed, flat, out, act = refs[2 * teams + 1 :]
     tall = CAP * SEGMENTS
     wide = packed.shape[1]
     units = gate_ref.shape[1]
-    for b, ref in enumerate(blocks):
-        packed[b * tall : (b + 1) * tall, :] = ref[...].astype(jnp.float32)
-    start = own * tall
-    for ref in joined:
+    start = 0
+    for ref in pieces:
         packed[start : start + ref.shape[0], :] = ref[...].astype(jnp.float32)
         start += ref.shape[0]
-    count = 2 * own * CAP
+    known = first_ref.shape[0]
+    count = known * teams
     gate_act = jnp.zeros((count, units), jnp.float32)
     up_act = jnp.zeros((count, units), jnp.float32)
     for s in range(SEGMENTS):
         slot = flat.at[s % 2]
-        for b in range(2 * own):
+        columns = slice(s * wide, (s + 1) * wide)
+        slot[:known, :] = first_ref[:, columns]
+        for b in range((count - known) // CAP):
             start = b * tall + s * CAP
-            slot[b * CAP : (b + 1) * CAP, :] = packed[start : start + CAP, :]
+            slot[known + b * CAP : known + (b + 1) * CAP, :] = packed[start : start + CAP, :]
         rows = slot[...].astype(jnp.bfloat16)
-        columns = slice(s * wide, (s + 1) * wide)
         gate_act += jnp.dot(rows, gate_ref[columns, :], preferred_element_type=jnp.float32)
         up_act += jnp.dot(rows, up_ref[columns, :], preferred_element_type=jnp.float32)
-    hidden = (jax.nn.silu(gate_act) * up_act).astype(jnp.bfloat16)
+    act[:count, :] = jax.nn.silu(gate_act) * up_act
+    half = known // 2
+    for k in range(teams):
+        for core in range(CORES):
+            source = (CORES * k + core) * half
+            target = count + (core * teams + k) * half
+            act[target : target + half, :] = act[source : source + half, :]
+    hidden = act[count:, :].astype(jnp.bfloat16)
     half = count // 2
     hidden_ref[...] = hidden[:half]
     packed_down(hidden[half:], down_ref, out, flat.at[:, :half, :])
-    given_ref[...] = out[...].astype(jnp.bfloat16)
-
-
-def expert_half(blocks, joined, w_gate, w_up, w_down):
-    own = len(blocks)
-    tall, wide = blocks[0].shape
+    for k, given_ref in enumerate(given_refs):
+        rows = given_ref.shape[0]
+        given_ref[...] = out[k * rows : (k + 1) * rows, :].astype(jnp.bfloat16)
+
+
+def expert_half(first, pieces, w_gate, w_up, w_down):
+    teams = 1 + len(pieces) // 2
+    block, wide = pieces[0].shape
     features, units = w_gate.shape
-    rows = 2 * own * CAP
-    return pl.pallas_call(
-        functools.partial(expert_kernel, own),
-        out_shape=[
-            jax.ShapeDtypeStruct((own * tall, wide), jnp.bfloat16),
-            jax.ShapeDtypeStruct((own * CAP, units), jnp.bfloat16),
+    rows = first.shape[0] * teams
+    return pl.pallas_call(
+        functools.partial(expert_kernel, teams),
+        out_shape=[jax.ShapeDtypeStruct((block, wide), jnp.bfloat16)] * teams
+        + [jax.ShapeDtypeStruct((rows // 2, units), jnp.bfloat16)],
+        in_specs=[VMEM] * (len(pieces) + 4),
+        out_specs=[VMEM] * (teams + 1),
+        scratch_shapes=[
+            pltpu.VMEM((block * len(pieces), wide), jnp.float32),
+            pltpu.VMEM((2, rows, wide), jnp.float32),
+            pltpu.VMEM((block * teams, wide), jnp.float32),
+            pltpu.VMEM((2 * rows, units), jnp.float32),
         ],
-        in_specs=[VMEM] * (own + len(joined) + 3),
-        out_specs=[VMEM] * 2,
-        scratch_shapes=[
-            pltpu.VMEM((2 * own * tall, wide), jnp.float32),
-            pltpu.VMEM((2, rows, wide), jnp.float32),
-            pltpu.VMEM((own * tall, wide), jnp.float32),
-        ],
-        compiler_params=params(16 + own),
+        compiler_params=params(16 + 4 * teams),
         cost_estimate=pl.CostEstimate(
             flops=5 * rows * units * features,
             bytes_accessed=6 * features * units,
             transcendentals=rows * units,
         ),
         name="expert_half",
-    )(*blocks, *joined, w_gate, w_up, w_down)
+    )(first, *pieces, w_gate, w_up, w_down)
 
 
 def kept_kernel(hidden_ref, down_ref, kept_ref, flat):
@@ -280,27 +316,25 @@
     )(hidden, w_down)
 
 
-def add_kernel(kept_ref, taken_ref, *out_refs):
+def add_kernel(first, kept_ref, taken_ref, *out_refs):
     tall = out_refs[0].shape[0]
     for b, out_ref in enumerate(out_refs):
         rows = slice(b * tall, (b + 1) * tall)
-        total = kept_ref[rows, :] + taken_ref[rows, :].astype(jnp.float32)
+        total = kept_ref[first + b * tall : first + (b + 1) * tall, :] + taken_ref[
+            rows, :
+        ].astype(jnp.float32)
         out_ref[...] = total.astype(out_ref.dtype)
 
 
-def add_cores(kept, taken, teams, chips):
+def add_cores(kept, taken, k, chips):
     shape = (CAP * SEGMENTS, kept.shape[1])
-    outs = [
-        jax.ShapeDtypeStruct(shape, jnp.bfloat16 if m else jnp.float32)
-        for k in range(teams)
-        for m in range(chips)
-    ]
-    return pl.pallas_call(
-        add_kernel,
+    outs = [jax.ShapeDtypeStruct(shape, jnp.bfloat16 if m else jnp.float32) for m in range(chips)]
+    return pl.pallas_call(
+        functools.partial(add_kernel, k * taken.shape[0]),
         out_shape=outs,
         in_specs=[VMEM] * 2,
         out_specs=[VMEM] * len(outs),
-        compiler_params=params(4 + 4 * teams),
+        compiler_params=params(6),
         name="add_cores",
     )(kept, taken)
 
@@ -321,6 +355,11 @@
         compiler_params=params(4),
         name="sum_blocks",
     )(*blocks)
+
+
+def halves(wide):
+    cut = 128 * pl.cdiv(wide // 128, 2)
+    return slice(0, cut), slice(cut, wide)
 
 
 def blend_kernel(chips, weight_ref, *refs):
@@ -336,15 +375,18 @@
         terms += [ref[...].astype(jnp.float32)] * 2
     rows = jnp.concatenate(terms, axis=0).astype(jnp.bfloat16)
     copies = []
-    for s in range(SEGMENTS):
-        columns = pl.ds(s * wide, wide)
-        out_ref[:, columns] = jnp.dot(
-            weight_ref[s * count : (s + 1) * count, :], rows, preferred_element_type=jnp.float32
-        ).astype(jnp.bfloat16)
-        copies.append(
-            pltpu.make_async_copy(out_ref.at[:, columns], out_hbm.at[:, columns], sem.at[s])
-        )
-        copies[-1].start()
+    for columns in halves(wide):
+        size = columns.stop - columns.start
+        total = jnp.dot(weight_ref[...], rows[:, columns], preferred_element_type=jnp.float32)
+        for s in range(SEGMENTS):
+            part = pl.ds(s * wide + columns.start, size)
+            out_ref[:, part] = total[s * count : (s + 1) * count].astype(jnp.bfloat16)
+            copies.append(
+                pltpu.make_async_copy(
+                    out_ref.at[:, part], out_hbm.at[:, part], sem.at[len(copies)]
+                )
+            )
+            copies[-1].start()
     wait_all(copies)
 
 
@@ -358,7 +400,7 @@
         out_specs=HBM,
         scratch_shapes=[
             pltpu.VMEM((count, features), jnp.bfloat16),
-            pltpu.SemaphoreType.DMA((SEGMENTS,)),
+            pltpu.SemaphoreType.DMA((2 * SEGMENTS,)),
         ],
         compiler_params=params(16),
         name="blend",
@@ -372,38 +414,38 @@
     other_core = [(i, i ^ 1) for i in range(devices)]
     other_chip = [[(i, i ^ (m * CORES)) for i in range(devices)] for m in range(chips)]
     packed, table = pack_rows(expert_ids.T, route_logits.T, tokens, teams)
+    def gather(block):
+        return [block] + [lax.ppermute(block, "expert", other_chip[m]) for m in range(1, chips)]
+
+    own = gather(packed[0])
     crowds = []
-    for k in range(teams):
-        block = packed[k]
-        if k > 0:
-            pairs = [(i, (i + k * SPLIT) % devices) for i in range(devices)]
-            block = lax.ppermute(block, "expert", pairs)
+    for k in range(1, teams):
+        pairs = [(i, (i + k * SPLIT) % devices) for i in range(devices)]
+        block = lax.ppermute(packed[k], "expert", pairs)
         if k == teams - 1:
             block, table = lax.optimization_barrier((block, table))
             weights = blend_weights(table, teams)
-        team = [block]
-        for m in range(1, chips):
-            team.append(lax.ppermute(block, "expert", other_chip[m]))
-        crowds.append(team)
-    crowds[0], weights = lax.optimization_barrier((crowds[0], weights))
-    blocks, joined = [], []
-    for team in crowds:
-        if joined:
-            team, joined = lax.optimization_barrier((team, joined))
-        blocks += team
-        joined.append(join(team))
-    swapped = [lax.ppermute(j, "expert", other_core) for j in joined]
-    given, hidden = expert_half(blocks, swapped, w_gate, w_up, w_down)
-    taken = lax.ppermute(given, "expert", other_core)
+        crowds.append(gather(block))
+    own, crowds, weights = lax.optimization_barrier((own, crowds, weights))
+    own = join(own)
+    first = unpack(own, lax.ppermute(own, "expert", other_core))
+    pieces = []
+    for crowd in crowds:
+        crowd = join(crowd)
+        pieces += [crowd, lax.ppermute(crowd, "expert", other_core)]
+    *given, hidden = expert_half(first, pieces, w_gate, w_up, w_down)
+    taken = [lax.ppermute(piece, "expert", other_core) for piece in given]
     kept = kept_half(hidden, w_down)
-    parts = add_cores(kept, taken, teams, chips)
     others = []
     for k in range(1, teams):
-        team = [parts[k * chips]]
+        parts = add_cores(kept, taken[k], k, chips)
+        parts, taken[0] = lax.optimization_barrier((parts, taken[0]))
+        team = [parts[0]]
         for m in range(1, chips):
-            team.append(lax.ppermute(parts[k * chips + m], "expert", other_chip[m]))
+            team.append(lax.ppermute(parts[m], "expert", other_chip[m]))
         pairs = [(i, (i - k * SPLIT) % devices) for i in range(devices)]
         others.append(lax.ppermute(sum_blocks(team), "expert", pairs))
+    parts = add_cores(kept, taken[0], 0, chips)
     own = [parts[0]]
     for m in range(1, chips):
         own.append(lax.ppermute(parts[m], "expert", other_chip[m]))

time: 40 us -> 39.5 us (0.988)
  waiting for transfers between devices: 8.84 us -> 7.71 us
  starting transfers between devices: 22.7 us -> 23.4 us
    ppermute x13 -> x14, waiting for transfers between devices: 5.76 us -> 4.63 us  [the longest x6 2.35 us: gather(): lax.ppermute(block, 'expert', other_chip[m])]
    ppermute x13 -> x14, starting transfers between devices: 16.2 us -> 16.6 us  [the longest x6 7.81 us: gather(): lax.ppermute(block, 'expert', other_chip[m])]
    pallas_call x2 -> x4, Pallas kernels: 2.63 us -> 2.8 us  [the longest x1 2.33 us: expert_half(): pl.pallas_call(functools.partial(expert_kernel, teams), out_shape=[jax.Sh...]
  transfers between devices with their start and end apart: 17 -> 18, of which waited for: 9 -> 11; matrix products, arithmetic and copies ran while one was open for 0% -> 0% of each run, Pallas kernels for 3% -> 4%
where the time goes in v11:
time: 39.5 us; the launch traced here: 39.3 us
  starting transfers between devices  23.4 us (59%)
  waiting for transfers between devices  7.71 us (20%)
  Pallas kernels  7.43 us (19%)
  local copies, waits for them, and re-layouts  0.71 us (2%)
    ppermute x6, starting transfers between devices, gather(): lax.ppermute(block, 'expert', other_chip[m])  7.81 us
    ppermute x1, starting transfers between devices, body(): block = lax.ppermute(packed[k], 'expert', pairs)  4.1 us
    ppermute x3, starting transfers between devices, body(): own.append(lax.ppermute(parts[m], 'expert', other_chip[m]))  3.55 us
    ppermute x3, starting transfers between devices, body(): team.append(lax.ppermute(parts[m], 'expert', other_chip[m]))  3.49 us
    ppermute x1, starting transfers between devices, body(): others.append(lax.ppermute(sum_blocks(team), 'expert', pairs))  3.19 us
    ppermute x1, waiting for transfers between devices, body(): others.append(lax.ppermute(sum_blocks(team), 'expert', pairs))  2.54 us
    ppermute x6, waiting for transfers between devices, gather(): lax.ppermute(block, 'expert', other_chip[m])  2.35 us
    pallas_call x1, Pallas kernels, expert_half(): pl.pallas_call(functools.partial(expert_kernel, teams), out_shape=[jax.Sh...  2.33 us
  transfers between devices with their start and end apart: 18, of which 11 were waited for; matrix products, arithmetic and copies ran while one was open for 0% of the time, Pallas kernels for 4%

profile of v11, /device:TPU:0, one launch (start us, length us, event | category | flops | bytes accessed | tf_op | source)
XLA Modules:
  0.0 39.3 jit_solution(8321861119505855853)
XLA Ops:
  0.0 2.3 %pack_rows.1 = (bf16[40,896]{1,0:T(8,128)(2,1)}, bf16[40,896]{1,0:T(8,128)(2,1)}, f32[16,64]{1,0:T(8,128)}) custom-call(s32[8,64]{1,0:T(8,128)} %bitcast.2, f32[8,64]{1,0:T(8,128)} %bitcast.3, bf16[64,7168]{1,0:T(8,128)(2,1)} %tokens_hbm.1), custom_call_target="tpu_custom_call" | custom-call | tf_op jit(solution)/shard_map/pack_rows/pallas_call | solution.py:110
  2.3 4.1 %collective-permute-start.3 = (bf16[40,896]{1,0:T(8,128)(2,1)}, bf16[40,896]{1,0:T(8,128)(2,1)S(1)}, u32[]{:S(2)}, u32[]{:S(2)}) collective-permute-start(bf16[40,896]{1,0:T(8,128)(2,1)} %get-tuple-element.36), channel_id=1, source_target_pairs={{0,8},{1,9},{2,10},{3,11},{4,12},{5,13},{6,14},{7,15},{8,0},{9,1},... | collective-permute-start | bytes 215048 | tf_op jit(solution)/shard_map/ppermute | solution.py:424
  6.4 2.5 %collective-permute-start.2 = (bf16[40,896]{1,0:T(8,128)(2,1)}, bf16[40,896]{1,0:T(8,128)(2,1)S(1)}, u32[]{:S(2)}, u32[]{:S(2)}) collective-permute-start(bf16[40,896]{1,0:T(8,128)(2,1)} %get-tuple-element.41.refs_0_), channel_id=1, source_target_pairs={{0,6},{1,7},{2,4},{3,5},{4,2},{5,3},{6,0},{7,1},{8,14},{9,15},{10,... | collective-permute-start | bytes 215048 | tf_op jit(solution)/shard_map/ppermute | solution.py:418
  8.9 0.4 %collective-permute-start.1 = (bf16[40,896]{1,0:T(8,128)(2,1)}, bf16[40,896]{1,0:T(8,128)(2,1)S(1)}, u32[]{:S(2)}, u32[]{:S(2)}) collective-permute-start(bf16[40,896]{1,0:T(8,128)(2,1)} %get-tuple-element.41.refs_0_), channel_id=1, source_target_pairs={{0,4},{1,5},{2,6},{3,7},{4,0},{5,1},{6,2},{7,3},{8,12},{9,13},{10,... | collective-permute-start | bytes 215048 | tf_op jit(solution)/shard_map/ppermute | solution.py:418
  9.4 0.5 %collective-permute-start = (bf16[40,896]{1,0:T(8,128)(2,1)}, bf16[40,896]{1,0:T(8,128)(2,1)S(1)}, u32[]{:S(2)}, u32[]{:S(2)}) collective-permute-start(bf16[40,896]{1,0:T(8,128)(2,1)} %get-tuple-element.41.refs_0_), channel_id=1, source_target_pairs={{0,2},{1,3},{2,0},{3,1},{4,6},{5,7},{6,4},{7,5},{8,10},{9,11},{10,... | collective-permute-start | bytes 215048 | tf_op jit(solution)/shard_map/ppermute | solution.py:418
  9.9 0.0 collective-permute-done.3.refs_0_
  9.9 2.7 %collective-permute-start.6 = (bf16[40,896]{1,0:T(8,128)(2,1)S(1)}, bf16[40,896]{1,0:T(8,128)(2,1)S(1)}, u32[]{:S(2)}, u32[]{:S(2)}) collective-permute-start(bf16[40,896]{1,0:T(8,128)(2,1)S(1)} %collective-permute-done.3.refs_0_), channel_id=1, source_target_pairs={{0,6},{1,7},{2,4},{3,5},{4,2},{5,3},{6,0},{7,1},{8,14},{9,15},{10,... | collective-permute-start | bytes 215048 | tf_op jit(solution)/shard_map/ppermute | solution.py:418
  12.6 0.7 %collective-permute-start.5 = (bf16[40,896]{1,0:T(8,128)(2,1)S(1)}, bf16[40,896]{1,0:T(8,128)(2,1)S(1)}, u32[]{:S(2)}, u32[]{:S(2)}) collective-permute-start(bf16[40,896]{1,0:T(8,128)(2,1)S(1)} %collective-permute-done.3.refs_0_), channel_id=1, source_target_pairs={{0,4},{1,5},{2,6},{3,7},{4,0},{5,1},{6,2},{7,3},{8,12},{9,13},{10,... | collective-permute-start | bytes 215048 | tf_op jit(solution)/shard_map/ppermute | solution.py:418
  13.3 0.0 collective-permute-done.2.refs_3_
  13.3 1.0 %collective-permute-start.4 = (bf16[40,896]{1,0:T(8,128)(2,1)S(1)}, bf16[40,896]{1,0:T(8,128)(2,1)S(1)}, u32[]{:S(2)}, u32[]{:S(2)}) collective-permute-start(bf16[40,896]{1,0:T(8,128)(2,1)S(1)} %collective-permute-done.3.refs_0_), channel_id=1, source_target_pairs={{0,2},{1,3},{2,0},{3,1},{4,6},{5,7},{6,4},{7,5},{8,10},{9,11},{10,... | collective-permute-start | bytes 215048 | tf_op jit(solution)/shard_map/ppermute | solution.py:418
  14.2 0.7 %copy-done.4 = f32[16,64]{1,0:T(8,128)S(1)} copy-done((f32[16,64]{1,0:T(8,128)S(1)}, f32[16,64]{1,0:T(8,128)}, u32[]{:S(2)}) %copy-start.4) | copy-done | bytes 4120
  14.9 0.3 blend_weights.1.weight_ref
  15.2 0.0 collective-permute-done.1.refs_2_
  15.2 0.1 collective-permute-done.refs_1_
  15.3 0.5 %collective-permute-done.6.refs_3_ = bf16[40,896]{1,0:T(8,128)(2,1)S(1)} collective-permute-done((bf16[40,896]{1,0:T(8,128)(2,1)S(1)}, bf16[40,896]{1,0:T(8,128)(2,1)S(1)}, u32[]{:S(2)}, u32[]{:S(2)}) %collective-permute-start.6) | collective-permute-done | bytes 71712 | tf_op jit(solution)/shard_map/ppermute | solution.py:418
  15.9 1.0 %collective-permute-done.5.refs_2_ = bf16[40,896]{1,0:T(8,128)(2,1)S(1)} collective-permute-done((bf16[40,896]{1,0:T(8,128)(2,1)S(1)}, bf16[40,896]{1,0:T(8,128)(2,1)S(1)}, u32[]{:S(2)}, u32[]{:S(2)}) %collective-permute-start.5) | collective-permute-done | bytes 71712 | tf_op jit(solution)/shard_map/ppermute | solution.py:418
  16.9 0.7 %collective-permute-done.4.refs_1_ = bf16[40,896]{1,0:T(8,128)(2,1)S(1)} collective-permute-done((bf16[40,896]{1,0:T(8,128)(2,1)S(1)}, bf16[40,896]{1,0:T(8,128)(2,1)S(1)}, u32[]{:S(2)}, u32[]{:S(2)}) %collective-permute-start.4) | collective-permute-done | bytes 71712 | tf_op jit(solution)/shard_map/ppermute | solution.py:418
  17.6 0.0 copy-done.3
  17.6 0.1 collective-permute-start.7
  17.7 0.6 %collective-permute-start.8 = (bf16[160,896]{1,0:T(8,128)(2,1)S(1)}, bf16[160,896]{1,0:T(8,128)(2,1)S(1)}, u32[]{:S(2)}, u32[]{:S(2)}) collective-permute-start(bf16[160,896]{1,0:T(8,128)(2,1)S(1)} %join.3.refs_0_), channel_id=1, source_target_pairs={{0,1},{1,0},{2,3},{3,2},{4,5},{5,4},{6,7},{7,6},{8,9},{9,8},{10,11... | collective-permute-start | bytes 860168 | tf_op jit(solution)/shard_map/ppermute | solution.py:435
  18.3 1.0 %collective-permute-done.7.other_ref = bf16[160,896]{1,0:T(8,128)(2,1)S(1)} collective-permute-done((bf16[160,896]{1,0:T(8,128)(2,1)S(1)}, bf16[160,896]{1,0:T(8,128)(2,1)S(1)}, u32[]{:S(2)}, u32[]{:S(2)}) %collective-permute-start.7) | collective-permute-done | bytes 286752 | tf_op jit(solution)/shard_map/ppermute | solution.py:431
  19.3 0.3 unpack.1.first_ref
  19.6 0.1 collective-permute-done.8.refs_1_
  19.7 0.0 copy-done
  19.7 0.0 copy-done.1
  19.7 2.3 %expert_half.1 = (bf16[160,896]{1,0:T(8,128)(2,1)S(1)}, bf16[160,896]{1,0:T(8,128)(2,1)S(1)}, bf16[40,256]{1,0:T(8,128)(2,1)S(1)}) custom-call(f32[40,7168]{1,0:T(8,128)S(1)} %unpack.1.first_ref, bf16[160,896]{1,0:T(8,128)(2,1)S(1)} %join.3.refs_0_, bf16[160,896]{1,0:T(8,128)(2,1)S(1)} %collective-permute-done.8.refs_1_, bf16[7168,256]{1,0:T(8,128)(2,1)S(1)} %copy-done.1, ...), custom_call_target="tpu_custom_call" | custom-call | flops 734003200 | bytes 11010048 | tf_op jit(solution)/shard_map/expert_half/pallas_call | solution.py:273
  22.0 0.3 collective-permute-start.9
  22.3 0.3 collective-permute-start.10
  22.6 0.7 %kept_half.1.kept_ref = f32[320,896]{1,0:T(8,128)S(1)} custom-call(bf16[40,256]{1,0:T(8,128)(2,1)S(1)} %get-tuple-element.49.hidden_ref, bf16[256,7168]{1,0:T(8,128)(2,1)S(1)} %copy-done), custom_call_target="tpu_custom_call" | custom-call | flops 146800640 | bytes 3670016 | tf_op jit(solution)/shard_map/kept_half/pallas_call | solution.py:303
  23.3 0.3 collective-permute-done.9.taken_ref
  23.6 0.1 add_cores.2
  23.7 0.3 collective-permute-done.10.taken_ref
  24.1 1.0 %collective-permute-start.14 = (bf16[40,896]{1,0:T(8,128)(2,1)S(1)}, bf16[40,896]{1,0:T(8,128)(2,1)S(1)}, u32[]{:S(2)}, u32[]{:S(2)}) collective-permute-start(bf16[40,896]{1,0:T(8,128)(2,1)S(1)} %get-tuple-element.62), channel_id=1, source_target_pairs={{0,2},{1,3},{2,0},{3,1},{4,6},{5,7},{6,4},{7,5},{8,10},{9,11},{10,... | collective-permute-start | bytes 215048 | tf_op jit(solution)/shard_map/ppermute | solution.py:445
  25.0 0.9 %collective-permute-start.15 = (bf16[40,896]{1,0:T(8,128)(2,1)S(1)}, bf16[40,896]{1,0:T(8,128)(2,1)S(1)}, u32[]{:S(2)}, u32[]{:S(2)}) collective-permute-start(bf16[40,896]{1,0:T(8,128)(2,1)S(1)} %get-tuple-element.63), channel_id=1, source_target_pairs={{0,4},{1,5},{2,6},{3,7},{4,0},{5,1},{6,2},{7,3},{8,12},{9,13},{10,... | collective-permute-start | bytes 215048 | tf_op jit(solution)/shard_map/ppermute | solution.py:445
  25.9 1.6 %collective-permute-start.16 = (bf16[40,896]{1,0:T(8,128)(2,1)S(1)}, bf16[40,896]{1,0:T(8,128)(2,1)S(1)}, u32[]{:S(2)}, u32[]{:S(2)}) collective-permute-start(bf16[40,896]{1,0:T(8,128)(2,1)S(1)} %get-tuple-element.64), channel_id=1, source_target_pairs={{0,6},{1,7},{2,4},{3,5},{4,2},{5,3},{6,0},{7,1},{8,14},{9,15},{10,... | collective-permute-start | bytes 215048 | tf_op jit(solution)/shard_map/ppermute | solution.py:445
  27.5 0.1 add_cores.3
  27.6 1.0 %collective-permute-start.11 = (bf16[40,896]{1,0:T(8,128)(2,1)S(1)}, bf16[40,896]{1,0:T(8,128)(2,1)S(1)}, u32[]{:S(2)}, u32[]{:S(2)}) collective-permute-start(bf16[40,896]{1,0:T(8,128)(2,1)S(1)} %get-tuple-element.58), channel_id=1, source_target_pairs={{0,2},{1,3},{2,0},{3,1},{4,6},{5,7},{6,4},{7,5},{8,10},{9,11},{10,... | collective-permute-start | bytes 215048 | tf_op jit(solution)/shard_map/ppermute | solution.py:451
  28.6 0.9 %collective-permute-start.12 = (bf16[40,896]{1,0:T(8,128)(2,1)S(1)}, bf16[40,896]{1,0:T(8,128)(2,1)S(1)}, u32[]{:S(2)}, u32[]{:S(2)}) collective-permute-start(bf16[40,896]{1,0:T(8,128)(2,1)S(1)} %get-tuple-element.59), channel_id=1, source_target_pairs={{0,4},{1,5},{2,6},{3,7},{4,0},{5,1},{6,2},{7,3},{8,12},{9,13},{10,... | collective-permute-start | bytes 215048 | tf_op jit(solution)/shard_map/ppermute | solution.py:451
  29.5 0.0 collective-permute-done.14.refs_1_
  29.5 1.6 %collective-permute-start.13 = (bf16[40,896]{1,0:T(8,128)(2,1)S(1)}, bf16[40,896]{1,0:T(8,128)(2,1)S(1)}, u32[]{:S(2)}, u32[]{:S(2)}) collective-permute-start(bf16[40,896]{1,0:T(8,128)(2,1)S(1)} %get-tuple-element.60), channel_id=1, source_target_pairs={{0,6},{1,7},{2,4},{3,5},{4,2},{5,3},{6,0},{7,1},{8,14},{9,15},{10,... | collective-permute-start | bytes 215048 | tf_op jit(solution)/shard_map/ppermute | solution.py:451
  31.2 0.0 collective-permute-done.15.refs_2_
  31.2 0.6 %collective-permute-done.16.refs_3_ = bf16[40,896]{1,0:T(8,128)(2,1)S(1)} collective-permute-done((bf16[40,896]{1,0:T(8,128)(2,1)S(1)}, bf16[40,896]{1,0:T(8,128)(2,1)S(1)}, u32[]{:S(2)}, u32[]{:S(2)}) %collective-permute-start.16) | collective-permute-done | bytes 71712 | tf_op jit(solution)/shard_map/ppermute | solution.py:445
  31.8 3.2 %collective-permute-start.17 = (bf16[40,896]{1,0:T(8,128)(2,1)S(1)}, bf16[40,896]{1,0:T(8,128)(2,1)S(1)}, u32[]{:S(2)}, u32[]{:S(2)}) collective-permute-start(bf16[40,896]{1,0:T(8,128)(2,1)S(1)} %sum_blocks.1), channel_id=1, source_target_pairs={{0,8},{1,9},{2,10},{3,11},{4,12},{5,13},{6,14},{7,15},{8,0},{9,1},... | collective-permute-start | bytes 215048 | tf_op jit(solution)/shard_map/ppermute | solution.py:447
  35.0 0.0 collective-permute-done.11.refs_1_
  35.0 0.0 collective-permute-done.12.refs_2_
  35.0 0.5 %collective-permute-done.13.refs_3_ = bf16[40,896]{1,0:T(8,128)(2,1)S(1)} collective-permute-done((bf16[40,896]{1,0:T(8,128)(2,1)S(1)}, bf16[40,896]{1,0:T(8,128)(2,1)S(1)}, u32[]{:S(2)}, u32[]{:S(2)}) %collective-permute-start.13) | collective-permute-done | bytes 71712 | tf_op jit(solution)/shard_map/ppermute | solution.py:451
  35.5 2.5 %collective-permute-done.17.refs_4_ = bf16[40,896]{1,0:T(8,128)(2,1)S(1)} collective-permute-done((bf16[40,896]{1,0:T(8,128)(2,1)S(1)}, bf16[40,896]{1,0:T(8,128)(2,1)S(1)}, u32[]{:S(2)}, u32[]{:S(2)}) %collective-permute-start.17) | collective-permute-done | bytes 71712 | tf_op jit(solution)/shard_map/ppermute | solution.py:447
  38.1 1.2 %blend.1 = bf16[64,7168]{1,0:T(8,128)(2,1)} custom-call(bf16[512,200]{1,0:T(8,128)(2,1)S(1)} %blend_weights.1.weight_ref, f32[40,896]{1,0:T(8,128)S(1)} %get-tuple-element.57.refs_0_, bf16[40,896]{1,0:T(8,128)(2,1)S(1)} %collective-permute-done.11.refs_1_, bf16[40,896]{1,0:T(8,128)(2,1)S(1)} %collective-permute-done.12.refs_2_, ...), custom_call_target="tpu_custom_call" | custom-call | tf_op jit(solution)/shard_map/blend/pallas_call | solution.py:396
  (9 shorter events, 0.1 us)
Async XLA Ops:
  2.3 7.6 %collective-permute-start.3 = (bf16[40,896]{1,0:T(8,128)(2,1)}, bf16[40,896]{1,0:T(8,128)(2,1)S(1)}, u32[]{:S(2)}, u32[]{:S(2)}) collective-permute-start(bf16[40,896]{1,0:T(8,128)(2,1)} %get-tuple-element.36), channel_id=1, source_target_pairs={{0,8},{1,9},{2,10},{3,11},{4,12},{5,13},{6,14},{7,15},{8,0},{9,1},... | collective-permute-start | bytes 215048 | tf_op jit(solution)/shard_map/ppermute | solution.py:424
  6.4 6.9 %collective-permute-start.2 = (bf16[40,896]{1,0:T(8,128)(2,1)}, bf16[40,896]{1,0:T(8,128)(2,1)S(1)}, u32[]{:S(2)}, u32[]{:S(2)}) collective-permute-start(bf16[40,896]{1,0:T(8,128)(2,1)} %get-tuple-element.41.refs_0_), channel_id=1, source_target_pairs={{0,6},{1,7},{2,4},{3,5},{4,2},{5,3},{6,0},{7,1},{8,14},{9,15},{10,... | collective-permute-start | bytes 215048 | tf_op jit(solution)/shard_map/ppermute | solution.py:418
  8.9 6.3 %collective-permute-start.1 = (bf16[40,896]{1,0:T(8,128)(2,1)}, bf16[40,896]{1,0:T(8,128)(2,1)S(1)}, u32[]{:S(2)}, u32[]{:S(2)}) collective-permute-start(bf16[40,896]{1,0:T(8,128)(2,1)} %get-tuple-element.41.refs_0_), channel_id=1, source_target_pairs={{0,4},{1,5},{2,6},{3,7},{4,0},{5,1},{6,2},{7,3},{8,12},{9,13},{10,... | collective-permute-start | bytes 215048 | tf_op jit(solution)/shard_map/ppermute | solution.py:418
  9.4 6.0 %collective-permute-start = (bf16[40,896]{1,0:T(8,128)(2,1)}, bf16[40,896]{1,0:T(8,128)(2,1)S(1)}, u32[]{:S(2)}, u32[]{:S(2)}) collective-permute-start(bf16[40,896]{1,0:T(8,128)(2,1)} %get-tuple-element.41.refs_0_), channel_id=1, source_target_pairs={{0,2},{1,3},{2,0},{3,1},{4,6},{5,7},{6,4},{7,5},{8,10},{9,11},{10,... | collective-permute-start | bytes 215048 | tf_op jit(solution)/shard_map/ppermute | solution.py:418
  9.9 7.7 %copy-start.3 = (bf16[40,896]{1,0:T(8,128)(2,1)S(1)}, bf16[40,896]{1,0:T(8,128)(2,1)}, u32[]{:S(2)}) copy-start(bf16[40,896]{1,0:T(8,128)(2,1)} %get-tuple-element.41.refs_0_) | copy-start | bytes 215044
  9.9 6.0 %collective-permute-start.6 = (bf16[40,896]{1,0:T(8,128)(2,1)S(1)}, bf16[40,896]{1,0:T(8,128)(2,1)S(1)}, u32[]{:S(2)}, u32[]{:S(2)}) collective-permute-start(bf16[40,896]{1,0:T(8,128)(2,1)S(1)} %collective-permute-done.3.refs_0_), channel_id=1, source_target_pairs={{0,6},{1,7},{2,4},{3,5},{4,2},{5,3},{6,0},{7,1},{8,14},{9,15},{10,... | collective-permute-start | bytes 215048 | tf_op jit(solution)/shard_map/ppermute | solution.py:418
  12.6 4.3 %collective-permute-start.5 = (bf16[40,896]{1,0:T(8,128)(2,1)S(1)}, bf16[40,896]{1,0:T(8,128)(2,1)S(1)}, u32[]{:S(2)}, u32[]{:S(2)}) collective-permute-start(bf16[40,896]{1,0:T(8,128)(2,1)S(1)} %collective-permute-done.3.refs_0_), channel_id=1, source_target_pairs={{0,4},{1,5},{2,6},{3,7},{4,0},{5,1},{6,2},{7,3},{8,12},{9,13},{10,... | collective-permute-start | bytes 215048 | tf_op jit(solution)/shard_map/ppermute | solution.py:418
  13.3 4.3 %collective-permute-start.4 = (bf16[40,896]{1,0:T(8,128)(2,1)S(1)}, bf16[40,896]{1,0:T(8,128)(2,1)S(1)}, u32[]{:S(2)}, u32[]{:S(2)}) collective-permute-start(bf16[40,896]{1,0:T(8,128)(2,1)S(1)} %collective-permute-done.3.refs_0_), channel_id=1, source_target_pairs={{0,2},{1,3},{2,0},{3,1},{4,6},{5,7},{6,4},{7,5},{8,10},{9,11},{10,... | collective-permute-start | bytes 215048 | tf_op jit(solution)/shard_map/ppermute | solution.py:418
  14.2 0.7 %copy-start.4 = (f32[16,64]{1,0:T(8,128)S(1)}, f32[16,64]{1,0:T(8,128)}, u32[]{:S(2)}) copy-start(f32[16,64]{1,0:T(8,128)} %get-tuple-element.39.table_ref) | copy-start | bytes 12292
  14.9 4.8 %copy-start = (bf16[256,7168]{1,0:T(8,128)(2,1)S(1)}, bf16[256,7168]{1,0:T(8,128)(2,1)}, u32[]{:S(2)}) copy-start(bf16[256,7168]{1,0:T(8,128)(2,1)} %down_ref.1) | copy-start | bytes 11010052
  14.9 4.8 %copy-start.1 = (bf16[7168,256]{1,0:T(8,128)(2,1)S(1)}, bf16[7168,256]{1,0:T(8,128)(2,1)}, u32[]{:S(2)}) copy-start(bf16[7168,256]{1,0:T(8,128)(2,1)} %refs_2_.1) | copy-start | bytes 11010052
  14.9 4.8 %copy-start.2 = (bf16[7168,256]{1,0:T(8,128)(2,1)S(1)}, bf16[7168,256]{1,0:T(8,128)(2,1)}, u32[]{:S(2)}) copy-start(bf16[7168,256]{1,0:T(8,128)(2,1)} %refs_3_.1) | copy-start | bytes 11010052
  17.6 1.6 %collective-permute-start.7 = (bf16[160,896]{1,0:T(8,128)(2,1)S(1)}, bf16[160,896]{1,0:T(8,128)(2,1)S(1)}, u32[]{:S(2)}, u32[]{:S(2)}) collective-permute-start(bf16[160,896]{1,0:T(8,128)(2,1)S(1)} %join.2.own_ref), channel_id=1, source_target_pairs={{0,1},{1,0},{2,3},{3,2},{4,5},{5,4},{6,7},{7,6},{8,9},{9,8},{10,11... | collective-permute-start | bytes 860168 | tf_op jit(solution)/shard_map/ppermute | solution.py:431
  17.7 1.9 %collective-permute-start.8 = (bf16[160,896]{1,0:T(8,128)(2,1)S(1)}, bf16[160,896]{1,0:T(8,128)(2,1)S(1)}, u32[]{:S(2)}, u32[]{:S(2)}) collective-permute-start(bf16[160,896]{1,0:T(8,128)(2,1)S(1)} %join.3.refs_0_), channel_id=1, source_target_pairs={{0,1},{1,0},{2,3},{3,2},{4,5},{5,4},{6,7},{7,6},{8,9},{9,8},{10,11... | collective-permute-start | bytes 860168 | tf_op jit(solution)/shard_map/ppermute | solution.py:435
  22.0 1.6 %collective-permute-start.9 = (bf16[160,896]{1,0:T(8,128)(2,1)S(1)}, bf16[160,896]{1,0:T(8,128)(2,1)S(1)}, u32[]{:S(2)}, u32[]{:S(2)}) collective-permute-start(bf16[160,896]{1,0:T(8,128)(2,1)S(1)} %get-tuple-element.50), channel_id=1, source_target_pairs={{0,1},{1,0},{2,3},{3,2},{4,5},{5,4},{6,7},{7,6},{8,9},{9,8},{10,11... | collective-permute-start | bytes 860168 | tf_op jit(solution)/shard_map/ppermute | solution.py:437
  22.3 1.8 %collective-permute-start.10 = (bf16[160,896]{1,0:T(8,128)(2,1)S(1)}, bf16[160,896]{1,0:T(8,128)(2,1)S(1)}, u32[]{:S(2)}, u32[]{:S(2)}) collective-permute-start(bf16[160,896]{1,0:T(8,128)(2,1)S(1)} %get-tuple-element.55), channel_id=1, source_target_pairs={{0,1},{1,0},{2,3},{3,2},{4,5},{5,4},{6,7},{7,6},{8,9},{9,8},{10,11... | collective-permute-start | bytes 860168 | tf_op jit(solution)/shard_map/ppermute | solution.py:437
  24.1 5.5 %collective-permute-start.14 = (bf16[40,896]{1,0:T(8,128)(2,1)S(1)}, bf16[40,896]{1,0:T(8,128)(2,1)S(1)}, u32[]{:S(2)}, u32[]{:S(2)}) collective-permute-start(bf16[40,896]{1,0:T(8,128)(2,1)S(1)} %get-tuple-element.62), channel_id=1, source_target_pairs={{0,2},{1,3},{2,0},{3,1},{4,6},{5,7},{6,4},{7,5},{8,10},{9,11},{10,... | collective-permute-start | bytes 215048 | tf_op jit(solution)/shard_map/ppermute | solution.py:445
  25.0 6.1 %collective-permute-start.15 = (bf16[40,896]{1,0:T(8,128)(2,1)S(1)}, bf16[40,896]{1,0:T(8,128)(2,1)S(1)}, u32[]{:S(2)}, u32[]{:S(2)}) collective-permute-start(bf16[40,896]{1,0:T(8,128)(2,1)S(1)} %get-tuple-element.63), channel_id=1, source_target_pairs={{0,4},{1,5},{2,6},{3,7},{4,0},{5,1},{6,2},{7,3},{8,12},{9,13},{10,... | collective-permute-start | bytes 215048 | tf_op jit(solution)/shard_map/ppermute | solution.py:445
  25.9 5.8 %collective-permute-start.16 = (bf16[40,896]{1,0:T(8,128)(2,1)S(1)}, bf16[40,896]{1,0:T(8,128)(2,1)S(1)}, u32[]{:S(2)}, u32[]{:S(2)}) collective-permute-start(bf16[40,896]{1,0:T(8,128)(2,1)S(1)} %get-tuple-element.64), channel_id=1, source_target_pairs={{0,6},{1,7},{2,4},{3,5},{4,2},{5,3},{6,0},{7,1},{8,14},{9,15},{10,... | collective-permute-start | bytes 215048 | tf_op jit(solution)/shard_map/ppermute | solution.py:445
  27.6 7.4 %collective-permute-start.11 = (bf16[40,896]{1,0:T(8,128)(2,1)S(1)}, bf16[40,896]{1,0:T(8,128)(2,1)S(1)}, u32[]{:S(2)}, u32[]{:S(2)}) collective-permute-start(bf16[40,896]{1,0:T(8,128)(2,1)S(1)} %get-tuple-element.58), channel_id=1, source_target_pairs={{0,2},{1,3},{2,0},{3,1},{4,6},{5,7},{6,4},{7,5},{8,10},{9,11},{10,... | collective-permute-start | bytes 215048 | tf_op jit(solution)/shard_map/ppermute | solution.py:451
  28.6 6.3 %collective-permute-start.12 = (bf16[40,896]{1,0:T(8,128)(2,1)S(1)}, bf16[40,896]{1,0:T(8,128)(2,1)S(1)}, u32[]{:S(2)}, u32[]{:S(2)}) collective-permute-start(bf16[40,896]{1,0:T(8,128)(2,1)S(1)} %get-tuple-element.59), channel_id=1, source_target_pairs={{0,4},{1,5},{2,6},{3,7},{4,0},{5,1},{6,2},{7,3},{8,12},{9,13},{10,... | collective-permute-start | bytes 215048 | tf_op jit(solution)/shard_map/ppermute | solution.py:451
  29.5 6.0 %collective-permute-start.13 = (bf16[40,896]{1,0:T(8,128)(2,1)S(1)}, bf16[40,896]{1,0:T(8,128)(2,1)S(1)}, u32[]{:S(2)}, u32[]{:S(2)}) collective-permute-start(bf16[40,896]{1,0:T(8,128)(2,1)S(1)} %get-tuple-element.60), channel_id=1, source_target_pairs={{0,6},{1,7},{2,4},{3,5},{4,2},{5,3},{6,0},{7,1},{8,14},{9,15},{10,... | collective-permute-start | bytes 215048 | tf_op jit(solution)/shard_map/ppermute | solution.py:451
  31.8 6.3 %collective-permute-start.17 = (bf16[40,896]{1,0:T(8,128)(2,1)S(1)}, bf16[40,896]{1,0:T(8,128)(2,1)S(1)}, u32[]{:S(2)}, u32[]{:S(2)}) collective-permute-start(bf16[40,896]{1,0:T(8,128)(2,1)S(1)} %sum_blocks.1), channel_id=1, source_target_pairs={{0,8},{1,9},{2,10},{3,11},{4,12},{5,13},{6,14},{7,15},{8,0},{9,1},... | collective-permute-start | bytes 215048 | tf_op jit(solution)/shard_map/ppermute | solution.py:447

commit v12 on v11

--- a/solution.py
+++ b/solution.py
@@ -426,7 +426,7 @@
             block, table = lax.optimization_barrier((block, table))
             weights = blend_weights(table, teams)
         crowds.append(gather(block))
-    own, crowds, weights = lax.optimization_barrier((own, crowds, weights))
+    own, weights, crowds[-1][-1] = lax.optimization_barrier((own, weights, crowds[-1][-1]))
     own = join(own)
     first = unpack(own, lax.ppermute(own, "expert", other_core))
     pieces = []
@@ -439,13 +439,13 @@
     others = []
     for k in range(1, teams):
         parts = add_cores(kept, taken[k], k, chips)
-        parts, taken[0] = lax.optimization_barrier((parts, taken[0]))
+        parts, later = lax.optimization_barrier((parts, kept))
         team = [parts[0]]
         for m in range(1, chips):
             team.append(lax.ppermute(parts[m], "expert", other_chip[m]))
         pairs = [(i, (i - k * SPLIT) % devices) for i in range(devices)]
         others.append(lax.ppermute(sum_blocks(team), "expert", pairs))
-    parts = add_cores(kept, taken[0], 0, chips)
+    parts = add_cores(later, taken[0], 0, chips)
     own = [parts[0]]
     for m in range(1, chips):
         own.append(lax.ppermute(parts[m], "expert", other_chip[m]))

time: 39.5 us -> 40.2 us (1.018)
  waiting for transfers between devices: 7.71 us -> 8.8 us
  starting transfers between devices: 23.4 us -> 22.9 us
    ppermute x1, starting transfers between devices: 3.19 us -> 2.19 us  [body(): others.append(lax.ppermute(sum_blocks(team), 'expert', pairs))]
    ppermute x3, waiting for transfers between devices: 0.54 us -> 1.49 us  [body(): own.append(lax.ppermute(parts[m], 'expert', other_chip[m]))]
    ppermute x6, starting transfers between devices: 7.81 us -> 8.34 us  [gather(): lax.ppermute(block, 'expert', other_chip[m])]
  transfers between devices with their start and end apart: 18 -> 18, of which waited for: 11 -> 7; matrix products, arithmetic and copies ran while one was open for 0% -> 0% of each run, Pallas kernels for 4% -> 4%
where the time goes in v12:
time: 40.2 us; the launch traced here: 40 us
  starting transfers between devices  22.9 us (57%)
  waiting for transfers between devices  8.8 us (22%)
  Pallas kernels  7.43 us (18%)
  local copies, waits for them, and re-layouts  0.71 us (2%)
    ppermute x6, starting transfers between devices, gather(): lax.ppermute(block, 'expert', other_chip[m])  8.34 us
    ppermute x1, starting transfers between devices, body(): block = lax.ppermute(packed[k], 'expert', pairs)  4.1 us
    ppermute x3, starting transfers between devices, body(): own.append(lax.ppermute(parts[m], 'expert', other_chip[m]))  3.55 us
    ppermute x3, starting transfers between devices, body(): team.append(lax.ppermute(parts[m], 'expert', other_chip[m]))  3.55 us
    ppermute x6, waiting for transfers between devices, gather(): lax.ppermute(block, 'expert', other_chip[m])  2.59 us
    ppermute x1, waiting for transfers between devices, body(): others.append(lax.ppermute(sum_blocks(team), 'expert', pairs))  2.39 us
    pallas_call x1, Pallas kernels, expert_half(): pl.pallas_call(functools.partial(expert_kernel, teams), out_shape=[jax.Sh...  2.33 us
    pallas_call x1, Pallas kernels, pack_rows(): pl.pallas_call(functools.partial(pack_kernel, teams), out_shape=[block] *...  2.28 us
  transfers between devices with their start and end apart: 18, of which 7 were waited for; matrix products, arithmetic and copies ran while one was open for 0% of the time, Pallas kernels for 4%

profile of v12, /device:TPU:0, one launch (start us, length us, event | category | flops | bytes accessed | tf_op | source)
XLA Modules:
  0.0 40.0 jit_solution(6012246279557269930)
XLA Ops:
  0.0 2.3 %pack_rows.1 = (bf16[40,896]{1,0:T(8,128)(2,1)}, bf16[40,896]{1,0:T(8,128)(2,1)}, f32[16,64]{1,0:T(8,128)}) custom-call(s32[8,64]{1,0:T(8,128)} %bitcast.2, f32[8,64]{1,0:T(8,128)} %bitcast.3, bf16[64,7168]{1,0:T(8,128)(2,1)} %tokens_hbm.1), custom_call_target="tpu_custom_call" | custom-call | tf_op jit(solution)/shard_map/pack_rows/pallas_call | solution.py:110
  2.3 4.1 %collective-permute-start.3 = (bf16[40,896]{1,0:T(8,128)(2,1)}, bf16[40,896]{1,0:T(8,128)(2,1)S(1)}, u32[]{:S(2)}, u32[]{:S(2)}) collective-permute-start(bf16[40,896]{1,0:T(8,128)(2,1)} %get-tuple-element.33), channel_id=1, source_target_pairs={{0,8},{1,9},{2,10},{3,11},{4,12},{5,13},{6,14},{7,15},{8,0},{9,1},... | collective-permute-start | bytes 215048 | tf_op jit(solution)/shard_map/ppermute | solution.py:424
  6.4 2.5 %collective-permute-start.2 = (bf16[40,896]{1,0:T(8,128)(2,1)}, bf16[40,896]{1,0:T(8,128)(2,1)S(1)}, u32[]{:S(2)}, u32[]{:S(2)}) collective-permute-start(bf16[40,896]{1,0:T(8,128)(2,1)} %get-tuple-element.38.refs_0_), channel_id=1, source_target_pairs={{0,6},{1,7},{2,4},{3,5},{4,2},{5,3},{6,0},{7,1},{8,14},{9,15},{10,... | collective-permute-start | bytes 215048 | tf_op jit(solution)/shard_map/ppermute | solution.py:418
  8.9 0.4 %collective-permute-start.1 = (bf16[40,896]{1,0:T(8,128)(2,1)}, bf16[40,896]{1,0:T(8,128)(2,1)S(1)}, u32[]{:S(2)}, u32[]{:S(2)}) collective-permute-start(bf16[40,896]{1,0:T(8,128)(2,1)} %get-tuple-element.38.refs_0_), channel_id=1, source_target_pairs={{0,4},{1,5},{2,6},{3,7},{4,0},{5,1},{6,2},{7,3},{8,12},{9,13},{10,... | collective-permute-start | bytes 215048 | tf_op jit(solution)/shard_map/ppermute | solution.py:418
  9.4 0.5 %collective-permute-start = (bf16[40,896]{1,0:T(8,128)(2,1)}, bf16[40,896]{1,0:T(8,128)(2,1)S(1)}, u32[]{:S(2)}, u32[]{:S(2)}) collective-permute-start(bf16[40,896]{1,0:T(8,128)(2,1)} %get-tuple-element.38.refs_0_), channel_id=1, source_target_pairs={{0,2},{1,3},{2,0},{3,1},{4,6},{5,7},{6,4},{7,5},{8,10},{9,11},{10,... | collective-permute-start | bytes 215048 | tf_op jit(solution)/shard_map/ppermute | solution.py:418
  9.9 0.0 collective-permute-done.3.refs_0_
  9.9 1.7 %collective-permute-start.7 = (bf16[40,896]{1,0:T(8,128)(2,1)S(1)}, bf16[40,896]{1,0:T(8,128)(2,1)S(1)}, u32[]{:S(2)}, u32[]{:S(2)}) collective-permute-start(bf16[40,896]{1,0:T(8,128)(2,1)S(1)} %collective-permute-done.3.refs_0_), channel_id=1, source_target_pairs={{0,4},{1,5},{2,6},{3,7},{4,0},{5,1},{6,2},{7,3},{8,12},{9,13},{10,... | collective-permute-start | bytes 215048 | tf_op jit(solution)/shard_map/ppermute | solution.py:418
  11.6 1.6 %collective-permute-start.6 = (bf16[40,896]{1,0:T(8,128)(2,1)S(1)}, bf16[40,896]{1,0:T(8,128)(2,1)S(1)}, u32[]{:S(2)}, u32[]{:S(2)}) collective-permute-start(bf16[40,896]{1,0:T(8,128)(2,1)S(1)} %collective-permute-done.3.refs_0_), channel_id=1, source_target_pairs={{0,2},{1,3},{2,0},{3,1},{4,6},{5,7},{6,4},{7,5},{8,10},{9,11},{10,... | collective-permute-start | bytes 215048 | tf_op jit(solution)/shard_map/ppermute | solution.py:418
  13.1 0.0 collective-permute-done.2.refs_3_
  13.1 1.6 %collective-permute-start.4 = (bf16[40,896]{1,0:T(8,128)(2,1)S(1)}, bf16[40,896]{1,0:T(8,128)(2,1)S(1)}, u32[]{:S(2)}, u32[]{:S(2)}) collective-permute-start(bf16[40,896]{1,0:T(8,128)(2,1)S(1)} %collective-permute-done.3.refs_0_), channel_id=1, source_target_pairs={{0,6},{1,7},{2,4},{3,5},{4,2},{5,3},{6,0},{7,1},{8,14},{9,15},{10,... | collective-permute-start | bytes 215048 | tf_op jit(solution)/shard_map/ppermute | solution.py:418
  14.8 0.7 %copy-done.4 = f32[16,64]{1,0:T(8,128)S(1)} copy-done((f32[16,64]{1,0:T(8,128)S(1)}, f32[16,64]{1,0:T(8,128)}, u32[]{:S(2)}) %copy-start.4) | copy-done | bytes 4120
  15.5 0.3 blend_weights.1.weight_ref
  15.8 0.0 collective-permute-done.1.refs_2_
  15.8 0.0 collective-permute-done.refs_1_
  15.8 2.6 %collective-permute-done.4.refs_3_ = bf16[40,896]{1,0:T(8,128)(2,1)S(1)} collective-permute-done((bf16[40,896]{1,0:T(8,128)(2,1)S(1)}, bf16[40,896]{1,0:T(8,128)(2,1)S(1)}, u32[]{:S(2)}, u32[]{:S(2)}) %collective-permute-start.4) | collective-permute-done | bytes 71712 | tf_op jit(solution)/shard_map/ppermute | solution.py:418
  18.4 0.0 copy-done.3
  18.4 0.1 collective-permute-start.5
  18.5 0.0 collective-permute-done.7.refs_2_
  18.5 0.0 collective-permute-done.6.refs_1_
  18.5 0.5 %collective-permute-start.8 = (bf16[160,896]{1,0:T(8,128)(2,1)S(1)}, bf16[160,896]{1,0:T(8,128)(2,1)S(1)}, u32[]{:S(2)}, u32[]{:S(2)}) collective-permute-start(bf16[160,896]{1,0:T(8,128)(2,1)S(1)} %join.3.refs_0_), channel_id=1, source_target_pairs={{0,1},{1,0},{2,3},{3,2},{4,5},{5,4},{6,7},{7,6},{8,9},{9,8},{10,11... | collective-permute-start | bytes 860168 | tf_op jit(solution)/shard_map/ppermute | solution.py:435
  19.1 1.0 %collective-permute-done.5.other_ref = bf16[160,896]{1,0:T(8,128)(2,1)S(1)} collective-permute-done((bf16[160,896]{1,0:T(8,128)(2,1)S(1)}, bf16[160,896]{1,0:T(8,128)(2,1)S(1)}, u32[]{:S(2)}, u32[]{:S(2)}) %collective-permute-start.5) | collective-permute-done | bytes 286752 | tf_op jit(solution)/shard_map/ppermute | solution.py:431
  20.0 0.3 unpack.1.first_ref
  20.4 0.1 collective-permute-done.8.refs_1_
  20.4 0.0 copy-done
  20.4 0.0 copy-done.2
  20.5 2.3 %expert_half.1 = (bf16[160,896]{1,0:T(8,128)(2,1)S(1)}, bf16[160,896]{1,0:T(8,128)(2,1)S(1)}, bf16[40,256]{1,0:T(8,128)(2,1)S(1)}) custom-call(f32[40,7168]{1,0:T(8,128)S(1)} %unpack.1.first_ref, bf16[160,896]{1,0:T(8,128)(2,1)S(1)} %join.3.refs_0_, bf16[160,896]{1,0:T(8,128)(2,1)S(1)} %collective-permute-done.8.refs_1_, bf16[7168,256]{1,0:T(8,128)(2,1)S(1)} %copy-done.1, ...), custom_call_target="tpu_custom_call" | custom-call | flops 734003200 | bytes 11010048 | tf_op jit(solution)/shard_map/expert_half/pallas_call | solution.py:273
  22.8 0.3 collective-permute-start.9
  23.1 0.3 collective-permute-start.10
  23.4 0.7 %kept_half.1.kept_ref = f32[320,896]{1,0:T(8,128)S(1)} custom-call(bf16[40,256]{1,0:T(8,128)(2,1)S(1)} %get-tuple-element.43.hidden_ref, bf16[256,7168]{1,0:T(8,128)(2,1)S(1)} %copy-done), custom_call_target="tpu_custom_call" | custom-call | flops 146800640 | bytes 3670016 | tf_op jit(solution)/shard_map/kept_half/pallas_call | solution.py:303
  24.1 0.3 collective-permute-done.9.taken_ref
  24.4 0.1 add_cores.2
  24.5 1.1 %collective-permute-start.14 = (bf16[40,896]{1,0:T(8,128)(2,1)S(1)}, bf16[40,896]{1,0:T(8,128)(2,1)S(1)}, u32[]{:S(2)}, u32[]{:S(2)}) collective-permute-start(bf16[40,896]{1,0:T(8,128)(2,1)S(1)} %get-tuple-element.56), channel_id=1, source_target_pairs={{0,2},{1,3},{2,0},{3,1},{4,6},{5,7},{6,4},{7,5},{8,10},{9,11},{10,... | collective-permute-start | bytes 215048 | tf_op jit(solution)/shard_map/ppermute | solution.py:445
  25.6 1.2 %collective-permute-start.15 = (bf16[40,896]{1,0:T(8,128)(2,1)S(1)}, bf16[40,896]{1,0:T(8,128)(2,1)S(1)}, u32[]{:S(2)}, u32[]{:S(2)}) collective-permute-start(bf16[40,896]{1,0:T(8,128)(2,1)S(1)} %get-tuple-element.57), channel_id=1, source_target_pairs={{0,4},{1,5},{2,6},{3,7},{4,0},{5,1},{6,2},{7,3},{8,12},{9,13},{10,... | collective-permute-start | bytes 215048 | tf_op jit(solution)/shard_map/ppermute | solution.py:445
  26.7 1.3 %collective-permute-start.16 = (bf16[40,896]{1,0:T(8,128)(2,1)S(1)}, bf16[40,896]{1,0:T(8,128)(2,1)S(1)}, u32[]{:S(2)}, u32[]{:S(2)}) collective-permute-start(bf16[40,896]{1,0:T(8,128)(2,1)S(1)} %get-tuple-element.58), channel_id=1, source_target_pairs={{0,6},{1,7},{2,4},{3,5},{4,2},{5,3},{6,0},{7,1},{8,14},{9,15},{10,... | collective-permute-start | bytes 215048 | tf_op jit(solution)/shard_map/ppermute | solution.py:445
  28.1 0.0 collective-permute-done.10.taken_ref
  28.1 0.1 add_cores.3
  28.1 1.1 %collective-permute-start.11 = (bf16[40,896]{1,0:T(8,128)(2,1)S(1)}, bf16[40,896]{1,0:T(8,128)(2,1)S(1)}, u32[]{:S(2)}, u32[]{:S(2)}) collective-permute-start(bf16[40,896]{1,0:T(8,128)(2,1)S(1)} %get-tuple-element.52), channel_id=1, source_target_pairs={{0,2},{1,3},{2,0},{3,1},{4,6},{5,7},{6,4},{7,5},{8,10},{9,11},{10,... | collective-permute-start | bytes 215048 | tf_op jit(solution)/shard_map/ppermute | solution.py:451
  29.2 1.2 %collective-permute-start.12 = (bf16[40,896]{1,0:T(8,128)(2,1)S(1)}, bf16[40,896]{1,0:T(8,128)(2,1)S(1)}, u32[]{:S(2)}, u32[]{:S(2)}) collective-permute-start(bf16[40,896]{1,0:T(8,128)(2,1)S(1)} %get-tuple-element.53), channel_id=1, source_target_pairs={{0,4},{1,5},{2,6},{3,7},{4,0},{5,1},{6,2},{7,3},{8,12},{9,13},{10,... | collective-permute-start | bytes 215048 | tf_op jit(solution)/shard_map/ppermute | solution.py:451
  30.4 0.0 collective-permute-done.14.refs_1_
  30.4 1.3 %collective-permute-start.13 = (bf16[40,896]{1,0:T(8,128)(2,1)S(1)}, bf16[40,896]{1,0:T(8,128)(2,1)S(1)}, u32[]{:S(2)}, u32[]{:S(2)}) collective-permute-start(bf16[40,896]{1,0:T(8,128)(2,1)S(1)} %get-tuple-element.54), channel_id=1, source_target_pairs={{0,6},{1,7},{2,4},{3,5},{4,2},{5,3},{6,0},{7,1},{8,14},{9,15},{10,... | collective-permute-start | bytes 215048 | tf_op jit(solution)/shard_map/ppermute | solution.py:451
  31.7 0.0 collective-permute-done.15.refs_2_
  31.7 1.0 %collective-permute-done.16.refs_3_ = bf16[40,896]{1,0:T(8,128)(2,1)S(1)} collective-permute-done((bf16[40,896]{1,0:T(8,128)(2,1)S(1)}, bf16[40,896]{1,0:T(8,128)(2,1)S(1)}, u32[]{:S(2)}, u32[]{:S(2)}) %collective-permute-start.16) | collective-permute-done | bytes 71712 | tf_op jit(solution)/shard_map/ppermute | solution.py:445
  32.7 2.2 %collective-permute-start.17 = (bf16[40,896]{1,0:T(8,128)(2,1)S(1)}, bf16[40,896]{1,0:T(8,128)(2,1)S(1)}, u32[]{:S(2)}, u32[]{:S(2)}) collective-permute-start(bf16[40,896]{1,0:T(8,128)(2,1)S(1)} %sum_blocks.1), channel_id=1, source_target_pairs={{0,8},{1,9},{2,10},{3,11},{4,12},{5,13},{6,14},{7,15},{8,0},{9,1},... | collective-permute-start | bytes 215048 | tf_op jit(solution)/shard_map/ppermute | solution.py:447
  34.9 0.0 collective-permute-done.11.refs_1_
  34.9 0.0 collective-permute-done.12.refs_2_
  34.9 1.5 %collective-permute-done.13.refs_3_ = bf16[40,896]{1,0:T(8,128)(2,1)S(1)} collective-permute-done((bf16[40,896]{1,0:T(8,128)(2,1)S(1)}, bf16[40,896]{1,0:T(8,128)(2,1)S(1)}, u32[]{:S(2)}, u32[]{:S(2)}) %collective-permute-start.13) | collective-permute-done | bytes 71712 | tf_op jit(solution)/shard_map/ppermute | solution.py:451
  36.4 2.4 %collective-permute-done.17.refs_4_ = bf16[40,896]{1,0:T(8,128)(2,1)S(1)} collective-permute-done((bf16[40,896]{1,0:T(8,128)(2,1)S(1)}, bf16[40,896]{1,0:T(8,128)(2,1)S(1)}, u32[]{:S(2)}, u32[]{:S(2)}) %collective-permute-start.17) | collective-permute-done | bytes 71712 | tf_op jit(solution)/shard_map/ppermute | solution.py:447
  38.7 1.2 %blend.1 = bf16[64,7168]{1,0:T(8,128)(2,1)} custom-call(bf16[512,200]{1,0:T(8,128)(2,1)S(1)} %blend_weights.1.weight_ref, f32[40,896]{1,0:T(8,128)S(1)} %get-tuple-element.51.refs_0_, bf16[40,896]{1,0:T(8,128)(2,1)S(1)} %collective-permute-done.11.refs_1_, bf16[40,896]{1,0:T(8,128)(2,1)S(1)} %collective-permute-done.12.refs_2_, ...), custom_call_target="tpu_custom_call" | custom-call | tf_op jit(solution)/shard_map/blend/pallas_call | solution.py:396
  (9 shorter events, 0.1 us)
Async XLA Ops:
  2.3 7.6 %collective-permute-start.3 = (bf16[40,896]{1,0:T(8,128)(2,1)}, bf16[40,896]{1,0:T(8,128)(2,1)S(1)}, u32[]{:S(2)}, u32[]{:S(2)}) collective-permute-start(bf16[40,896]{1,0:T(8,128)(2,1)} %get-tuple-element.33), channel_id=1, source_target_pairs={{0,8},{1,9},{2,10},{3,11},{4,12},{5,13},{6,14},{7,15},{8,0},{9,1},... | collective-permute-start | bytes 215048 | tf_op jit(solution)/shard_map/ppermute | solution.py:424
  6.4 6.7 %collective-permute-start.2 = (bf16[40,896]{1,0:T(8,128)(2,1)}, bf16[40,896]{1,0:T(8,128)(2,1)S(1)}, u32[]{:S(2)}, u32[]{:S(2)}) collective-permute-start(bf16[40,896]{1,0:T(8,128)(2,1)} %get-tuple-element.38.refs_0_), channel_id=1, source_target_pairs={{0,6},{1,7},{2,4},{3,5},{4,2},{5,3},{6,0},{7,1},{8,14},{9,15},{10,... | collective-permute-start | bytes 215048 | tf_op jit(solution)/shard_map/ppermute | solution.py:418
  8.9 6.8 %collective-permute-start.1 = (bf16[40,896]{1,0:T(8,128)(2,1)}, bf16[40,896]{1,0:T(8,128)(2,1)S(1)}, u32[]{:S(2)}, u32[]{:S(2)}) collective-permute-start(bf16[40,896]{1,0:T(8,128)(2,1)} %get-tuple-element.38.refs_0_), channel_id=1, source_target_pairs={{0,4},{1,5},{2,6},{3,7},{4,0},{5,1},{6,2},{7,3},{8,12},{9,13},{10,... | collective-permute-start | bytes 215048 | tf_op jit(solution)/shard_map/ppermute | solution.py:418
  9.4 6.4 %collective-permute-start = (bf16[40,896]{1,0:T(8,128)(2,1)}, bf16[40,896]{1,0:T(8,128)(2,1)S(1)}, u32[]{:S(2)}, u32[]{:S(2)}) collective-permute-start(bf16[40,896]{1,0:T(8,128)(2,1)} %get-tuple-element.38.refs_0_), channel_id=1, source_target_pairs={{0,2},{1,3},{2,0},{3,1},{4,6},{5,7},{6,4},{7,5},{8,10},{9,11},{10,... | collective-permute-start | bytes 215048 | tf_op jit(solution)/shard_map/ppermute | solution.py:418
  9.9 8.5 %copy-start.3 = (bf16[40,896]{1,0:T(8,128)(2,1)S(1)}, bf16[40,896]{1,0:T(8,128)(2,1)}, u32[]{:S(2)}) copy-start(bf16[40,896]{1,0:T(8,128)(2,1)} %get-tuple-element.38.refs_0_) | copy-start | bytes 215044
  9.9 8.6 %collective-permute-start.7 = (bf16[40,896]{1,0:T(8,128)(2,1)S(1)}, bf16[40,896]{1,0:T(8,128)(2,1)S(1)}, u32[]{:S(2)}, u32[]{:S(2)}) collective-permute-start(bf16[40,896]{1,0:T(8,128)(2,1)S(1)} %collective-permute-done.3.refs_0_), channel_id=1, source_target_pairs={{0,4},{1,5},{2,6},{3,7},{4,0},{5,1},{6,2},{7,3},{8,12},{9,13},{10,... | collective-permute-start | bytes 215048 | tf_op jit(solution)/shard_map/ppermute | solution.py:418
  11.6 6.9 %collective-permute-start.6 = (bf16[40,896]{1,0:T(8,128)(2,1)S(1)}, bf16[40,896]{1,0:T(8,128)(2,1)S(1)}, u32[]{:S(2)}, u32[]{:S(2)}) collective-permute-start(bf16[40,896]{1,0:T(8,128)(2,1)S(1)} %collective-permute-done.3.refs_0_), channel_id=1, source_target_pairs={{0,2},{1,3},{2,0},{3,1},{4,6},{5,7},{6,4},{7,5},{8,10},{9,11},{10,... | collective-permute-start | bytes 215048 | tf_op jit(solution)/shard_map/ppermute | solution.py:418
  13.1 5.2 %collective-permute-start.4 = (bf16[40,896]{1,0:T(8,128)(2,1)S(1)}, bf16[40,896]{1,0:T(8,128)(2,1)S(1)}, u32[]{:S(2)}, u32[]{:S(2)}) collective-permute-start(bf16[40,896]{1,0:T(8,128)(2,1)S(1)} %collective-permute-done.3.refs_0_), channel_id=1, source_target_pairs={{0,6},{1,7},{2,4},{3,5},{4,2},{5,3},{6,0},{7,1},{8,14},{9,15},{10,... | collective-permute-start | bytes 215048 | tf_op jit(solution)/shard_map/ppermute | solution.py:418
  14.7 0.7 %copy-start.4 = (f32[16,64]{1,0:T(8,128)S(1)}, f32[16,64]{1,0:T(8,128)}, u32[]{:S(2)}) copy-start(f32[16,64]{1,0:T(8,128)} %get-tuple-element.35.table_ref) | copy-start | bytes 12292
  15.4 5.0 %copy-start = (bf16[256,7168]{1,0:T(8,128)(2,1)S(1)}, bf16[256,7168]{1,0:T(8,128)(2,1)}, u32[]{:S(2)}) copy-start(bf16[256,7168]{1,0:T(8,128)(2,1)} %down_ref.1) | copy-start | bytes 11010052
  15.4 5.0 %copy-start.1 = (bf16[7168,256]{1,0:T(8,128)(2,1)S(1)}, bf16[7168,256]{1,0:T(8,128)(2,1)}, u32[]{:S(2)}) copy-start(bf16[7168,256]{1,0:T(8,128)(2,1)} %refs_2_.1) | copy-start | bytes 11010052
  15.4 5.0 %copy-start.2 = (bf16[7168,256]{1,0:T(8,128)(2,1)S(1)}, bf16[7168,256]{1,0:T(8,128)(2,1)}, u32[]{:S(2)}) copy-start(bf16[7168,256]{1,0:T(8,128)(2,1)} %refs_3_.1) | copy-start | bytes 11010052
  18.4 1.6 %collective-permute-start.5 = (bf16[160,896]{1,0:T(8,128)(2,1)S(1)}, bf16[160,896]{1,0:T(8,128)(2,1)S(1)}, u32[]{:S(2)}, u32[]{:S(2)}) collective-permute-start(bf16[160,896]{1,0:T(8,128)(2,1)S(1)} %join.2.own_ref), channel_id=1, source_target_pairs={{0,1},{1,0},{2,3},{3,2},{4,5},{5,4},{6,7},{7,6},{8,9},{9,8},{10,11... | collective-permute-start | bytes 860168 | tf_op jit(solution)/shard_map/ppermute | solution.py:431
  18.5 1.9 %collective-permute-start.8 = (bf16[160,896]{1,0:T(8,128)(2,1)S(1)}, bf16[160,896]{1,0:T(8,128)(2,1)S(1)}, u32[]{:S(2)}, u32[]{:S(2)}) collective-permute-start(bf16[160,896]{1,0:T(8,128)(2,1)S(1)} %join.3.refs_0_), channel_id=1, source_target_pairs={{0,1},{1,0},{2,3},{3,2},{4,5},{5,4},{6,7},{7,6},{8,9},{9,8},{10,11... | collective-permute-start | bytes 860168 | tf_op jit(solution)/shard_map/ppermute | solution.py:435
  22.8 1.6 %collective-permute-start.9 = (bf16[160,896]{1,0:T(8,128)(2,1)S(1)}, bf16[160,896]{1,0:T(8,128)(2,1)S(1)}, u32[]{:S(2)}, u32[]{:S(2)}) collective-permute-start(bf16[160,896]{1,0:T(8,128)(2,1)S(1)} %get-tuple-element.44), channel_id=1, source_target_pairs={{0,1},{1,0},{2,3},{3,2},{4,5},{5,4},{6,7},{7,6},{8,9},{9,8},{10,11... | collective-permute-start | bytes 860168 | tf_op jit(solution)/shard_map/ppermute | solution.py:437
  23.1 5.0 %collective-permute-start.10 = (bf16[160,896]{1,0:T(8,128)(2,1)S(1)}, bf16[160,896]{1,0:T(8,128)(2,1)S(1)}, u32[]{:S(2)}, u32[]{:S(2)}) collective-permute-start(bf16[160,896]{1,0:T(8,128)(2,1)S(1)} %get-tuple-element.50), channel_id=1, source_target_pairs={{0,1},{1,0},{2,3},{3,2},{4,5},{5,4},{6,7},{7,6},{8,9},{9,8},{10,11... | collective-permute-start | bytes 860168 | tf_op jit(solution)/shard_map/ppermute | solution.py:437
  24.5 5.9 %collective-permute-start.14 = (bf16[40,896]{1,0:T(8,128)(2,1)S(1)}, bf16[40,896]{1,0:T(8,128)(2,1)S(1)}, u32[]{:S(2)}, u32[]{:S(2)}) collective-permute-start(bf16[40,896]{1,0:T(8,128)(2,1)S(1)} %get-tuple-element.56), channel_id=1, source_target_pairs={{0,2},{1,3},{2,0},{3,1},{4,6},{5,7},{6,4},{7,5},{8,10},{9,11},{10,... | collective-permute-start | bytes 215048 | tf_op jit(solution)/shard_map/ppermute | solution.py:445
  25.6 6.1 %collective-permute-start.15 = (bf16[40,896]{1,0:T(8,128)(2,1)S(1)}, bf16[40,896]{1,0:T(8,128)(2,1)S(1)}, u32[]{:S(2)}, u32[]{:S(2)}) collective-permute-start(bf16[40,896]{1,0:T(8,128)(2,1)S(1)} %get-tuple-element.57), channel_id=1, source_target_pairs={{0,4},{1,5},{2,6},{3,7},{4,0},{5,1},{6,2},{7,3},{8,12},{9,13},{10,... | collective-permute-start | bytes 215048 | tf_op jit(solution)/shard_map/ppermute | solution.py:445
  26.7 5.9 %collective-permute-start.16 = (bf16[40,896]{1,0:T(8,128)(2,1)S(1)}, bf16[40,896]{1,0:T(8,128)(2,1)S(1)}, u32[]{:S(2)}, u32[]{:S(2)}) collective-permute-start(bf16[40,896]{1,0:T(8,128)(2,1)S(1)} %get-tuple-element.58), channel_id=1, source_target_pairs={{0,6},{1,7},{2,4},{3,5},{4,2},{5,3},{6,0},{7,1},{8,14},{9,15},{10,... | collective-permute-start | bytes 215048 | tf_op jit(solution)/shard_map/ppermute | solution.py:445
  28.1 6.8 %collective-permute-start.11 = (bf16[40,896]{1,0:T(8,128)(2,1)S(1)}, bf16[40,896]{1,0:T(8,128)(2,1)S(1)}, u32[]{:S(2)}, u32[]{:S(2)}) collective-permute-start(bf16[40,896]{1,0:T(8,128)(2,1)S(1)} %get-tuple-element.52), channel_id=1, source_target_pairs={{0,2},{1,3},{2,0},{3,1},{4,6},{5,7},{6,4},{7,5},{8,10},{9,11},{10,... | collective-permute-start | bytes 215048 | tf_op jit(solution)/shard_map/ppermute | solution.py:451
  29.2 5.7 %collective-permute-start.12 = (bf16[40,896]{1,0:T(8,128)(2,1)S(1)}, bf16[40,896]{1,0:T(8,128)(2,1)S(1)}, u32[]{:S(2)}, u32[]{:S(2)}) collective-permute-start(bf16[40,896]{1,0:T(8,128)(2,1)S(1)} %get-tuple-element.53), channel_id=1, source_target_pairs={{0,4},{1,5},{2,6},{3,7},{4,0},{5,1},{6,2},{7,3},{8,12},{9,13},{10,... | collective-permute-start | bytes 215048 | tf_op jit(solution)/shard_map/ppermute | solution.py:451
  30.4 6.0 %collective-permute-start.13 = (bf16[40,896]{1,0:T(8,128)(2,1)S(1)}, bf16[40,896]{1,0:T(8,128)(2,1)S(1)}, u32[]{:S(2)}, u32[]{:S(2)}) collective-permute-start(bf16[40,896]{1,0:T(8,128)(2,1)S(1)} %get-tuple-element.54), channel_id=1, source_target_pairs={{0,6},{1,7},{2,4},{3,5},{4,2},{5,3},{6,0},{7,1},{8,14},{9,15},{10,... | collective-permute-start | bytes 215048 | tf_op jit(solution)/shard_map/ppermute | solution.py:451
  32.7 6.1 %collective-permute-start.17 = (bf16[40,896]{1,0:T(8,128)(2,1)S(1)}, bf16[40,896]{1,0:T(8,128)(2,1)S(1)}, u32[]{:S(2)}, u32[]{:S(2)}) collective-permute-start(bf16[40,896]{1,0:T(8,128)(2,1)S(1)} %sum_blocks.1), channel_id=1, source_target_pairs={{0,8},{1,9},{2,10},{3,11},{4,12},{5,13},{6,14},{7,15},{8,0},{9,1},... | collective-permute-start | bytes 215048 | tf_op jit(solution)/shard_map/ppermute | solution.py:447

commit v13 on v12

--- a/solution.py
+++ b/solution.py
@@ -426,7 +426,7 @@
             block, table = lax.optimization_barrier((block, table))
             weights = blend_weights(table, teams)
         crowds.append(gather(block))
-    own, weights, crowds[-1][-1] = lax.optimization_barrier((own, weights, crowds[-1][-1]))
+    own, crowds, weights = lax.optimization_barrier((own, crowds, weights))
     own = join(own)
     first = unpack(own, lax.ppermute(own, "expert", other_core))
     pieces = []
@@ -441,13 +441,13 @@
         parts = add_cores(kept, taken[k], k, chips)
         parts, later = lax.optimization_barrier((parts, kept))
         team = [parts[0]]
-        for m in range(1, chips):
+        for m in reversed(range(1, chips)):
             team.append(lax.ppermute(parts[m], "expert", other_chip[m]))
         pairs = [(i, (i - k * SPLIT) % devices) for i in range(devices)]
         others.append(lax.ppermute(sum_blocks(team), "expert", pairs))
     parts = add_cores(later, taken[0], 0, chips)
     own = [parts[0]]
-    for m in range(1, chips):
+    for m in reversed(range(1, chips)):
         own.append(lax.ppermute(parts[m], "expert", other_chip[m]))
     return blend(weights, own, others, tokens.shape[0])
 

time: 40.2 us -> 38.9 us (0.968)
  waiting for transfers between devices: 8.8 us -> 7.89 us
    ppermute x3, waiting for transfers between devices: 0.97 us -> 0.01 us  [body(): team.append(lax.ppermute(parts[m], 'expert', other_chip[m]))]
    ppermute x1, waiting for transfers between devices: 2.39 us -> 3.24 us  [body(): others.append(lax.ppermute(sum_blocks(team), 'expert', pairs))]
    ppermute x3, waiting for transfers between devices: 1.49 us -> 0.91 us  [body(): own.append(lax.ppermute(parts[m], 'expert', other_chip[m]))]
    ppermute x6, starting transfers between devices: 8.34 us -> 7.81 us  [gather(): lax.ppermute(block, 'expert', other_chip[m])]
  transfers between devices with their start and end apart: 18 -> 18, of which waited for: 7 -> 9; matrix products, arithmetic and copies ran while one was open for 0% -> 0% of each run, Pallas kernels for 4% -> 4%
where the time goes in v13:
time: 38.9 us; the launch traced here: 38.7 us
  starting transfers between devices  22.5 us (58%)
  waiting for transfers between devices  7.89 us (20%)
  Pallas kernels  7.43 us (19%)
  local copies, waits for them, and re-layouts  0.71 us (2%)
    ppermute x6, starting transfers between devices, gather(): lax.ppermute(block, 'expert', other_chip[m])  7.81 us
    ppermute x1, starting transfers between devices, body(): block = lax.ppermute(packed[k], 'expert', pairs)  4.1 us
    ppermute x3, starting transfers between devices, body(): own.append(lax.ppermute(parts[m], 'expert', other_chip[m]))  3.55 us
    ppermute x3, starting transfers between devices, body(): team.append(lax.ppermute(parts[m], 'expert', other_chip[m]))  3.55 us
    ppermute x1, waiting for transfers between devices, body(): others.append(lax.ppermute(sum_blocks(team), 'expert', pairs))  3.24 us
    ppermute x6, waiting for transfers between devices, gather(): lax.ppermute(block, 'expert', other_chip[m])  2.35 us
    pallas_call x1, Pallas kernels, expert_half(): pl.pallas_call(functools.partial(expert_kernel, teams), out_shape=[jax.Sh...  2.33 us
    ppermute x1, starting transfers between devices, body(): others.append(lax.ppermute(sum_blocks(team), 'expert', pairs))  2.3 us
  transfers between devices with their start and end apart: 18, of which 9 were waited for; matrix products, arithmetic and copies ran while one was open for 0% of the time, Pallas kernels for 4%

profile of v13, /device:TPU:0, one launch (start us, length us, event | category | flops | bytes accessed | tf_op | source)
XLA Modules:
  0.0 38.7 jit_solution(1132282887040064124)
XLA Ops:
  0.0 2.3 %pack_rows.1 = (bf16[40,896]{1,0:T(8,128)(2,1)}, bf16[40,896]{1,0:T(8,128)(2,1)}, f32[16,64]{1,0:T(8,128)}) custom-call(s32[8,64]{1,0:T(8,128)} %bitcast.2, f32[8,64]{1,0:T(8,128)} %bitcast.3, bf16[64,7168]{1,0:T(8,128)(2,1)} %tokens_hbm.1), custom_call_target="tpu_custom_call" | custom-call | tf_op jit(solution)/shard_map/pack_rows/pallas_call | solution.py:110
  2.3 4.1 %collective-permute-start.3 = (bf16[40,896]{1,0:T(8,128)(2,1)}, bf16[40,896]{1,0:T(8,128)(2,1)S(1)}, u32[]{:S(2)}, u32[]{:S(2)}) collective-permute-start(bf16[40,896]{1,0:T(8,128)(2,1)} %get-tuple-element.36), channel_id=1, source_target_pairs={{0,8},{1,9},{2,10},{3,11},{4,12},{5,13},{6,14},{7,15},{8,0},{9,1},... | collective-permute-start | bytes 215048 | tf_op jit(solution)/shard_map/ppermute | solution.py:424
  6.4 2.5 %collective-permute-start.2 = (bf16[40,896]{1,0:T(8,128)(2,1)}, bf16[40,896]{1,0:T(8,128)(2,1)S(1)}, u32[]{:S(2)}, u32[]{:S(2)}) collective-permute-start(bf16[40,896]{1,0:T(8,128)(2,1)} %get-tuple-element.41.refs_0_), channel_id=1, source_target_pairs={{0,6},{1,7},{2,4},{3,5},{4,2},{5,3},{6,0},{7,1},{8,14},{9,15},{10,... | collective-permute-start | bytes 215048 | tf_op jit(solution)/shard_map/ppermute | solution.py:418
  8.9 0.4 %collective-permute-start.1 = (bf16[40,896]{1,0:T(8,128)(2,1)}, bf16[40,896]{1,0:T(8,128)(2,1)S(1)}, u32[]{:S(2)}, u32[]{:S(2)}) collective-permute-start(bf16[40,896]{1,0:T(8,128)(2,1)} %get-tuple-element.41.refs_0_), channel_id=1, source_target_pairs={{0,4},{1,5},{2,6},{3,7},{4,0},{5,1},{6,2},{7,3},{8,12},{9,13},{10,... | collective-permute-start | bytes 215048 | tf_op jit(solution)/shard_map/ppermute | solution.py:418
  9.4 0.5 %collective-permute-start = (bf16[40,896]{1,0:T(8,128)(2,1)}, bf16[40,896]{1,0:T(8,128)(2,1)S(1)}, u32[]{:S(2)}, u32[]{:S(2)}) collective-permute-start(bf16[40,896]{1,0:T(8,128)(2,1)} %get-tuple-element.41.refs_0_), channel_id=1, source_target_pairs={{0,2},{1,3},{2,0},{3,1},{4,6},{5,7},{6,4},{7,5},{8,10},{9,11},{10,... | collective-permute-start | bytes 215048 | tf_op jit(solution)/shard_map/ppermute | solution.py:418
  9.9 0.0 collective-permute-done.3.refs_0_
  9.9 2.7 %collective-permute-start.6 = (bf16[40,896]{1,0:T(8,128)(2,1)S(1)}, bf16[40,896]{1,0:T(8,128)(2,1)S(1)}, u32[]{:S(2)}, u32[]{:S(2)}) collective-permute-start(bf16[40,896]{1,0:T(8,128)(2,1)S(1)} %collective-permute-done.3.refs_0_), channel_id=1, source_target_pairs={{0,6},{1,7},{2,4},{3,5},{4,2},{5,3},{6,0},{7,1},{8,14},{9,15},{10,... | collective-permute-start | bytes 215048 | tf_op jit(solution)/shard_map/ppermute | solution.py:418
  12.6 0.7 %collective-permute-start.5 = (bf16[40,896]{1,0:T(8,128)(2,1)S(1)}, bf16[40,896]{1,0:T(8,128)(2,1)S(1)}, u32[]{:S(2)}, u32[]{:S(2)}) collective-permute-start(bf16[40,896]{1,0:T(8,128)(2,1)S(1)} %collective-permute-done.3.refs_0_), channel_id=1, source_target_pairs={{0,4},{1,5},{2,6},{3,7},{4,0},{5,1},{6,2},{7,3},{8,12},{9,13},{10,... | collective-permute-start | bytes 215048 | tf_op jit(solution)/shard_map/ppermute | solution.py:418
  13.3 0.0 collective-permute-done.2.refs_3_
  13.3 1.0 %collective-permute-start.4 = (bf16[40,896]{1,0:T(8,128)(2,1)S(1)}, bf16[40,896]{1,0:T(8,128)(2,1)S(1)}, u32[]{:S(2)}, u32[]{:S(2)}) collective-permute-start(bf16[40,896]{1,0:T(8,128)(2,1)S(1)} %collective-permute-done.3.refs_0_), channel_id=1, source_target_pairs={{0,2},{1,3},{2,0},{3,1},{4,6},{5,7},{6,4},{7,5},{8,10},{9,11},{10,... | collective-permute-start | bytes 215048 | tf_op jit(solution)/shard_map/ppermute | solution.py:418
  14.2 0.7 %copy-done.4 = f32[16,64]{1,0:T(8,128)S(1)} copy-done((f32[16,64]{1,0:T(8,128)S(1)}, f32[16,64]{1,0:T(8,128)}, u32[]{:S(2)}) %copy-start.4) | copy-done | bytes 4120
  14.9 0.3 blend_weights.1.weight_ref
  15.2 0.0 collective-permute-done.1.refs_2_
  15.2 0.1 collective-permute-done.refs_1_
  15.3 0.5 %collective-permute-done.6.refs_3_ = bf16[40,896]{1,0:T(8,128)(2,1)S(1)} collective-permute-done((bf16[40,896]{1,0:T(8,128)(2,1)S(1)}, bf16[40,896]{1,0:T(8,128)(2,1)S(1)}, u32[]{:S(2)}, u32[]{:S(2)}) %collective-permute-start.6) | collective-permute-done | bytes 71712 | tf_op jit(solution)/shard_map/ppermute | solution.py:418
  15.9 1.0 %collective-permute-done.5.refs_2_ = bf16[40,896]{1,0:T(8,128)(2,1)S(1)} collective-permute-done((bf16[40,896]{1,0:T(8,128)(2,1)S(1)}, bf16[40,896]{1,0:T(8,128)(2,1)S(1)}, u32[]{:S(2)}, u32[]{:S(2)}) %collective-permute-start.5) | collective-permute-done | bytes 71712 | tf_op jit(solution)/shard_map/ppermute | solution.py:418
  16.9 0.7 %collective-permute-done.4.refs_1_ = bf16[40,896]{1,0:T(8,128)(2,1)S(1)} collective-permute-done((bf16[40,896]{1,0:T(8,128)(2,1)S(1)}, bf16[40,896]{1,0:T(8,128)(2,1)S(1)}, u32[]{:S(2)}, u32[]{:S(2)}) %collective-permute-start.4) | collective-permute-done | bytes 71712 | tf_op jit(solution)/shard_map/ppermute | solution.py:418
  17.6 0.0 copy-done.3
  17.6 0.1 collective-permute-start.7
  17.7 0.6 %collective-permute-start.8 = (bf16[160,896]{1,0:T(8,128)(2,1)S(1)}, bf16[160,896]{1,0:T(8,128)(2,1)S(1)}, u32[]{:S(2)}, u32[]{:S(2)}) collective-permute-start(bf16[160,896]{1,0:T(8,128)(2,1)S(1)} %join.3.refs_0_), channel_id=1, source_target_pairs={{0,1},{1,0},{2,3},{3,2},{4,5},{5,4},{6,7},{7,6},{8,9},{9,8},{10,11... | collective-permute-start | bytes 860168 | tf_op jit(solution)/shard_map/ppermute | solution.py:435
  18.3 1.0 %collective-permute-done.7.other_ref = bf16[160,896]{1,0:T(8,128)(2,1)S(1)} collective-permute-done((bf16[160,896]{1,0:T(8,128)(2,1)S(1)}, bf16[160,896]{1,0:T(8,128)(2,1)S(1)}, u32[]{:S(2)}, u32[]{:S(2)}) %collective-permute-start.7) | collective-permute-done | bytes 286752 | tf_op jit(solution)/shard_map/ppermute | solution.py:431
  19.3 0.3 unpack.1.first_ref
  19.6 0.1 collective-permute-done.8.refs_1_
  19.7 0.0 copy-done
  19.7 0.0 copy-done.1
  19.7 2.3 %expert_half.1 = (bf16[160,896]{1,0:T(8,128)(2,1)S(1)}, bf16[160,896]{1,0:T(8,128)(2,1)S(1)}, bf16[40,256]{1,0:T(8,128)(2,1)S(1)}) custom-call(f32[40,7168]{1,0:T(8,128)S(1)} %unpack.1.first_ref, bf16[160,896]{1,0:T(8,128)(2,1)S(1)} %join.3.refs_0_, bf16[160,896]{1,0:T(8,128)(2,1)S(1)} %collective-permute-done.8.refs_1_, bf16[7168,256]{1,0:T(8,128)(2,1)S(1)} %copy-done.1, ...), custom_call_target="tpu_custom_call" | custom-call | flops 734003200 | bytes 11010048 | tf_op jit(solution)/shard_map/expert_half/pallas_call | solution.py:273
  22.0 0.3 collective-permute-start.9
  22.3 0.3 collective-permute-start.10
  22.6 0.7 %kept_half.1.kept_ref = f32[320,896]{1,0:T(8,128)S(1)} custom-call(bf16[40,256]{1,0:T(8,128)(2,1)S(1)} %get-tuple-element.49.hidden_ref, bf16[256,7168]{1,0:T(8,128)(2,1)S(1)} %copy-done), custom_call_target="tpu_custom_call" | custom-call | flops 146800640 | bytes 3670016 | tf_op jit(solution)/shard_map/kept_half/pallas_call | solution.py:303
  23.3 0.3 collective-permute-done.9.taken_ref
  23.6 0.1 add_cores.2
  23.7 1.3 %collective-permute-start.14 = (bf16[40,896]{1,0:T(8,128)(2,1)S(1)}, bf16[40,896]{1,0:T(8,128)(2,1)S(1)}, u32[]{:S(2)}, u32[]{:S(2)}) collective-permute-start(bf16[40,896]{1,0:T(8,128)(2,1)S(1)} %get-tuple-element.62), channel_id=1, source_target_pairs={{0,6},{1,7},{2,4},{3,5},{4,2},{5,3},{6,0},{7,1},{8,14},{9,15},{10,... | collective-permute-start | bytes 215048 | tf_op jit(solution)/shard_map/ppermute | solution.py:445
  25.1 1.1 %collective-permute-start.15 = (bf16[40,896]{1,0:T(8,128)(2,1)S(1)}, bf16[40,896]{1,0:T(8,128)(2,1)S(1)}, u32[]{:S(2)}, u32[]{:S(2)}) collective-permute-start(bf16[40,896]{1,0:T(8,128)(2,1)S(1)} %get-tuple-element.63), channel_id=1, source_target_pairs={{0,4},{1,5},{2,6},{3,7},{4,0},{5,1},{6,2},{7,3},{8,12},{9,13},{10,... | collective-permute-start | bytes 215048 | tf_op jit(solution)/shard_map/ppermute | solution.py:445
  26.2 1.1 %collective-permute-start.16 = (bf16[40,896]{1,0:T(8,128)(2,1)S(1)}, bf16[40,896]{1,0:T(8,128)(2,1)S(1)}, u32[]{:S(2)}, u32[]{:S(2)}) collective-permute-start(bf16[40,896]{1,0:T(8,128)(2,1)S(1)} %get-tuple-element.64), channel_id=1, source_target_pairs={{0,2},{1,3},{2,0},{3,1},{4,6},{5,7},{6,4},{7,5},{8,10},{9,11},{10,... | collective-permute-start | bytes 215048 | tf_op jit(solution)/shard_map/ppermute | solution.py:445
  27.3 0.0 collective-permute-done.10.taken_ref
  27.3 0.1 add_cores.3
  27.3 1.3 %collective-permute-start.11 = (bf16[40,896]{1,0:T(8,128)(2,1)S(1)}, bf16[40,896]{1,0:T(8,128)(2,1)S(1)}, u32[]{:S(2)}, u32[]{:S(2)}) collective-permute-start(bf16[40,896]{1,0:T(8,128)(2,1)S(1)} %get-tuple-element.58), channel_id=1, source_target_pairs={{0,6},{1,7},{2,4},{3,5},{4,2},{5,3},{6,0},{7,1},{8,14},{9,15},{10,... | collective-permute-start | bytes 215048 | tf_op jit(solution)/shard_map/ppermute | solution.py:451
  28.7 1.1 %collective-permute-start.12 = (bf16[40,896]{1,0:T(8,128)(2,1)S(1)}, bf16[40,896]{1,0:T(8,128)(2,1)S(1)}, u32[]{:S(2)}, u32[]{:S(2)}) collective-permute-start(bf16[40,896]{1,0:T(8,128)(2,1)S(1)} %get-tuple-element.59), channel_id=1, source_target_pairs={{0,4},{1,5},{2,6},{3,7},{4,0},{5,1},{6,2},{7,3},{8,12},{9,13},{10,... | collective-permute-start | bytes 215048 | tf_op jit(solution)/shard_map/ppermute | solution.py:451
  29.8 0.0 collective-permute-done.14.refs_1_
  29.8 1.1 %collective-permute-start.13 = (bf16[40,896]{1,0:T(8,128)(2,1)S(1)}, bf16[40,896]{1,0:T(8,128)(2,1)S(1)}, u32[]{:S(2)}, u32[]{:S(2)}) collective-permute-start(bf16[40,896]{1,0:T(8,128)(2,1)S(1)} %get-tuple-element.60), channel_id=1, source_target_pairs={{0,2},{1,3},{2,0},{3,1},{4,6},{5,7},{6,4},{7,5},{8,10},{9,11},{10,... | collective-permute-start | bytes 215048 | tf_op jit(solution)/shard_map/ppermute | solution.py:451
  30.9 0.0 collective-permute-done.15.refs_2_
  30.9 0.0 collective-permute-done.16.refs_3_
  31.0 2.3 %collective-permute-start.17 = (bf16[40,896]{1,0:T(8,128)(2,1)S(1)}, bf16[40,896]{1,0:T(8,128)(2,1)S(1)}, u32[]{:S(2)}, u32[]{:S(2)}) collective-permute-start(bf16[40,896]{1,0:T(8,128)(2,1)S(1)} %sum_blocks.1), channel_id=1, source_target_pairs={{0,8},{1,9},{2,10},{3,11},{4,12},{5,13},{6,14},{7,15},{8,0},{9,1},... | collective-permute-start | bytes 215048 | tf_op jit(solution)/shard_map/ppermute | solution.py:447
  33.2 0.0 collective-permute-done.11.refs_1_
  33.3 0.0 collective-permute-done.12.refs_2_
  33.3 0.9 %collective-permute-done.13.refs_3_ = bf16[40,896]{1,0:T(8,128)(2,1)S(1)} collective-permute-done((bf16[40,896]{1,0:T(8,128)(2,1)S(1)}, bf16[40,896]{1,0:T(8,128)(2,1)S(1)}, u32[]{:S(2)}, u32[]{:S(2)}) %collective-permute-start.13) | collective-permute-done | bytes 71712 | tf_op jit(solution)/shard_map/ppermute | solution.py:451
  34.2 3.2 %collective-permute-done.17.refs_4_ = bf16[40,896]{1,0:T(8,128)(2,1)S(1)} collective-permute-done((bf16[40,896]{1,0:T(8,128)(2,1)S(1)}, bf16[40,896]{1,0:T(8,128)(2,1)S(1)}, u32[]{:S(2)}, u32[]{:S(2)}) %collective-permute-start.17) | collective-permute-done | bytes 71712 | tf_op jit(solution)/shard_map/ppermute | solution.py:447
  37.4 1.2 %blend.1 = bf16[64,7168]{1,0:T(8,128)(2,1)} custom-call(bf16[512,200]{1,0:T(8,128)(2,1)S(1)} %blend_weights.1.weight_ref, f32[40,896]{1,0:T(8,128)S(1)} %get-tuple-element.57.refs_0_, bf16[40,896]{1,0:T(8,128)(2,1)S(1)} %collective-permute-done.11.refs_1_, bf16[40,896]{1,0:T(8,128)(2,1)S(1)} %collective-permute-done.12.refs_2_, ...), custom_call_target="tpu_custom_call" | custom-call | tf_op jit(solution)/shard_map/blend/pallas_call | solution.py:396
  (9 shorter events, 0.1 us)
Async XLA Ops:
  2.3 7.6 %collective-permute-start.3 = (bf16[40,896]{1,0:T(8,128)(2,1)}, bf16[40,896]{1,0:T(8,128)(2,1)S(1)}, u32[]{:S(2)}, u32[]{:S(2)}) collective-permute-start(bf16[40,896]{1,0:T(8,128)(2,1)} %get-tuple-element.36), channel_id=1, source_target_pairs={{0,8},{1,9},{2,10},{3,11},{4,12},{5,13},{6,14},{7,15},{8,0},{9,1},... | collective-permute-start | bytes 215048 | tf_op jit(solution)/shard_map/ppermute | solution.py:424
  6.4 6.9 %collective-permute-start.2 = (bf16[40,896]{1,0:T(8,128)(2,1)}, bf16[40,896]{1,0:T(8,128)(2,1)S(1)}, u32[]{:S(2)}, u32[]{:S(2)}) collective-permute-start(bf16[40,896]{1,0:T(8,128)(2,1)} %get-tuple-element.41.refs_0_), channel_id=1, source_target_pairs={{0,6},{1,7},{2,4},{3,5},{4,2},{5,3},{6,0},{7,1},{8,14},{9,15},{10,... | collective-permute-start | bytes 215048 | tf_op jit(solution)/shard_map/ppermute | solution.py:418
  8.9 6.3 %collective-permute-start.1 = (bf16[40,896]{1,0:T(8,128)(2,1)}, bf16[40,896]{1,0:T(8,128)(2,1)S(1)}, u32[]{:S(2)}, u32[]{:S(2)}) collective-permute-start(bf16[40,896]{1,0:T(8,128)(2,1)} %get-tuple-element.41.refs_0_), channel_id=1, source_target_pairs={{0,4},{1,5},{2,6},{3,7},{4,0},{5,1},{6,2},{7,3},{8,12},{9,13},{10,... | collective-permute-start | bytes 215048 | tf_op jit(solution)/shard_map/ppermute | solution.py:418
  9.4 6.0 %collective-permute-start = (bf16[40,896]{1,0:T(8,128)(2,1)}, bf16[40,896]{1,0:T(8,128)(2,1)S(1)}, u32[]{:S(2)}, u32[]{:S(2)}) collective-permute-start(bf16[40,896]{1,0:T(8,128)(2,1)} %get-tuple-element.41.refs_0_), channel_id=1, source_target_pairs={{0,2},{1,3},{2,0},{3,1},{4,6},{5,7},{6,4},{7,5},{8,10},{9,11},{10,... | collective-permute-start | bytes 215048 | tf_op jit(solution)/shard_map/ppermute | solution.py:418
  9.9 7.7 %copy-start.3 = (bf16[40,896]{1,0:T(8,128)(2,1)S(1)}, bf16[40,896]{1,0:T(8,128)(2,1)}, u32[]{:S(2)}) copy-start(bf16[40,896]{1,0:T(8,128)(2,1)} %get-tuple-element.41.refs_0_) | copy-start | bytes 215044
  9.9 6.0 %collective-permute-start.6 = (bf16[40,896]{1,0:T(8,128)(2,1)S(1)}, bf16[40,896]{1,0:T(8,128)(2,1)S(1)}, u32[]{:S(2)}, u32[]{:S(2)}) collective-permute-start(bf16[40,896]{1,0:T(8,128)(2,1)S(1)} %collective-permute-done.3.refs_0_), channel_id=1, source_target_pairs={{0,6},{1,7},{2,4},{3,5},{4,2},{5,3},{6,0},{7,1},{8,14},{9,15},{10,... | collective-permute-start | bytes 215048 | tf_op jit(solution)/shard_map/ppermute | solution.py:418
  12.6 4.3 %collective-permute-start.5 = (bf16[40,896]{1,0:T(8,128)(2,1)S(1)}, bf16[40,896]{1,0:T(8,128)(2,1)S(1)}, u32[]{:S(2)}, u32[]{:S(2)}) collective-permute-start(bf16[40,896]{1,0:T(8,128)(2,1)S(1)} %collective-permute-done.3.refs_0_), channel_id=1, source_target_pairs={{0,4},{1,5},{2,6},{3,7},{4,0},{5,1},{6,2},{7,3},{8,12},{9,13},{10,... | collective-permute-start | bytes 215048 | tf_op jit(solution)/shard_map/ppermute | solution.py:418
  13.3 4.3 %collective-permute-start.4 = (bf16[40,896]{1,0:T(8,128)(2,1)S(1)}, bf16[40,896]{1,0:T(8,128)(2,1)S(1)}, u32[]{:S(2)}, u32[]{:S(2)}) collective-permute-start(bf16[40,896]{1,0:T(8,128)(2,1)S(1)} %collective-permute-done.3.refs_0_), channel_id=1, source_target_pairs={{0,2},{1,3},{2,0},{3,1},{4,6},{5,7},{6,4},{7,5},{8,10},{9,11},{10,... | collective-permute-start | bytes 215048 | tf_op jit(solution)/shard_map/ppermute | solution.py:418
  14.2 0.7 %copy-start.4 = (f32[16,64]{1,0:T(8,128)S(1)}, f32[16,64]{1,0:T(8,128)}, u32[]{:S(2)}) copy-start(f32[16,64]{1,0:T(8,128)} %get-tuple-element.39.table_ref) | copy-start | bytes 12292
  14.9 4.8 %copy-start = (bf16[256,7168]{1,0:T(8,128)(2,1)S(1)}, bf16[256,7168]{1,0:T(8,128)(2,1)}, u32[]{:S(2)}) copy-start(bf16[256,7168]{1,0:T(8,128)(2,1)} %down_ref.1) | copy-start | bytes 11010052
  14.9 4.8 %copy-start.1 = (bf16[7168,256]{1,0:T(8,128)(2,1)S(1)}, bf16[7168,256]{1,0:T(8,128)(2,1)}, u32[]{:S(2)}) copy-start(bf16[7168,256]{1,0:T(8,128)(2,1)} %refs_2_.1) | copy-start | bytes 11010052
  14.9 4.8 %copy-start.2 = (bf16[7168,256]{1,0:T(8,128)(2,1)S(1)}, bf16[7168,256]{1,0:T(8,128)(2,1)}, u32[]{:S(2)}) copy-start(bf16[7168,256]{1,0:T(8,128)(2,1)} %refs_3_.1) | copy-start | bytes 11010052
  17.6 1.6 %collective-permute-start.7 = (bf16[160,896]{1,0:T(8,128)(2,1)S(1)}, bf16[160,896]{1,0:T(8,128)(2,1)S(1)}, u32[]{:S(2)}, u32[]{:S(2)}) collective-permute-start(bf16[160,896]{1,0:T(8,128)(2,1)S(1)} %join.2.own_ref), channel_id=1, source_target_pairs={{0,1},{1,0},{2,3},{3,2},{4,5},{5,4},{6,7},{7,6},{8,9},{9,8},{10,11... | collective-permute-start | bytes 860168 | tf_op jit(solution)/shard_map/ppermute | solution.py:431
  17.7 1.9 %collective-permute-start.8 = (bf16[160,896]{1,0:T(8,128)(2,1)S(1)}, bf16[160,896]{1,0:T(8,128)(2,1)S(1)}, u32[]{:S(2)}, u32[]{:S(2)}) collective-permute-start(bf16[160,896]{1,0:T(8,128)(2,1)S(1)} %join.3.refs_0_), channel_id=1, source_target_pairs={{0,1},{1,0},{2,3},{3,2},{4,5},{5,4},{6,7},{7,6},{8,9},{9,8},{10,11... | collective-permute-start | bytes 860168 | tf_op jit(solution)/shard_map/ppermute | solution.py:435
  22.0 1.6 %collective-permute-start.9 = (bf16[160,896]{1,0:T(8,128)(2,1)S(1)}, bf16[160,896]{1,0:T(8,128)(2,1)S(1)}, u32[]{:S(2)}, u32[]{:S(2)}) collective-permute-start(bf16[160,896]{1,0:T(8,128)(2,1)S(1)} %get-tuple-element.50), channel_id=1, source_target_pairs={{0,1},{1,0},{2,3},{3,2},{4,5},{5,4},{6,7},{7,6},{8,9},{9,8},{10,11... | collective-permute-start | bytes 860168 | tf_op jit(solution)/shard_map/ppermute | solution.py:437
  22.3 5.0 %collective-permute-start.10 = (bf16[160,896]{1,0:T(8,128)(2,1)S(1)}, bf16[160,896]{1,0:T(8,128)(2,1)S(1)}, u32[]{:S(2)}, u32[]{:S(2)}) collective-permute-start(bf16[160,896]{1,0:T(8,128)(2,1)S(1)} %get-tuple-element.56), channel_id=1, source_target_pairs={{0,1},{1,0},{2,3},{3,2},{4,5},{5,4},{6,7},{7,6},{8,9},{9,8},{10,11... | collective-permute-start | bytes 860168 | tf_op jit(solution)/shard_map/ppermute | solution.py:437
  23.7 6.1 %collective-permute-start.14 = (bf16[40,896]{1,0:T(8,128)(2,1)S(1)}, bf16[40,896]{1,0:T(8,128)(2,1)S(1)}, u32[]{:S(2)}, u32[]{:S(2)}) collective-permute-start(bf16[40,896]{1,0:T(8,128)(2,1)S(1)} %get-tuple-element.62), channel_id=1, source_target_pairs={{0,6},{1,7},{2,4},{3,5},{4,2},{5,3},{6,0},{7,1},{8,14},{9,15},{10,... | collective-permute-start | bytes 215048 | tf_op jit(solution)/shard_map/ppermute | solution.py:445
  25.1 5.8 %collective-permute-start.15 = (bf16[40,896]{1,0:T(8,128)(2,1)S(1)}, bf16[40,896]{1,0:T(8,128)(2,1)S(1)}, u32[]{:S(2)}, u32[]{:S(2)}) collective-permute-start(bf16[40,896]{1,0:T(8,128)(2,1)S(1)} %get-tuple-element.63), channel_id=1, source_target_pairs={{0,4},{1,5},{2,6},{3,7},{4,0},{5,1},{6,2},{7,3},{8,12},{9,13},{10,... | collective-permute-start | bytes 215048 | tf_op jit(solution)/shard_map/ppermute | solution.py:445
  26.2 4.7 %collective-permute-start.16 = (bf16[40,896]{1,0:T(8,128)(2,1)S(1)}, bf16[40,896]{1,0:T(8,128)(2,1)S(1)}, u32[]{:S(2)}, u32[]{:S(2)}) collective-permute-start(bf16[40,896]{1,0:T(8,128)(2,1)S(1)} %get-tuple-element.64), channel_id=1, source_target_pairs={{0,2},{1,3},{2,0},{3,1},{4,6},{5,7},{6,4},{7,5},{8,10},{9,11},{10,... | collective-permute-start | bytes 215048 | tf_op jit(solution)/shard_map/ppermute | solution.py:445
  27.3 5.9 %collective-permute-start.11 = (bf16[40,896]{1,0:T(8,128)(2,1)S(1)}, bf16[40,896]{1,0:T(8,128)(2,1)S(1)}, u32[]{:S(2)}, u32[]{:S(2)}) collective-permute-start(bf16[40,896]{1,0:T(8,128)(2,1)S(1)} %get-tuple-element.58), channel_id=1, source_target_pairs={{0,6},{1,7},{2,4},{3,5},{4,2},{5,3},{6,0},{7,1},{8,14},{9,15},{10,... | collective-permute-start | bytes 215048 | tf_op jit(solution)/shard_map/ppermute | solution.py:451
  28.7 4.6 %collective-permute-start.12 = (bf16[40,896]{1,0:T(8,128)(2,1)S(1)}, bf16[40,896]{1,0:T(8,128)(2,1)S(1)}, u32[]{:S(2)}, u32[]{:S(2)}) collective-permute-start(bf16[40,896]{1,0:T(8,128)(2,1)S(1)} %get-tuple-element.59), channel_id=1, source_target_pairs={{0,4},{1,5},{2,6},{3,7},{4,0},{5,1},{6,2},{7,3},{8,12},{9,13},{10,... | collective-permute-start | bytes 215048 | tf_op jit(solution)/shard_map/ppermute | solution.py:451
  29.8 4.3 %collective-permute-start.13 = (bf16[40,896]{1,0:T(8,128)(2,1)S(1)}, bf16[40,896]{1,0:T(8,128)(2,1)S(1)}, u32[]{:S(2)}, u32[]{:S(2)}) collective-permute-start(bf16[40,896]{1,0:T(8,128)(2,1)S(1)} %get-tuple-element.60), channel_id=1, source_target_pairs={{0,2},{1,3},{2,0},{3,1},{4,6},{5,7},{6,4},{7,5},{8,10},{9,11},{10,... | collective-permute-start | bytes 215048 | tf_op jit(solution)/shard_map/ppermute | solution.py:451
  31.0 6.5 %collective-permute-start.17 = (bf16[40,896]{1,0:T(8,128)(2,1)S(1)}, bf16[40,896]{1,0:T(8,128)(2,1)S(1)}, u32[]{:S(2)}, u32[]{:S(2)}) collective-permute-start(bf16[40,896]{1,0:T(8,128)(2,1)S(1)} %sum_blocks.1), channel_id=1, source_target_pairs={{0,8},{1,9},{2,10},{3,11},{4,12},{5,13},{6,14},{7,15},{8,0},{9,1},... | collective-permute-start | bytes 215048 | tf_op jit(solution)/shard_map/ppermute | solution.py:447

commit v14 on v13

--- a/solution.py
+++ b/solution.py
@@ -417,15 +417,16 @@
     def gather(block):
         return [block] + [lax.ppermute(block, "expert", other_chip[m]) for m in range(1, chips)]
 
-    own = gather(packed[0])
+    own = [packed[0]] + [lax.ppermute(packed[0], "expert", other_chip[m]) for m in range(2, chips)]
     crowds = []
     for k in range(1, teams):
         pairs = [(i, (i + k * SPLIT) % devices) for i in range(devices)]
         block = lax.ppermute(packed[k], "expert", pairs)
         if k == teams - 1:
-            block, table = lax.optimization_barrier((block, table))
+            block, table, last = lax.optimization_barrier((block, table, packed[0]))
             weights = blend_weights(table, teams)
         crowds.append(gather(block))
+    own.insert(1, lax.ppermute(last, "expert", other_chip[1]))
     own, crowds, weights = lax.optimization_barrier((own, crowds, weights))
     own = join(own)
     first = unpack(own, lax.ppermute(own, "expert", other_core))

time: 38.9 us -> 39.4 us (1.013)
  starting transfers between devices: 22.5 us -> 23 us
    ppermute x0 -> x3, starting transfers between devices: none -> 4.88 us  [the longest x2 2.98 us: body(): lax.ppermute(packed[0], 'expert', other_chip[m])]
    ppermute x6 -> x3, starting transfers between devices: 7.81 us -> 3.49 us  [gather(): lax.ppermute(block, 'expert', other_chip[m])]
    ppermute x6 -> x3, waiting for transfers between devices: 2.35 us -> 0.01 us  [gather(): lax.ppermute(block, 'expert', other_chip[m])]
    ppermute x0 -> x3, waiting for transfers between devices: none -> 2.05 us  [the longest x1 2.04 us: body(): own.insert(1, lax.ppermute(last, 'expert', other_chip[1]))]
    ppermute x1, waiting for transfers between devices: 3.24 us -> 2.37 us  [body(): others.append(lax.ppermute(sum_blocks(team), 'expert', pairs))]
    ppermute x3, waiting for transfers between devices: 0.01 us -> 0.8 us  [body(): team.append(lax.ppermute(parts[m], 'expert', other_chip[m]))]
    ppermute x1, waiting for transfers between devices: 0.01 us -> 0.51 us  [body(): block = lax.ppermute(packed[k], 'expert', pairs)]
  transfers between devices with their start and end apart: 18 -> 18, of which waited for: 9 -> 8; matrix products, arithmetic and copies ran while one was open for 0% -> 0% of each run, Pallas kernels for 4% -> 4%
where the time goes in v14:
time: 39.4 us; the launch traced here: 39.2 us
  starting transfers between devices  23 us (58%)
  waiting for transfers between devices  7.95 us (20%)
  Pallas kernels  7.43 us (19%)
  local copies, waits for them, and re-layouts  0.71 us (2%)
    ppermute x1, starting transfers between devices, body(): block = lax.ppermute(packed[k], 'expert', pairs)  4.1 us
    ppermute x3, starting transfers between devices, body(): own.append(lax.ppermute(parts[m], 'expert', other_chip[m]))  3.64 us
    ppermute x3, starting transfers between devices, body(): team.append(lax.ppermute(parts[m], 'expert', other_chip[m]))  3.55 us
    ppermute x3, starting transfers between devices, gather(): lax.ppermute(block, 'expert', other_chip[m])  3.49 us
    ppermute x2, starting transfers between devices, body(): lax.ppermute(packed[0], 'expert', other_chip[m])  2.98 us
    ppermute x1, waiting for transfers between devices, body(): others.append(lax.ppermute(sum_blocks(team), 'expert', pairs))  2.37 us
    pallas_call x1, Pallas kernels, expert_half(): pl.pallas_call(functools.partial(expert_kernel, teams), out_shape=[jax.Sh...  2.33 us
    pallas_call x1, Pallas kernels, pack_rows(): pl.pallas_call(functools.partial(pack_kernel, teams), out_shape=[block] *...  2.28 us
  transfers between devices with their start and end apart: 18, of which 8 were waited for; matrix products, arithmetic and copies ran while one was open for 0% of the time, Pallas kernels for 4%

profile of v14, /device:TPU:0, one launch (start us, length us, event | category | flops | bytes accessed | tf_op | source)
XLA Modules:
  0.0 39.2 jit_solution(11469949042437124717)
XLA Ops:
  0.0 2.3 %pack_rows.1 = (bf16[40,896]{1,0:T(8,128)(2,1)}, bf16[40,896]{1,0:T(8,128)(2,1)}, f32[16,64]{1,0:T(8,128)}) custom-call(s32[8,64]{1,0:T(8,128)} %bitcast.2, f32[8,64]{1,0:T(8,128)} %bitcast.3, bf16[64,7168]{1,0:T(8,128)(2,1)} %tokens_hbm.1), custom_call_target="tpu_custom_call" | custom-call | tf_op jit(solution)/shard_map/pack_rows/pallas_call | solution.py:110
  2.3 4.1 %collective-permute-start = (bf16[40,896]{1,0:T(8,128)(2,1)}, bf16[40,896]{1,0:T(8,128)(2,1)S(1)}, u32[]{:S(2)}, u32[]{:S(2)}) collective-permute-start(bf16[40,896]{1,0:T(8,128)(2,1)} %get-tuple-element.37), channel_id=1, source_target_pairs={{0,8},{1,9},{2,10},{3,11},{4,12},{5,13},{6,14},{7,15},{8,0},{9,1},... | collective-permute-start | bytes 215048 | tf_op jit(solution)/shard_map/ppermute | solution.py:424
  6.4 2.5 %collective-permute-start.3 = (bf16[40,896]{1,0:T(8,128)(2,1)}, bf16[40,896]{1,0:T(8,128)(2,1)S(1)}, u32[]{:S(2)}, u32[]{:S(2)}) collective-permute-start(bf16[40,896]{1,0:T(8,128)(2,1)} %get-tuple-element.43.refs_0_), channel_id=1, source_target_pairs={{0,6},{1,7},{2,4},{3,5},{4,2},{5,3},{6,0},{7,1},{8,14},{9,15},{10,... | collective-permute-start | bytes 215048 | tf_op jit(solution)/shard_map/ppermute | solution.py:420
  8.9 0.4 %collective-permute-start.2 = (bf16[40,896]{1,0:T(8,128)(2,1)}, bf16[40,896]{1,0:T(8,128)(2,1)S(1)}, u32[]{:S(2)}, u32[]{:S(2)}) collective-permute-start(bf16[40,896]{1,0:T(8,128)(2,1)} %get-tuple-element.43.refs_0_), channel_id=1, source_target_pairs={{0,4},{1,5},{2,6},{3,7},{4,0},{5,1},{6,2},{7,3},{8,12},{9,13},{10,... | collective-permute-start | bytes 215048 | tf_op jit(solution)/shard_map/ppermute | solution.py:420
  9.4 0.5 %collective-permute-done.refs_0_ = bf16[40,896]{1,0:T(8,128)(2,1)S(1)} collective-permute-done((bf16[40,896]{1,0:T(8,128)(2,1)}, bf16[40,896]{1,0:T(8,128)(2,1)S(1)}, u32[]{:S(2)}, u32[]{:S(2)}) %collective-permute-start) | collective-permute-done | bytes 71712 | tf_op jit(solution)/shard_map/ppermute | solution.py:424
  9.9 2.7 %collective-permute-start.6 = (bf16[40,896]{1,0:T(8,128)(2,1)S(1)}, bf16[40,896]{1,0:T(8,128)(2,1)S(1)}, u32[]{:S(2)}, u32[]{:S(2)}) collective-permute-start(bf16[40,896]{1,0:T(8,128)(2,1)S(1)} %collective-permute-done.refs_0_), channel_id=1, source_target_pairs={{0,6},{1,7},{2,4},{3,5},{4,2},{5,3},{6,0},{7,1},{8,14},{9,15},{10,... | collective-permute-start | bytes 215048 | tf_op jit(solution)/shard_map/ppermute | solution.py:418
  12.6 0.7 %collective-permute-start.5 = (bf16[40,896]{1,0:T(8,128)(2,1)S(1)}, bf16[40,896]{1,0:T(8,128)(2,1)S(1)}, u32[]{:S(2)}, u32[]{:S(2)}) collective-permute-start(bf16[40,896]{1,0:T(8,128)(2,1)S(1)} %collective-permute-done.refs_0_), channel_id=1, source_target_pairs={{0,4},{1,5},{2,6},{3,7},{4,0},{5,1},{6,2},{7,3},{8,12},{9,13},{10,... | collective-permute-start | bytes 215048 | tf_op jit(solution)/shard_map/ppermute | solution.py:418
  13.3 0.1 collective-permute-start.4
  13.4 0.0 collective-permute-done.3.refs_3_
  13.4 1.9 %collective-permute-start.1 = (bf16[40,896]{1,0:T(8,128)(2,1)}, bf16[40,896]{1,0:T(8,128)(2,1)S(1)}, u32[]{:S(2)}, u32[]{:S(2)}) collective-permute-start(bf16[40,896]{1,0:T(8,128)(2,1)} %get-tuple-element.43.refs_0_), channel_id=1, source_target_pairs={{0,2},{1,3},{2,0},{3,1},{4,6},{5,7},{6,4},{7,5},{8,10},{9,11},{10,... | collective-permute-start | bytes 215048 | tf_op jit(solution)/shard_map/ppermute | solution.py:429
  15.3 0.7 %copy-done.4 = f32[16,64]{1,0:T(8,128)S(1)} copy-done((f32[16,64]{1,0:T(8,128)S(1)}, f32[16,64]{1,0:T(8,128)}, u32[]{:S(2)}) %copy-start.4) | copy-done | bytes 4120
  16.0 0.3 blend_weights.1.weight_ref
  16.3 0.0 collective-permute-done.2.refs_2_
  16.3 2.0 %collective-permute-done.1.refs_1_ = bf16[40,896]{1,0:T(8,128)(2,1)S(1)} collective-permute-done((bf16[40,896]{1,0:T(8,128)(2,1)}, bf16[40,896]{1,0:T(8,128)(2,1)S(1)}, u32[]{:S(2)}, u32[]{:S(2)}) %collective-permute-start.1) | collective-permute-done | bytes 71712 | tf_op jit(solution)/shard_map/ppermute | solution.py:429
  18.4 0.0 collective-permute-done.6.refs_3_
  18.4 0.0 collective-permute-done.5.refs_2_
  18.4 0.0 collective-permute-done.4.refs_1_
  18.4 0.0 copy-done.3
  18.4 0.1 collective-permute-start.7
  18.5 0.6 %collective-permute-start.8 = (bf16[160,896]{1,0:T(8,128)(2,1)S(1)}, bf16[160,896]{1,0:T(8,128)(2,1)S(1)}, u32[]{:S(2)}, u32[]{:S(2)}) collective-permute-start(bf16[160,896]{1,0:T(8,128)(2,1)S(1)} %join.3.refs_0_), channel_id=1, source_target_pairs={{0,1},{1,0},{2,3},{3,2},{4,5},{5,4},{6,7},{7,6},{8,9},{9,8},{10,11... | collective-permute-start | bytes 860168 | tf_op jit(solution)/shard_map/ppermute | solution.py:436
  19.1 1.0 %collective-permute-done.7.other_ref = bf16[160,896]{1,0:T(8,128)(2,1)S(1)} collective-permute-done((bf16[160,896]{1,0:T(8,128)(2,1)S(1)}, bf16[160,896]{1,0:T(8,128)(2,1)S(1)}, u32[]{:S(2)}, u32[]{:S(2)}) %collective-permute-start.7) | collective-permute-done | bytes 286752 | tf_op jit(solution)/shard_map/ppermute | solution.py:432
  20.0 0.3 unpack.1.first_ref
  20.4 0.1 collective-permute-done.8.refs_1_
  20.5 0.0 copy-done
  20.5 0.0 copy-done.1
  20.5 2.3 %expert_half.1 = (bf16[160,896]{1,0:T(8,128)(2,1)S(1)}, bf16[160,896]{1,0:T(8,128)(2,1)S(1)}, bf16[40,256]{1,0:T(8,128)(2,1)S(1)}) custom-call(f32[40,7168]{1,0:T(8,128)S(1)} %unpack.1.first_ref, bf16[160,896]{1,0:T(8,128)(2,1)S(1)} %join.3.refs_0_, bf16[160,896]{1,0:T(8,128)(2,1)S(1)} %collective-permute-done.8.refs_1_, bf16[7168,256]{1,0:T(8,128)(2,1)S(1)} %copy-done.1, ...), custom_call_target="tpu_custom_call" | custom-call | flops 734003200 | bytes 11010048 | tf_op jit(solution)/shard_map/expert_half/pallas_call | solution.py:273
  22.8 0.3 collective-permute-start.9
  23.1 0.3 collective-permute-start.10
  23.4 0.7 %kept_half.1.kept_ref = f32[320,896]{1,0:T(8,128)S(1)} custom-call(bf16[40,256]{1,0:T(8,128)(2,1)S(1)} %get-tuple-element.51.hidden_ref, bf16[256,7168]{1,0:T(8,128)(2,1)S(1)} %copy-done), custom_call_target="tpu_custom_call" | custom-call | flops 146800640 | bytes 3670016 | tf_op jit(solution)/shard_map/kept_half/pallas_call | solution.py:303
  24.1 0.3 collective-permute-done.9.taken_ref
  24.4 0.1 add_cores.2
  24.5 2.3 %collective-permute-start.14 = (bf16[40,896]{1,0:T(8,128)(2,1)S(1)}, bf16[40,896]{1,0:T(8,128)(2,1)S(1)}, u32[]{:S(2)}, u32[]{:S(2)}) collective-permute-start(bf16[40,896]{1,0:T(8,128)(2,1)S(1)} %get-tuple-element.64), channel_id=1, source_target_pairs={{0,6},{1,7},{2,4},{3,5},{4,2},{5,3},{6,0},{7,1},{8,14},{9,15},{10,... | collective-permute-start | bytes 215048 | tf_op jit(solution)/shard_map/ppermute | solution.py:446
  26.8 0.7 %collective-permute-start.15 = (bf16[40,896]{1,0:T(8,128)(2,1)S(1)}, bf16[40,896]{1,0:T(8,128)(2,1)S(1)}, u32[]{:S(2)}, u32[]{:S(2)}) collective-permute-start(bf16[40,896]{1,0:T(8,128)(2,1)S(1)} %get-tuple-element.65), channel_id=1, source_target_pairs={{0,4},{1,5},{2,6},{3,7},{4,0},{5,1},{6,2},{7,3},{8,12},{9,13},{10,... | collective-permute-start | bytes 215048 | tf_op jit(solution)/shard_map/ppermute | solution.py:446
  27.5 0.6 %collective-permute-start.16 = (bf16[40,896]{1,0:T(8,128)(2,1)S(1)}, bf16[40,896]{1,0:T(8,128)(2,1)S(1)}, u32[]{:S(2)}, u32[]{:S(2)}) collective-permute-start(bf16[40,896]{1,0:T(8,128)(2,1)S(1)} %get-tuple-element.66), channel_id=1, source_target_pairs={{0,2},{1,3},{2,0},{3,1},{4,6},{5,7},{6,4},{7,5},{8,10},{9,11},{10,... | collective-permute-start | bytes 215048 | tf_op jit(solution)/shard_map/ppermute | solution.py:446
  28.1 0.0 collective-permute-done.10.taken_ref
  28.1 0.1 add_cores.3
  28.1 2.3 %collective-permute-start.11 = (bf16[40,896]{1,0:T(8,128)(2,1)S(1)}, bf16[40,896]{1,0:T(8,128)(2,1)S(1)}, u32[]{:S(2)}, u32[]{:S(2)}) collective-permute-start(bf16[40,896]{1,0:T(8,128)(2,1)S(1)} %get-tuple-element.60), channel_id=1, source_target_pairs={{0,6},{1,7},{2,4},{3,5},{4,2},{5,3},{6,0},{7,1},{8,14},{9,15},{10,... | collective-permute-start | bytes 215048 | tf_op jit(solution)/shard_map/ppermute | solution.py:452
  30.4 0.7 %collective-permute-start.12 = (bf16[40,896]{1,0:T(8,128)(2,1)S(1)}, bf16[40,896]{1,0:T(8,128)(2,1)S(1)}, u32[]{:S(2)}, u32[]{:S(2)}) collective-permute-start(bf16[40,896]{1,0:T(8,128)(2,1)S(1)} %get-tuple-element.61), channel_id=1, source_target_pairs={{0,4},{1,5},{2,6},{3,7},{4,0},{5,1},{6,2},{7,3},{8,12},{9,13},{10,... | collective-permute-start | bytes 215048 | tf_op jit(solution)/shard_map/ppermute | solution.py:452
  31.1 0.0 collective-permute-done.14.refs_1_
  31.1 0.6 %collective-permute-start.13 = (bf16[40,896]{1,0:T(8,128)(2,1)S(1)}, bf16[40,896]{1,0:T(8,128)(2,1)S(1)}, u32[]{:S(2)}, u32[]{:S(2)}) collective-permute-start(bf16[40,896]{1,0:T(8,128)(2,1)S(1)} %get-tuple-element.62), channel_id=1, source_target_pairs={{0,2},{1,3},{2,0},{3,1},{4,6},{5,7},{6,4},{7,5},{8,10},{9,11},{10,... | collective-permute-start | bytes 215048 | tf_op jit(solution)/shard_map/ppermute | solution.py:452
  31.8 0.0 collective-permute-done.15.refs_2_
  31.8 0.8 %collective-permute-done.16.refs_3_ = bf16[40,896]{1,0:T(8,128)(2,1)S(1)} collective-permute-done((bf16[40,896]{1,0:T(8,128)(2,1)S(1)}, bf16[40,896]{1,0:T(8,128)(2,1)S(1)}, u32[]{:S(2)}, u32[]{:S(2)}) %collective-permute-start.16) | collective-permute-done | bytes 71712 | tf_op jit(solution)/shard_map/ppermute | solution.py:446
  32.6 2.1 %collective-permute-start.17 = (bf16[40,896]{1,0:T(8,128)(2,1)S(1)}, bf16[40,896]{1,0:T(8,128)(2,1)S(1)}, u32[]{:S(2)}, u32[]{:S(2)}) collective-permute-start(bf16[40,896]{1,0:T(8,128)(2,1)S(1)} %sum_blocks.1), channel_id=1, source_target_pairs={{0,8},{1,9},{2,10},{3,11},{4,12},{5,13},{6,14},{7,15},{8,0},{9,1},... | collective-permute-start | bytes 215048 | tf_op jit(solution)/shard_map/ppermute | solution.py:448
  34.7 0.0 collective-permute-done.11.refs_1_
  34.7 0.8 %collective-permute-done.12.refs_2_ = bf16[40,896]{1,0:T(8,128)(2,1)S(1)} collective-permute-done((bf16[40,896]{1,0:T(8,128)(2,1)S(1)}, bf16[40,896]{1,0:T(8,128)(2,1)S(1)}, u32[]{:S(2)}, u32[]{:S(2)}) %collective-permute-start.12) | collective-permute-done | bytes 71712 | tf_op jit(solution)/shard_map/ppermute | solution.py:452
  35.5 0.0 collective-permute-done.13.refs_3_
  35.5 2.4 %collective-permute-done.17.refs_4_ = bf16[40,896]{1,0:T(8,128)(2,1)S(1)} collective-permute-done((bf16[40,896]{1,0:T(8,128)(2,1)S(1)}, bf16[40,896]{1,0:T(8,128)(2,1)S(1)}, u32[]{:S(2)}, u32[]{:S(2)}) %collective-permute-start.17) | collective-permute-done | bytes 71712 | tf_op jit(solution)/shard_map/ppermute | solution.py:448
  37.9 1.2 %blend.1 = bf16[64,7168]{1,0:T(8,128)(2,1)} custom-call(bf16[512,200]{1,0:T(8,128)(2,1)S(1)} %blend_weights.1.weight_ref, f32[40,896]{1,0:T(8,128)S(1)} %get-tuple-element.59.refs_0_, bf16[40,896]{1,0:T(8,128)(2,1)S(1)} %collective-permute-done.11.refs_1_, bf16[40,896]{1,0:T(8,128)(2,1)S(1)} %collective-permute-done.12.refs_2_, ...), custom_call_target="tpu_custom_call" | custom-call | tf_op jit(solution)/shard_map/blend/pallas_call | solution.py:396
  (9 shorter events, 0.1 us)
Async XLA Ops:
  2.3 7.6 %collective-permute-start = (bf16[40,896]{1,0:T(8,128)(2,1)}, bf16[40,896]{1,0:T(8,128)(2,1)S(1)}, u32[]{:S(2)}, u32[]{:S(2)}) collective-permute-start(bf16[40,896]{1,0:T(8,128)(2,1)} %get-tuple-element.37), channel_id=1, source_target_pairs={{0,8},{1,9},{2,10},{3,11},{4,12},{5,13},{6,14},{7,15},{8,0},{9,1},... | collective-permute-start | bytes 215048 | tf_op jit(solution)/shard_map/ppermute | solution.py:424
  6.4 7.0 %collective-permute-start.3 = (bf16[40,896]{1,0:T(8,128)(2,1)}, bf16[40,896]{1,0:T(8,128)(2,1)S(1)}, u32[]{:S(2)}, u32[]{:S(2)}) collective-permute-start(bf16[40,896]{1,0:T(8,128)(2,1)} %get-tuple-element.43.refs_0_), channel_id=1, source_target_pairs={{0,6},{1,7},{2,4},{3,5},{4,2},{5,3},{6,0},{7,1},{8,14},{9,15},{10,... | collective-permute-start | bytes 215048 | tf_op jit(solution)/shard_map/ppermute | solution.py:420
  8.9 7.4 %collective-permute-start.2 = (bf16[40,896]{1,0:T(8,128)(2,1)}, bf16[40,896]{1,0:T(8,128)(2,1)S(1)}, u32[]{:S(2)}, u32[]{:S(2)}) collective-permute-start(bf16[40,896]{1,0:T(8,128)(2,1)} %get-tuple-element.43.refs_0_), channel_id=1, source_target_pairs={{0,4},{1,5},{2,6},{3,7},{4,0},{5,1},{6,2},{7,3},{8,12},{9,13},{10,... | collective-permute-start | bytes 215048 | tf_op jit(solution)/shard_map/ppermute | solution.py:420
  9.9 8.5 %copy-start.3 = (bf16[40,896]{1,0:T(8,128)(2,1)S(1)}, bf16[40,896]{1,0:T(8,128)(2,1)}, u32[]{:S(2)}) copy-start(bf16[40,896]{1,0:T(8,128)(2,1)} %get-tuple-element.43.refs_0_) | copy-start | bytes 215044
  9.9 8.5 %collective-permute-start.6 = (bf16[40,896]{1,0:T(8,128)(2,1)S(1)}, bf16[40,896]{1,0:T(8,128)(2,1)S(1)}, u32[]{:S(2)}, u32[]{:S(2)}) collective-permute-start(bf16[40,896]{1,0:T(8,128)(2,1)S(1)} %collective-permute-done.refs_0_), channel_id=1, source_target_pairs={{0,6},{1,7},{2,4},{3,5},{4,2},{5,3},{6,0},{7,1},{8,14},{9,15},{10,... | collective-permute-start | bytes 215048 | tf_op jit(solution)/shard_map/ppermute | solution.py:418
  12.6 5.8 %collective-permute-start.5 = (bf16[40,896]{1,0:T(8,128)(2,1)S(1)}, bf16[40,896]{1,0:T(8,128)(2,1)S(1)}, u32[]{:S(2)}, u32[]{:S(2)}) collective-permute-start(bf16[40,896]{1,0:T(8,128)(2,1)S(1)} %collective-permute-done.refs_0_), channel_id=1, source_target_pairs={{0,4},{1,5},{2,6},{3,7},{4,0},{5,1},{6,2},{7,3},{8,12},{9,13},{10,... | collective-permute-start | bytes 215048 | tf_op jit(solution)/shard_map/ppermute | solution.py:418
  13.3 5.1 %collective-permute-start.4 = (bf16[40,896]{1,0:T(8,128)(2,1)S(1)}, bf16[40,896]{1,0:T(8,128)(2,1)S(1)}, u32[]{:S(2)}, u32[]{:S(2)}) collective-permute-start(bf16[40,896]{1,0:T(8,128)(2,1)S(1)} %collective-permute-done.refs_0_), channel_id=1, source_target_pairs={{0,2},{1,3},{2,0},{3,1},{4,6},{5,7},{6,4},{7,5},{8,10},{9,11},{10,... | collective-permute-start | bytes 215048 | tf_op jit(solution)/shard_map/ppermute | solution.py:418
  13.4 5.0 %collective-permute-start.1 = (bf16[40,896]{1,0:T(8,128)(2,1)}, bf16[40,896]{1,0:T(8,128)(2,1)S(1)}, u32[]{:S(2)}, u32[]{:S(2)}) collective-permute-start(bf16[40,896]{1,0:T(8,128)(2,1)} %get-tuple-element.43.refs_0_), channel_id=1, source_target_pairs={{0,2},{1,3},{2,0},{3,1},{4,6},{5,7},{6,4},{7,5},{8,10},{9,11},{10,... | collective-permute-start | bytes 215048 | tf_op jit(solution)/shard_map/ppermute | solution.py:429
  15.3 0.7 %copy-start.4 = (f32[16,64]{1,0:T(8,128)S(1)}, f32[16,64]{1,0:T(8,128)}, u32[]{:S(2)}) copy-start(f32[16,64]{1,0:T(8,128)} %get-tuple-element.41.table_ref) | copy-start | bytes 12292
  16.0 4.5 %copy-start = (bf16[256,7168]{1,0:T(8,128)(2,1)S(1)}, bf16[256,7168]{1,0:T(8,128)(2,1)}, u32[]{:S(2)}) copy-start(bf16[256,7168]{1,0:T(8,128)(2,1)} %down_ref.1) | copy-start | bytes 11010052
  16.0 4.5 %copy-start.1 = (bf16[7168,256]{1,0:T(8,128)(2,1)S(1)}, bf16[7168,256]{1,0:T(8,128)(2,1)}, u32[]{:S(2)}) copy-start(bf16[7168,256]{1,0:T(8,128)(2,1)} %refs_2_.1) | copy-start | bytes 11010052
  16.0 4.5 %copy-start.2 = (bf16[7168,256]{1,0:T(8,128)(2,1)S(1)}, bf16[7168,256]{1,0:T(8,128)(2,1)}, u32[]{:S(2)}) copy-start(bf16[7168,256]{1,0:T(8,128)(2,1)} %refs_3_.1) | copy-start | bytes 11010052
  18.4 1.6 %collective-permute-start.7 = (bf16[160,896]{1,0:T(8,128)(2,1)S(1)}, bf16[160,896]{1,0:T(8,128)(2,1)S(1)}, u32[]{:S(2)}, u32[]{:S(2)}) collective-permute-start(bf16[160,896]{1,0:T(8,128)(2,1)S(1)} %join.2.own_ref), channel_id=1, source_target_pairs={{0,1},{1,0},{2,3},{3,2},{4,5},{5,4},{6,7},{7,6},{8,9},{9,8},{10,11... | collective-permute-start | bytes 860168 | tf_op jit(solution)/shard_map/ppermute | solution.py:432
  18.5 1.9 %collective-permute-start.8 = (bf16[160,896]{1,0:T(8,128)(2,1)S(1)}, bf16[160,896]{1,0:T(8,128)(2,1)S(1)}, u32[]{:S(2)}, u32[]{:S(2)}) collective-permute-start(bf16[160,896]{1,0:T(8,128)(2,1)S(1)} %join.3.refs_0_), channel_id=1, source_target_pairs={{0,1},{1,0},{2,3},{3,2},{4,5},{5,4},{6,7},{7,6},{8,9},{9,8},{10,11... | collective-permute-start | bytes 860168 | tf_op jit(solution)/shard_map/ppermute | solution.py:436
  22.8 1.6 %collective-permute-start.9 = (bf16[160,896]{1,0:T(8,128)(2,1)S(1)}, bf16[160,896]{1,0:T(8,128)(2,1)S(1)}, u32[]{:S(2)}, u32[]{:S(2)}) collective-permute-start(bf16[160,896]{1,0:T(8,128)(2,1)S(1)} %get-tuple-element.52), channel_id=1, source_target_pairs={{0,1},{1,0},{2,3},{3,2},{4,5},{5,4},{6,7},{7,6},{8,9},{9,8},{10,11... | collective-permute-start | bytes 860168 | tf_op jit(solution)/shard_map/ppermute | solution.py:438
  23.1 5.0 %collective-permute-start.10 = (bf16[160,896]{1,0:T(8,128)(2,1)S(1)}, bf16[160,896]{1,0:T(8,128)(2,1)S(1)}, u32[]{:S(2)}, u32[]{:S(2)}) collective-permute-start(bf16[160,896]{1,0:T(8,128)(2,1)S(1)} %get-tuple-element.58), channel_id=1, source_target_pairs={{0,1},{1,0},{2,3},{3,2},{4,5},{5,4},{6,7},{7,6},{8,9},{9,8},{10,11... | collective-permute-start | bytes 860168 | tf_op jit(solution)/shard_map/ppermute | solution.py:438
  24.5 6.6 %collective-permute-start.14 = (bf16[40,896]{1,0:T(8,128)(2,1)S(1)}, bf16[40,896]{1,0:T(8,128)(2,1)S(1)}, u32[]{:S(2)}, u32[]{:S(2)}) collective-permute-start(bf16[40,896]{1,0:T(8,128)(2,1)S(1)} %get-tuple-element.64), channel_id=1, source_target_pairs={{0,6},{1,7},{2,4},{3,5},{4,2},{5,3},{6,0},{7,1},{8,14},{9,15},{10,... | collective-permute-start | bytes 215048 | tf_op jit(solution)/shard_map/ppermute | solution.py:446
  26.8 5.0 %collective-permute-start.15 = (bf16[40,896]{1,0:T(8,128)(2,1)S(1)}, bf16[40,896]{1,0:T(8,128)(2,1)S(1)}, u32[]{:S(2)}, u32[]{:S(2)}) collective-permute-start(bf16[40,896]{1,0:T(8,128)(2,1)S(1)} %get-tuple-element.65), channel_id=1, source_target_pairs={{0,4},{1,5},{2,6},{3,7},{4,0},{5,1},{6,2},{7,3},{8,12},{9,13},{10,... | collective-permute-start | bytes 215048 | tf_op jit(solution)/shard_map/ppermute | solution.py:446
  27.5 5.1 %collective-permute-start.16 = (bf16[40,896]{1,0:T(8,128)(2,1)S(1)}, bf16[40,896]{1,0:T(8,128)(2,1)S(1)}, u32[]{:S(2)}, u32[]{:S(2)}) collective-permute-start(bf16[40,896]{1,0:T(8,128)(2,1)S(1)} %get-tuple-element.66), channel_id=1, source_target_pairs={{0,2},{1,3},{2,0},{3,1},{4,6},{5,7},{6,4},{7,5},{8,10},{9,11},{10,... | collective-permute-start | bytes 215048 | tf_op jit(solution)/shard_map/ppermute | solution.py:446
  28.1 6.6 %collective-permute-start.11 = (bf16[40,896]{1,0:T(8,128)(2,1)S(1)}, bf16[40,896]{1,0:T(8,128)(2,1)S(1)}, u32[]{:S(2)}, u32[]{:S(2)}) collective-permute-start(bf16[40,896]{1,0:T(8,128)(2,1)S(1)} %get-tuple-element.60), channel_id=1, source_target_pairs={{0,6},{1,7},{2,4},{3,5},{4,2},{5,3},{6,0},{7,1},{8,14},{9,15},{10,... | collective-permute-start | bytes 215048 | tf_op jit(solution)/shard_map/ppermute | solution.py:452
  30.4 5.1 %collective-permute-start.12 = (bf16[40,896]{1,0:T(8,128)(2,1)S(1)}, bf16[40,896]{1,0:T(8,128)(2,1)S(1)}, u32[]{:S(2)}, u32[]{:S(2)}) collective-permute-start(bf16[40,896]{1,0:T(8,128)(2,1)S(1)} %get-tuple-element.61), channel_id=1, source_target_pairs={{0,4},{1,5},{2,6},{3,7},{4,0},{5,1},{6,2},{7,3},{8,12},{9,13},{10,... | collective-permute-start | bytes 215048 | tf_op jit(solution)/shard_map/ppermute | solution.py:452
  31.1 4.4 %collective-permute-start.13 = (bf16[40,896]{1,0:T(8,128)(2,1)S(1)}, bf16[40,896]{1,0:T(8,128)(2,1)S(1)}, u32[]{:S(2)}, u32[]{:S(2)}) collective-permute-start(bf16[40,896]{1,0:T(8,128)(2,1)S(1)} %get-tuple-element.62), channel_id=1, source_target_pairs={{0,2},{1,3},{2,0},{3,1},{4,6},{5,7},{6,4},{7,5},{8,10},{9,11},{10,... | collective-permute-start | bytes 215048 | tf_op jit(solution)/shard_map/ppermute | solution.py:452
  32.6 5.3 %collective-permute-start.17 = (bf16[40,896]{1,0:T(8,128)(2,1)S(1)}, bf16[40,896]{1,0:T(8,128)(2,1)S(1)}, u32[]{:S(2)}, u32[]{:S(2)}) collective-permute-start(bf16[40,896]{1,0:T(8,128)(2,1)S(1)} %sum_blocks.1), channel_id=1, source_target_pairs={{0,8},{1,9},{2,10},{3,11},{4,12},{5,13},{6,14},{7,15},{8,0},{9,1},... | collective-permute-start | bytes 215048 | tf_op jit(solution)/shard_map/ppermute | solution.py:448

commit v15 on v13

--- a/solution.py
+++ b/solution.py
@@ -426,7 +426,7 @@
             block, table = lax.optimization_barrier((block, table))
             weights = blend_weights(table, teams)
         crowds.append(gather(block))
-    own, crowds, weights = lax.optimization_barrier((own, crowds, weights))
+    own, weights = lax.optimization_barrier((own, weights))
     own = join(own)
     first = unpack(own, lax.ppermute(own, "expert", other_core))
     pieces = []

time: 38.9 us -> 37.4 us (0.961)
  waiting for transfers between devices: 7.89 us -> 6.85 us
  starting transfers between devices: 22.5 us -> 22.1 us
    ppermute x1, waiting for transfers between devices: 0.06 us -> 1.19 us  [body(): pieces += [crowd, lax.ppermute(crowd, 'expert', other_core)]]
    ppermute x1, waiting for transfers between devices: 3.24 us -> 2.24 us  [body(): others.append(lax.ppermute(sum_blocks(team), 'expert', pairs))]
    ppermute x1, waiting for transfers between devices: 0.97 us -> 0.01 us  [body(): first = unpack(own, lax.ppermute(own, 'expert', other_core))]
    ppermute x1, starting transfers between devices: 0.56 us -> 0.07 us  [body(): pieces += [crowd, lax.ppermute(crowd, 'expert', other_core)]]
where the time goes in v15:
time: 37.4 us; the launch traced here: 37.2 us
  starting transfers between devices  22.1 us (59%)
  Pallas kernels  7.42 us (20%)
  waiting for transfers between devices  6.85 us (18%)
  local copies, waits for them, and re-layouts  0.71 us (2%)
    ppermute x6, starting transfers between devices, gather(): lax.ppermute(block, 'expert', other_chip[m])  7.81 us
    ppermute x1, starting transfers between devices, body(): block = lax.ppermute(packed[k], 'expert', pairs)  4.1 us
    ppermute x3, starting transfers between devices, body(): own.append(lax.ppermute(parts[m], 'expert', other_chip[m]))  3.55 us
    ppermute x3, starting transfers between devices, body(): team.append(lax.ppermute(parts[m], 'expert', other_chip[m]))  3.55 us
    ppermute x1, starting transfers between devices, body(): others.append(lax.ppermute(sum_blocks(team), 'expert', pairs))  2.4 us
    pallas_call x1, Pallas kernels, expert_half(): pl.pallas_call(functools.partial(expert_kernel, teams), out_shape=[jax.Sh...  2.33 us
    pallas_call x1, Pallas kernels, pack_rows(): pl.pallas_call(functools.partial(pack_kernel, teams), out_shape=[block] *...  2.28 us
    ppermute x6, waiting for transfers between devices, gather(): lax.ppermute(block, 'expert', other_chip[m])  2.24 us
  transfers between devices with their start and end apart: 18, of which 9 were waited for; matrix products, arithmetic and copies ran while one was open for 0% of the time, Pallas kernels for 4%

profile of v15, /device:TPU:0, one launch (start us, length us, event | category | flops | bytes accessed | tf_op | source)
XLA Modules:
  0.0 37.2 jit_solution(11615774488222581662)
XLA Ops:
  0.0 2.3 %pack_rows.1 = (bf16[40,896]{1,0:T(8,128)(2,1)}, bf16[40,896]{1,0:T(8,128)(2,1)}, f32[16,64]{1,0:T(8,128)}) custom-call(s32[8,64]{1,0:T(8,128)} %bitcast.2, f32[8,64]{1,0:T(8,128)} %bitcast.3, bf16[64,7168]{1,0:T(8,128)(2,1)} %tokens_hbm.1), custom_call_target="tpu_custom_call" | custom-call | tf_op jit(solution)/shard_map/pack_rows/pallas_call | solution.py:110
  2.3 4.1 %collective-permute-start.3 = (bf16[40,896]{1,0:T(8,128)(2,1)}, bf16[40,896]{1,0:T(8,128)(2,1)S(1)}, u32[]{:S(2)}, u32[]{:S(2)}) collective-permute-start(bf16[40,896]{1,0:T(8,128)(2,1)} %get-tuple-element.32), channel_id=1, source_target_pairs={{0,8},{1,9},{2,10},{3,11},{4,12},{5,13},{6,14},{7,15},{8,0},{9,1},... | collective-permute-start | bytes 215048 | tf_op jit(solution)/shard_map/ppermute | solution.py:424
  6.4 2.5 %collective-permute-start.2 = (bf16[40,896]{1,0:T(8,128)(2,1)}, bf16[40,896]{1,0:T(8,128)(2,1)S(1)}, u32[]{:S(2)}, u32[]{:S(2)}) collective-permute-start(bf16[40,896]{1,0:T(8,128)(2,1)} %get-tuple-element.36.refs_0_), channel_id=1, source_target_pairs={{0,6},{1,7},{2,4},{3,5},{4,2},{5,3},{6,0},{7,1},{8,14},{9,15},{10,... | collective-permute-start | bytes 215048 | tf_op jit(solution)/shard_map/ppermute | solution.py:418
  8.9 0.4 %collective-permute-start.1 = (bf16[40,896]{1,0:T(8,128)(2,1)}, bf16[40,896]{1,0:T(8,128)(2,1)S(1)}, u32[]{:S(2)}, u32[]{:S(2)}) collective-permute-start(bf16[40,896]{1,0:T(8,128)(2,1)} %get-tuple-element.36.refs_0_), channel_id=1, source_target_pairs={{0,4},{1,5},{2,6},{3,7},{4,0},{5,1},{6,2},{7,3},{8,12},{9,13},{10,... | collective-permute-start | bytes 215048 | tf_op jit(solution)/shard_map/ppermute | solution.py:418
  9.4 0.5 %collective-permute-start = (bf16[40,896]{1,0:T(8,128)(2,1)}, bf16[40,896]{1,0:T(8,128)(2,1)S(1)}, u32[]{:S(2)}, u32[]{:S(2)}) collective-permute-start(bf16[40,896]{1,0:T(8,128)(2,1)} %get-tuple-element.36.refs_0_), channel_id=1, source_target_pairs={{0,2},{1,3},{2,0},{3,1},{4,6},{5,7},{6,4},{7,5},{8,10},{9,11},{10,... | collective-permute-start | bytes 215048 | tf_op jit(solution)/shard_map/ppermute | solution.py:418
  9.9 0.0 collective-permute-done.3.refs_0_
  9.9 2.7 %collective-permute-start.7 = (bf16[40,896]{1,0:T(8,128)(2,1)S(1)}, bf16[40,896]{1,0:T(8,128)(2,1)S(1)}, u32[]{:S(2)}, u32[]{:S(2)}) collective-permute-start(bf16[40,896]{1,0:T(8,128)(2,1)S(1)} %collective-permute-done.3.refs_0_), channel_id=1, source_target_pairs={{0,6},{1,7},{2,4},{3,5},{4,2},{5,3},{6,0},{7,1},{8,14},{9,15},{10,... | collective-permute-start | bytes 215048 | tf_op jit(solution)/shard_map/ppermute | solution.py:418
  12.6 0.7 %collective-permute-start.6 = (bf16[40,896]{1,0:T(8,128)(2,1)S(1)}, bf16[40,896]{1,0:T(8,128)(2,1)S(1)}, u32[]{:S(2)}, u32[]{:S(2)}) collective-permute-start(bf16[40,896]{1,0:T(8,128)(2,1)S(1)} %collective-permute-done.3.refs_0_), channel_id=1, source_target_pairs={{0,4},{1,5},{2,6},{3,7},{4,0},{5,1},{6,2},{7,3},{8,12},{9,13},{10,... | collective-permute-start | bytes 215048 | tf_op jit(solution)/shard_map/ppermute | solution.py:418
  13.3 0.0 collective-permute-done.2.refs_3_
  13.3 1.0 %collective-permute-start.5 = (bf16[40,896]{1,0:T(8,128)(2,1)S(1)}, bf16[40,896]{1,0:T(8,128)(2,1)S(1)}, u32[]{:S(2)}, u32[]{:S(2)}) collective-permute-start(bf16[40,896]{1,0:T(8,128)(2,1)S(1)} %collective-permute-done.3.refs_0_), channel_id=1, source_target_pairs={{0,2},{1,3},{2,0},{3,1},{4,6},{5,7},{6,4},{7,5},{8,10},{9,11},{10,... | collective-permute-start | bytes 215048 | tf_op jit(solution)/shard_map/ppermute | solution.py:418
  14.2 0.7 %copy-done.4 = f32[16,64]{1,0:T(8,128)S(1)} copy-done((f32[16,64]{1,0:T(8,128)S(1)}, f32[16,64]{1,0:T(8,128)}, u32[]{:S(2)}) %copy-start.4) | copy-done | bytes 4120
  14.9 0.3 blend_weights.1.weight_ref
  15.2 0.0 collective-permute-done.1.refs_2_
  15.2 0.1 collective-permute-done.refs_1_
  15.3 0.0 copy-done.3
  15.4 0.1 collective-permute-start.4
  15.5 0.4 %collective-permute-done.7.refs_3_ = bf16[40,896]{1,0:T(8,128)(2,1)S(1)} collective-permute-done((bf16[40,896]{1,0:T(8,128)(2,1)S(1)}, bf16[40,896]{1,0:T(8,128)(2,1)S(1)}, u32[]{:S(2)}, u32[]{:S(2)}) %collective-permute-start.7) | collective-permute-done | bytes 71712 | tf_op jit(solution)/shard_map/ppermute | solution.py:418
  15.9 1.0 %collective-permute-done.6.refs_2_ = bf16[40,896]{1,0:T(8,128)(2,1)S(1)} collective-permute-done((bf16[40,896]{1,0:T(8,128)(2,1)S(1)}, bf16[40,896]{1,0:T(8,128)(2,1)S(1)}, u32[]{:S(2)}, u32[]{:S(2)}) %collective-permute-start.6) | collective-permute-done | bytes 71712 | tf_op jit(solution)/shard_map/ppermute | solution.py:418
  16.9 0.7 %collective-permute-done.5.refs_1_ = bf16[40,896]{1,0:T(8,128)(2,1)S(1)} collective-permute-done((bf16[40,896]{1,0:T(8,128)(2,1)S(1)}, bf16[40,896]{1,0:T(8,128)(2,1)S(1)}, u32[]{:S(2)}, u32[]{:S(2)}) %collective-permute-start.5) | collective-permute-done | bytes 71712 | tf_op jit(solution)/shard_map/ppermute | solution.py:418
  17.6 0.1 collective-permute-start.8
  17.7 0.0 collective-permute-done.4.other_ref
  17.7 0.3 unpack.1.first_ref
  18.1 1.2 %collective-permute-done.8.refs_1_ = bf16[160,896]{1,0:T(8,128)(2,1)S(1)} collective-permute-done((bf16[160,896]{1,0:T(8,128)(2,1)S(1)}, bf16[160,896]{1,0:T(8,128)(2,1)S(1)}, u32[]{:S(2)}, u32[]{:S(2)}) %collective-permute-start.8) | collective-permute-done | bytes 286752 | tf_op jit(solution)/shard_map/ppermute | solution.py:435
  19.3 0.0 copy-done
  19.3 0.0 copy-done.2
  19.3 2.3 %expert_half.1 = (bf16[160,896]{1,0:T(8,128)(2,1)S(1)}, bf16[160,896]{1,0:T(8,128)(2,1)S(1)}, bf16[40,256]{1,0:T(8,128)(2,1)S(1)}) custom-call(f32[40,7168]{1,0:T(8,128)S(1)} %unpack.1.first_ref, bf16[160,896]{1,0:T(8,128)(2,1)S(1)} %join.3.refs_0_, bf16[160,896]{1,0:T(8,128)(2,1)S(1)} %collective-permute-done.8.refs_1_, bf16[7168,256]{1,0:T(8,128)(2,1)S(1)} %copy-done.1, ...), custom_call_target="tpu_custom_call" | custom-call | flops 734003200 | bytes 11010048 | tf_op jit(solution)/shard_map/expert_half/pallas_call | solution.py:273
  21.6 0.2 collective-permute-start.9
  21.8 0.4 %collective-permute-start.10 = (bf16[160,896]{1,0:T(8,128)(2,1)S(1)}, bf16[160,896]{1,0:T(8,128)(2,1)S(1)}, u32[]{:S(2)}, u32[]{:S(2)}) collective-permute-start(bf16[160,896]{1,0:T(8,128)(2,1)S(1)} %get-tuple-element.48), channel_id=1, source_target_pairs={{0,1},{1,0},{2,3},{3,2},{4,5},{5,4},{6,7},{7,6},{8,9},{9,8},{10,11... | collective-permute-start | bytes 860168 | tf_op jit(solution)/shard_map/ppermute | solution.py:437
  22.2 0.7 %kept_half.1.kept_ref = f32[320,896]{1,0:T(8,128)S(1)} custom-call(bf16[40,256]{1,0:T(8,128)(2,1)S(1)} %get-tuple-element.41.hidden_ref, bf16[256,7168]{1,0:T(8,128)(2,1)S(1)} %copy-done), custom_call_target="tpu_custom_call" | custom-call | flops 146800640 | bytes 3670016 | tf_op jit(solution)/shard_map/kept_half/pallas_call | solution.py:303
  22.9 0.3 collective-permute-done.9.taken_ref
  23.2 0.1 add_cores.2
  23.3 1.8 %collective-permute-start.14 = (bf16[40,896]{1,0:T(8,128)(2,1)S(1)}, bf16[40,896]{1,0:T(8,128)(2,1)S(1)}, u32[]{:S(2)}, u32[]{:S(2)}) collective-permute-start(bf16[40,896]{1,0:T(8,128)(2,1)S(1)} %get-tuple-element.54), channel_id=1, source_target_pairs={{0,6},{1,7},{2,4},{3,5},{4,2},{5,3},{6,0},{7,1},{8,14},{9,15},{10,... | collective-permute-start | bytes 215048 | tf_op jit(solution)/shard_map/ppermute | solution.py:445
  25.1 0.7 %collective-permute-start.15 = (bf16[40,896]{1,0:T(8,128)(2,1)S(1)}, bf16[40,896]{1,0:T(8,128)(2,1)S(1)}, u32[]{:S(2)}, u32[]{:S(2)}) collective-permute-start(bf16[40,896]{1,0:T(8,128)(2,1)S(1)} %get-tuple-element.55), channel_id=1, source_target_pairs={{0,4},{1,5},{2,6},{3,7},{4,0},{5,1},{6,2},{7,3},{8,12},{9,13},{10,... | collective-permute-start | bytes 215048 | tf_op jit(solution)/shard_map/ppermute | solution.py:445
  25.8 1.1 %collective-permute-start.16 = (bf16[40,896]{1,0:T(8,128)(2,1)S(1)}, bf16[40,896]{1,0:T(8,128)(2,1)S(1)}, u32[]{:S(2)}, u32[]{:S(2)}) collective-permute-start(bf16[40,896]{1,0:T(8,128)(2,1)S(1)} %get-tuple-element.56), channel_id=1, source_target_pairs={{0,2},{1,3},{2,0},{3,1},{4,6},{5,7},{6,4},{7,5},{8,10},{9,11},{10,... | collective-permute-start | bytes 215048 | tf_op jit(solution)/shard_map/ppermute | solution.py:445
  26.9 0.0 collective-permute-done.10.taken_ref
  26.9 0.1 add_cores.3
  26.9 1.8 %collective-permute-start.11 = (bf16[40,896]{1,0:T(8,128)(2,1)S(1)}, bf16[40,896]{1,0:T(8,128)(2,1)S(1)}, u32[]{:S(2)}, u32[]{:S(2)}) collective-permute-start(bf16[40,896]{1,0:T(8,128)(2,1)S(1)} %get-tuple-element.50), channel_id=1, source_target_pairs={{0,6},{1,7},{2,4},{3,5},{4,2},{5,3},{6,0},{7,1},{8,14},{9,15},{10,... | collective-permute-start | bytes 215048 | tf_op jit(solution)/shard_map/ppermute | solution.py:451
  28.7 0.7 %collective-permute-start.12 = (bf16[40,896]{1,0:T(8,128)(2,1)S(1)}, bf16[40,896]{1,0:T(8,128)(2,1)S(1)}, u32[]{:S(2)}, u32[]{:S(2)}) collective-permute-start(bf16[40,896]{1,0:T(8,128)(2,1)S(1)} %get-tuple-element.51), channel_id=1, source_target_pairs={{0,4},{1,5},{2,6},{3,7},{4,0},{5,1},{6,2},{7,3},{8,12},{9,13},{10,... | collective-permute-start | bytes 215048 | tf_op jit(solution)/shard_map/ppermute | solution.py:451
  29.4 0.0 collective-permute-done.14.refs_1_
  29.4 1.1 %collective-permute-start.13 = (bf16[40,896]{1,0:T(8,128)(2,1)S(1)}, bf16[40,896]{1,0:T(8,128)(2,1)S(1)}, u32[]{:S(2)}, u32[]{:S(2)}) collective-permute-start(bf16[40,896]{1,0:T(8,128)(2,1)S(1)} %get-tuple-element.52), channel_id=1, source_target_pairs={{0,2},{1,3},{2,0},{3,1},{4,6},{5,7},{6,4},{7,5},{8,10},{9,11},{10,... | collective-permute-start | bytes 215048 | tf_op jit(solution)/shard_map/ppermute | solution.py:451
  30.5 0.0 collective-permute-done.15.refs_2_
  30.5 0.1 collective-permute-done.16.refs_3_
  30.6 2.4 %collective-permute-start.17 = (bf16[40,896]{1,0:T(8,128)(2,1)S(1)}, bf16[40,896]{1,0:T(8,128)(2,1)S(1)}, u32[]{:S(2)}, u32[]{:S(2)}) collective-permute-start(bf16[40,896]{1,0:T(8,128)(2,1)S(1)} %sum_blocks.1), channel_id=1, source_target_pairs={{0,8},{1,9},{2,10},{3,11},{4,12},{5,13},{6,14},{7,15},{8,0},{9,1},... | collective-permute-start | bytes 215048 | tf_op jit(solution)/shard_map/ppermute | solution.py:447
  33.0 0.0 collective-permute-done.11.refs_1_
  33.0 0.0 collective-permute-done.12.refs_2_
  33.0 0.7 %collective-permute-done.13.refs_3_ = bf16[40,896]{1,0:T(8,128)(2,1)S(1)} collective-permute-done((bf16[40,896]{1,0:T(8,128)(2,1)S(1)}, bf16[40,896]{1,0:T(8,128)(2,1)S(1)}, u32[]{:S(2)}, u32[]{:S(2)}) %collective-permute-start.13) | collective-permute-done | bytes 71712 | tf_op jit(solution)/shard_map/ppermute | solution.py:451
  33.8 2.2 %collective-permute-done.17.refs_4_ = bf16[40,896]{1,0:T(8,128)(2,1)S(1)} collective-permute-done((bf16[40,896]{1,0:T(8,128)(2,1)S(1)}, bf16[40,896]{1,0:T(8,128)(2,1)S(1)}, u32[]{:S(2)}, u32[]{:S(2)}) %collective-permute-start.17) | collective-permute-done | bytes 71712 | tf_op jit(solution)/shard_map/ppermute | solution.py:447
  36.0 1.2 %blend.1 = bf16[64,7168]{1,0:T(8,128)(2,1)} custom-call(bf16[512,200]{1,0:T(8,128)(2,1)S(1)} %blend_weights.1.weight_ref, f32[40,896]{1,0:T(8,128)S(1)} %get-tuple-element.49.refs_0_, bf16[40,896]{1,0:T(8,128)(2,1)S(1)} %collective-permute-done.11.refs_1_, bf16[40,896]{1,0:T(8,128)(2,1)S(1)} %collective-permute-done.12.refs_2_, ...), custom_call_target="tpu_custom_call" | custom-call | tf_op jit(solution)/shard_map/blend/pallas_call | solution.py:396
  (9 shorter events, 0.1 us)
Async XLA Ops:
  2.3 7.6 %collective-permute-start.3 = (bf16[40,896]{1,0:T(8,128)(2,1)}, bf16[40,896]{1,0:T(8,128)(2,1)S(1)}, u32[]{:S(2)}, u32[]{:S(2)}) collective-permute-start(bf16[40,896]{1,0:T(8,128)(2,1)} %get-tuple-element.32), channel_id=1, source_target_pairs={{0,8},{1,9},{2,10},{3,11},{4,12},{5,13},{6,14},{7,15},{8,0},{9,1},... | collective-permute-start | bytes 215048 | tf_op jit(solution)/shard_map/ppermute | solution.py:424
  6.4 6.9 %collective-permute-start.2 = (bf16[40,896]{1,0:T(8,128)(2,1)}, bf16[40,896]{1,0:T(8,128)(2,1)S(1)}, u32[]{:S(2)}, u32[]{:S(2)}) collective-permute-start(bf16[40,896]{1,0:T(8,128)(2,1)} %get-tuple-element.36.refs_0_), channel_id=1, source_target_pairs={{0,6},{1,7},{2,4},{3,5},{4,2},{5,3},{6,0},{7,1},{8,14},{9,15},{10,... | collective-permute-start | bytes 215048 | tf_op jit(solution)/shard_map/ppermute | solution.py:418
  8.9 6.3 %collective-permute-start.1 = (bf16[40,896]{1,0:T(8,128)(2,1)}, bf16[40,896]{1,0:T(8,128)(2,1)S(1)}, u32[]{:S(2)}, u32[]{:S(2)}) collective-permute-start(bf16[40,896]{1,0:T(8,128)(2,1)} %get-tuple-element.36.refs_0_), channel_id=1, source_target_pairs={{0,4},{1,5},{2,6},{3,7},{4,0},{5,1},{6,2},{7,3},{8,12},{9,13},{10,... | collective-permute-start | bytes 215048 | tf_op jit(solution)/shard_map/ppermute | solution.py:418
  9.4 6.0 %collective-permute-start = (bf16[40,896]{1,0:T(8,128)(2,1)}, bf16[40,896]{1,0:T(8,128)(2,1)S(1)}, u32[]{:S(2)}, u32[]{:S(2)}) collective-permute-start(bf16[40,896]{1,0:T(8,128)(2,1)} %get-tuple-element.36.refs_0_), channel_id=1, source_target_pairs={{0,2},{1,3},{2,0},{3,1},{4,6},{5,7},{6,4},{7,5},{8,10},{9,11},{10,... | collective-permute-start | bytes 215048 | tf_op jit(solution)/shard_map/ppermute | solution.py:418
  9.9 5.5 %copy-start.3 = (bf16[40,896]{1,0:T(8,128)(2,1)S(1)}, bf16[40,896]{1,0:T(8,128)(2,1)}, u32[]{:S(2)}) copy-start(bf16[40,896]{1,0:T(8,128)(2,1)} %get-tuple-element.36.refs_0_) | copy-start | bytes 215044
  9.9 6.0 %collective-permute-start.7 = (bf16[40,896]{1,0:T(8,128)(2,1)S(1)}, bf16[40,896]{1,0:T(8,128)(2,1)S(1)}, u32[]{:S(2)}, u32[]{:S(2)}) collective-permute-start(bf16[40,896]{1,0:T(8,128)(2,1)S(1)} %collective-permute-done.3.refs_0_), channel_id=1, source_target_pairs={{0,6},{1,7},{2,4},{3,5},{4,2},{5,3},{6,0},{7,1},{8,14},{9,15},{10,... | collective-permute-start | bytes 215048 | tf_op jit(solution)/shard_map/ppermute | solution.py:418
  12.6 4.3 %collective-permute-start.6 = (bf16[40,896]{1,0:T(8,128)(2,1)S(1)}, bf16[40,896]{1,0:T(8,128)(2,1)S(1)}, u32[]{:S(2)}, u32[]{:S(2)}) collective-permute-start(bf16[40,896]{1,0:T(8,128)(2,1)S(1)} %collective-permute-done.3.refs_0_), channel_id=1, source_target_pairs={{0,4},{1,5},{2,6},{3,7},{4,0},{5,1},{6,2},{7,3},{8,12},{9,13},{10,... | collective-permute-start | bytes 215048 | tf_op jit(solution)/shard_map/ppermute | solution.py:418
  13.3 4.3 %collective-permute-start.5 = (bf16[40,896]{1,0:T(8,128)(2,1)S(1)}, bf16[40,896]{1,0:T(8,128)(2,1)S(1)}, u32[]{:S(2)}, u32[]{:S(2)}) collective-permute-start(bf16[40,896]{1,0:T(8,128)(2,1)S(1)} %collective-permute-done.3.refs_0_), channel_id=1, source_target_pairs={{0,2},{1,3},{2,0},{3,1},{4,6},{5,7},{6,4},{7,5},{8,10},{9,11},{10,... | collective-permute-start | bytes 215048 | tf_op jit(solution)/shard_map/ppermute | solution.py:418
  14.2 0.7 %copy-start.4 = (f32[16,64]{1,0:T(8,128)S(1)}, f32[16,64]{1,0:T(8,128)}, u32[]{:S(2)}) copy-start(f32[16,64]{1,0:T(8,128)} %get-tuple-element.34.table_ref) | copy-start | bytes 12292
  14.9 4.3 %copy-start = (bf16[256,7168]{1,0:T(8,128)(2,1)S(1)}, bf16[256,7168]{1,0:T(8,128)(2,1)}, u32[]{:S(2)}) copy-start(bf16[256,7168]{1,0:T(8,128)(2,1)} %down_ref.1) | copy-start | bytes 11010052
  14.9 4.3 %copy-start.1 = (bf16[7168,256]{1,0:T(8,128)(2,1)S(1)}, bf16[7168,256]{1,0:T(8,128)(2,1)}, u32[]{:S(2)}) copy-start(bf16[7168,256]{1,0:T(8,128)(2,1)} %refs_2_.1) | copy-start | bytes 11010052
  14.9 4.3 %copy-start.2 = (bf16[7168,256]{1,0:T(8,128)(2,1)S(1)}, bf16[7168,256]{1,0:T(8,128)(2,1)}, u32[]{:S(2)}) copy-start(bf16[7168,256]{1,0:T(8,128)(2,1)} %refs_3_.1) | copy-start | bytes 11010052
  15.4 2.3 %collective-permute-start.4 = (bf16[160,896]{1,0:T(8,128)(2,1)S(1)}, bf16[160,896]{1,0:T(8,128)(2,1)S(1)}, u32[]{:S(2)}, u32[]{:S(2)}) collective-permute-start(bf16[160,896]{1,0:T(8,128)(2,1)S(1)} %join.2.own_ref), channel_id=1, source_target_pairs={{0,1},{1,0},{2,3},{3,2},{4,5},{5,4},{6,7},{7,6},{8,9},{9,8},{10,11... | collective-permute-start | bytes 860168 | tf_op jit(solution)/shard_map/ppermute | solution.py:431
  17.6 1.6 %collective-permute-start.8 = (bf16[160,896]{1,0:T(8,128)(2,1)S(1)}, bf16[160,896]{1,0:T(8,128)(2,1)S(1)}, u32[]{:S(2)}, u32[]{:S(2)}) collective-permute-start(bf16[160,896]{1,0:T(8,128)(2,1)S(1)} %join.3.refs_0_), channel_id=1, source_target_pairs={{0,1},{1,0},{2,3},{3,2},{4,5},{5,4},{6,7},{7,6},{8,9},{9,8},{10,11... | collective-permute-start | bytes 860168 | tf_op jit(solution)/shard_map/ppermute | solution.py:435
  21.6 1.6 %collective-permute-start.9 = (bf16[160,896]{1,0:T(8,128)(2,1)S(1)}, bf16[160,896]{1,0:T(8,128)(2,1)S(1)}, u32[]{:S(2)}, u32[]{:S(2)}) collective-permute-start(bf16[160,896]{1,0:T(8,128)(2,1)S(1)} %get-tuple-element.42), channel_id=1, source_target_pairs={{0,1},{1,0},{2,3},{3,2},{4,5},{5,4},{6,7},{7,6},{8,9},{9,8},{10,11... | collective-permute-start | bytes 860168 | tf_op jit(solution)/shard_map/ppermute | solution.py:437
  21.8 5.1 %collective-permute-start.10 = (bf16[160,896]{1,0:T(8,128)(2,1)S(1)}, bf16[160,896]{1,0:T(8,128)(2,1)S(1)}, u32[]{:S(2)}, u32[]{:S(2)}) collective-permute-start(bf16[160,896]{1,0:T(8,128)(2,1)S(1)} %get-tuple-element.48), channel_id=1, source_target_pairs={{0,1},{1,0},{2,3},{3,2},{4,5},{5,4},{6,7},{7,6},{8,9},{9,8},{10,11... | collective-permute-start | bytes 860168 | tf_op jit(solution)/shard_map/ppermute | solution.py:437
  23.3 6.1 %collective-permute-start.14 = (bf16[40,896]{1,0:T(8,128)(2,1)S(1)}, bf16[40,896]{1,0:T(8,128)(2,1)S(1)}, u32[]{:S(2)}, u32[]{:S(2)}) collective-permute-start(bf16[40,896]{1,0:T(8,128)(2,1)S(1)} %get-tuple-element.54), channel_id=1, source_target_pairs={{0,6},{1,7},{2,4},{3,5},{4,2},{5,3},{6,0},{7,1},{8,14},{9,15},{10,... | collective-permute-start | bytes 215048 | tf_op jit(solution)/shard_map/ppermute | solution.py:445
  25.1 5.4 %collective-permute-start.15 = (bf16[40,896]{1,0:T(8,128)(2,1)S(1)}, bf16[40,896]{1,0:T(8,128)(2,1)S(1)}, u32[]{:S(2)}, u32[]{:S(2)}) collective-permute-start(bf16[40,896]{1,0:T(8,128)(2,1)S(1)} %get-tuple-element.55), channel_id=1, source_target_pairs={{0,4},{1,5},{2,6},{3,7},{4,0},{5,1},{6,2},{7,3},{8,12},{9,13},{10,... | collective-permute-start | bytes 215048 | tf_op jit(solution)/shard_map/ppermute | solution.py:445
  25.8 4.8 %collective-permute-start.16 = (bf16[40,896]{1,0:T(8,128)(2,1)S(1)}, bf16[40,896]{1,0:T(8,128)(2,1)S(1)}, u32[]{:S(2)}, u32[]{:S(2)}) collective-permute-start(bf16[40,896]{1,0:T(8,128)(2,1)S(1)} %get-tuple-element.56), channel_id=1, source_target_pairs={{0,2},{1,3},{2,0},{3,1},{4,6},{5,7},{6,4},{7,5},{8,10},{9,11},{10,... | collective-permute-start | bytes 215048 | tf_op jit(solution)/shard_map/ppermute | solution.py:445
  26.9 6.1 %collective-permute-start.11 = (bf16[40,896]{1,0:T(8,128)(2,1)S(1)}, bf16[40,896]{1,0:T(8,128)(2,1)S(1)}, u32[]{:S(2)}, u32[]{:S(2)}) collective-permute-start(bf16[40,896]{1,0:T(8,128)(2,1)S(1)} %get-tuple-element.50), channel_id=1, source_target_pairs={{0,6},{1,7},{2,4},{3,5},{4,2},{5,3},{6,0},{7,1},{8,14},{9,15},{10,... | collective-permute-start | bytes 215048 | tf_op jit(solution)/shard_map/ppermute | solution.py:451
  28.7 4.3 %collective-permute-start.12 = (bf16[40,896]{1,0:T(8,128)(2,1)S(1)}, bf16[40,896]{1,0:T(8,128)(2,1)S(1)}, u32[]{:S(2)}, u32[]{:S(2)}) collective-permute-start(bf16[40,896]{1,0:T(8,128)(2,1)S(1)} %get-tuple-element.51), channel_id=1, source_target_pairs={{0,4},{1,5},{2,6},{3,7},{4,0},{5,1},{6,2},{7,3},{8,12},{9,13},{10,... | collective-permute-start | bytes 215048 | tf_op jit(solution)/shard_map/ppermute | solution.py:451
  29.4 4.3 %collective-permute-start.13 = (bf16[40,896]{1,0:T(8,128)(2,1)S(1)}, bf16[40,896]{1,0:T(8,128)(2,1)S(1)}, u32[]{:S(2)}, u32[]{:S(2)}) collective-permute-start(bf16[40,896]{1,0:T(8,128)(2,1)S(1)} %get-tuple-element.52), channel_id=1, source_target_pairs={{0,2},{1,3},{2,0},{3,1},{4,6},{5,7},{6,4},{7,5},{8,10},{9,11},{10,... | collective-permute-start | bytes 215048 | tf_op jit(solution)/shard_map/ppermute | solution.py:451
  30.6 5.4 %collective-permute-start.17 = (bf16[40,896]{1,0:T(8,128)(2,1)S(1)}, bf16[40,896]{1,0:T(8,128)(2,1)S(1)}, u32[]{:S(2)}, u32[]{:S(2)}) collective-permute-start(bf16[40,896]{1,0:T(8,128)(2,1)S(1)} %sum_blocks.1), channel_id=1, source_target_pairs={{0,8},{1,9},{2,10},{3,11},{4,12},{5,13},{6,14},{7,15},{8,0},{9,1},... | collective-permute-start | bytes 215048 | tf_op jit(solution)/shard_map/ppermute | solution.py:447

commit v16 on v15

--- a/solution.py
+++ b/solution.py
@@ -225,9 +225,9 @@
 
 
 def expert_kernel(teams, first_ref, *refs):
-    pieces = refs[: 2 * (teams - 1)]
-    gate_ref, up_ref, down_ref = refs[2 * (teams - 1) : 2 * teams + 1]
-    *given_refs, hidden_ref, packed, flat, out, act = refs[2 * teams + 1 :]
+    pieces = refs[: 4 * (teams - 1)]
+    gate_ref, up_ref, down_ref = refs[4 * (teams - 1) : 4 * teams - 1]
+    *given_refs, hidden_ref, packed, flat, out, act = refs[4 * teams - 1 :]
     tall = CAP * SEGMENTS
     wide = packed.shape[1]
     units = gate_ref.shape[1]
@@ -266,8 +266,8 @@
 
 
 def expert_half(first, pieces, w_gate, w_up, w_down):
-    teams = 1 + len(pieces) // 2
-    block, wide = pieces[0].shape
+    teams = 1 + len(pieces) // 4
+    block, wide = first.shape[0] // 2 * SEGMENTS, pieces[0].shape[1]
     features, units = w_gate.shape
     rows = first.shape[0] * teams
     return pl.pallas_call(
@@ -277,7 +277,7 @@
         in_specs=[VMEM] * (len(pieces) + 4),
         out_specs=[VMEM] * (teams + 1),
         scratch_shapes=[
-            pltpu.VMEM((block * len(pieces), wide), jnp.float32),
+            pltpu.VMEM((2 * block * (teams - 1), wide), jnp.float32),
             pltpu.VMEM((2, rows, wide), jnp.float32),
             pltpu.VMEM((block * teams, wide), jnp.float32),
             pltpu.VMEM((2 * rows, units), jnp.float32),
@@ -429,10 +429,12 @@
     own, weights = lax.optimization_barrier((own, weights))
     own = join(own)
     first = unpack(own, lax.ppermute(own, "expert", other_core))
+    order = [0, *reversed(range(1, chips))]
     pieces = []
     for crowd in crowds:
-        crowd = join(crowd)
-        pieces += [crowd, lax.ppermute(crowd, "expert", other_core)]
+        early, late = join([crowd[m] for m in order[:-1]]), crowd[order[-1]]
+        pieces += [early, late]
+        pieces += [lax.ppermute(piece, "expert", other_core) for piece in (early, late)]
     *given, hidden = expert_half(first, pieces, w_gate, w_up, w_down)
     taken = [lax.ppermute(piece, "expert", other_core) for piece in given]
     kept = kept_half(hidden, w_down)
@@ -441,8 +443,8 @@
         parts = add_cores(kept, taken[k], k, chips)
         parts, later = lax.optimization_barrier((parts, kept))
         team = [parts[0]]
-        for m in reversed(range(1, chips)):
-            team.append(lax.ppermute(parts[m], "expert", other_chip[m]))
+        for m, part in zip(order[1:], parts[1:]):
+            team.append(lax.ppermute(part, "expert", other_chip[m]))
         pairs = [(i, (i - k * SPLIT) % devices) for i in range(devices)]
         others.append(lax.ppermute(sum_blocks(team), "expert", pairs))
     parts = add_cores(later, taken[0], 0, chips)

time: 37.4 us -> 45.1 us (1.21)
  waiting for transfers between devices: 6.85 us -> 16.3 us
  starting transfers between devices: 22.1 us -> 20.1 us
    ppermute x6, waiting for transfers between devices: 2.24 us -> 11.4 us  [gather(): lax.ppermute(block, 'expert', other_chip[m])]
    ppermute x6, starting transfers between devices: 7.81 us -> 6.59 us  [gather(): lax.ppermute(block, 'expert', other_chip[m])]
    ppermute x1, starting transfers between devices: 2.4 us -> 1.72 us  [body(): others.append(lax.ppermute(sum_blocks(team), 'expert', pairs))]
    ppermute x3, waiting for transfers between devices: 0.75 us -> 1.39 us  [body(): own.append(lax.ppermute(parts[m], 'expert', other_chip[m]))]
    ppermute x4 -> x5, waiting for transfers between devices: 1.27 us -> 1.01 us  [the longest x2 0.91 us: body(): lax.ppermute(piece, 'expert', other_core)]
    ppermute x4 -> x5, starting transfers between devices: 3.62 us -> 3.63 us  [the longest x3 3.55 us: body(): team.append(lax.ppermute(part, 'expert', other_chip[m]))]
  transfers between devices with their start and end apart: 18 -> 19, of which waited for: 9 -> 13; matrix products, arithmetic and copies ran while one was open for 0% -> 0% of each run, Pallas kernels for 4% -> 4%
where the time goes in v16:
time: 45.1 us; the launch traced here: 44.9 us
  starting transfers between devices  20.1 us (45%)
  waiting for transfers between devices  16.3 us (36%)
  Pallas kernels  7.63 us (17%)
  local copies, waits for them, and re-layouts  0.71 us (2%)
    ppermute x6, waiting for transfers between devices, gather(): lax.ppermute(block, 'expert', other_chip[m])  11.4 us
    ppermute x6, starting transfers between devices, gather(): lax.ppermute(block, 'expert', other_chip[m])  6.59 us
    ppermute x1, starting transfers between devices, body(): block = lax.ppermute(packed[k], 'expert', pairs)  4.1 us
    ppermute x3, starting transfers between devices, body(): team.append(lax.ppermute(part, 'expert', other_chip[m]))  3.55 us
    ppermute x3, starting transfers between devices, body(): own.append(lax.ppermute(parts[m], 'expert', other_chip[m]))  3.46 us
    pallas_call x1, Pallas kernels, expert_half(): pl.pallas_call(functools.partial(expert_kernel, teams), out_shape=[jax.Sh...  2.5 us
    pallas_call x1, Pallas kernels, pack_rows(): pl.pallas_call(functools.partial(pack_kernel, teams), out_shape=[block] *...  2.27 us
    ppermute x1, waiting for transfers between devices, body(): others.append(lax.ppermute(sum_blocks(team), 'expert', pairs))  2.19 us
  transfers between devices with their start and end apart: 19, of which 13 were waited for; matrix products, arithmetic and copies ran while one was open for 0% of the time, Pallas kernels for 4%

profile of v16, /device:TPU:0, one launch (start us, length us, event | category | flops | bytes accessed | tf_op | source)
XLA Modules:
  0.0 44.9 jit_solution(5594998048443316000)
XLA Ops:
  0.0 2.3 %pack_rows.1 = (bf16[40,896]{1,0:T(8,128)(2,1)}, bf16[40,896]{1,0:T(8,128)(2,1)}, f32[16,64]{1,0:T(8,128)}) custom-call(s32[8,64]{1,0:T(8,128)} %bitcast.2, f32[8,64]{1,0:T(8,128)} %bitcast.3, bf16[64,7168]{1,0:T(8,128)(2,1)} %tokens_hbm.1), custom_call_target="tpu_custom_call" | custom-call | tf_op jit(solution)/shard_map/pack_rows/pallas_call | solution.py:110
  2.3 4.1 %collective-permute-start.3 = (bf16[40,896]{1,0:T(8,128)(2,1)}, bf16[40,896]{1,0:T(8,128)(2,1)S(1)}, u32[]{:S(2)}, u32[]{:S(2)}) collective-permute-start(bf16[40,896]{1,0:T(8,128)(2,1)} %get-tuple-element.32), channel_id=1, source_target_pairs={{0,8},{1,9},{2,10},{3,11},{4,12},{5,13},{6,14},{7,15},{8,0},{9,1},... | collective-permute-start | bytes 215048 | tf_op jit(solution)/shard_map/ppermute | solution.py:424
  6.4 2.5 %collective-permute-start.2 = (bf16[40,896]{1,0:T(8,128)(2,1)}, bf16[40,896]{1,0:T(8,128)(2,1)S(1)}, u32[]{:S(2)}, u32[]{:S(2)}) collective-permute-start(bf16[40,896]{1,0:T(8,128)(2,1)} %get-tuple-element.36.refs_0_), channel_id=1, source_target_pairs={{0,6},{1,7},{2,4},{3,5},{4,2},{5,3},{6,0},{7,1},{8,14},{9,15},{10,... | collective-permute-start | bytes 215048 | tf_op jit(solution)/shard_map/ppermute | solution.py:418
  8.9 0.4 collective-permute-start.1
  9.4 0.5 %collective-permute-start = (bf16[40,896]{1,0:T(8,128)(2,1)}, bf16[40,896]{1,0:T(8,128)(2,1)S(1)}, u32[]{:S(2)}, u32[]{:S(2)}) collective-permute-start(bf16[40,896]{1,0:T(8,128)(2,1)} %get-tuple-element.36.refs_0_), channel_id=1, source_target_pairs={{0,2},{1,3},{2,0},{3,1},{4,6},{5,7},{6,4},{7,5},{8,10},{9,11},{10,... | collective-permute-start | bytes 215048 | tf_op jit(solution)/shard_map/ppermute | solution.py:418
  9.9 0.0 collective-permute-done.3.refs_0_
  9.9 0.7 %copy-done.4 = f32[16,64]{1,0:T(8,128)S(1)} copy-done((f32[16,64]{1,0:T(8,128)S(1)}, f32[16,64]{1,0:T(8,128)}, u32[]{:S(2)}) %copy-start.4) | copy-done | bytes 4120
  10.6 0.3 blend_weights.1.weight_ref
  10.9 1.8 %collective-permute-done.2.refs_3_ = bf16[40,896]{1,0:T(8,128)(2,1)S(1)} collective-permute-done((bf16[40,896]{1,0:T(8,128)(2,1)}, bf16[40,896]{1,0:T(8,128)(2,1)S(1)}, u32[]{:S(2)}, u32[]{:S(2)}) %collective-permute-start.2) | collective-permute-done | bytes 71712 | tf_op jit(solution)/shard_map/ppermute | solution.py:418
  12.7 0.8 %collective-permute-done.1.refs_2_ = bf16[40,896]{1,0:T(8,128)(2,1)S(1)} collective-permute-done((bf16[40,896]{1,0:T(8,128)(2,1)}, bf16[40,896]{1,0:T(8,128)(2,1)S(1)}, u32[]{:S(2)}, u32[]{:S(2)}) %collective-permute-start.1) | collective-permute-done | bytes 71712 | tf_op jit(solution)/shard_map/ppermute | solution.py:418
  13.5 0.4 collective-permute-done.refs_1_
  13.9 0.0 copy-done.3
  13.9 0.1 collective-permute-start.4
  14.0 1.6 %collective-permute-start.6 = (bf16[40,896]{1,0:T(8,128)(2,1)S(1)}, bf16[40,896]{1,0:T(8,128)(2,1)S(1)}, u32[]{:S(2)}, u32[]{:S(2)}) collective-permute-start(bf16[40,896]{1,0:T(8,128)(2,1)S(1)} %collective-permute-done.3.refs_0_), channel_id=1, source_target_pairs={{0,4},{1,5},{2,6},{3,7},{4,0},{5,1},{6,2},{7,3},{8,12},{9,13},{10,... | collective-permute-start | bytes 215048 | tf_op jit(solution)/shard_map/ppermute | solution.py:418
  15.7 0.6 %collective-permute-start.5 = (bf16[40,896]{1,0:T(8,128)(2,1)S(1)}, bf16[40,896]{1,0:T(8,128)(2,1)S(1)}, u32[]{:S(2)}, u32[]{:S(2)}) collective-permute-start(bf16[40,896]{1,0:T(8,128)(2,1)S(1)} %collective-permute-done.3.refs_0_), channel_id=1, source_target_pairs={{0,6},{1,7},{2,4},{3,5},{4,2},{5,3},{6,0},{7,1},{8,14},{9,15},{10,... | collective-permute-start | bytes 215048 | tf_op jit(solution)/shard_map/ppermute | solution.py:418
  16.3 2.7 %collective-permute-done.6.refs_2_ = bf16[40,896]{1,0:T(8,128)(2,1)S(1)} collective-permute-done((bf16[40,896]{1,0:T(8,128)(2,1)S(1)}, bf16[40,896]{1,0:T(8,128)(2,1)S(1)}, u32[]{:S(2)}, u32[]{:S(2)}) %collective-permute-start.6) | collective-permute-done | bytes 71712 | tf_op jit(solution)/shard_map/ppermute | solution.py:418
  19.0 1.9 %collective-permute-done.5.refs_1_ = bf16[40,896]{1,0:T(8,128)(2,1)S(1)} collective-permute-done((bf16[40,896]{1,0:T(8,128)(2,1)S(1)}, bf16[40,896]{1,0:T(8,128)(2,1)S(1)}, u32[]{:S(2)}, u32[]{:S(2)}) %collective-permute-start.5) | collective-permute-done | bytes 71712 | tf_op jit(solution)/shard_map/ppermute | solution.py:418
  20.9 0.1 collective-permute-start.8
  21.0 0.8 %collective-permute-start.7 = (bf16[40,896]{1,0:T(8,128)(2,1)S(1)}, bf16[40,896]{1,0:T(8,128)(2,1)S(1)}, u32[]{:S(2)}, u32[]{:S(2)}) collective-permute-start(bf16[40,896]{1,0:T(8,128)(2,1)S(1)} %collective-permute-done.3.refs_0_), channel_id=1, source_target_pairs={{0,2},{1,3},{2,0},{3,1},{4,6},{5,7},{6,4},{7,5},{8,10},{9,11},{10,... | collective-permute-start | bytes 215048 | tf_op jit(solution)/shard_map/ppermute | solution.py:418
  21.8 3.8 %collective-permute-done.7.refs_1_ = bf16[40,896]{1,0:T(8,128)(2,1)S(1)} collective-permute-done((bf16[40,896]{1,0:T(8,128)(2,1)S(1)}, bf16[40,896]{1,0:T(8,128)(2,1)S(1)}, u32[]{:S(2)}, u32[]{:S(2)}) %collective-permute-start.7) | collective-permute-done | bytes 71712 | tf_op jit(solution)/shard_map/ppermute | solution.py:418
  25.6 0.0 collective-permute-start.9
  25.6 0.0 collective-permute-done.4.other_ref
  25.6 0.3 unpack.1.first_ref
  26.0 0.9 %collective-permute-done.9.refs_3_ = bf16[40,896]{1,0:T(8,128)(2,1)S(1)} collective-permute-done((bf16[40,896]{1,0:T(8,128)(2,1)S(1)}, bf16[40,896]{1,0:T(8,128)(2,1)S(1)}, u32[]{:S(2)}, u32[]{:S(2)}) %collective-permute-start.9) | collective-permute-done | bytes 71712 | tf_op jit(solution)/shard_map/ppermute | solution.py:437
  26.9 0.0 collective-permute-done.8.refs_2_
  26.9 2.5 %expert_half.1 = (bf16[160,896]{1,0:T(8,128)(2,1)S(1)}, bf16[160,896]{1,0:T(8,128)(2,1)S(1)}, bf16[40,256]{1,0:T(8,128)(2,1)S(1)}) custom-call(f32[40,7168]{1,0:T(8,128)S(1)} %unpack.1.first_ref, bf16[120,896]{1,0:T(8,128)(2,1)S(1)} %join.3.refs_0_, bf16[40,896]{1,0:T(8,128)(2,1)S(1)} %collective-permute-done.7.refs_1_, ...), custom_call_target="tpu_custom_call" | custom-call | flops 734003200 | bytes 11010048 | tf_op jit(solution)/shard_map/expert_half/pallas_call | solution.py:273
  29.4 0.2 collective-permute-start.10
  29.6 0.4 collective-permute-start.11
  30.0 0.8 %kept_half.1.kept_ref = f32[320,896]{1,0:T(8,128)S(1)} custom-call(bf16[40,256]{1,0:T(8,128)(2,1)S(1)} %get-tuple-element.41.hidden_ref, bf16[256,7168]{1,0:T(8,128)(2,1)S(1)} %copy-done), custom_call_target="tpu_custom_call" | custom-call | flops 146800640 | bytes 3670016 | tf_op jit(solution)/shard_map/kept_half/pallas_call | solution.py:303
  30.8 0.3 collective-permute-done.10.taken_ref
  31.1 0.1 add_cores.2
  31.1 1.8 %collective-permute-start.15 = (bf16[40,896]{1,0:T(8,128)(2,1)S(1)}, bf16[40,896]{1,0:T(8,128)(2,1)S(1)}, u32[]{:S(2)}, u32[]{:S(2)}) collective-permute-start(bf16[40,896]{1,0:T(8,128)(2,1)S(1)} %get-tuple-element.54), channel_id=1, source_target_pairs={{0,6},{1,7},{2,4},{3,5},{4,2},{5,3},{6,0},{7,1},{8,14},{9,15},{10,... | collective-permute-start | bytes 215048 | tf_op jit(solution)/shard_map/ppermute | solution.py:447
  33.0 0.4 collective-permute-start.16
  33.4 1.3 %collective-permute-start.17 = (bf16[40,896]{1,0:T(8,128)(2,1)S(1)}, bf16[40,896]{1,0:T(8,128)(2,1)S(1)}, u32[]{:S(2)}, u32[]{:S(2)}) collective-permute-start(bf16[40,896]{1,0:T(8,128)(2,1)S(1)} %get-tuple-element.56), channel_id=1, source_target_pairs={{0,2},{1,3},{2,0},{3,1},{4,6},{5,7},{6,4},{7,5},{8,10},{9,11},{10,... | collective-permute-start | bytes 215048 | tf_op jit(solution)/shard_map/ppermute | solution.py:447
  34.7 0.0 collective-permute-done.11.taken_ref
  34.7 0.1 add_cores.3
  34.7 1.8 %collective-permute-start.12 = (bf16[40,896]{1,0:T(8,128)(2,1)S(1)}, bf16[40,896]{1,0:T(8,128)(2,1)S(1)}, u32[]{:S(2)}, u32[]{:S(2)}) collective-permute-start(bf16[40,896]{1,0:T(8,128)(2,1)S(1)} %get-tuple-element.50), channel_id=1, source_target_pairs={{0,6},{1,7},{2,4},{3,5},{4,2},{5,3},{6,0},{7,1},{8,14},{9,15},{10,... | collective-permute-start | bytes 215048 | tf_op jit(solution)/shard_map/ppermute | solution.py:453
  36.6 0.4 collective-permute-start.13
  37.0 0.1 collective-permute-done.15.refs_1_
  37.1 1.2 %collective-permute-start.14 = (bf16[40,896]{1,0:T(8,128)(2,1)S(1)}, bf16[40,896]{1,0:T(8,128)(2,1)S(1)}, u32[]{:S(2)}, u32[]{:S(2)}) collective-permute-start(bf16[40,896]{1,0:T(8,128)(2,1)S(1)} %get-tuple-element.52), channel_id=1, source_target_pairs={{0,2},{1,3},{2,0},{3,1},{4,6},{5,7},{6,4},{7,5},{8,10},{9,11},{10,... | collective-permute-start | bytes 215048 | tf_op jit(solution)/shard_map/ppermute | solution.py:453
  38.3 0.0 collective-permute-done.16.refs_2_
  38.3 0.0 collective-permute-done.17.refs_3_
  38.4 1.7 %collective-permute-start.18 = (bf16[40,896]{1,0:T(8,128)(2,1)S(1)}, bf16[40,896]{1,0:T(8,128)(2,1)S(1)}, u32[]{:S(2)}, u32[]{:S(2)}) collective-permute-start(bf16[40,896]{1,0:T(8,128)(2,1)S(1)} %sum_blocks.1), channel_id=1, source_target_pairs={{0,8},{1,9},{2,10},{3,11},{4,12},{5,13},{6,14},{7,15},{8,0},{9,1},... | collective-permute-start | bytes 215048 | tf_op jit(solution)/shard_map/ppermute | solution.py:449
  40.1 0.1 collective-permute-done.12.refs_1_
  40.2 0.7 %collective-permute-done.13.refs_2_ = bf16[40,896]{1,0:T(8,128)(2,1)S(1)} collective-permute-done((bf16[40,896]{1,0:T(8,128)(2,1)S(1)}, bf16[40,896]{1,0:T(8,128)(2,1)S(1)}, u32[]{:S(2)}, u32[]{:S(2)}) %collective-permute-start.13) | collective-permute-done | bytes 71712 | tf_op jit(solution)/shard_map/ppermute | solution.py:453
  40.9 0.5 %collective-permute-done.14.refs_3_ = bf16[40,896]{1,0:T(8,128)(2,1)S(1)} collective-permute-done((bf16[40,896]{1,0:T(8,128)(2,1)S(1)}, bf16[40,896]{1,0:T(8,128)(2,1)S(1)}, u32[]{:S(2)}, u32[]{:S(2)}) %collective-permute-start.14) | collective-permute-done | bytes 71712 | tf_op jit(solution)/shard_map/ppermute | solution.py:453
  41.5 2.2 %collective-permute-done.18.refs_4_ = bf16[40,896]{1,0:T(8,128)(2,1)S(1)} collective-permute-done((bf16[40,896]{1,0:T(8,128)(2,1)S(1)}, bf16[40,896]{1,0:T(8,128)(2,1)S(1)}, u32[]{:S(2)}, u32[]{:S(2)}) %collective-permute-start.18) | collective-permute-done | bytes 71712 | tf_op jit(solution)/shard_map/ppermute | solution.py:449
  43.7 1.2 %blend.1 = bf16[64,7168]{1,0:T(8,128)(2,1)} custom-call(bf16[512,200]{1,0:T(8,128)(2,1)S(1)} %blend_weights.1.weight_ref, f32[40,896]{1,0:T(8,128)S(1)} %get-tuple-element.49.refs_0_, bf16[40,896]{1,0:T(8,128)(2,1)S(1)} %collective-permute-done.12.refs_1_, bf16[40,896]{1,0:T(8,128)(2,1)S(1)} %collective-permute-done.13.refs_2_, ...), custom_call_target="tpu_custom_call" | custom-call | tf_op jit(solution)/shard_map/blend/pallas_call | solution.py:396
  (11 shorter events, 0.1 us)
Async XLA Ops:
  2.3 7.6 %collective-permute-start.3 = (bf16[40,896]{1,0:T(8,128)(2,1)}, bf16[40,896]{1,0:T(8,128)(2,1)S(1)}, u32[]{:S(2)}, u32[]{:S(2)}) collective-permute-start(bf16[40,896]{1,0:T(8,128)(2,1)} %get-tuple-element.32), channel_id=1, source_target_pairs={{0,8},{1,9},{2,10},{3,11},{4,12},{5,13},{6,14},{7,15},{8,0},{9,1},... | collective-permute-start | bytes 215048 | tf_op jit(solution)/shard_map/ppermute | solution.py:424
  6.4 6.3 %collective-permute-start.2 = (bf16[40,896]{1,0:T(8,128)(2,1)}, bf16[40,896]{1,0:T(8,128)(2,1)S(1)}, u32[]{:S(2)}, u32[]{:S(2)}) collective-permute-start(bf16[40,896]{1,0:T(8,128)(2,1)} %get-tuple-element.36.refs_0_), channel_id=1, source_target_pairs={{0,6},{1,7},{2,4},{3,5},{4,2},{5,3},{6,0},{7,1},{8,14},{9,15},{10,... | collective-permute-start | bytes 215048 | tf_op jit(solution)/shard_map/ppermute | solution.py:418
  8.9 4.5 %collective-permute-start.1 = (bf16[40,896]{1,0:T(8,128)(2,1)}, bf16[40,896]{1,0:T(8,128)(2,1)S(1)}, u32[]{:S(2)}, u32[]{:S(2)}) collective-permute-start(bf16[40,896]{1,0:T(8,128)(2,1)} %get-tuple-element.36.refs_0_), channel_id=1, source_target_pairs={{0,4},{1,5},{2,6},{3,7},{4,0},{5,1},{6,2},{7,3},{8,12},{9,13},{10,... | collective-permute-start | bytes 215048 | tf_op jit(solution)/shard_map/ppermute | solution.py:418
  9.4 4.5 %collective-permute-start = (bf16[40,896]{1,0:T(8,128)(2,1)}, bf16[40,896]{1,0:T(8,128)(2,1)S(1)}, u32[]{:S(2)}, u32[]{:S(2)}) collective-permute-start(bf16[40,896]{1,0:T(8,128)(2,1)} %get-tuple-element.36.refs_0_), channel_id=1, source_target_pairs={{0,2},{1,3},{2,0},{3,1},{4,6},{5,7},{6,4},{7,5},{8,10},{9,11},{10,... | collective-permute-start | bytes 215048 | tf_op jit(solution)/shard_map/ppermute | solution.py:418
  9.9 0.7 %copy-start.4 = (f32[16,64]{1,0:T(8,128)S(1)}, f32[16,64]{1,0:T(8,128)}, u32[]{:S(2)}) copy-start(f32[16,64]{1,0:T(8,128)} %get-tuple-element.34.table_ref) | copy-start | bytes 12292
  10.6 3.3 %copy-start.3 = (bf16[40,896]{1,0:T(8,128)(2,1)S(1)}, bf16[40,896]{1,0:T(8,128)(2,1)}, u32[]{:S(2)}) copy-start(bf16[40,896]{1,0:T(8,128)(2,1)} %get-tuple-element.36.refs_0_) | copy-start | bytes 215044
  10.6 16.3 %copy-start = (bf16[256,7168]{1,0:T(8,128)(2,1)S(1)}, bf16[256,7168]{1,0:T(8,128)(2,1)}, u32[]{:S(2)}) copy-start(bf16[256,7168]{1,0:T(8,128)(2,1)} %down_ref.1) | copy-start | bytes 11010052
  10.6 16.3 %copy-start.1 = (bf16[7168,256]{1,0:T(8,128)(2,1)S(1)}, bf16[7168,256]{1,0:T(8,128)(2,1)}, u32[]{:S(2)}) copy-start(bf16[7168,256]{1,0:T(8,128)(2,1)} %refs_4_.1) | copy-start | bytes 11010052
  10.6 16.3 %copy-start.2 = (bf16[7168,256]{1,0:T(8,128)(2,1)S(1)}, bf16[7168,256]{1,0:T(8,128)(2,1)}, u32[]{:S(2)}) copy-start(bf16[7168,256]{1,0:T(8,128)(2,1)} %refs_5_.1) | copy-start | bytes 11010052
  13.9 11.7 %collective-permute-start.4 = (bf16[160,896]{1,0:T(8,128)(2,1)S(1)}, bf16[160,896]{1,0:T(8,128)(2,1)S(1)}, u32[]{:S(2)}, u32[]{:S(2)}) collective-permute-start(bf16[160,896]{1,0:T(8,128)(2,1)S(1)} %join.2.own_ref), channel_id=1, source_target_pairs={{0,1},{1,0},{2,3},{3,2},{4,5},{5,4},{6,7},{7,6},{8,9},{9,8},{10,11... | collective-permute-start | bytes 860168 | tf_op jit(solution)/shard_map/ppermute | solution.py:431
  14.0 5.0 %collective-permute-start.6 = (bf16[40,896]{1,0:T(8,128)(2,1)S(1)}, bf16[40,896]{1,0:T(8,128)(2,1)S(1)}, u32[]{:S(2)}, u32[]{:S(2)}) collective-permute-start(bf16[40,896]{1,0:T(8,128)(2,1)S(1)} %collective-permute-done.3.refs_0_), channel_id=1, source_target_pairs={{0,4},{1,5},{2,6},{3,7},{4,0},{5,1},{6,2},{7,3},{8,12},{9,13},{10,... | collective-permute-start | bytes 215048 | tf_op jit(solution)/shard_map/ppermute | solution.py:418
  15.7 5.2 %collective-permute-start.5 = (bf16[40,896]{1,0:T(8,128)(2,1)S(1)}, bf16[40,896]{1,0:T(8,128)(2,1)S(1)}, u32[]{:S(2)}, u32[]{:S(2)}) collective-permute-start(bf16[40,896]{1,0:T(8,128)(2,1)S(1)} %collective-permute-done.3.refs_0_), channel_id=1, source_target_pairs={{0,6},{1,7},{2,4},{3,5},{4,2},{5,3},{6,0},{7,1},{8,14},{9,15},{10,... | collective-permute-start | bytes 215048 | tf_op jit(solution)/shard_map/ppermute | solution.py:418
  20.9 6.0 %collective-permute-start.8 = (bf16[120,896]{1,0:T(8,128)(2,1)S(1)}, bf16[120,896]{1,0:T(8,128)(2,1)S(1)}, u32[]{:S(2)}, u32[]{:S(2)}) collective-permute-start(bf16[120,896]{1,0:T(8,128)(2,1)S(1)} %join.3.refs_0_), channel_id=1, source_target_pairs={{0,1},{1,0},{2,3},{3,2},{4,5},{5,4},{6,7},{7,6},{8,9},{9,8},{10,11... | collective-permute-start | bytes 645128 | tf_op jit(solution)/shard_map/ppermute | solution.py:437
  21.0 4.6 %collective-permute-start.7 = (bf16[40,896]{1,0:T(8,128)(2,1)S(1)}, bf16[40,896]{1,0:T(8,128)(2,1)S(1)}, u32[]{:S(2)}, u32[]{:S(2)}) collective-permute-start(bf16[40,896]{1,0:T(8,128)(2,1)S(1)} %collective-permute-done.3.refs_0_), channel_id=1, source_target_pairs={{0,2},{1,3},{2,0},{3,1},{4,6},{5,7},{6,4},{7,5},{8,10},{9,11},{10,... | collective-permute-start | bytes 215048 | tf_op jit(solution)/shard_map/ppermute | solution.py:418
  25.6 1.3 %collective-permute-start.9 = (bf16[40,896]{1,0:T(8,128)(2,1)S(1)}, bf16[40,896]{1,0:T(8,128)(2,1)S(1)}, u32[]{:S(2)}, u32[]{:S(2)}) collective-permute-start(bf16[40,896]{1,0:T(8,128)(2,1)S(1)} %collective-permute-done.7.refs_1_), channel_id=1, source_target_pairs={{0,1},{1,0},{2,3},{3,2},{4,5},{5,4},{6,7},{7,6},{8,9},{9,8},{10,11... | collective-permute-start | bytes 215048 | tf_op jit(solution)/shard_map/ppermute | solution.py:437
  29.4 1.6 %collective-permute-start.10 = (bf16[160,896]{1,0:T(8,128)(2,1)S(1)}, bf16[160,896]{1,0:T(8,128)(2,1)S(1)}, u32[]{:S(2)}, u32[]{:S(2)}) collective-permute-start(bf16[160,896]{1,0:T(8,128)(2,1)S(1)} %get-tuple-element.42), channel_id=1, source_target_pairs={{0,1},{1,0},{2,3},{3,2},{4,5},{5,4},{6,7},{7,6},{8,9},{9,8},{10,11... | collective-permute-start | bytes 860168 | tf_op jit(solution)/shard_map/ppermute | solution.py:439
  29.6 5.1 %collective-permute-start.11 = (bf16[160,896]{1,0:T(8,128)(2,1)S(1)}, bf16[160,896]{1,0:T(8,128)(2,1)S(1)}, u32[]{:S(2)}, u32[]{:S(2)}) collective-permute-start(bf16[160,896]{1,0:T(8,128)(2,1)S(1)} %get-tuple-element.48), channel_id=1, source_target_pairs={{0,1},{1,0},{2,3},{3,2},{4,5},{5,4},{6,7},{7,6},{8,9},{9,8},{10,11... | collective-permute-start | bytes 860168 | tf_op jit(solution)/shard_map/ppermute | solution.py:439
  31.1 6.0 %collective-permute-start.15 = (bf16[40,896]{1,0:T(8,128)(2,1)S(1)}, bf16[40,896]{1,0:T(8,128)(2,1)S(1)}, u32[]{:S(2)}, u32[]{:S(2)}) collective-permute-start(bf16[40,896]{1,0:T(8,128)(2,1)S(1)} %get-tuple-element.54), channel_id=1, source_target_pairs={{0,6},{1,7},{2,4},{3,5},{4,2},{5,3},{6,0},{7,1},{8,14},{9,15},{10,... | collective-permute-start | bytes 215048 | tf_op jit(solution)/shard_map/ppermute | solution.py:447
  33.0 5.3 %collective-permute-start.16 = (bf16[40,896]{1,0:T(8,128)(2,1)S(1)}, bf16[40,896]{1,0:T(8,128)(2,1)S(1)}, u32[]{:S(2)}, u32[]{:S(2)}) collective-permute-start(bf16[40,896]{1,0:T(8,128)(2,1)S(1)} %get-tuple-element.55), channel_id=1, source_target_pairs={{0,4},{1,5},{2,6},{3,7},{4,0},{5,1},{6,2},{7,3},{8,12},{9,13},{10,... | collective-permute-start | bytes 215048 | tf_op jit(solution)/shard_map/ppermute | solution.py:447
  33.4 4.9 %collective-permute-start.17 = (bf16[40,896]{1,0:T(8,128)(2,1)S(1)}, bf16[40,896]{1,0:T(8,128)(2,1)S(1)}, u32[]{:S(2)}, u32[]{:S(2)}) collective-permute-start(bf16[40,896]{1,0:T(8,128)(2,1)S(1)} %get-tuple-element.56), channel_id=1, source_target_pairs={{0,2},{1,3},{2,0},{3,1},{4,6},{5,7},{6,4},{7,5},{8,10},{9,11},{10,... | collective-permute-start | bytes 215048 | tf_op jit(solution)/shard_map/ppermute | solution.py:447
  34.7 5.5 %collective-permute-start.12 = (bf16[40,896]{1,0:T(8,128)(2,1)S(1)}, bf16[40,896]{1,0:T(8,128)(2,1)S(1)}, u32[]{:S(2)}, u32[]{:S(2)}) collective-permute-start(bf16[40,896]{1,0:T(8,128)(2,1)S(1)} %get-tuple-element.50), channel_id=1, source_target_pairs={{0,6},{1,7},{2,4},{3,5},{4,2},{5,3},{6,0},{7,1},{8,14},{9,15},{10,... | collective-permute-start | bytes 215048 | tf_op jit(solution)/shard_map/ppermute | solution.py:453
  36.6 4.3 %collective-permute-start.13 = (bf16[40,896]{1,0:T(8,128)(2,1)S(1)}, bf16[40,896]{1,0:T(8,128)(2,1)S(1)}, u32[]{:S(2)}, u32[]{:S(2)}) collective-permute-start(bf16[40,896]{1,0:T(8,128)(2,1)S(1)} %get-tuple-element.51), channel_id=1, source_target_pairs={{0,4},{1,5},{2,6},{3,7},{4,0},{5,1},{6,2},{7,3},{8,12},{9,13},{10,... | collective-permute-start | bytes 215048 | tf_op jit(solution)/shard_map/ppermute | solution.py:453
  37.1 4.3 %collective-permute-start.14 = (bf16[40,896]{1,0:T(8,128)(2,1)S(1)}, bf16[40,896]{1,0:T(8,128)(2,1)S(1)}, u32[]{:S(2)}, u32[]{:S(2)}) collective-permute-start(bf16[40,896]{1,0:T(8,128)(2,1)S(1)} %get-tuple-element.52), channel_id=1, source_target_pairs={{0,2},{1,3},{2,0},{3,1},{4,6},{5,7},{6,4},{7,5},{8,10},{9,11},{10,... | collective-permute-start | bytes 215048 | tf_op jit(solution)/shard_map/ppermute | solution.py:453
  38.4 5.3 %collective-permute-start.18 = (bf16[40,896]{1,0:T(8,128)(2,1)S(1)}, bf16[40,896]{1,0:T(8,128)(2,1)S(1)}, u32[]{:S(2)}, u32[]{:S(2)}) collective-permute-start(bf16[40,896]{1,0:T(8,128)(2,1)S(1)} %sum_blocks.1), channel_id=1, source_target_pairs={{0,8},{1,9},{2,10},{3,11},{4,12},{5,13},{6,14},{7,15},{8,0},{9,1},... | collective-permute-start | bytes 215048 | tf_op jit(solution)/shard_map/ppermute | solution.py:449

commit v17 on v15

--- a/solution.py
+++ b/solution.py
@@ -13,6 +13,8 @@
 SEGMENTS = 8
 
 route_scale = 2.5
+
+ROOM = 8
 
 VMEM = pl.BlockSpec(memory_space=pltpu.VMEM)
 HBM = pl.BlockSpec(memory_space=pltpu.HBM)
@@ -167,9 +169,8 @@
 
 
 def join_kernel(*refs):
-    tall = refs[0].shape[0]
-    for i, ref in enumerate(refs[:-1]):
-        refs[-1][i * tall : (i + 1) * tall, :] = ref[...]
+    blocks = [ref[...].astype(jnp.float32) for ref in refs[:-1]]
+    refs[-1][...] = jnp.concatenate(blocks, axis=0).astype(refs[-1].dtype)
 
 
 def join(blocks):
@@ -185,11 +186,11 @@
 
 
 def packed_down(hidden, down_ref, out_ref, flat):
-    count, wide = flat.shape[1:]
+    count, wide = hidden.shape[0], flat.shape[2]
     tall = CAP * SEGMENTS
     for s in range(SEGMENTS):
         slot = flat.at[s % 2]
-        slot[...] = jnp.dot(
+        slot[:count, :] = jnp.dot(
             hidden, down_ref[:, s * wide : (s + 1) * wide], preferred_element_type=jnp.float32
         )
         for b in range(count // CAP):
@@ -202,7 +203,7 @@
     half = own_ref.shape[0]
     wide = own_ref.shape[1]
     packed[:half, :] = own_ref[...].astype(jnp.float32)
-    packed[half:, :] = other_ref[...].astype(jnp.float32)
+    packed[half : 2 * half, :] = other_ref[...].astype(jnp.float32)
     for s in range(SEGMENTS):
         for b in range(2 * half // tall):
             start = b * tall + s * CAP
@@ -215,10 +216,12 @@
     rows, wide = own.shape
     return pl.pallas_call(
         unpack_kernel,
-        out_shape=jax.ShapeDtypeStruct((2 * rows // SEGMENTS, wide * SEGMENTS), jnp.float32),
+        out_shape=jax.ShapeDtypeStruct(
+            (2 * rows // SEGMENTS + ROOM, wide * SEGMENTS), jnp.float32
+        ),
         in_specs=[VMEM] * 2,
         out_specs=VMEM,
-        scratch_shapes=[pltpu.VMEM((2 * rows, wide), jnp.float32)],
+        scratch_shapes=[pltpu.VMEM((2 * rows + ROOM, wide), jnp.float32)],
         compiler_params=params(6),
         name="unpack",
     )(own, other)
@@ -235,18 +238,18 @@
     for ref in pieces:
         packed[start : start + ref.shape[0], :] = ref[...].astype(jnp.float32)
         start += ref.shape[0]
-    known = first_ref.shape[0]
+    known = first_ref.shape[0] - ROOM
     count = known * teams
     gate_act = jnp.zeros((count, units), jnp.float32)
     up_act = jnp.zeros((count, units), jnp.float32)
     for s in range(SEGMENTS):
         slot = flat.at[s % 2]
         columns = slice(s * wide, (s + 1) * wide)
-        slot[:known, :] = first_ref[:, columns]
+        slot[:known, :] = first_ref[:known, columns]
         for b in range((count - known) // CAP):
             start = b * tall + s * CAP
             slot[known + b * CAP : known + (b + 1) * CAP, :] = packed[start : start + CAP, :]
-        rows = slot[...].astype(jnp.bfloat16)
+        rows = slot[:count, :].astype(jnp.bfloat16)
         gate_act += jnp.dot(rows, gate_ref[columns, :], preferred_element_type=jnp.float32)
         up_act += jnp.dot(rows, up_ref[columns, :], preferred_element_type=jnp.float32)
     act[:count, :] = jax.nn.silu(gate_act) * up_act
@@ -256,10 +259,10 @@
             source = (CORES * k + core) * half
             target = count + (core * teams + k) * half
             act[target : target + half, :] = act[source : source + half, :]
-    hidden = act[count:, :].astype(jnp.bfloat16)
     half = count // 2
-    hidden_ref[...] = hidden[:half]
-    packed_down(hidden[half:], down_ref, out, flat.at[:, :half, :])
+    hidden_ref[...] = act[count : count + half, :].astype(jnp.bfloat16)
+    given = act[count + half : 2 * count, :].astype(jnp.bfloat16)
+    packed_down(given, down_ref, out, flat)
     for k, given_ref in enumerate(given_refs):
         rows = given_ref.shape[0]
         given_ref[...] = out[k * rows : (k + 1) * rows, :].astype(jnp.bfloat16)
@@ -269,7 +272,7 @@
     teams = 1 + len(pieces) // 2
     block, wide = pieces[0].shape
     features, units = w_gate.shape
-    rows = first.shape[0] * teams
+    rows = (first.shape[0] - ROOM) * teams
     return pl.pallas_call(
         functools.partial(expert_kernel, teams),
         out_shape=[jax.ShapeDtypeStruct((block, wide), jnp.bfloat16)] * teams
@@ -277,10 +280,10 @@
         in_specs=[VMEM] * (len(pieces) + 4),
         out_specs=[VMEM] * (teams + 1),
         scratch_shapes=[
-            pltpu.VMEM((block * len(pieces), wide), jnp.float32),
-            pltpu.VMEM((2, rows, wide), jnp.float32),
-            pltpu.VMEM((block * teams, wide), jnp.float32),
-            pltpu.VMEM((2 * rows, units), jnp.float32),
+            pltpu.VMEM((block * len(pieces) + ROOM, wide), jnp.float32),
+            pltpu.VMEM((2, rows + ROOM, wide), jnp.float32),
+            pltpu.VMEM((block * teams + ROOM, wide), jnp.float32),
+            pltpu.VMEM((2 * rows + ROOM, units), jnp.float32),
         ],
         compiler_params=params(16 + 4 * teams),
         cost_estimate=pl.CostEstimate(
@@ -302,10 +305,10 @@
     wide = features // SEGMENTS
     return pl.pallas_call(
         kept_kernel,
-        out_shape=jax.ShapeDtypeStruct((count * SEGMENTS, wide), jnp.float32),
+        out_shape=jax.ShapeDtypeStruct((count * SEGMENTS + ROOM, wide), jnp.float32),
         in_specs=[VMEM] * 2,
         out_specs=VMEM,
-        scratch_shapes=[pltpu.VMEM((2, count, wide), jnp.float32)],
+        scratch_shapes=[pltpu.VMEM((2, count + ROOM, wide), jnp.float32)],
         compiler_params=params(8 + count // 10),
         cost_estimate=pl.CostEstimate(
             flops=2 * count * units * features,
@@ -318,12 +321,9 @@
 
 def add_kernel(first, kept_ref, taken_ref, *out_refs):
     tall = out_refs[0].shape[0]
+    total = kept_ref[first : first + taken_ref.shape[0], :] + taken_ref[...].astype(jnp.float32)
     for b, out_ref in enumerate(out_refs):
-        rows = slice(b * tall, (b + 1) * tall)
-        total = kept_ref[first + b * tall : first + (b + 1) * tall, :] + taken_ref[
-            rows, :
-        ].astype(jnp.float32)
-        out_ref[...] = total.astype(out_ref.dtype)
+        out_ref[...] = total[b * tall : (b + 1) * tall].astype(out_ref.dtype)
 
 
 def add_cores(kept, taken, k, chips):

time: 37.4 us -> 38.2 us (1.021)
  waiting for transfers between devices: 6.85 us -> 7.58 us
    ppermute x1, waiting for transfers between devices: 2.24 us -> 2.97 us  [body(): others.append(lax.ppermute(sum_blocks(team), 'expert', pairs))]
  transfers between devices with their start and end apart: 18 -> 18, of which waited for: 9 -> 8; matrix products, arithmetic and copies ran while one was open for 0% -> 0% of each run, Pallas kernels for 4% -> 4%
where the time goes in v17:
time: 38.2 us; the launch traced here: 38 us
  starting transfers between devices  22.1 us (58%)
  waiting for transfers between devices  7.58 us (20%)
  Pallas kernels  7.43 us (19%)
  local copies, waits for them, and re-layouts  0.71 us (2%)
    ppermute x6, starting transfers between devices, gather(): lax.ppermute(block, 'expert', other_chip[m])  7.81 us
    ppermute x1, starting transfers between devices, body(): block = lax.ppermute(packed[k], 'expert', pairs)  4.1 us
    ppermute x3, starting transfers between devices, body(): own.append(lax.ppermute(parts[m], 'expert', other_chip[m]))  3.55 us
    ppermute x3, starting transfers between devices, body(): team.append(lax.ppermute(parts[m], 'expert', other_chip[m]))  3.55 us
    ppermute x1, waiting for transfers between devices, body(): others.append(lax.ppermute(sum_blocks(team), 'expert', pairs))  2.97 us
    ppermute x1, starting transfers between devices, body(): others.append(lax.ppermute(sum_blocks(team), 'expert', pairs))  2.4 us
    pallas_call x1, Pallas kernels, expert_half(): pl.pallas_call(functools.partial(expert_kernel, teams), out_shape=[jax.Sh...  2.31 us
    pallas_call x1, Pallas kernels, pack_rows(): pl.pallas_call(functools.partial(pack_kernel, teams), out_shape=[block] *...  2.28 us
  transfers between devices with their start and end apart: 18, of which 8 were waited for; matrix products, arithmetic and copies ran while one was open for 0% of the time, Pallas kernels for 4%

profile of v17, /device:TPU:0, one launch (start us, length us, event | category | flops | bytes accessed | tf_op | source)
XLA Modules:
  0.0 38.0 jit_solution(8580173346874221672)
XLA Ops:
  0.0 2.3 %pack_rows.1 = (bf16[40,896]{1,0:T(8,128)(2,1)}, bf16[40,896]{1,0:T(8,128)(2,1)}, f32[16,64]{1,0:T(8,128)}) custom-call(s32[8,64]{1,0:T(8,128)} %bitcast.2, f32[8,64]{1,0:T(8,128)} %bitcast.3, bf16[64,7168]{1,0:T(8,128)(2,1)} %tokens_hbm.1), custom_call_target="tpu_custom_call" | custom-call | tf_op jit(solution)/shard_map/pack_rows/pallas_call | solution.py:112
  2.3 4.1 %collective-permute-start.3 = (bf16[40,896]{1,0:T(8,128)(2,1)}, bf16[40,896]{1,0:T(8,128)(2,1)S(1)}, u32[]{:S(2)}, u32[]{:S(2)}) collective-permute-start(bf16[40,896]{1,0:T(8,128)(2,1)} %get-tuple-element.32), channel_id=1, source_target_pairs={{0,8},{1,9},{2,10},{3,11},{4,12},{5,13},{6,14},{7,15},{8,0},{9,1},... | collective-permute-start | bytes 215048 | tf_op jit(solution)/shard_map/ppermute | solution.py:424
  6.4 2.5 %collective-permute-start.2 = (bf16[40,896]{1,0:T(8,128)(2,1)}, bf16[40,896]{1,0:T(8,128)(2,1)S(1)}, u32[]{:S(2)}, u32[]{:S(2)}) collective-permute-start(bf16[40,896]{1,0:T(8,128)(2,1)} %get-tuple-element.36.refs_0_), channel_id=1, source_target_pairs={{0,6},{1,7},{2,4},{3,5},{4,2},{5,3},{6,0},{7,1},{8,14},{9,15},{10,... | collective-permute-start | bytes 215048 | tf_op jit(solution)/shard_map/ppermute | solution.py:418
  8.9 0.4 %collective-permute-start.1 = (bf16[40,896]{1,0:T(8,128)(2,1)}, bf16[40,896]{1,0:T(8,128)(2,1)S(1)}, u32[]{:S(2)}, u32[]{:S(2)}) collective-permute-start(bf16[40,896]{1,0:T(8,128)(2,1)} %get-tuple-element.36.refs_0_), channel_id=1, source_target_pairs={{0,4},{1,5},{2,6},{3,7},{4,0},{5,1},{6,2},{7,3},{8,12},{9,13},{10,... | collective-permute-start | bytes 215048 | tf_op jit(solution)/shard_map/ppermute | solution.py:418
  9.4 0.5 %collective-permute-start = (bf16[40,896]{1,0:T(8,128)(2,1)}, bf16[40,896]{1,0:T(8,128)(2,1)S(1)}, u32[]{:S(2)}, u32[]{:S(2)}) collective-permute-start(bf16[40,896]{1,0:T(8,128)(2,1)} %get-tuple-element.36.refs_0_), channel_id=1, source_target_pairs={{0,2},{1,3},{2,0},{3,1},{4,6},{5,7},{6,4},{7,5},{8,10},{9,11},{10,... | collective-permute-start | bytes 215048 | tf_op jit(solution)/shard_map/ppermute | solution.py:418
  9.9 0.0 collective-permute-done.3.refs_0_
  9.9 2.7 %collective-permute-start.7 = (bf16[40,896]{1,0:T(8,128)(2,1)S(1)}, bf16[40,896]{1,0:T(8,128)(2,1)S(1)}, u32[]{:S(2)}, u32[]{:S(2)}) collective-permute-start(bf16[40,896]{1,0:T(8,128)(2,1)S(1)} %collective-permute-done.3.refs_0_), channel_id=1, source_target_pairs={{0,6},{1,7},{2,4},{3,5},{4,2},{5,3},{6,0},{7,1},{8,14},{9,15},{10,... | collective-permute-start | bytes 215048 | tf_op jit(solution)/shard_map/ppermute | solution.py:418
  12.6 0.7 %collective-permute-start.6 = (bf16[40,896]{1,0:T(8,128)(2,1)S(1)}, bf16[40,896]{1,0:T(8,128)(2,1)S(1)}, u32[]{:S(2)}, u32[]{:S(2)}) collective-permute-start(bf16[40,896]{1,0:T(8,128)(2,1)S(1)} %collective-permute-done.3.refs_0_), channel_id=1, source_target_pairs={{0,4},{1,5},{2,6},{3,7},{4,0},{5,1},{6,2},{7,3},{8,12},{9,13},{10,... | collective-permute-start | bytes 215048 | tf_op jit(solution)/shard_map/ppermute | solution.py:418
  13.3 0.0 collective-permute-done.2.refs_3_
  13.3 1.0 %collective-permute-start.5 = (bf16[40,896]{1,0:T(8,128)(2,1)S(1)}, bf16[40,896]{1,0:T(8,128)(2,1)S(1)}, u32[]{:S(2)}, u32[]{:S(2)}) collective-permute-start(bf16[40,896]{1,0:T(8,128)(2,1)S(1)} %collective-permute-done.3.refs_0_), channel_id=1, source_target_pairs={{0,2},{1,3},{2,0},{3,1},{4,6},{5,7},{6,4},{7,5},{8,10},{9,11},{10,... | collective-permute-start | bytes 215048 | tf_op jit(solution)/shard_map/ppermute | solution.py:418
  14.2 0.7 %copy-done.4 = f32[16,64]{1,0:T(8,128)S(1)} copy-done((f32[16,64]{1,0:T(8,128)S(1)}, f32[16,64]{1,0:T(8,128)}, u32[]{:S(2)}) %copy-start.4) | copy-done | bytes 4120
  14.9 0.3 blend_weights.1.weight_ref
  15.2 0.0 collective-permute-done.1.refs_2_
  15.2 0.1 collective-permute-done.refs_1_
  15.3 0.0 copy-done.3
  15.4 0.1 collective-permute-start.4
  15.5 0.4 %collective-permute-done.7.refs_3_ = bf16[40,896]{1,0:T(8,128)(2,1)S(1)} collective-permute-done((bf16[40,896]{1,0:T(8,128)(2,1)S(1)}, bf16[40,896]{1,0:T(8,128)(2,1)S(1)}, u32[]{:S(2)}, u32[]{:S(2)}) %collective-permute-start.7) | collective-permute-done | bytes 71712 | tf_op jit(solution)/shard_map/ppermute | solution.py:418
  15.9 1.0 %collective-permute-done.6.refs_2_ = bf16[40,896]{1,0:T(8,128)(2,1)S(1)} collective-permute-done((bf16[40,896]{1,0:T(8,128)(2,1)S(1)}, bf16[40,896]{1,0:T(8,128)(2,1)S(1)}, u32[]{:S(2)}, u32[]{:S(2)}) %collective-permute-start.6) | collective-permute-done | bytes 71712 | tf_op jit(solution)/shard_map/ppermute | solution.py:418
  16.9 0.7 %collective-permute-done.5.refs_1_ = bf16[40,896]{1,0:T(8,128)(2,1)S(1)} collective-permute-done((bf16[40,896]{1,0:T(8,128)(2,1)S(1)}, bf16[40,896]{1,0:T(8,128)(2,1)S(1)}, u32[]{:S(2)}, u32[]{:S(2)}) %collective-permute-start.5) | collective-permute-done | bytes 71712 | tf_op jit(solution)/shard_map/ppermute | solution.py:418
  17.6 0.1 collective-permute-start.8
  17.7 0.0 collective-permute-done.4.other_ref
  17.7 0.3 unpack.1.first_ref
  18.1 1.2 %collective-permute-done.8.refs_1_ = bf16[160,896]{1,0:T(8,128)(2,1)S(1)} collective-permute-done((bf16[160,896]{1,0:T(8,128)(2,1)S(1)}, bf16[160,896]{1,0:T(8,128)(2,1)S(1)}, u32[]{:S(2)}, u32[]{:S(2)}) %collective-permute-start.8) | collective-permute-done | bytes 286752 | tf_op jit(solution)/shard_map/ppermute | solution.py:435
  19.3 0.0 copy-done
  19.3 0.0 copy-done.1
  19.3 2.3 %expert_half.1 = (bf16[160,896]{1,0:T(8,128)(2,1)S(1)}, bf16[160,896]{1,0:T(8,128)(2,1)S(1)}, bf16[40,256]{1,0:T(8,128)(2,1)S(1)}) custom-call(f32[48,7168]{1,0:T(8,128)S(1)} %unpack.1.first_ref, bf16[160,896]{1,0:T(8,128)(2,1)S(1)} %join.3.refs_0_, bf16[160,896]{1,0:T(8,128)(2,1)S(1)} %collective-permute-done.8.refs_1_, bf16[7168,256]{1,0:T(8,128)(2,1)S(1)} %copy-done.1, ...), custom_call_target="tpu_custom_call" | custom-call | flops 734003200 | bytes 11010048 | tf_op jit(solution)/shard_map/expert_half/pallas_call | solution.py:276
  21.6 0.2 collective-permute-start.9
  21.8 0.4 collective-permute-start.10
  22.2 0.7 %kept_half.1.kept_ref = f32[328,896]{1,0:T(8,128)S(1)} custom-call(bf16[40,256]{1,0:T(8,128)(2,1)S(1)} %get-tuple-element.41.hidden_ref, bf16[256,7168]{1,0:T(8,128)(2,1)S(1)} %copy-done), custom_call_target="tpu_custom_call" | custom-call | flops 146800640 | bytes 3670016 | tf_op jit(solution)/shard_map/kept_half/pallas_call | solution.py:306
  22.9 0.3 collective-permute-done.9.taken_ref
  23.2 0.1 add_cores.2
  23.3 1.8 %collective-permute-start.14 = (bf16[40,896]{1,0:T(8,128)(2,1)S(1)}, bf16[40,896]{1,0:T(8,128)(2,1)S(1)}, u32[]{:S(2)}, u32[]{:S(2)}) collective-permute-start(bf16[40,896]{1,0:T(8,128)(2,1)S(1)} %get-tuple-element.54), channel_id=1, source_target_pairs={{0,6},{1,7},{2,4},{3,5},{4,2},{5,3},{6,0},{7,1},{8,14},{9,15},{10,... | collective-permute-start | bytes 215048 | tf_op jit(solution)/shard_map/ppermute | solution.py:445
  25.0 0.7 %collective-permute-start.15 = (bf16[40,896]{1,0:T(8,128)(2,1)S(1)}, bf16[40,896]{1,0:T(8,128)(2,1)S(1)}, u32[]{:S(2)}, u32[]{:S(2)}) collective-permute-start(bf16[40,896]{1,0:T(8,128)(2,1)S(1)} %get-tuple-element.55), channel_id=1, source_target_pairs={{0,4},{1,5},{2,6},{3,7},{4,0},{5,1},{6,2},{7,3},{8,12},{9,13},{10,... | collective-permute-start | bytes 215048 | tf_op jit(solution)/shard_map/ppermute | solution.py:445
  25.8 1.1 %collective-permute-start.16 = (bf16[40,896]{1,0:T(8,128)(2,1)S(1)}, bf16[40,896]{1,0:T(8,128)(2,1)S(1)}, u32[]{:S(2)}, u32[]{:S(2)}) collective-permute-start(bf16[40,896]{1,0:T(8,128)(2,1)S(1)} %get-tuple-element.56), channel_id=1, source_target_pairs={{0,2},{1,3},{2,0},{3,1},{4,6},{5,7},{6,4},{7,5},{8,10},{9,11},{10,... | collective-permute-start | bytes 215048 | tf_op jit(solution)/shard_map/ppermute | solution.py:445
  26.8 0.0 collective-permute-done.10.taken_ref
  26.9 0.1 add_cores.3
  26.9 1.8 %collective-permute-start.11 = (bf16[40,896]{1,0:T(8,128)(2,1)S(1)}, bf16[40,896]{1,0:T(8,128)(2,1)S(1)}, u32[]{:S(2)}, u32[]{:S(2)}) collective-permute-start(bf16[40,896]{1,0:T(8,128)(2,1)S(1)} %get-tuple-element.50), channel_id=1, source_target_pairs={{0,6},{1,7},{2,4},{3,5},{4,2},{5,3},{6,0},{7,1},{8,14},{9,15},{10,... | collective-permute-start | bytes 215048 | tf_op jit(solution)/shard_map/ppermute | solution.py:451
  28.7 0.7 %collective-permute-start.12 = (bf16[40,896]{1,0:T(8,128)(2,1)S(1)}, bf16[40,896]{1,0:T(8,128)(2,1)S(1)}, u32[]{:S(2)}, u32[]{:S(2)}) collective-permute-start(bf16[40,896]{1,0:T(8,128)(2,1)S(1)} %get-tuple-element.51), channel_id=1, source_target_pairs={{0,4},{1,5},{2,6},{3,7},{4,0},{5,1},{6,2},{7,3},{8,12},{9,13},{10,... | collective-permute-start | bytes 215048 | tf_op jit(solution)/shard_map/ppermute | solution.py:451
  29.4 0.0 collective-permute-done.14.refs_1_
  29.4 1.1 %collective-permute-start.13 = (bf16[40,896]{1,0:T(8,128)(2,1)S(1)}, bf16[40,896]{1,0:T(8,128)(2,1)S(1)}, u32[]{:S(2)}, u32[]{:S(2)}) collective-permute-start(bf16[40,896]{1,0:T(8,128)(2,1)S(1)} %get-tuple-element.52), channel_id=1, source_target_pairs={{0,2},{1,3},{2,0},{3,1},{4,6},{5,7},{6,4},{7,5},{8,10},{9,11},{10,... | collective-permute-start | bytes 215048 | tf_op jit(solution)/shard_map/ppermute | solution.py:451
  30.5 0.0 collective-permute-done.15.refs_2_
  30.5 0.0 collective-permute-done.16.refs_3_
  30.6 2.4 %collective-permute-start.17 = (bf16[40,896]{1,0:T(8,128)(2,1)S(1)}, bf16[40,896]{1,0:T(8,128)(2,1)S(1)}, u32[]{:S(2)}, u32[]{:S(2)}) collective-permute-start(bf16[40,896]{1,0:T(8,128)(2,1)S(1)} %sum_blocks.1), channel_id=1, source_target_pairs={{0,8},{1,9},{2,10},{3,11},{4,12},{5,13},{6,14},{7,15},{8,0},{9,1},... | collective-permute-start | bytes 215048 | tf_op jit(solution)/shard_map/ppermute | solution.py:447
  33.0 0.0 collective-permute-done.11.refs_1_
  33.0 0.0 collective-permute-done.12.refs_2_
  33.0 0.7 %collective-permute-done.13.refs_3_ = bf16[40,896]{1,0:T(8,128)(2,1)S(1)} collective-permute-done((bf16[40,896]{1,0:T(8,128)(2,1)S(1)}, bf16[40,896]{1,0:T(8,128)(2,1)S(1)}, u32[]{:S(2)}, u32[]{:S(2)}) %collective-permute-start.13) | collective-permute-done | bytes 71712 | tf_op jit(solution)/shard_map/ppermute | solution.py:451
  33.7 3.0 %collective-permute-done.17.refs_4_ = bf16[40,896]{1,0:T(8,128)(2,1)S(1)} collective-permute-done((bf16[40,896]{1,0:T(8,128)(2,1)S(1)}, bf16[40,896]{1,0:T(8,128)(2,1)S(1)}, u32[]{:S(2)}, u32[]{:S(2)}) %collective-permute-start.17) | collective-permute-done | bytes 71712 | tf_op jit(solution)/shard_map/ppermute | solution.py:447
  36.7 1.2 %blend.1 = bf16[64,7168]{1,0:T(8,128)(2,1)} custom-call(bf16[512,200]{1,0:T(8,128)(2,1)S(1)} %blend_weights.1.weight_ref, f32[40,896]{1,0:T(8,128)S(1)} %get-tuple-element.49.refs_0_, bf16[40,896]{1,0:T(8,128)(2,1)S(1)} %collective-permute-done.11.refs_1_, bf16[40,896]{1,0:T(8,128)(2,1)S(1)} %collective-permute-done.12.refs_2_, ...), custom_call_target="tpu_custom_call" | custom-call | tf_op jit(solution)/shard_map/blend/pallas_call | solution.py:396
  (9 shorter events, 0.1 us)
Async XLA Ops:
  2.3 7.6 %collective-permute-start.3 = (bf16[40,896]{1,0:T(8,128)(2,1)}, bf16[40,896]{1,0:T(8,128)(2,1)S(1)}, u32[]{:S(2)}, u32[]{:S(2)}) collective-permute-start(bf16[40,896]{1,0:T(8,128)(2,1)} %get-tuple-element.32), channel_id=1, source_target_pairs={{0,8},{1,9},{2,10},{3,11},{4,12},{5,13},{6,14},{7,15},{8,0},{9,1},... | collective-permute-start | bytes 215048 | tf_op jit(solution)/shard_map/ppermute | solution.py:424
  6.4 6.9 %collective-permute-start.2 = (bf16[40,896]{1,0:T(8,128)(2,1)}, bf16[40,896]{1,0:T(8,128)(2,1)S(1)}, u32[]{:S(2)}, u32[]{:S(2)}) collective-permute-start(bf16[40,896]{1,0:T(8,128)(2,1)} %get-tuple-element.36.refs_0_), channel_id=1, source_target_pairs={{0,6},{1,7},{2,4},{3,5},{4,2},{5,3},{6,0},{7,1},{8,14},{9,15},{10,... | collective-permute-start | bytes 215048 | tf_op jit(solution)/shard_map/ppermute | solution.py:418
  8.9 6.3 %collective-permute-start.1 = (bf16[40,896]{1,0:T(8,128)(2,1)}, bf16[40,896]{1,0:T(8,128)(2,1)S(1)}, u32[]{:S(2)}, u32[]{:S(2)}) collective-permute-start(bf16[40,896]{1,0:T(8,128)(2,1)} %get-tuple-element.36.refs_0_), channel_id=1, source_target_pairs={{0,4},{1,5},{2,6},{3,7},{4,0},{5,1},{6,2},{7,3},{8,12},{9,13},{10,... | collective-permute-start | bytes 215048 | tf_op jit(solution)/shard_map/ppermute | solution.py:418
  9.4 6.0 %collective-permute-start = (bf16[40,896]{1,0:T(8,128)(2,1)}, bf16[40,896]{1,0:T(8,128)(2,1)S(1)}, u32[]{:S(2)}, u32[]{:S(2)}) collective-permute-start(bf16[40,896]{1,0:T(8,128)(2,1)} %get-tuple-element.36.refs_0_), channel_id=1, source_target_pairs={{0,2},{1,3},{2,0},{3,1},{4,6},{5,7},{6,4},{7,5},{8,10},{9,11},{10,... | collective-permute-start | bytes 215048 | tf_op jit(solution)/shard_map/ppermute | solution.py:418
  9.9 5.5 %copy-start.3 = (bf16[40,896]{1,0:T(8,128)(2,1)S(1)}, bf16[40,896]{1,0:T(8,128)(2,1)}, u32[]{:S(2)}) copy-start(bf16[40,896]{1,0:T(8,128)(2,1)} %get-tuple-element.36.refs_0_) | copy-start | bytes 215044
  9.9 6.0 %collective-permute-start.7 = (bf16[40,896]{1,0:T(8,128)(2,1)S(1)}, bf16[40,896]{1,0:T(8,128)(2,1)S(1)}, u32[]{:S(2)}, u32[]{:S(2)}) collective-permute-start(bf16[40,896]{1,0:T(8,128)(2,1)S(1)} %collective-permute-done.3.refs_0_), channel_id=1, source_target_pairs={{0,6},{1,7},{2,4},{3,5},{4,2},{5,3},{6,0},{7,1},{8,14},{9,15},{10,... | collective-permute-start | bytes 215048 | tf_op jit(solution)/shard_map/ppermute | solution.py:418
  12.6 4.3 %collective-permute-start.6 = (bf16[40,896]{1,0:T(8,128)(2,1)S(1)}, bf16[40,896]{1,0:T(8,128)(2,1)S(1)}, u32[]{:S(2)}, u32[]{:S(2)}) collective-permute-start(bf16[40,896]{1,0:T(8,128)(2,1)S(1)} %collective-permute-done.3.refs_0_), channel_id=1, source_target_pairs={{0,4},{1,5},{2,6},{3,7},{4,0},{5,1},{6,2},{7,3},{8,12},{9,13},{10,... | collective-permute-start | bytes 215048 | tf_op jit(solution)/shard_map/ppermute | solution.py:418
  13.3 4.3 %collective-permute-start.5 = (bf16[40,896]{1,0:T(8,128)(2,1)S(1)}, bf16[40,896]{1,0:T(8,128)(2,1)S(1)}, u32[]{:S(2)}, u32[]{:S(2)}) collective-permute-start(bf16[40,896]{1,0:T(8,128)(2,1)S(1)} %collective-permute-done.3.refs_0_), channel_id=1, source_target_pairs={{0,2},{1,3},{2,0},{3,1},{4,6},{5,7},{6,4},{7,5},{8,10},{9,11},{10,... | collective-permute-start | bytes 215048 | tf_op jit(solution)/shard_map/ppermute | solution.py:418
  14.2 0.7 %copy-start.4 = (f32[16,64]{1,0:T(8,128)S(1)}, f32[16,64]{1,0:T(8,128)}, u32[]{:S(2)}) copy-start(f32[16,64]{1,0:T(8,128)} %get-tuple-element.34.table_ref) | copy-start | bytes 12292
  14.9 4.3 %copy-start = (bf16[256,7168]{1,0:T(8,128)(2,1)S(1)}, bf16[256,7168]{1,0:T(8,128)(2,1)}, u32[]{:S(2)}) copy-start(bf16[256,7168]{1,0:T(8,128)(2,1)} %down_ref.1) | copy-start | bytes 11010052
  14.9 4.3 %copy-start.1 = (bf16[7168,256]{1,0:T(8,128)(2,1)S(1)}, bf16[7168,256]{1,0:T(8,128)(2,1)}, u32[]{:S(2)}) copy-start(bf16[7168,256]{1,0:T(8,128)(2,1)} %refs_2_.1) | copy-start | bytes 11010052
  14.9 4.3 %copy-start.2 = (bf16[7168,256]{1,0:T(8,128)(2,1)S(1)}, bf16[7168,256]{1,0:T(8,128)(2,1)}, u32[]{:S(2)}) copy-start(bf16[7168,256]{1,0:T(8,128)(2,1)} %refs_3_.1) | copy-start | bytes 11010052
  15.4 2.3 %collective-permute-start.4 = (bf16[160,896]{1,0:T(8,128)(2,1)S(1)}, bf16[160,896]{1,0:T(8,128)(2,1)S(1)}, u32[]{:S(2)}, u32[]{:S(2)}) collective-permute-start(bf16[160,896]{1,0:T(8,128)(2,1)S(1)} %join.2.own_ref), channel_id=1, source_target_pairs={{0,1},{1,0},{2,3},{3,2},{4,5},{5,4},{6,7},{7,6},{8,9},{9,8},{10,11... | collective-permute-start | bytes 860168 | tf_op jit(solution)/shard_map/ppermute | solution.py:431
  17.6 1.6 %collective-permute-start.8 = (bf16[160,896]{1,0:T(8,128)(2,1)S(1)}, bf16[160,896]{1,0:T(8,128)(2,1)S(1)}, u32[]{:S(2)}, u32[]{:S(2)}) collective-permute-start(bf16[160,896]{1,0:T(8,128)(2,1)S(1)} %join.3.refs_0_), channel_id=1, source_target_pairs={{0,1},{1,0},{2,3},{3,2},{4,5},{5,4},{6,7},{7,6},{8,9},{9,8},{10,11... | collective-permute-start | bytes 860168 | tf_op jit(solution)/shard_map/ppermute | solution.py:435
  21.6 1.6 %collective-permute-start.9 = (bf16[160,896]{1,0:T(8,128)(2,1)S(1)}, bf16[160,896]{1,0:T(8,128)(2,1)S(1)}, u32[]{:S(2)}, u32[]{:S(2)}) collective-permute-start(bf16[160,896]{1,0:T(8,128)(2,1)S(1)} %get-tuple-element.42), channel_id=1, source_target_pairs={{0,1},{1,0},{2,3},{3,2},{4,5},{5,4},{6,7},{7,6},{8,9},{9,8},{10,11... | collective-permute-start | bytes 860168 | tf_op jit(solution)/shard_map/ppermute | solution.py:437
  21.8 5.1 %collective-permute-start.10 = (bf16[160,896]{1,0:T(8,128)(2,1)S(1)}, bf16[160,896]{1,0:T(8,128)(2,1)S(1)}, u32[]{:S(2)}, u32[]{:S(2)}) collective-permute-start(bf16[160,896]{1,0:T(8,128)(2,1)S(1)} %get-tuple-element.48), channel_id=1, source_target_pairs={{0,1},{1,0},{2,3},{3,2},{4,5},{5,4},{6,7},{7,6},{8,9},{9,8},{10,11... | collective-permute-start | bytes 860168 | tf_op jit(solution)/shard_map/ppermute | solution.py:437
  23.3 6.1 %collective-permute-start.14 = (bf16[40,896]{1,0:T(8,128)(2,1)S(1)}, bf16[40,896]{1,0:T(8,128)(2,1)S(1)}, u32[]{:S(2)}, u32[]{:S(2)}) collective-permute-start(bf16[40,896]{1,0:T(8,128)(2,1)S(1)} %get-tuple-element.54), channel_id=1, source_target_pairs={{0,6},{1,7},{2,4},{3,5},{4,2},{5,3},{6,0},{7,1},{8,14},{9,15},{10,... | collective-permute-start | bytes 215048 | tf_op jit(solution)/shard_map/ppermute | solution.py:445
  25.0 5.4 %collective-permute-start.15 = (bf16[40,896]{1,0:T(8,128)(2,1)S(1)}, bf16[40,896]{1,0:T(8,128)(2,1)S(1)}, u32[]{:S(2)}, u32[]{:S(2)}) collective-permute-start(bf16[40,896]{1,0:T(8,128)(2,1)S(1)} %get-tuple-element.55), channel_id=1, source_target_pairs={{0,4},{1,5},{2,6},{3,7},{4,0},{5,1},{6,2},{7,3},{8,12},{9,13},{10,... | collective-permute-start | bytes 215048 | tf_op jit(solution)/shard_map/ppermute | solution.py:445
  25.8 4.7 %collective-permute-start.16 = (bf16[40,896]{1,0:T(8,128)(2,1)S(1)}, bf16[40,896]{1,0:T(8,128)(2,1)S(1)}, u32[]{:S(2)}, u32[]{:S(2)}) collective-permute-start(bf16[40,896]{1,0:T(8,128)(2,1)S(1)} %get-tuple-element.56), channel_id=1, source_target_pairs={{0,2},{1,3},{2,0},{3,1},{4,6},{5,7},{6,4},{7,5},{8,10},{9,11},{10,... | collective-permute-start | bytes 215048 | tf_op jit(solution)/shard_map/ppermute | solution.py:445
  26.9 6.0 %collective-permute-start.11 = (bf16[40,896]{1,0:T(8,128)(2,1)S(1)}, bf16[40,896]{1,0:T(8,128)(2,1)S(1)}, u32[]{:S(2)}, u32[]{:S(2)}) collective-permute-start(bf16[40,896]{1,0:T(8,128)(2,1)S(1)} %get-tuple-element.50), channel_id=1, source_target_pairs={{0,6},{1,7},{2,4},{3,5},{4,2},{5,3},{6,0},{7,1},{8,14},{9,15},{10,... | collective-permute-start | bytes 215048 | tf_op jit(solution)/shard_map/ppermute | solution.py:451
  28.7 4.3 %collective-permute-start.12 = (bf16[40,896]{1,0:T(8,128)(2,1)S(1)}, bf16[40,896]{1,0:T(8,128)(2,1)S(1)}, u32[]{:S(2)}, u32[]{:S(2)}) collective-permute-start(bf16[40,896]{1,0:T(8,128)(2,1)S(1)} %get-tuple-element.51), channel_id=1, source_target_pairs={{0,4},{1,5},{2,6},{3,7},{4,0},{5,1},{6,2},{7,3},{8,12},{9,13},{10,... | collective-permute-start | bytes 215048 | tf_op jit(solution)/shard_map/ppermute | solution.py:451
  29.4 4.3 %collective-permute-start.13 = (bf16[40,896]{1,0:T(8,128)(2,1)S(1)}, bf16[40,896]{1,0:T(8,128)(2,1)S(1)}, u32[]{:S(2)}, u32[]{:S(2)}) collective-permute-start(bf16[40,896]{1,0:T(8,128)(2,1)S(1)} %get-tuple-element.52), channel_id=1, source_target_pairs={{0,2},{1,3},{2,0},{3,1},{4,6},{5,7},{6,4},{7,5},{8,10},{9,11},{10,... | collective-permute-start | bytes 215048 | tf_op jit(solution)/shard_map/ppermute | solution.py:451
  30.6 6.2 %collective-permute-start.17 = (bf16[40,896]{1,0:T(8,128)(2,1)S(1)}, bf16[40,896]{1,0:T(8,128)(2,1)S(1)}, u32[]{:S(2)}, u32[]{:S(2)}) collective-permute-start(bf16[40,896]{1,0:T(8,128)(2,1)S(1)} %sum_blocks.1), channel_id=1, source_target_pairs={{0,8},{1,9},{2,10},{3,11},{4,12},{5,13},{6,14},{7,15},{8,0},{9,1},... | collective-permute-start | bytes 215048 | tf_op jit(solution)/shard_map/ppermute | solution.py:447

commit v18 on v17

--- a/solution.py
+++ b/solution.py
@@ -357,6 +357,41 @@
     )(*blocks)
 
 
+def settle_kernel(block_ref, out_ref):
+    out_ref[...] = block_ref[...].astype(jnp.float32)
+
+
+def settle(block):
+    return pl.pallas_call(
+        settle_kernel,
+        out_shape=jax.ShapeDtypeStruct(block.shape, jnp.float32),
+        in_specs=[VMEM],
+        out_specs=VMEM,
+        compiler_params=params(4),
+        cost_estimate=pl.CostEstimate(flops=3 * 10**9, bytes_accessed=MIB, transcendentals=0),
+        name="settle",
+    )(block)
+
+
+def partial_kernel(*refs):
+    total = refs[0][...]
+    for ref in refs[1:-1]:
+        total = total + ref[...].astype(jnp.float32)
+    refs[-1][...] = total
+
+
+def partial_sum(blocks):
+    return pl.pallas_call(
+        partial_kernel,
+        out_shape=jax.ShapeDtypeStruct(blocks[0].shape, jnp.float32),
+        in_specs=[VMEM] * len(blocks),
+        out_specs=VMEM,
+        compiler_params=params(4),
+        cost_estimate=pl.CostEstimate(flops=300 * 10**6, bytes_accessed=MIB, transcendentals=0),
+        name="partial_sum",
+    )(*blocks)
+
+
 def halves(wide):
     cut = 128 * pl.cdiv(wide // 128, 2)
     return slice(0, cut), slice(cut, wide)
@@ -436,19 +471,24 @@
     *given, hidden = expert_half(first, pieces, w_gate, w_up, w_down)
     taken = [lax.ppermute(piece, "expert", other_core) for piece in given]
     kept = kept_half(hidden, w_down)
-    others = []
+    totals = []
     for k in range(1, teams):
         parts = add_cores(kept, taken[k], k, chips)
         parts, later = lax.optimization_barrier((parts, kept))
         team = [parts[0]]
         for m in reversed(range(1, chips)):
             team.append(lax.ppermute(parts[m], "expert", other_chip[m]))
+        totals.append(sum_blocks(team))
+    parts = list(add_cores(later, taken[0], 0, chips))
+    totals, parts[1] = lax.optimization_barrier((totals, parts[1]))
+    others = []
+    for k in range(1, teams):
         pairs = [(i, (i - k * SPLIT) % devices) for i in range(devices)]
-        others.append(lax.ppermute(sum_blocks(team), "expert", pairs))
-    parts = add_cores(later, taken[0], 0, chips)
+        others.append(settle(lax.ppermute(totals[k - 1], "expert", pairs)))
     own = [parts[0]]
-    for m in reversed(range(1, chips)):
+    for m in reversed(range(2, chips)):
         own.append(lax.ppermute(parts[m], "expert", other_chip[m]))
+    own = [partial_sum(own), lax.ppermute(parts[1], "expert", other_chip[1])]
     return blend(weights, own, others, tokens.shape[0])
 
 

time: 38.2 us -> 38.7 us (1.013)
  waiting for transfers between devices: 7.58 us -> 8.07 us
    ppermute x1 -> x2, starting transfers between devices: 2.4 us -> 3.51 us  [the longest x1 2.4 us: body(): others.append(settle(lax.ppermute(totals[k - 1], 'expert', pairs)))]
    ppermute x3, waiting for transfers between devices: 0.04 us -> 1.11 us  [body(): team.append(lax.ppermute(parts[m], 'expert', other_chip[m]))]
    ppermute x3 -> x2, starting transfers between devices: 3.55 us -> 2.49 us  [body(): own.append(lax.ppermute(parts[m], 'expert', other_chip[m]))]
    ppermute x3 -> x2, waiting for transfers between devices: 0.78 us -> 0.01 us  [body(): own.append(lax.ppermute(parts[m], 'expert', other_chip[m]))]
    ppermute x1 -> x2, waiting for transfers between devices: 2.97 us -> 3.17 us  [the longest x1 2.6 us: body(): others.append(settle(lax.ppermute(totals[k - 1], 'expert', pairs)))]
  transfers between devices with their start and end apart: 18 -> 18, of which waited for: 8 -> 10; matrix products, arithmetic and copies ran while one was open for 0% -> 0% of each run, Pallas kernels for 4% -> 4%
where the time goes in v18:
time: 38.7 us; the launch traced here: 38.5 us
  starting transfers between devices  22.2 us (57%)
  waiting for transfers between devices  8.07 us (21%)
  Pallas kernels  7.45 us (19%)
  local copies, waits for them, and re-layouts  0.71 us (2%)
    ppermute x6, starting transfers between devices, gather(): lax.ppermute(block, 'expert', other_chip[m])  7.81 us
    ppermute x1, starting transfers between devices, body(): block = lax.ppermute(packed[k], 'expert', pairs)  4.1 us
    ppermute x3, starting transfers between devices, body(): team.append(lax.ppermute(parts[m], 'expert', other_chip[m]))  3.55 us
    ppermute x1, waiting for transfers between devices, body(): others.append(settle(lax.ppermute(totals[k - 1], 'expert', pairs)))  2.6 us
    ppermute x2, starting transfers between devices, body(): own.append(lax.ppermute(parts[m], 'expert', other_chip[m]))  2.49 us
    ppermute x1, starting transfers between devices, body(): others.append(settle(lax.ppermute(totals[k - 1], 'expert', pairs)))  2.4 us
    pallas_call x1, Pallas kernels, expert_half(): pl.pallas_call(functools.partial(expert_kernel, teams), out_shape=[jax.Sh...  2.31 us
    pallas_call x1, Pallas kernels, pack_rows(): pl.pallas_call(functools.partial(pack_kernel, teams), out_shape=[block] *...  2.28 us
  transfers between devices with their start and end apart: 18, of which 10 were waited for; matrix products, arithmetic and copies ran while one was open for 0% of the time, Pallas kernels for 4%

profile of v18, /device:TPU:0, one launch (start us, length us, event | category | flops | bytes accessed | tf_op | source)
XLA Modules:
  0.0 38.5 jit_solution(2110420822377623539)
XLA Ops:
  0.0 2.3 %pack_rows.1 = (bf16[40,896]{1,0:T(8,128)(2,1)}, bf16[40,896]{1,0:T(8,128)(2,1)}, f32[16,64]{1,0:T(8,128)}) custom-call(s32[8,64]{1,0:T(8,128)} %bitcast.2, f32[8,64]{1,0:T(8,128)} %bitcast.3, bf16[64,7168]{1,0:T(8,128)(2,1)} %tokens_hbm.1), custom_call_target="tpu_custom_call" | custom-call | tf_op jit(solution)/shard_map/pack_rows/pallas_call | solution.py:112
  2.3 4.1 %collective-permute-start.3 = (bf16[40,896]{1,0:T(8,128)(2,1)}, bf16[40,896]{1,0:T(8,128)(2,1)S(1)}, u32[]{:S(2)}, u32[]{:S(2)}) collective-permute-start(bf16[40,896]{1,0:T(8,128)(2,1)} %get-tuple-element.34), channel_id=1, source_target_pairs={{0,8},{1,9},{2,10},{3,11},{4,12},{5,13},{6,14},{7,15},{8,0},{9,1},... | collective-permute-start | bytes 215048 | tf_op jit(solution)/shard_map/ppermute | solution.py:459
  6.4 2.5 %collective-permute-start.2 = (bf16[40,896]{1,0:T(8,128)(2,1)}, bf16[40,896]{1,0:T(8,128)(2,1)S(1)}, u32[]{:S(2)}, u32[]{:S(2)}) collective-permute-start(bf16[40,896]{1,0:T(8,128)(2,1)} %get-tuple-element.38.refs_0_), channel_id=1, source_target_pairs={{0,6},{1,7},{2,4},{3,5},{4,2},{5,3},{6,0},{7,1},{8,14},{9,15},{10,... | collective-permute-start | bytes 215048 | tf_op jit(solution)/shard_map/ppermute | solution.py:453
  8.9 0.4 %collective-permute-start.1 = (bf16[40,896]{1,0:T(8,128)(2,1)}, bf16[40,896]{1,0:T(8,128)(2,1)S(1)}, u32[]{:S(2)}, u32[]{:S(2)}) collective-permute-start(bf16[40,896]{1,0:T(8,128)(2,1)} %get-tuple-element.38.refs_0_), channel_id=1, source_target_pairs={{0,4},{1,5},{2,6},{3,7},{4,0},{5,1},{6,2},{7,3},{8,12},{9,13},{10,... | collective-permute-start | bytes 215048 | tf_op jit(solution)/shard_map/ppermute | solution.py:453
  9.4 0.5 %collective-permute-start = (bf16[40,896]{1,0:T(8,128)(2,1)}, bf16[40,896]{1,0:T(8,128)(2,1)S(1)}, u32[]{:S(2)}, u32[]{:S(2)}) collective-permute-start(bf16[40,896]{1,0:T(8,128)(2,1)} %get-tuple-element.38.refs_0_), channel_id=1, source_target_pairs={{0,2},{1,3},{2,0},{3,1},{4,6},{5,7},{6,4},{7,5},{8,10},{9,11},{10,... | collective-permute-start | bytes 215048 | tf_op jit(solution)/shard_map/ppermute | solution.py:453
  9.9 0.0 collective-permute-done.3.refs_0_
  9.9 2.7 %collective-permute-start.7 = (bf16[40,896]{1,0:T(8,128)(2,1)S(1)}, bf16[40,896]{1,0:T(8,128)(2,1)S(1)}, u32[]{:S(2)}, u32[]{:S(2)}) collective-permute-start(bf16[40,896]{1,0:T(8,128)(2,1)S(1)} %collective-permute-done.3.refs_0_), channel_id=1, source_target_pairs={{0,6},{1,7},{2,4},{3,5},{4,2},{5,3},{6,0},{7,1},{8,14},{9,15},{10,... | collective-permute-start | bytes 215048 | tf_op jit(solution)/shard_map/ppermute | solution.py:453
  12.6 0.7 %collective-permute-start.6 = (bf16[40,896]{1,0:T(8,128)(2,1)S(1)}, bf16[40,896]{1,0:T(8,128)(2,1)S(1)}, u32[]{:S(2)}, u32[]{:S(2)}) collective-permute-start(bf16[40,896]{1,0:T(8,128)(2,1)S(1)} %collective-permute-done.3.refs_0_), channel_id=1, source_target_pairs={{0,4},{1,5},{2,6},{3,7},{4,0},{5,1},{6,2},{7,3},{8,12},{9,13},{10,... | collective-permute-start | bytes 215048 | tf_op jit(solution)/shard_map/ppermute | solution.py:453
  13.3 0.0 collective-permute-done.2.refs_3_
  13.3 1.0 %collective-permute-start.5 = (bf16[40,896]{1,0:T(8,128)(2,1)S(1)}, bf16[40,896]{1,0:T(8,128)(2,1)S(1)}, u32[]{:S(2)}, u32[]{:S(2)}) collective-permute-start(bf16[40,896]{1,0:T(8,128)(2,1)S(1)} %collective-permute-done.3.refs_0_), channel_id=1, source_target_pairs={{0,2},{1,3},{2,0},{3,1},{4,6},{5,7},{6,4},{7,5},{8,10},{9,11},{10,... | collective-permute-start | bytes 215048 | tf_op jit(solution)/shard_map/ppermute | solution.py:453
  14.2 0.7 %copy-done.4 = f32[16,64]{1,0:T(8,128)S(1)} copy-done((f32[16,64]{1,0:T(8,128)S(1)}, f32[16,64]{1,0:T(8,128)}, u32[]{:S(2)}) %copy-start.4) | copy-done | bytes 4120
  14.9 0.3 blend_weights.1.weight_ref
  15.2 0.0 collective-permute-done.1.refs_2_
  15.2 0.1 collective-permute-done.refs_1_
  15.3 0.0 copy-done.3
  15.4 0.1 collective-permute-start.4
  15.5 0.4 %collective-permute-done.7.refs_3_ = bf16[40,896]{1,0:T(8,128)(2,1)S(1)} collective-permute-done((bf16[40,896]{1,0:T(8,128)(2,1)S(1)}, bf16[40,896]{1,0:T(8,128)(2,1)S(1)}, u32[]{:S(2)}, u32[]{:S(2)}) %collective-permute-start.7) | collective-permute-done | bytes 71712 | tf_op jit(solution)/shard_map/ppermute | solution.py:453
  15.9 1.0 %collective-permute-done.6.refs_2_ = bf16[40,896]{1,0:T(8,128)(2,1)S(1)} collective-permute-done((bf16[40,896]{1,0:T(8,128)(2,1)S(1)}, bf16[40,896]{1,0:T(8,128)(2,1)S(1)}, u32[]{:S(2)}, u32[]{:S(2)}) %collective-permute-start.6) | collective-permute-done | bytes 71712 | tf_op jit(solution)/shard_map/ppermute | solution.py:453
  16.9 0.7 %collective-permute-done.5.refs_1_ = bf16[40,896]{1,0:T(8,128)(2,1)S(1)} collective-permute-done((bf16[40,896]{1,0:T(8,128)(2,1)S(1)}, bf16[40,896]{1,0:T(8,128)(2,1)S(1)}, u32[]{:S(2)}, u32[]{:S(2)}) %collective-permute-start.5) | collective-permute-done | bytes 71712 | tf_op jit(solution)/shard_map/ppermute | solution.py:453
  17.6 0.1 collective-permute-start.8
  17.7 0.0 collective-permute-done.4.other_ref
  17.7 0.3 unpack.1.first_ref
  18.1 1.2 %collective-permute-done.8.refs_1_ = bf16[160,896]{1,0:T(8,128)(2,1)S(1)} collective-permute-done((bf16[160,896]{1,0:T(8,128)(2,1)S(1)}, bf16[160,896]{1,0:T(8,128)(2,1)S(1)}, u32[]{:S(2)}, u32[]{:S(2)}) %collective-permute-start.8) | collective-permute-done | bytes 286752 | tf_op jit(solution)/shard_map/ppermute | solution.py:470
  19.3 0.0 copy-done
  19.3 0.0 copy-done.1
  19.3 2.3 %expert_half.1 = (bf16[160,896]{1,0:T(8,128)(2,1)S(1)}, bf16[160,896]{1,0:T(8,128)(2,1)S(1)}, bf16[40,256]{1,0:T(8,128)(2,1)S(1)}) custom-call(f32[48,7168]{1,0:T(8,128)S(1)} %unpack.1.first_ref, bf16[160,896]{1,0:T(8,128)(2,1)S(1)} %join.3.refs_0_, bf16[160,896]{1,0:T(8,128)(2,1)S(1)} %collective-permute-done.8.refs_1_, bf16[7168,256]{1,0:T(8,128)(2,1)S(1)} %copy-done.1, ...), custom_call_target="tpu_custom_call" | custom-call | flops 734003200 | bytes 11010048 | tf_op jit(solution)/shard_map/expert_half/pallas_call | solution.py:276
  21.6 0.2 collective-permute-start.9
  21.8 0.4 collective-permute-start.10
  22.2 0.7 %kept_half.1.kept_ref = f32[328,896]{1,0:T(8,128)S(1)} custom-call(bf16[40,256]{1,0:T(8,128)(2,1)S(1)} %get-tuple-element.43.hidden_ref, bf16[256,7168]{1,0:T(8,128)(2,1)S(1)} %copy-done), custom_call_target="tpu_custom_call" | custom-call | flops 146800640 | bytes 3670016 | tf_op jit(solution)/shard_map/kept_half/pallas_call | solution.py:306
  22.9 0.3 collective-permute-done.9.taken_ref
  23.2 0.1 add_cores.2
  23.3 1.8 %collective-permute-start.13 = (bf16[40,896]{1,0:T(8,128)(2,1)S(1)}, bf16[40,896]{1,0:T(8,128)(2,1)S(1)}, u32[]{:S(2)}, u32[]{:S(2)}) collective-permute-start(bf16[40,896]{1,0:T(8,128)(2,1)S(1)} %get-tuple-element.55), channel_id=1, source_target_pairs={{0,6},{1,7},{2,4},{3,5},{4,2},{5,3},{6,0},{7,1},{8,14},{9,15},{10,... | collective-permute-start | bytes 215048 | tf_op jit(solution)/shard_map/ppermute | solution.py:480
  25.0 0.7 %collective-permute-start.14 = (bf16[40,896]{1,0:T(8,128)(2,1)S(1)}, bf16[40,896]{1,0:T(8,128)(2,1)S(1)}, u32[]{:S(2)}, u32[]{:S(2)}) collective-permute-start(bf16[40,896]{1,0:T(8,128)(2,1)S(1)} %get-tuple-element.56), channel_id=1, source_target_pairs={{0,4},{1,5},{2,6},{3,7},{4,0},{5,1},{6,2},{7,3},{8,12},{9,13},{10,... | collective-permute-start | bytes 215048 | tf_op jit(solution)/shard_map/ppermute | solution.py:480
  25.8 1.1 %collective-permute-start.15 = (bf16[40,896]{1,0:T(8,128)(2,1)S(1)}, bf16[40,896]{1,0:T(8,128)(2,1)S(1)}, u32[]{:S(2)}, u32[]{:S(2)}) collective-permute-start(bf16[40,896]{1,0:T(8,128)(2,1)S(1)} %get-tuple-element.57), channel_id=1, source_target_pairs={{0,2},{1,3},{2,0},{3,1},{4,6},{5,7},{6,4},{7,5},{8,10},{9,11},{10,... | collective-permute-start | bytes 215048 | tf_op jit(solution)/shard_map/ppermute | solution.py:480
  26.8 0.0 collective-permute-done.10.taken_ref
  26.9 0.1 add_cores.3
  26.9 1.8 %collective-permute-start.11 = (bf16[40,896]{1,0:T(8,128)(2,1)S(1)}, bf16[40,896]{1,0:T(8,128)(2,1)S(1)}, u32[]{:S(2)}, u32[]{:S(2)}) collective-permute-start(bf16[40,896]{1,0:T(8,128)(2,1)S(1)} %get-tuple-element.52), channel_id=1, source_target_pairs={{0,6},{1,7},{2,4},{3,5},{4,2},{5,3},{6,0},{7,1},{8,14},{9,15},{10,... | collective-permute-start | bytes 215048 | tf_op jit(solution)/shard_map/ppermute | solution.py:490
  28.7 0.7 %collective-permute-start.12 = (bf16[40,896]{1,0:T(8,128)(2,1)S(1)}, bf16[40,896]{1,0:T(8,128)(2,1)S(1)}, u32[]{:S(2)}, u32[]{:S(2)}) collective-permute-start(bf16[40,896]{1,0:T(8,128)(2,1)S(1)} %get-tuple-element.53), channel_id=1, source_target_pairs={{0,4},{1,5},{2,6},{3,7},{4,0},{5,1},{6,2},{7,3},{8,12},{9,13},{10,... | collective-permute-start | bytes 215048 | tf_op jit(solution)/shard_map/ppermute | solution.py:490
  29.4 0.0 collective-permute-done.13.refs_1_
  29.4 0.5 %collective-permute-done.14.refs_2_ = bf16[40,896]{1,0:T(8,128)(2,1)S(1)} collective-permute-done((bf16[40,896]{1,0:T(8,128)(2,1)S(1)}, bf16[40,896]{1,0:T(8,128)(2,1)S(1)}, u32[]{:S(2)}, u32[]{:S(2)}) %collective-permute-start.14) | collective-permute-done | bytes 71712 | tf_op jit(solution)/shard_map/ppermute | solution.py:480
  29.9 0.6 %collective-permute-done.15.refs_3_ = bf16[40,896]{1,0:T(8,128)(2,1)S(1)} collective-permute-done((bf16[40,896]{1,0:T(8,128)(2,1)S(1)}, bf16[40,896]{1,0:T(8,128)(2,1)S(1)}, u32[]{:S(2)}, u32[]{:S(2)}) %collective-permute-start.15) | collective-permute-done | bytes 71712 | tf_op jit(solution)/shard_map/ppermute | solution.py:480
  30.6 2.4 %collective-permute-start.17 = (bf16[40,896]{1,0:T(8,128)(2,1)S(1)}, bf16[40,896]{1,0:T(8,128)(2,1)S(1)}, u32[]{:S(2)}, u32[]{:S(2)}) collective-permute-start(bf16[40,896]{1,0:T(8,128)(2,1)S(1)} %sum_blocks.1), channel_id=1, source_target_pairs={{0,8},{1,9},{2,10},{3,11},{4,12},{5,13},{6,14},{7,15},{8,0},{9,1},... | collective-permute-start | bytes 215048 | tf_op jit(solution)/shard_map/ppermute | solution.py:487
  33.0 1.1 %collective-permute-start.16 = (bf16[40,896]{1,0:T(8,128)(2,1)S(1)}, bf16[40,896]{1,0:T(8,128)(2,1)S(1)}, u32[]{:S(2)}, u32[]{:S(2)}) collective-permute-start(bf16[40,896]{1,0:T(8,128)(2,1)S(1)} %get-tuple-element.59), channel_id=1, source_target_pairs={{0,2},{1,3},{2,0},{3,1},{4,6},{5,7},{6,4},{7,5},{8,10},{9,11},{10,... | collective-permute-start | bytes 215048 | tf_op jit(solution)/shard_map/ppermute | solution.py:491
  34.1 0.0 collective-permute-done.11.refs_1_
  34.1 0.0 collective-permute-done.12.refs_2_
  34.1 2.6 %collective-permute-done.17.block_ref = bf16[40,896]{1,0:T(8,128)(2,1)S(1)} collective-permute-done((bf16[40,896]{1,0:T(8,128)(2,1)S(1)}, bf16[40,896]{1,0:T(8,128)(2,1)S(1)}, u32[]{:S(2)}, u32[]{:S(2)}) %collective-permute-start.17) | collective-permute-done | bytes 71712 | tf_op jit(solution)/shard_map/ppermute | solution.py:487
  36.7 0.6 %collective-permute-done.16.refs_1_ = bf16[40,896]{1,0:T(8,128)(2,1)S(1)} collective-permute-done((bf16[40,896]{1,0:T(8,128)(2,1)S(1)}, bf16[40,896]{1,0:T(8,128)(2,1)S(1)}, u32[]{:S(2)}, u32[]{:S(2)}) %collective-permute-start.16) | collective-permute-done | bytes 71712 | tf_op jit(solution)/shard_map/ppermute | solution.py:491
  37.3 1.2 %blend.1 = bf16[64,7168]{1,0:T(8,128)(2,1)} custom-call(bf16[512,200]{1,0:T(8,128)(2,1)S(1)} %blend_weights.1.weight_ref, f32[40,896]{1,0:T(8,128)S(1)} %partial_sum.1.refs_0_, bf16[40,896]{1,0:T(8,128)(2,1)S(1)} %collective-permute-done.16.refs_1_, f32[40,896]{1,0:T(8,128)S(1)} %settle.1.refs_2_), custom_call_target="tpu_custom_call" | custom-call | tf_op jit(solution)/shard_map/blend/pallas_call | solution.py:431
  (11 shorter events, 0.1 us)
Async XLA Ops:
  2.3 7.6 %collective-permute-start.3 = (bf16[40,896]{1,0:T(8,128)(2,1)}, bf16[40,896]{1,0:T(8,128)(2,1)S(1)}, u32[]{:S(2)}, u32[]{:S(2)}) collective-permute-start(bf16[40,896]{1,0:T(8,128)(2,1)} %get-tuple-element.34), channel_id=1, source_target_pairs={{0,8},{1,9},{2,10},{3,11},{4,12},{5,13},{6,14},{7,15},{8,0},{9,1},... | collective-permute-start | bytes 215048 | tf_op jit(solution)/shard_map/ppermute | solution.py:459
  6.4 6.9 %collective-permute-start.2 = (bf16[40,896]{1,0:T(8,128)(2,1)}, bf16[40,896]{1,0:T(8,128)(2,1)S(1)}, u32[]{:S(2)}, u32[]{:S(2)}) collective-permute-start(bf16[40,896]{1,0:T(8,128)(2,1)} %get-tuple-element.38.refs_0_), channel_id=1, source_target_pairs={{0,6},{1,7},{2,4},{3,5},{4,2},{5,3},{6,0},{7,1},{8,14},{9,15},{10,... | collective-permute-start | bytes 215048 | tf_op jit(solution)/shard_map/ppermute | solution.py:453
  8.9 6.3 %collective-permute-start.1 = (bf16[40,896]{1,0:T(8,128)(2,1)}, bf16[40,896]{1,0:T(8,128)(2,1)S(1)}, u32[]{:S(2)}, u32[]{:S(2)}) collective-permute-start(bf16[40,896]{1,0:T(8,128)(2,1)} %get-tuple-element.38.refs_0_), channel_id=1, source_target_pairs={{0,4},{1,5},{2,6},{3,7},{4,0},{5,1},{6,2},{7,3},{8,12},{9,13},{10,... | collective-permute-start | bytes 215048 | tf_op jit(solution)/shard_map/ppermute | solution.py:453
  9.4 6.0 %collective-permute-start = (bf16[40,896]{1,0:T(8,128)(2,1)}, bf16[40,896]{1,0:T(8,128)(2,1)S(1)}, u32[]{:S(2)}, u32[]{:S(2)}) collective-permute-start(bf16[40,896]{1,0:T(8,128)(2,1)} %get-tuple-element.38.refs_0_), channel_id=1, source_target_pairs={{0,2},{1,3},{2,0},{3,1},{4,6},{5,7},{6,4},{7,5},{8,10},{9,11},{10,... | collective-permute-start | bytes 215048 | tf_op jit(solution)/shard_map/ppermute | solution.py:453
  9.9 5.5 %copy-start.3 = (bf16[40,896]{1,0:T(8,128)(2,1)S(1)}, bf16[40,896]{1,0:T(8,128)(2,1)}, u32[]{:S(2)}) copy-start(bf16[40,896]{1,0:T(8,128)(2,1)} %get-tuple-element.38.refs_0_) | copy-start | bytes 215044
  9.9 6.0 %collective-permute-start.7 = (bf16[40,896]{1,0:T(8,128)(2,1)S(1)}, bf16[40,896]{1,0:T(8,128)(2,1)S(1)}, u32[]{:S(2)}, u32[]{:S(2)}) collective-permute-start(bf16[40,896]{1,0:T(8,128)(2,1)S(1)} %collective-permute-done.3.refs_0_), channel_id=1, source_target_pairs={{0,6},{1,7},{2,4},{3,5},{4,2},{5,3},{6,0},{7,1},{8,14},{9,15},{10,... | collective-permute-start | bytes 215048 | tf_op jit(solution)/shard_map/ppermute | solution.py:453
  12.6 4.3 %collective-permute-start.6 = (bf16[40,896]{1,0:T(8,128)(2,1)S(1)}, bf16[40,896]{1,0:T(8,128)(2,1)S(1)}, u32[]{:S(2)}, u32[]{:S(2)}) collective-permute-start(bf16[40,896]{1,0:T(8,128)(2,1)S(1)} %collective-permute-done.3.refs_0_), channel_id=1, source_target_pairs={{0,4},{1,5},{2,6},{3,7},{4,0},{5,1},{6,2},{7,3},{8,12},{9,13},{10,... | collective-permute-start | bytes 215048 | tf_op jit(solution)/shard_map/ppermute | solution.py:453
  13.3 4.3 %collective-permute-start.5 = (bf16[40,896]{1,0:T(8,128)(2,1)S(1)}, bf16[40,896]{1,0:T(8,128)(2,1)S(1)}, u32[]{:S(2)}, u32[]{:S(2)}) collective-permute-start(bf16[40,896]{1,0:T(8,128)(2,1)S(1)} %collective-permute-done.3.refs_0_), channel_id=1, source_target_pairs={{0,2},{1,3},{2,0},{3,1},{4,6},{5,7},{6,4},{7,5},{8,10},{9,11},{10,... | collective-permute-start | bytes 215048 | tf_op jit(solution)/shard_map/ppermute | solution.py:453
  14.2 0.7 %copy-start.4 = (f32[16,64]{1,0:T(8,128)S(1)}, f32[16,64]{1,0:T(8,128)}, u32[]{:S(2)}) copy-start(f32[16,64]{1,0:T(8,128)} %get-tuple-element.36.table_ref) | copy-start | bytes 12292
  14.9 4.3 %copy-start = (bf16[256,7168]{1,0:T(8,128)(2,1)S(1)}, bf16[256,7168]{1,0:T(8,128)(2,1)}, u32[]{:S(2)}) copy-start(bf16[256,7168]{1,0:T(8,128)(2,1)} %down_ref.1) | copy-start | bytes 11010052
  14.9 4.3 %copy-start.1 = (bf16[7168,256]{1,0:T(8,128)(2,1)S(1)}, bf16[7168,256]{1,0:T(8,128)(2,1)}, u32[]{:S(2)}) copy-start(bf16[7168,256]{1,0:T(8,128)(2,1)} %refs_2_.1) | copy-start | bytes 11010052
  14.9 4.3 %copy-start.2 = (bf16[7168,256]{1,0:T(8,128)(2,1)S(1)}, bf16[7168,256]{1,0:T(8,128)(2,1)}, u32[]{:S(2)}) copy-start(bf16[7168,256]{1,0:T(8,128)(2,1)} %refs_3_.1) | copy-start | bytes 11010052
  15.4 2.3 %collective-permute-start.4 = (bf16[160,896]{1,0:T(8,128)(2,1)S(1)}, bf16[160,896]{1,0:T(8,128)(2,1)S(1)}, u32[]{:S(2)}, u32[]{:S(2)}) collective-permute-start(bf16[160,896]{1,0:T(8,128)(2,1)S(1)} %join.2.own_ref), channel_id=1, source_target_pairs={{0,1},{1,0},{2,3},{3,2},{4,5},{5,4},{6,7},{7,6},{8,9},{9,8},{10,11... | collective-permute-start | bytes 860168 | tf_op jit(solution)/shard_map/ppermute | solution.py:466
  17.6 1.6 %collective-permute-start.8 = (bf16[160,896]{1,0:T(8,128)(2,1)S(1)}, bf16[160,896]{1,0:T(8,128)(2,1)S(1)}, u32[]{:S(2)}, u32[]{:S(2)}) collective-permute-start(bf16[160,896]{1,0:T(8,128)(2,1)S(1)} %join.3.refs_0_), channel_id=1, source_target_pairs={{0,1},{1,0},{2,3},{3,2},{4,5},{5,4},{6,7},{7,6},{8,9},{9,8},{10,11... | collective-permute-start | bytes 860168 | tf_op jit(solution)/shard_map/ppermute | solution.py:470
  21.6 1.6 %collective-permute-start.9 = (bf16[160,896]{1,0:T(8,128)(2,1)S(1)}, bf16[160,896]{1,0:T(8,128)(2,1)S(1)}, u32[]{:S(2)}, u32[]{:S(2)}) collective-permute-start(bf16[160,896]{1,0:T(8,128)(2,1)S(1)} %get-tuple-element.44), channel_id=1, source_target_pairs={{0,1},{1,0},{2,3},{3,2},{4,5},{5,4},{6,7},{7,6},{8,9},{9,8},{10,11... | collective-permute-start | bytes 860168 | tf_op jit(solution)/shard_map/ppermute | solution.py:472
  21.8 5.1 %collective-permute-start.10 = (bf16[160,896]{1,0:T(8,128)(2,1)S(1)}, bf16[160,896]{1,0:T(8,128)(2,1)S(1)}, u32[]{:S(2)}, u32[]{:S(2)}) collective-permute-start(bf16[160,896]{1,0:T(8,128)(2,1)S(1)} %get-tuple-element.50), channel_id=1, source_target_pairs={{0,1},{1,0},{2,3},{3,2},{4,5},{5,4},{6,7},{7,6},{8,9},{9,8},{10,11... | collective-permute-start | bytes 860168 | tf_op jit(solution)/shard_map/ppermute | solution.py:472
  23.3 6.1 %collective-permute-start.13 = (bf16[40,896]{1,0:T(8,128)(2,1)S(1)}, bf16[40,896]{1,0:T(8,128)(2,1)S(1)}, u32[]{:S(2)}, u32[]{:S(2)}) collective-permute-start(bf16[40,896]{1,0:T(8,128)(2,1)S(1)} %get-tuple-element.55), channel_id=1, source_target_pairs={{0,6},{1,7},{2,4},{3,5},{4,2},{5,3},{6,0},{7,1},{8,14},{9,15},{10,... | collective-permute-start | bytes 215048 | tf_op jit(solution)/shard_map/ppermute | solution.py:480
  25.0 4.9 %collective-permute-start.14 = (bf16[40,896]{1,0:T(8,128)(2,1)S(1)}, bf16[40,896]{1,0:T(8,128)(2,1)S(1)}, u32[]{:S(2)}, u32[]{:S(2)}) collective-permute-start(bf16[40,896]{1,0:T(8,128)(2,1)S(1)} %get-tuple-element.56), channel_id=1, source_target_pairs={{0,4},{1,5},{2,6},{3,7},{4,0},{5,1},{6,2},{7,3},{8,12},{9,13},{10,... | collective-permute-start | bytes 215048 | tf_op jit(solution)/shard_map/ppermute | solution.py:480
  25.8 4.7 %collective-permute-start.15 = (bf16[40,896]{1,0:T(8,128)(2,1)S(1)}, bf16[40,896]{1,0:T(8,128)(2,1)S(1)}, u32[]{:S(2)}, u32[]{:S(2)}) collective-permute-start(bf16[40,896]{1,0:T(8,128)(2,1)S(1)} %get-tuple-element.57), channel_id=1, source_target_pairs={{0,2},{1,3},{2,0},{3,1},{4,6},{5,7},{6,4},{7,5},{8,10},{9,11},{10,... | collective-permute-start | bytes 215048 | tf_op jit(solution)/shard_map/ppermute | solution.py:480
  26.9 7.2 %collective-permute-start.11 = (bf16[40,896]{1,0:T(8,128)(2,1)S(1)}, bf16[40,896]{1,0:T(8,128)(2,1)S(1)}, u32[]{:S(2)}, u32[]{:S(2)}) collective-permute-start(bf16[40,896]{1,0:T(8,128)(2,1)S(1)} %get-tuple-element.52), channel_id=1, source_target_pairs={{0,6},{1,7},{2,4},{3,5},{4,2},{5,3},{6,0},{7,1},{8,14},{9,15},{10,... | collective-permute-start | bytes 215048 | tf_op jit(solution)/shard_map/ppermute | solution.py:490
  28.7 5.4 %collective-permute-start.12 = (bf16[40,896]{1,0:T(8,128)(2,1)S(1)}, bf16[40,896]{1,0:T(8,128)(2,1)S(1)}, u32[]{:S(2)}, u32[]{:S(2)}) collective-permute-start(bf16[40,896]{1,0:T(8,128)(2,1)S(1)} %get-tuple-element.53), channel_id=1, source_target_pairs={{0,4},{1,5},{2,6},{3,7},{4,0},{5,1},{6,2},{7,3},{8,12},{9,13},{10,... | collective-permute-start | bytes 215048 | tf_op jit(solution)/shard_map/ppermute | solution.py:490
  30.6 6.2 %collective-permute-start.17 = (bf16[40,896]{1,0:T(8,128)(2,1)S(1)}, bf16[40,896]{1,0:T(8,128)(2,1)S(1)}, u32[]{:S(2)}, u32[]{:S(2)}) collective-permute-start(bf16[40,896]{1,0:T(8,128)(2,1)S(1)} %sum_blocks.1), channel_id=1, source_target_pairs={{0,8},{1,9},{2,10},{3,11},{4,12},{5,13},{6,14},{7,15},{8,0},{9,1},... | collective-permute-start | bytes 215048 | tf_op jit(solution)/shard_map/ppermute | solution.py:487
  33.0 4.3 %collective-permute-start.16 = (bf16[40,896]{1,0:T(8,128)(2,1)S(1)}, bf16[40,896]{1,0:T(8,128)(2,1)S(1)}, u32[]{:S(2)}, u32[]{:S(2)}) collective-permute-start(bf16[40,896]{1,0:T(8,128)(2,1)S(1)} %get-tuple-element.59), channel_id=1, source_target_pairs={{0,2},{1,3},{2,0},{3,1},{4,6},{5,7},{6,4},{7,5},{8,10},{9,11},{10,... | collective-permute-start | bytes 215048 | tf_op jit(solution)/shard_map/ppermute | solution.py:491
